TPU v7x, 32 devices: a whole 2x2x4 slice. The times are simulated.
32 devices in a mesh: rows: 8 (over z, y), filt: 4 (over x, core).
Axes of the slice: x: 2, y: 2, z: 4, core: 2. Of those that a mesh axis runs over, the one named last changes fastest.
Arguments:
- features: bfloat16 [512, 8, 512], P('filt', 'rows'), may hold values from -6 to 6
- first_weight: bfloat16 [512, 3, 3, 512], P('filt'), may hold values from -0.09375 to 0.09375
- second_weight: bfloat16 [512, 3, 3, 512], P('filt'), may hold values from -0.09375 to 0.09375
- out_grad: bfloat16 [512, 8, 512], P('filt', 'rows'), may hold values from -0.09375 to 0.09375
Outputs:
- block_out: bfloat16 [512, 8, 512], P('filt', 'rows')
- first_grad: float32 [512, 3, 3, 512], P('filt')
- second_grad: float32 [512, 3, 3, 512], P('filt')
All inputs are finite; a program needn't handle non-finite values.
Results may differ from a plain program's by a relative error of at most 0.024.
The roundings to bfloat16 on the way count: a program that leaves them out, or rounds other values in their place, can miss the bound.
Values may be sent and summed in bfloat16 or wider, within the bound.
No kernel may reach another device: no remote copies, remote signals or barrier semaphores. Data moves between devices by JAX's collectives and lax.ppermute only.
A program may use at most 64 MiB of HBM per device.

v0:
```python
import jax
import jax.numpy as jnp
from jax import lax
from jax.sharding import PartitionSpec as P


def extended(cells, sides, width):
    for axis, dim in sides:
        count = lax.axis_size(axis)
        ends = count - 1
        head = lax.slice_in_dim(cells, 0, width, axis=dim)
        tail = lax.slice_in_dim(cells, cells.shape[dim] - width, cells.shape[dim], axis=dim)
        cells = jnp.concatenate(
            [
                lax.ppermute(tail, axis, [(i, (i + 1) % count) for i in range(ends)]),
                cells,
                lax.ppermute(head, axis, [((i + 1) % count, i) for i in range(ends)]),
            ],
            axis=dim,
        )
    return cells


def shift_cols(value, offset):
    if offset == 0:
        return value
    if offset > 0:
        return jnp.pad(value[..., offset:], ((0, 0), (0, 0), (0, offset)))
    return jnp.pad(value[..., :offset], ((0, 0), (0, 0), (-offset, 0)))


def conv_forward(weight, padded, count):
    total = jnp.zeros((weight.shape[0], count, padded.shape[2]), jnp.float32)
    for a in range(3):
        for b in range(3):
            part = jnp.einsum(
                "oi,ihw->ohw",
                weight[:, a, b, :],
                padded[:, a : a + count, :],
                preferred_element_type=jnp.float32,
            )
            total = total + shift_cols(part, b - 1)
    return total


def conv_backward(weight, padded, count):
    total = jnp.zeros((weight.shape[3], count, padded.shape[2]), jnp.float32)
    for a in range(3):
        for b in range(3):
            part = jnp.einsum(
                "oi,ohw->ihw",
                weight[:, a, b, :],
                padded[:, 2 - a : 2 - a + count, :],
                preferred_element_type=jnp.float32,
            )
            total = total + shift_cols(part, 1 - b)
    return total


def weight_terms(grad, padded, count):
    rows_out = []
    for a in range(3):
        cols_out = []
        for b in range(3):
            moved = shift_cols(grad, 1 - b)
            cols_out.append(
                jnp.einsum(
                    "ohw,ihw->oi",
                    moved,
                    padded[:, a : a + count, :],
                    preferred_element_type=jnp.float32,
                )
            )
        rows_out.append(jnp.stack(cols_out, axis=1))
    return jnp.stack(rows_out, axis=1)


def with_rims(value):
    return extended(value, (("rows", 1),), 1)


def all_channels(value):
    return lax.all_gather(with_rims(value), "filt", axis=0, tiled=True)


def per_device(features, first_weight, second_weight, out_grad):
    count = features.shape[1]
    padded_in = all_channels(features)
    pre_first = conv_forward(first_weight, padded_in, count)
    hidden = jnp.maximum(pre_first, 0.0).astype(jnp.bfloat16)
    padded_hidden = all_channels(hidden)
    pre_second = conv_forward(second_weight, padded_hidden, count) + features.astype(jnp.float32)
    block_out = jnp.maximum(pre_second, 0.0).astype(jnp.bfloat16)
    grad_second = jnp.where(pre_second > 0, out_grad.astype(jnp.float32), 0.0).astype(jnp.bfloat16)
    rimmed_grad = with_rims(grad_second)
    terms = conv_backward(second_weight, rimmed_grad, count)
    hidden_grad = lax.psum_scatter(terms, "filt", scatter_dimension=0, tiled=True)
    grad_first = jnp.where(pre_first > 0, hidden_grad, 0.0).astype(jnp.bfloat16)
    second_local = weight_terms(grad_second, padded_hidden, count)
    first_local = weight_terms(grad_first, padded_in, count)
    first_grad, second_grad = lax.psum((first_local, second_local), "rows")
    return (block_out, first_grad, second_grad)


def solution(mesh):
    in_specs = (
        P("filt", "rows", None),
        P("filt", None, None, None),
        P("filt", None, None, None),
        P("filt", "rows", None),
    )
    out_specs = (P("filt", "rows", None), P("filt", None, None, None), P("filt", None, None, None))
    return jax.shard_map(
        per_device, mesh=mesh, in_specs=in_specs, out_specs=out_specs, check_vma=False
    )
```

profile of v0, /device:TPU:0, one launch (start us, length us, event | category | flops | bytes accessed | tf_op | source)
XLA Modules:
  0.0 317.7 jit_solution(16708447323217496402)
XLA Ops:
  7.2 4.9 %collective-permute-start = (bf16[128,1,512]{2,0,1:T(8,128)(2,1)}, bf16[128,1,512]{2,0,1:T(8,128)(2,1)S(1)}, u32[]{:S(2)}, u32[]{:S(2)}) collective-permute-start(bf16[128,1,512]{2,0,1:T(8,128)(2,1)} %param.4), channel_id=1, source_target_pairs={{0,4},{4,8},{8,12},{12,16},{16,20},{20,24},{24,28},{1,5},{5,9},{9,... | collective-permute-start | bytes 393224 | tf_op jit(solution)/shard_map/ppermute | solution.py:15
  12.1 1.3 collective-permute-start.1
  13.4 1.7 collective-permute-done
  15.1 4.0 %collective-permute-done.1 = bf16[128,1,512]{2,0,1:T(8,128)(2,1)S(1)} collective-permute-done((bf16[128,1,512]{2,0,1:T(8,128)(2,1)}, bf16[128,1,512]{2,0,1:T(8,128)(2,1)S(1)}, u32[]{:S(2)}, u32[]{:S(2)}) %collective-permute-start.1) | collective-permute-done | bytes 131104 | tf_op jit(solution)/shard_map/ppermute | solution.py:17
  19.2 1.7 pad_maximum_fusion.2
  20.9 20.9 %all-gather.3.cloned.1.call-done = bf16[512,3,512]{2,0,1:T(8,128)(2,1)} async-done(((bf16[128,3,512]{2,0,1:T(8,128)(2,1)}), bf16[512,3,512]{2,0,1:T(8,128)(2,1)}) %all-gather.3.cloned.1.call-update) | async-done | bytes 1572880 | tf_op jit(solution)/shard_map/all_gather | solution.py:83
  41.8 1.5 convolution_bitcast_fusion.42
  43.4 1.4 convolution_bitcast_fusion.39
  44.8 1.2 convolution_bitcast_fusion.36
  46.1 1.2 convolution_bitcast_fusion.38
  47.3 1.2 convolution_bitcast_fusion.41
  48.6 1.2 convolution_bitcast_fusion.44
  49.8 1.2 convolution_bitcast_fusion.37
  51.1 1.2 convolution_bitcast_fusion.40
  52.3 1.3 maximum_convert_fusion.1
  53.7 3.4 %collective-permute-start.2 = (bf16[128,1,512]{0,2,1:T(8,128)(2,1)S(1)}, bf16[128,1,512]{0,2,1:T(8,128)(2,1)S(1)}, u32[]{:S(2)}, u32[]{:S(2)}) collective-permute-start(bf16[128,1,512]{0,2,1:T(8,128)(2,1)S(1)} %get-tuple-element.12), channel_id=1, source_target_pairs={{0,4},{4,8},{8,12},{12,16},{16,20},{20,24},{24,28},{1,5},{5,9},{9,... | collective-permute-start | bytes 393224 | tf_op jit(solution)/shard_map/ppermute | solution.py:15
  57.1 1.3 collective-permute-start.3
  58.4 1.8 collective-permute-done.2
  60.2 4.1 %collective-permute-done.3 = bf16[128,1,512]{0,2,1:T(8,128)(2,1)S(1)} collective-permute-done((bf16[128,1,512]{0,2,1:T(8,128)(2,1)S(1)}, bf16[128,1,512]{0,2,1:T(8,128)(2,1)S(1)}, u32[]{:S(2)}, u32[]{:S(2)}) %collective-permute-start.3) | collective-permute-done | bytes 131104 | tf_op jit(solution)/shard_map/ppermute | solution.py:17
  64.3 0.8 pad_maximum_fusion.3
  65.3 0.8 copy.8
  66.1 19.0 %all-gather.5.cloned.1.call-done = bf16[512,3,512]{0,2,1:T(8,128)(2,1)} async-done(((bf16[128,3,512]{0,2,1:T(8,128)(2,1)}), bf16[512,3,512]{0,2,1:T(8,128)(2,1)}) %all-gather.5.cloned.1.call-update) | async-done | bytes 1572880 | tf_op jit(solution)/shard_map/all_gather | solution.py:83
  85.1 1.5 convolution_bitcast_fusion.33
  86.6 1.5 convolution_bitcast_fusion.30
  88.1 1.2 convolution_bitcast_fusion.27
  89.4 0.3 convolution_bitcast_fusion.29
  89.7 0.3 convolution_bitcast_fusion.32
  90.0 0.3 convolution_bitcast_fusion.35
  90.3 0.3 convolution_bitcast_fusion.28
  90.6 0.3 convolution_bitcast_fusion.31
  90.9 1.0 maximum_convert_fusion
  91.9 1.3 collective-permute-start.4
  93.2 4.6 %collective-permute-start.5 = (bf16[128,1,512]{0,2,1:T(8,128)(2,1)S(1)}, bf16[128,1,512]{0,2,1:T(8,128)(2,1)S(1)}, u32[]{:S(2)}, u32[]{:S(2)}) collective-permute-start(bf16[128,1,512]{0,2,1:T(8,128)(2,1)S(1)} %select_convert_fusion.1), channel_id=1, source_target_pairs={{0,4},{4,8},{8,12},{12,16},{16,20},{20,24},{24,28},{1,5},{5,9},{9,... | collective-permute-start | bytes 393224 | tf_op jit(solution)/shard_map/ppermute | solution.py:15
  97.8 0.3 convolution_bitcast_fusion.5
  98.1 0.3 convolution_bitcast_fusion.3
  98.3 0.3 convolution_bitcast_fusion.4
  98.7 0.7 collective-permute-done.4
  99.5 0.3 convolution_bitcast_fusion.8
  99.9 2.3 collective-permute-done.5
  102.2 0.3 convolution_bitcast_fusion.2
  102.6 0.3 convolution_bitcast_fusion
  102.8 0.3 convolution_bitcast_fusion.6
  103.1 0.3 convolution_bitcast_fusion.7
  103.4 1.6 fusion.1
  105.4 0.3 convolution_bitcast_fusion.9
  106.5 0.3 convolution_bitcast_fusion.15
  107.7 1.6 pad_maximum_fusion.1
  109.3 21.2 %reduce-scatter.2.cloned.1.call-done = f32[128,1,512]{0,2,1:T(8,128)} async-done(((f32[512,1,512]{0,2,1:T(8,128)}), f32[128,1,512]{0,2,1:T(8,128)}) %reduce-scatter.2.cloned.1.call-update) | async-done | bytes 262160 | tf_op jit(solution)/shard_map/reduce_scatter | solution.py:97
  130.5 1.0 select_convert_fusion
  131.5 0.3 convolution_bitcast_fusion.19
  131.8 0.3 convolution_bitcast_fusion.20
  132.1 0.3 convolution_bitcast_fusion.18
  132.5 0.3 convolution_bitcast_fusion.21
  132.8 0.3 convolution_bitcast_fusion.23
  133.2 0.3 convolution_bitcast_fusion.24
  133.5 0.3 convolution_bitcast_fusion.26
  133.8 0.3 convolution_bitcast_fusion.22
  134.1 0.3 convolution_bitcast_fusion.25
  134.6 1.6 pad_maximum_fusion
  136.2 0.9 copy-done.4
  137.1 0.8 copy.9
  137.9 168.5 %all-reduce.25.cloned.1.call-done = (f32[128,3,3,512]{3,0,2,1:T(8,128)}, f32[128,3,3,512]{3,0,2,1:T(8,128)}) async-done(((f32[128,3,3,512]{3,0,2,1:T(8,128)}, f32[128,3,3,512]{3,0,2,1:T(8,128)}), (f32[128,3,3,512]{3,0,2,1:T(8,128)}, f32[128,3,3,512]{3,0,2,1:T(8,128)})) %all-reduce.25.cloned.1.call-update) | async-done | bytes 4718608 | tf_op jit(solution)/shard_map/psum | solution.py:101
  306.3 3.4 %copy.12 = f32[128,3,3,512]{3,0,2,1:T(8,128)} copy(f32[128,3,3,512]{3,0,2,1:T(8,128)} %get-tuple-element.21) | data formatting | bytes 4718592
  309.8 1.4 copy.13
  (47 shorter events, 3.1 us)
Async XLA Ops:
  7.2 34.7 %all-gather.3.cloned.1.call-start = ((), (), s32[]{:S(2)}) async-start(), calls=%async_computation.1 | async-start | bytes 1966080 | tf_op jit(solution)/shard_map/all_gather | solution.py:83
  7.2 7.9 %collective-permute-start = (bf16[128,1,512]{2,0,1:T(8,128)(2,1)}, bf16[128,1,512]{2,0,1:T(8,128)(2,1)S(1)}, u32[]{:S(2)}, u32[]{:S(2)}) collective-permute-start(bf16[128,1,512]{2,0,1:T(8,128)(2,1)} %param.4), channel_id=1, source_target_pairs={{0,4},{4,8},{8,12},{12,16},{16,20},{20,24},{24,28},{1,5},{5,9},{9,... | collective-permute-start | bytes 393224 | tf_op jit(solution)/shard_map/ppermute | solution.py:15
  12.1 7.1 %collective-permute-start.1 = (bf16[128,1,512]{2,0,1:T(8,128)(2,1)}, bf16[128,1,512]{2,0,1:T(8,128)(2,1)S(1)}, u32[]{:S(2)}, u32[]{:S(2)}) collective-permute-start(bf16[128,1,512]{2,0,1:T(8,128)(2,1)} %param.4), channel_id=1, source_target_pairs={{4,0},{8,4},{12,8},{16,12},{20,16},{24,20},{28,24},{5,1},{9,5},{13... | collective-permute-start | bytes 393224 | tf_op jit(solution)/shard_map/ppermute | solution.py:17
  20.9 64.2 %all-gather.5.cloned.1.call-start = ((), (), s32[]{:S(2)}) async-start(), calls=%async_computation.2 | async-start | bytes 1966080 | tf_op jit(solution)/shard_map/all_gather | solution.py:83
  41.8 3.0 copy-start
  52.3 12.9 %copy-start.5 = (bf16[128,1,512]{2,0,1:T(8,128)(2,1)S(1)}, bf16[128,1,512]{2,0,1:T(8,128)(2,1)}, u32[]{:S(2)}) copy-start(bf16[128,1,512]{2,0,1:T(8,128)(2,1)} %param.4) | copy-start | bytes 393220
  52.3 13.0 %copy-start.7 = (bf16[128,1,512]{2,0,1:T(8,128)(2,1)S(1)}, bf16[128,1,512]{2,0,1:T(8,128)(2,1)}, u32[]{:S(2)}) copy-start(bf16[128,1,512]{2,0,1:T(8,128)(2,1)} %param.7) | copy-start | bytes 393220
  53.7 6.5 %collective-permute-start.2 = (bf16[128,1,512]{0,2,1:T(8,128)(2,1)S(1)}, bf16[128,1,512]{0,2,1:T(8,128)(2,1)S(1)}, u32[]{:S(2)}, u32[]{:S(2)}) collective-permute-start(bf16[128,1,512]{0,2,1:T(8,128)(2,1)S(1)} %get-tuple-element.12), channel_id=1, source_target_pairs={{0,4},{4,8},{8,12},{12,16},{16,20},{20,24},{24,28},{1,5},{5,9},{9,... | collective-permute-start | bytes 393224 | tf_op jit(solution)/shard_map/ppermute | solution.py:15
  57.1 7.2 %collective-permute-start.3 = (bf16[128,1,512]{0,2,1:T(8,128)(2,1)S(1)}, bf16[128,1,512]{0,2,1:T(8,128)(2,1)S(1)}, u32[]{:S(2)}, u32[]{:S(2)}) collective-permute-start(bf16[128,1,512]{0,2,1:T(8,128)(2,1)S(1)} %get-tuple-element.12), channel_id=1, source_target_pairs={{4,0},{8,4},{12,8},{16,12},{20,16},{24,20},{28,24},{5,1},{9,5},{13... | collective-permute-start | bytes 393224 | tf_op jit(solution)/shard_map/ppermute | solution.py:17
  65.1 65.3 %reduce-scatter.2.cloned.1.call-start = ((), (), s32[]{:S(2)}) async-start(), calls=%async_computation.3 | async-start | bytes 1310720 | tf_op jit(solution)/shard_map/reduce_scatter | solution.py:97
  85.1 3.0 copy-start.1
  86.6 2.7 copy-start.3
  90.9 1.0 copy-start.6
  91.9 7.6 %collective-permute-start.4 = (bf16[128,1,512]{0,2,1:T(8,128)(2,1)S(1)}, bf16[128,1,512]{0,2,1:T(8,128)(2,1)S(1)}, u32[]{:S(2)}, u32[]{:S(2)}) collective-permute-start(bf16[128,1,512]{0,2,1:T(8,128)(2,1)S(1)} %select_convert_fusion.1), channel_id=1, source_target_pairs={{4,0},{8,4},{12,8},{16,12},{20,16},{24,20},{28,24},{5,1},{9,5},{13... | collective-permute-start | bytes 393224 | tf_op jit(solution)/shard_map/ppermute | solution.py:17
  93.2 9.0 %collective-permute-start.5 = (bf16[128,1,512]{0,2,1:T(8,128)(2,1)S(1)}, bf16[128,1,512]{0,2,1:T(8,128)(2,1)S(1)}, u32[]{:S(2)}, u32[]{:S(2)}) collective-permute-start(bf16[128,1,512]{0,2,1:T(8,128)(2,1)S(1)} %select_convert_fusion.1), channel_id=1, source_target_pairs={{0,4},{4,8},{8,12},{12,16},{16,20},{20,24},{24,28},{1,5},{5,9},{9,... | collective-permute-start | bytes 393224 | tf_op jit(solution)/shard_map/ppermute | solution.py:15
  105.0 201.3 %all-reduce.25.cloned.1.call-start = ((), (), s32[]{:S(2)}) async-start(), calls=%async_computation.4 | async-start | bytes 9437184 | tf_op jit(solution)/shard_map/psum | solution.py:101
  136.2 0.9 copy-start.4
  306.3 3.4 %copy-start.2 = (f32[128,3,3,512]{3,0,2,1:T(8,128)S(1)}, f32[128,3,3,512]{3,0,2,1:T(8,128)}, u32[]{:S(2)}) copy-start(f32[128,3,3,512]{3,0,2,1:T(8,128)} %get-tuple-element.22) | copy-start | bytes 7077892
Sparse Core Ops, SparseCore 0:
  21.0 20.7 all-gather.2
  65.3 19.8 all-gather.4
  105.1 25.2 reduce-scatter.1
  136.3 169.9 all-reduce.24
where the time goes:
time: 318 us
  waiting for transfers between devices  244 us (77%)
  matrix products  27.1 us (9%)
  starting transfers between devices  16.9 us (5%)
  between operations  14.2 us (4%)
  local copies, waits for them, and re-layouts  7.95 us (2%)
  other arithmetic  7.08 us (2%)
    psum x1, waiting for transfers between devices, per_device(): first_grad, second_grad = lax.psum((first_local, second_local), 'rows')  168 us
    all_gather x2, waiting for transfers between devices, all_channels(): return lax.all_gather(with_rims(value), 'filt', axis=0, tiled=True)  39.9 us
    reduce_scatter x1, waiting for transfers between devices, per_device(): lax.psum_scatter(terms, 'filt', scatter_dimension=0, tiled=True)  21.2 us
    dot_general x18, matrix products, conv_forward(): jnp.einsum('oi,ihw->ohw', weight[:, a, b, :], padded[:, a:a + count, :],...  18.3 us
    ppermute x3, starting transfers between devices, extended(): lax.ppermute(tail, axis, [(i, (i + 1) % count) for i in range(ends)])  12.8 us
    ppermute x3, waiting for transfers between devices, extended(): lax.ppermute(head, axis, [((i + 1) % count, i) for i in range(ends)])  8.89 us
    unnamed x21, local copies, waits for them, and re-layouts  7.39 us
  transfers between devices with their start and end apart: 10, of which 10 were waited for; matrix products, arithmetic and copies ran while one was open for 2% of the time, Pallas kernels for 0%

commit v1 on v0

v1 whole, which is shorter than its diff:
```python
import functools

import jax
import jax.numpy as jnp
from jax import lax
from jax.experimental import pallas as pl
from jax.experimental.pallas import tpu as pltpu
from jax.sharding import PartitionSpec as P

BF = jnp.bfloat16
F32 = jnp.float32
VMEM_BYTES = 56 * 1024 * 1024


def extended(cells, sides, width):
    for axis, dim in sides:
        count = lax.axis_size(axis)
        ends = count - 1
        head = lax.slice_in_dim(cells, 0, width, axis=dim)
        tail = lax.slice_in_dim(cells, cells.shape[dim] - width, cells.shape[dim], axis=dim)
        cells = jnp.concatenate(
            [
                lax.ppermute(tail, axis, [(i, (i + 1) % count) for i in range(ends)]),
                cells,
                lax.ppermute(head, axis, [((i + 1) % count, i) for i in range(ends)]),
            ],
            axis=dim,
        )
    return cells


def shift_cols(value, offset):
    if offset == 0:
        return value
    if offset > 0:
        return jnp.pad(value[..., offset:], ((0, 0), (0, 0), (0, offset)))
    return jnp.pad(value[..., :offset], ((0, 0), (0, 0), (-offset, 0)))


def conv_forward(weight, padded, count):
    total = jnp.zeros((weight.shape[0], count, padded.shape[2]), F32)
    for a in range(3):
        for b in range(3):
            part = jnp.einsum(
                "oi,ihw->ohw", weight[:, a, b, :], padded[:, a : a + count, :], preferred_element_type=F32
            )
            total = total + shift_cols(part, b - 1)
    return total


def conv_backward(weight, padded, count):
    total = jnp.zeros((weight.shape[3], count, padded.shape[2]), F32)
    for a in range(3):
        for b in range(3):
            part = jnp.einsum(
                "oi,ohw->ihw", weight[:, a, b, :], padded[:, 2 - a : 2 - a + count, :], preferred_element_type=F32
            )
            total = total + shift_cols(part, 1 - b)
    return total


def weight_terms(grad, padded, count):
    rows_out = []
    for a in range(3):
        cols_out = []
        for b in range(3):
            moved = shift_cols(grad, 1 - b)
            cols_out.append(
                jnp.einsum("ohw,ihw->oi", moved, padded[:, a : a + count, :], preferred_element_type=F32)
            )
        rows_out.append(jnp.stack(cols_out, axis=1))
    return jnp.stack(rows_out, axis=1)


def with_rims(value):
    return extended(value, (("rows", 1),), 1)


def all_channels(value):
    return lax.all_gather(with_rims(value), "filt", axis=0, tiled=True)


def split_rows(features, first_weight, second_weight, out_grad):
    count = features.shape[1]
    padded_in = all_channels(features)
    pre_first = conv_forward(first_weight, padded_in, count)
    hidden = jnp.maximum(pre_first, 0.0).astype(BF)
    padded_hidden = all_channels(hidden)
    pre_second = conv_forward(second_weight, padded_hidden, count) + features.astype(F32)
    block_out = jnp.maximum(pre_second, 0.0).astype(BF)
    grad_second = jnp.where(pre_second > 0, out_grad.astype(F32), 0.0).astype(BF)
    rimmed_grad = with_rims(grad_second)
    terms = conv_backward(second_weight, rimmed_grad, count)
    hidden_grad = lax.psum_scatter(terms, "filt", scatter_dimension=0, tiled=True)
    grad_first = jnp.where(pre_first > 0, hidden_grad, 0.0).astype(BF)
    second_local = weight_terms(grad_second, padded_hidden, count)
    first_local = weight_terms(grad_first, padded_in, count)
    first_grad, second_grad = lax.psum((first_local, second_local), "rows")
    return (block_out, first_grad, second_grad)


def swap(value, axis, bits):
    return lax.ppermute(value, axis, [(i, i ^ bits) for i in range(lax.axis_size(axis))])


def block_at(index, size):
    return pl.ds(pl.multiple_of(index * size, size), size)


def run_copies(copies):
    for c in copies:
        c.start()
    for c in copies:
        c.wait()


def conv_row(weight, x, r):
    acc = jnp.dot(weight[0], x[r], preferred_element_type=F32)
    acc += jnp.dot(weight[1], x[r + 1], preferred_element_type=F32)
    acc += jnp.dot(weight[2], x[r + 2], preferred_element_type=F32)
    return acc


def join_cols(left, mid, right):
    w = mid.shape[1]
    col = lax.broadcasted_iota(jnp.int32, mid.shape, 1)
    out = mid + jnp.where(col == 0, 0.0, pltpu.roll(left, 1, 1))
    return out + jnp.where(col == w - 1, 0.0, pltpu.roll(right, w - 1, 1))


def clear_rims(x):
    x[0] = jnp.zeros(x.shape[1:], x.dtype)
    x[x.shape[0] - 1] = jnp.zeros(x.shape[1:], x.dtype)


def first_kernel(places, n_pieces, *refs):
    pieces, weight = refs[:n_pieces], refs[n_pieces]
    full, hidden, mask, x, sems, out_sem = refs[n_pieces + 1 :]
    rows, own = hidden.shape[0], hidden.shape[1]
    r0, f0 = lax.axis_index("rows"), lax.axis_index("filt")
    copies = []
    for (piece, k, d, e, lo), ref in zip(places, [pieces[p[0]] for p in places]):
        size = ref.shape[1]
        at = pl.multiple_of((f0 ^ e) * own + lo, 16)
        copies.append(
            pltpu.make_async_copy(ref.at[k], x.at[1 + (r0 ^ d), pl.ds(at, size)], sems.at[len(copies)])
        )
    for c in copies:
        c.start()
    clear_rims(x)
    for c in copies:
        c.wait()
    out = pltpu.make_async_copy(x.at[pl.ds(1, rows)], full, out_sem)
    out.start()

    def step(r, carry):
        acc = conv_row(weight, x, r)
        pre = join_cols(acc[:own], acc[own : 2 * own], acc[2 * own :])
        hidden[r] = jnp.maximum(pre, 0.0).astype(BF)
        mask[r] = jnp.where(pre > 0, 1.0, 0.0).astype(BF)
        return carry

    lax.fori_loop(0, rows, step, 0)
    out.wait()


def load_filt(pieces, x, sems, own):
    f0 = lax.axis_index("filt")
    rows = pieces[0].shape[0]
    return [
        pltpu.make_async_copy(ref, x.at[pl.ds(1, rows), block_at(f0 ^ e, own)], sems.at[e])
        for e, ref in enumerate(pieces)
    ]


def second_kernel(places, n_grad, *refs):
    pieces, full, grads, weight = refs[:4], refs[4], refs[5 : 5 + n_grad], refs[5 + n_grad]
    block_out, grad_second, x, feat, grad, sems, sems_g = refs[6 + n_grad :]
    rows, own = grad_second.shape[0], grad_second.shape[1]
    r0, f0 = lax.axis_index("rows"), lax.axis_index("filt")
    copies = load_filt(pieces, x, sems, own)
    copies.append(pltpu.make_async_copy(full.at[:, block_at(f0, own)], feat, sems.at[4]))
    for n, (piece, k, d) in enumerate(places):
        copies.append(pltpu.make_async_copy(grads[piece].at[k], grad.at[r0 ^ d], sems_g.at[n]))
    for c in copies:
        c.start()
    clear_rims(x)
    for c in copies:
        c.wait()

    def step(r, carry):
        acc = conv_row(weight, x, r)
        pre = join_cols(acc[:own], acc[own : 2 * own], acc[2 * own :]) + feat[r].astype(F32)
        grad_second[r] = jnp.where(pre > 0, grad[r].astype(F32), 0.0).astype(BF)

        @pl.when(r == r0)
        def _():
            block_out[0] = jnp.maximum(pre, 0.0).astype(BF)

        return carry

    lax.fori_loop(0, rows, step, 0)


def turn_kernel(weight, *outs):
    own = weight.shape[1]
    f0 = lax.axis_index("filt")
    for e, out in enumerate(outs):
        for t in range(weight.shape[0]):
            out[t] = weight[t, :, block_at(f0 ^ e, own)].T


def back_kernel(*refs):
    pieces, turned, mask, grad_first, x, weight, sems, sems_w = refs[:4], refs[4:8], *refs[8:]
    rows, own = grad_first.shape[0], grad_first.shape[1]
    f0 = lax.axis_index("filt")
    copies = load_filt(pieces, x, sems, own)
    for e, ref in enumerate(turned):
        copies.append(pltpu.make_async_copy(ref, weight.at[:, :, block_at(f0 ^ e, own)], sems_w.at[e]))
    for c in copies:
        c.start()
    clear_rims(x)
    for c in copies:
        c.wait()
    c = weight.shape[2]

    def step(r, carry):
        acc = None
        for a in range(3):
            lhs = weight[3 * a : 3 * a + 3].reshape(3 * own, c)
            part = jnp.dot(lhs, x[r + 2 - a], preferred_element_type=F32)
            acc = part if acc is None else acc + part
        total = join_cols(acc[2 * own :], acc[own : 2 * own], acc[:own])
        grad_first[r] = jnp.where(mask[r] > 0, total, 0.0).astype(BF)
        return carry

    lax.fori_loop(0, rows, step, 0)


def fill_moved(grad, moved):
    rows, own, w = grad.shape
    clear_rims(moved)
    col = lax.broadcasted_iota(jnp.int32, (own, w), 1)

    def step(r, carry):
        g = grad[r].astype(F32)
        moved[r + 1, 0:own] = jnp.where(col == w - 1, 0.0, pltpu.roll(g, w - 1, 1)).astype(BF)
        moved[r + 1, own : 2 * own] = grad[r]
        moved[r + 1, 2 * own :] = jnp.where(col == 0, 0.0, pltpu.roll(g, 1, 1)).astype(BF)
        return carry

    lax.fori_loop(0, rows, step, 0)


def sum_terms(moved, x, first, out):
    rows, taps = moved.shape[0] - 2, moved.shape[1]
    for a in range(3):

        def step(h, acc, a=a):
            return acc + lax.dot_general(
                moved[h - a + 2], x[first + h], (((1,), (1,)), ((), ())), preferred_element_type=F32
            )

        out[a] = lax.fori_loop(0, rows, step, jnp.zeros((taps, x.shape[1]), F32))


def second_terms_kernel(*refs):
    pieces, grad, out, x, moved, sems = refs[:4], *refs[4:]
    copies = load_filt(pieces, x, sems, grad.shape[1])
    for c in copies:
        c.start()
    fill_moved(grad, moved)
    for c in copies:
        c.wait()
    sum_terms(moved, x, 1, out)


def first_terms_kernel(full, grad, out, x, moved, sem):
    copy = pltpu.make_async_copy(full, x, sem)
    copy.start()
    fill_moved(grad, moved)
    copy.wait()
    sum_terms(moved, x, 0, out)


ANY = pl.BlockSpec(memory_space=pl.ANY)
VM = pl.BlockSpec(memory_space=pltpu.VMEM)


def call(kernel, ins, outs, scratch, flops, name):
    nbytes = sum(v.size * v.dtype.itemsize for v, _ in ins)
    return pl.pallas_call(
        kernel,
        out_shape=[jax.ShapeDtypeStruct(s, d) for s, d, _ in outs],
        in_specs=[s for _, s in ins],
        out_specs=[s for _, _, s in outs],
        scratch_shapes=scratch,
        compiler_params=pltpu.CompilerParams(vmem_limit_bytes=VMEM_BYTES),
        cost_estimate=pl.CostEstimate(flops=flops, bytes_accessed=nbytes, transcendentals=0),
        name=name,
    )(*[v for v, _ in ins])


def all_rows(features, first_weight, second_weight, out_grad):
    c = first_weight.shape[3]
    own, _, w = features.shape
    rows = lax.axis_size("rows")
    flops = 2 * 9 * own * c * w * rows
    dma = pltpu.SemaphoreType.DMA
    feat = jnp.transpose(features, (1, 0, 2))
    ograd = jnp.transpose(out_grad, (1, 0, 2))
    w1 = jnp.transpose(first_weight, (1, 2, 0, 3)).reshape(3, 3 * own, c)
    w2 = jnp.transpose(second_weight, (1, 2, 0, 3))

    zs = tuple(range(0, rows, 2))
    own_z = jnp.concatenate([feat] + [swap(feat, "rows", d) for d in zs[1:]], axis=0)
    half = own // 2
    over_x = swap(own_z, "filt", 2)
    over_y = swap(own_z, "rows", 1)
    diag_lo = swap(over_x[:, :half], "rows", 1)
    diag_hi = swap(over_y[:, half:], "filt", 2)
    mine = [own_z, over_x, over_y, diag_lo, diag_hi]
    moves = [(0, 0, 0), (0, 2, 0), (1, 0, 0), (1, 2, 0), (1, 2, half)]
    pieces, places = [], []
    for core in (0, 1):
        for value, (d, e, lo) in zip(mine, moves):
            for k, z in enumerate(zs):
                places.append((len(pieces), k, z ^ d, e ^ core, lo))
            pieces.append(swap(value, "filt", 1) if core else value)
    full, hidden, mask = call(
        functools.partial(first_kernel, places, len(pieces)),
        [(v, ANY) for v in pieces] + [(w1, VM)],
        [((rows, c, w), BF, ANY), ((rows, own, w), BF, VM), ((rows, own, w), BF, VM)],
        [pltpu.VMEM((rows + 2, c, w), BF), dma((len(places),)), dma],
        flops,
        "first_conv",
    )

    grad_z = jnp.concatenate([ograd] + [swap(ograd, "rows", d) for d in zs[1:]], axis=0)
    grads = [grad_z, swap(grad_z, "rows", 1)]
    grad_places = [(p, k, z ^ p) for p in (0, 1) for k, z in enumerate(zs)]

    w2_blocks = w2.reshape(9, own, c)
    turned = call(
        turn_kernel, [(w2_blocks, VM)], [((9, own, own), BF, VM)] * 4, [], 0, "turn_weight"
    )
    turned = [turned[0]] + [swap(turned[e], "filt", e) for e in (1, 2, 3)]

    def over_filt(value):
        far = swap(value, "filt", 2)
        return [value, swap(value, "filt", 1), far, swap(far, "filt", 1)]

    hiddens = over_filt(hidden)
    block_out, grad_second = call(
        functools.partial(second_kernel, grad_places, len(grads)),
        [(v, ANY) for v in hiddens + [full] + grads] + [(w2.reshape(3, 3 * own, c), VM)],
        [((1, own, w), BF, VM), ((rows, own, w), BF, VM)],
        [
            pltpu.VMEM((rows + 2, c, w), BF),
            pltpu.VMEM((rows, own, w), BF),
            pltpu.VMEM((rows, own, w), BF),
            dma((5,)),
            dma((len(grad_places),)),
        ],
        flops,
        "second_conv",
    )
    seconds = over_filt(grad_second)
    (second_grad,) = call(
        second_terms_kernel,
        [(v, ANY) for v in hiddens] + [(grad_second, VM)],
        [((3, 3 * own, c), F32, VM)],
        [pltpu.VMEM((rows + 2, c, w), BF), pltpu.VMEM((rows + 2, 3 * own, w), BF), dma((4,))],
        flops,
        "second_terms",
    )
    (grad_first,) = call(
        back_kernel,
        [(v, ANY) for v in seconds + turned] + [(mask, VM)],
        [((rows, own, w), BF, VM)],
        [pltpu.VMEM((rows + 2, c, w), BF), pltpu.VMEM((9, own, c), BF), dma((4,)), dma((4,))],
        flops,
        "hidden_grad",
    )
    (first_grad,) = call(
        first_terms_kernel,
        [(full, ANY), (grad_first, VM)],
        [((3, 3 * own, c), F32, VM)],
        [pltpu.VMEM((rows, c, w), BF), pltpu.VMEM((rows + 2, 3 * own, w), BF), dma],
        flops,
        "first_terms",
    )

    def as_weight(value):
        return jnp.transpose(value.reshape(3, 3, own, c), (2, 0, 1, 3))

    return jnp.transpose(block_out, (1, 0, 2)), as_weight(first_grad), as_weight(second_grad)


def solution(mesh):
    in_specs = (
        P("filt", "rows", None),
        P("filt", None, None, None),
        P("filt", None, None, None),
        P("filt", "rows", None),
    )
    out_specs = (P("filt", "rows", None), P("filt", None, None, None), P("filt", None, None, None))

    def per_device(features, first_weight, second_weight, out_grad):
        rows, filt = mesh.shape["rows"], mesh.shape["filt"]
        small = rows == 8 and filt == 4 and features.shape[1] == 1 and features.shape[0] % 32 == 0
        plan = all_rows if small else split_rows
        return plan(features, first_weight, second_weight, out_grad)

    return jax.shard_map(per_device, mesh=mesh, in_specs=in_specs, out_specs=out_specs, check_vma=False)
```

time: 318 us -> 199 us (0.63)
  waiting for transfers between devices: 244 us -> 97.5 us
  Pallas kernels: 0 us -> 72.2 us
  matrix products: 27.1 us -> 0 us
  between operations: 14.2 us -> 0.96 us
  starting transfers between devices: 16.9 us -> 23.3 us
  other arithmetic: 7.08 us -> 1.04 us
  local copies, waits for them, and re-layouts: 7.95 us -> 3.7 us
    psum x1 -> x0, waiting for transfers between devices: 168 us -> none  [per_device(): first_grad, second_grad = lax.psum((first_local, second_local), 'rows')]
    ppermute x6 -> x25, waiting for transfers between devices: 14.8 us -> 97.5 us  [swap(): lax.ppermute(value, axis, [(i, i ^ bits) for i in range(lax.axis_size(axi...]
    pallas_call x0 -> x6, Pallas kernels: none -> 72.2 us  [call(): pl.pallas_call(kernel, out_shape=[jax.ShapeDtypeStruct(s, d) for s, d, _...]
    all_gather x2 -> x0, waiting for transfers between devices: 39.9 us -> none  [all_channels(): return lax.all_gather(with_rims(value), 'filt', axis=0, tiled=True)]
    dot_general x45 -> x0, matrix products: 27.1 us -> none  [the longest x18 18.3 us: conv_forward(): jnp.einsum('oi,ihw->ohw', weight[:, a, b, :], padded[:, a:a + count, :],...]
    reduce_scatter x1 -> x0, waiting for transfers between devices: 21.2 us -> none  [per_device(): lax.psum_scatter(terms, 'filt', scatter_dimension=0, tiled=True)]
    ppermute x6 -> x25, starting transfers between devices: 16.7 us -> 23.3 us  [swap(): lax.ppermute(value, axis, [(i, i ^ bits) for i in range(lax.axis_size(axi...]
    unnamed x21 -> x44, local copies, waits for them, and re-layouts: 7.39 us -> 3.67 us
  transfers between devices with their start and end apart: 10 -> 25, of which waited for: 10 -> 11; matrix products, arithmetic and copies ran while one was open for 2% -> 0% of each run, Pallas kernels for 0% -> 10%
where the time goes in v1:
time: 199 us
  waiting for transfers between devices  97.5 us (49%)
  Pallas kernels  72.2 us (36%)
  starting transfers between devices  23.3 us (12%)
  local copies, waits for them, and re-layouts  3.7 us (2%)
    ppermute x25, waiting for transfers between devices, swap(): lax.ppermute(value, axis, [(i, i ^ bits) for i in range(lax.axis_size(axi...  97.5 us
    pallas_call x6, Pallas kernels, call(): pl.pallas_call(kernel, out_shape=[jax.ShapeDtypeStruct(s, d) for s, d, _...  72.2 us
    ppermute x25, starting transfers between devices, swap(): lax.ppermute(value, axis, [(i, i ^ bits) for i in range(lax.axis_size(axi...  23.3 us
  transfers between devices with their start and end apart: 25, of which 11 were waited for; matrix products, arithmetic and copies ran while one was open for 0% of the time, Pallas kernels for 10%

profile of v1, /device:TPU:0, one launch (start us, length us, event | category | flops | bytes accessed | tf_op | source)
XLA Modules:
  0.0 198.6 jit_solution(2828591963721574232)
XLA Ops:
  0.6 5.1 %collective-permute-start.2 = (bf16[1,128,512]{2,1,0:T(8,128)(2,1)}, bf16[1,128,512]{2,1,0:T(8,128)(2,1)S(1)}, u32[]{:S(2)}, u32[]{:S(2)}) collective-permute-start(bf16[1,128,512]{2,1,0:T(8,128)(2,1)} %bitcast.19), channel_id=1, source_target_pairs={{0,24},{4,28},{8,16},{12,20},{16,8},{20,12},{24,0},{28,4},{1,25},{... | collective-permute-start | bytes 393224 | tf_op jit(solution)/shard_map/ppermute | solution.py:103
  5.7 0.0 collective-permute-start.1
  5.7 0.6 collective-permute-start
  6.4 4.0 %collective-permute-done.2 = bf16[1,128,512]{2,1,0:T(8,128)(2,1)S(1)} collective-permute-done((bf16[1,128,512]{2,1,0:T(8,128)(2,1)}, bf16[1,128,512]{2,1,0:T(8,128)(2,1)S(1)}, u32[]{:S(2)}, u32[]{:S(2)}) %collective-permute-start.2) | collective-permute-done | bytes 131104 | tf_op jit(solution)/shard_map/ppermute | solution.py:103
  10.4 6.6 %collective-permute-done.1 = bf16[1,128,512]{2,1,0:T(8,128)(2,1)S(1)} collective-permute-done((bf16[1,128,512]{2,1,0:T(8,128)(2,1)}, bf16[1,128,512]{2,1,0:T(8,128)(2,1)S(1)}, u32[]{:S(2)}, u32[]{:S(2)}) %collective-permute-start.1) | collective-permute-done | bytes 131104 | tf_op jit(solution)/shard_map/ppermute | solution.py:103
  17.0 0.0 collective-permute-done
  17.0 1.0 pad_maximum_fusion.refs_0_
  18.0 0.0 copy-start
  18.0 1.6 collective-permute-start.4
  19.6 1.5 collective-permute-start.3
  21.1 0.0 collective-permute-start.7
  21.1 10.0 %collective-permute-done.4.refs_2_ = bf16[4,128,512]{2,1,0:T(8,128)(2,1)S(1)} collective-permute-done((bf16[4,128,512]{2,1,0:T(8,128)(2,1)S(1)}, bf16[4,128,512]{2,1,0:T(8,128)(2,1)S(1)}, u32[]{:S(2)}, u32[]{:S(2)}) %collective-permute-start.4) | collective-permute-done | bytes 524320 | tf_op jit(solution)/shard_map/ppermute | solution.py:103
  31.1 1.6 collective-permute-start.6
  32.6 0.0 collective-permute-start.9
  32.6 0.0 collective-permute-done.3.refs_1_
  32.7 0.6 collective-permute-start.8
  33.2 1.5 collective-permute-start.5
  34.8 3.2 %collective-permute-done.6.refs_4_ = bf16[4,64,512]{2,1,0:T(8,128)(2,1)S(1)} collective-permute-done((bf16[4,64,512]{2,1,0:T(8,128)(2,1)S(1)}, bf16[4,64,512]{2,1,0:T(8,128)(2,1)S(1)}, u32[]{:S(2)}, u32[]{:S(2)}) %collective-permute-start.6) | collective-permute-done | bytes 262176 | tf_op jit(solution)/shard_map/ppermute | solution.py:103
  37.9 0.0 collective-permute-start.11
  37.9 3.6 %collective-permute-done.5.refs_3_ = bf16[4,64,512]{2,1,0:T(8,128)(2,1)S(1)} collective-permute-done((bf16[4,64,512]{2,1,0:T(8,128)(2,1)S(1)}, bf16[4,64,512]{2,1,0:T(8,128)(2,1)S(1)}, u32[]{:S(2)}, u32[]{:S(2)}) %collective-permute-start.5) | collective-permute-done | bytes 262176 | tf_op jit(solution)/shard_map/ppermute | solution.py:103
  41.5 0.0 collective-permute-start.10
  41.5 0.0 collective-permute-done.7.refs_5_
  41.6 0.0 collective-permute-done.9.refs_7_
  41.6 1.5 collective-permute-done.10.refs_8_
  43.1 0.6 copy-done.21
  43.8 12.2 %first_conv.1 = (bf16[8,512,512]{2,1,0:T(8,128)(2,1)}, bf16[8,128,512]{2,1,0:T(8,128)(2,1)}, bf16[8,128,512]{2,1,0:T(8,128)(2,1)}) custom-call(bf16[4,128,512]{2,1,0:T(8,128)(2,1)} %copy-done, bf16[4,128,512]{2,1,0:T(8,128)(2,1)} %copy-done.3, bf16[4,128,512]{2,1,0:T(8,128)(2,1)} %copy-done.2, bf16[4,64,512]{2,1,0:T(8,128)(2,1)} %copy-done.19, ...), custom_call_target="tpu_custom_call" | custom-call | flops 4831838208 | bytes 5373952 | tf_op jit(solution)/shard_map/first_conv/pallas_call | solution.py:292
  56.0 1.4 collective-permute-start.13
  57.4 0.0 collective-permute-start.12
  57.5 24.1 %collective-permute-done.13.refs_2_ = bf16[8,128,512]{2,1,0:T(8,128)(2,1)S(1)} collective-permute-done((bf16[8,128,512]{2,1,0:T(8,128)(2,1)}, bf16[8,128,512]{2,1,0:T(8,128)(2,1)S(1)}, u32[]{:S(2)}, u32[]{:S(2)}) %collective-permute-start.13) | collective-permute-done | bytes 1048608 | tf_op jit(solution)/shard_map/ppermute | solution.py:103
  81.5 0.0 collective-permute-start.14
  81.5 2.4 %collective-permute-start.17 = (bf16[1,128,512]{2,1,0:T(8,128)(2,1)S(1)}, bf16[1,128,512]{2,1,0:T(8,128)(2,1)S(1)}, u32[]{:S(2)}, u32[]{:S(2)}) collective-permute-start(bf16[1,128,512]{2,1,0:T(8,128)(2,1)S(1)} %bitcast.23), channel_id=1, source_target_pairs={{0,24},{4,28},{8,16},{12,20},{16,8},{20,12},{24,0},{28,4},{1,25},{... | collective-permute-start | bytes 393224 | tf_op jit(solution)/shard_map/ppermute | solution.py:103
  83.9 2.1 %collective-permute-start.15 = (bf16[1,128,512]{2,1,0:T(8,128)(2,1)S(1)}, bf16[1,128,512]{2,1,0:T(8,128)(2,1)S(1)}, u32[]{:S(2)}, u32[]{:S(2)}) collective-permute-start(bf16[1,128,512]{2,1,0:T(8,128)(2,1)S(1)} %bitcast.25), channel_id=1, source_target_pairs={{0,8},{4,12},{8,0},{12,4},{16,24},{20,28},{24,16},{28,20},{1,9},{5... | collective-permute-start | bytes 393224 | tf_op jit(solution)/shard_map/ppermute | solution.py:103
  86.0 3.9 %collective-permute-done.17 = bf16[1,128,512]{2,1,0:T(8,128)(2,1)S(1)} collective-permute-done((bf16[1,128,512]{2,1,0:T(8,128)(2,1)S(1)}, bf16[1,128,512]{2,1,0:T(8,128)(2,1)S(1)}, u32[]{:S(2)}, u32[]{:S(2)}) %collective-permute-start.17) | collective-permute-done | bytes 131104 | tf_op jit(solution)/shard_map/ppermute | solution.py:103
  89.8 5.1 %collective-permute-done.16 = bf16[1,128,512]{2,1,0:T(8,128)(2,1)S(1)} collective-permute-done((bf16[1,128,512]{2,1,0:T(8,128)(2,1)S(1)}, bf16[1,128,512]{2,1,0:T(8,128)(2,1)S(1)}, u32[]{:S(2)}, u32[]{:S(2)}) %collective-permute-start.16) | collective-permute-done | bytes 131104 | tf_op jit(solution)/shard_map/ppermute | solution.py:103
  95.0 0.0 collective-permute-done.15
  95.0 0.1 pad_maximum_fusion.1.refs_5_
  95.0 0.0 copy-start.1
  95.0 1.6 collective-permute-start.18
  96.6 12.4 %collective-permute-done.18.refs_6_ = bf16[4,128,512]{2,1,0:T(8,128)(2,1)S(1)} collective-permute-done((bf16[4,128,512]{2,1,0:T(8,128)(2,1)S(1)}, bf16[4,128,512]{2,1,0:T(8,128)(2,1)S(1)}, u32[]{:S(2)}, u32[]{:S(2)}) %collective-permute-start.18) | collective-permute-done | bytes 524320 | tf_op jit(solution)/shard_map/ppermute | solution.py:103
  109.1 0.0 collective-permute-done.12.refs_1_
  109.1 0.0 collective-permute-done.14.refs_3_
  109.1 0.7 copy-done.14
  109.8 0.4 copy-done.6
  110.2 0.3 copy-done.7
  110.5 12.4 %second_conv.1 = (bf16[1,128,512]{2,1,0:T(8,128)(2,1)}, bf16[8,128,512]{2,1,0:T(8,128)(2,1)}) custom-call(bf16[8,128,512]{2,1,0:T(8,128)(2,1)} %get-tuple-element.12.refs_0_, bf16[8,128,512]{2,1,0:T(8,128)(2,1)} %copy-done.6, bf16[8,128,512]{2,1,0:T(8,128)(2,1)} %copy-done.5, bf16[8,128,512]{2,1,0:T(8,128)(2,1)} %copy-done.7, ...), custom_call_target="tpu_custom_call" | custom-call | flops 4831838208 | bytes 10616832 | tf_op jit(solution)/shard_map/second_conv/pallas_call | solution.py:292
  122.9 1.5 collective-permute-start.20
  124.4 0.0 collective-permute-start.19
  124.4 23.2 %collective-permute-done.20.refs_2_ = bf16[8,128,512]{2,1,0:T(8,128)(2,1)S(1)} collective-permute-done((bf16[8,128,512]{2,1,0:T(8,128)(2,1)}, bf16[8,128,512]{2,1,0:T(8,128)(2,1)S(1)}, u32[]{:S(2)}, u32[]{:S(2)}) %collective-permute-start.20) | collective-permute-done | bytes 1048608 | tf_op jit(solution)/shard_map/ppermute | solution.py:103
  147.6 2.8 %turn_weight.1 = (bf16[9,128,128]{2,1,0:T(8,128)(2,1)}, bf16[9,128,128]{2,1,0:T(8,128)(2,1)}, bf16[9,128,128]{2,1,0:T(8,128)(2,1)}, bf16[9,128,128]{2,1,0:T(8,128)(2,1)}) custom-call(bf16[9,128,512]{2,1,0:T(8,128)(2,1)} %bitcast.18), custom_call_target="tpu_custom_call" | custom-call | bytes 1179648 | tf_op jit(solution)/shard_map/turn_weight/pallas_call | solution.py:292
  150.4 0.1 collective-permute-start.22
  150.5 1.3 collective-permute-start.23
  151.8 0.4 collective-permute-start.24
  152.2 16.5 %second_terms.1 = f32[3,384,512]{2,1,0:T(8,128)} custom-call(bf16[8,128,512]{2,1,0:T(8,128)(2,1)} %get-tuple-element.12.refs_0_, bf16[8,128,512]{2,1,0:T(8,128)(2,1)} %copy-done.6, bf16[8,128,512]{2,1,0:T(8,128)(2,1)} %copy-done.5, bf16[8,128,512]{2,1,0:T(8,128)(2,1)} %copy-done.7, bf16[8,128,512]{2,1,0:T(8,128)(2,1)} %get-tuple-element.15.refs_0_.refs_4_), custom_call_target="tpu_custom_call" | custom-call | flops 4831838208 | bytes 5242880 | tf_op jit(solution)/shard_map/second_terms/pallas_call | solution.py:292
  168.7 0.0 collective-permute-done.22.refs_5_
  168.7 0.0 collective-permute-done.23.refs_6_
  168.8 0.0 collective-permute-done.19.refs_1_
  168.8 0.0 copy-start.9
  168.8 0.6 copy-done.15
  169.4 0.1 copy-done.16
  169.6 0.1 copy-done.17
  169.7 0.3 copy-done.9
  170.0 0.3 copy-done.10
  170.3 11.9 %hidden_grad.1.grad = bf16[8,128,512]{2,1,0:T(8,128)(2,1)} custom-call(bf16[8,128,512]{2,1,0:T(8,128)(2,1)} %get-tuple-element.15.refs_0_.refs_4_, bf16[8,128,512]{2,1,0:T(8,128)(2,1)} %copy-done.9, bf16[8,128,512]{2,1,0:T(8,128)(2,1)} %copy-done.8, bf16[8,128,512]{2,1,0:T(8,128)(2,1)} %copy-done.10, bf16[9,128,128]{2,1,0:T(8,128)(2,1)} %get-tuple-element.16.refs_4_, ...), custom_call_target="tpu_custom_call" | custom-call | flops 4831838208 | bytes 6422528 | tf_op jit(solution)/shard_map/hidden_grad/pallas_call | solution.py:292
  182.2 16.4 %first_terms.1 = f32[3,384,512]{2,1,0:T(8,128)} custom-call(bf16[8,512,512]{2,1,0:T(8,128)(2,1)} %get-tuple-element.13.refs_4_.full, bf16[8,128,512]{2,1,0:T(8,128)(2,1)} %hidden_grad.1.grad), custom_call_target="tpu_custom_call" | custom-call | flops 4831838208 | bytes 5242880 | tf_op jit(solution)/shard_map/first_terms/pallas_call | solution.py:292
  (40 shorter events, 0.1 us)
Async XLA Ops:
  0.6 9.8 %collective-permute-start.2 = (bf16[1,128,512]{2,1,0:T(8,128)(2,1)}, bf16[1,128,512]{2,1,0:T(8,128)(2,1)S(1)}, u32[]{:S(2)}, u32[]{:S(2)}) collective-permute-start(bf16[1,128,512]{2,1,0:T(8,128)(2,1)} %bitcast.19), channel_id=1, source_target_pairs={{0,24},{4,28},{8,16},{12,20},{16,8},{20,12},{24,0},{28,4},{1,25},{... | collective-permute-start | bytes 393224 | tf_op jit(solution)/shard_map/ppermute | solution.py:103
  5.7 11.3 %collective-permute-start.1 = (bf16[1,128,512]{2,1,0:T(8,128)(2,1)}, bf16[1,128,512]{2,1,0:T(8,128)(2,1)S(1)}, u32[]{:S(2)}, u32[]{:S(2)}) collective-permute-start(bf16[1,128,512]{2,1,0:T(8,128)(2,1)} %bitcast.20), channel_id=1, source_target_pairs={{0,16},{4,20},{8,24},{12,28},{16,0},{20,4},{24,8},{28,12},{1,17},{... | collective-permute-start | bytes 393224 | tf_op jit(solution)/shard_map/ppermute | solution.py:103
  5.7 11.3 %collective-permute-start = (bf16[1,128,512]{2,1,0:T(8,128)(2,1)}, bf16[1,128,512]{2,1,0:T(8,128)(2,1)S(1)}, u32[]{:S(2)}, u32[]{:S(2)}) collective-permute-start(bf16[1,128,512]{2,1,0:T(8,128)(2,1)} %bitcast.21), channel_id=1, source_target_pairs={{0,8},{4,12},{8,0},{12,4},{16,24},{20,28},{24,16},{28,20},{1,9},{5... | collective-permute-start | bytes 393224 | tf_op jit(solution)/shard_map/ppermute | solution.py:103
  18.0 25.1 %copy-start = (bf16[4,128,512]{2,1,0:T(8,128)(2,1)}, bf16[4,128,512]{2,1,0:T(8,128)(2,1)S(1)}, u32[]{:S(2)}) copy-start(bf16[4,128,512]{2,1,0:T(8,128)(2,1)S(1)} %pad_maximum_fusion.refs_0_) | copy-start | bytes 1572868
  18.0 13.0 %collective-permute-start.4 = (bf16[4,128,512]{2,1,0:T(8,128)(2,1)S(1)}, bf16[4,128,512]{2,1,0:T(8,128)(2,1)S(1)}, u32[]{:S(2)}, u32[]{:S(2)}) collective-permute-start(bf16[4,128,512]{2,1,0:T(8,128)(2,1)S(1)} %pad_maximum_fusion.refs_0_), channel_id=1, source_target_pairs={{0,4},{4,0},{8,12},{12,8},{16,20},{20,16},{24,28},{28,24},{1,5},{5... | collective-permute-start | bytes 1572872 | tf_op jit(solution)/shard_map/ppermute | solution.py:103
  19.6 13.0 %collective-permute-start.3 = (bf16[4,128,512]{2,1,0:T(8,128)(2,1)S(1)}, bf16[4,128,512]{2,1,0:T(8,128)(2,1)S(1)}, u32[]{:S(2)}, u32[]{:S(2)}) collective-permute-start(bf16[4,128,512]{2,1,0:T(8,128)(2,1)S(1)} %pad_maximum_fusion.refs_0_), channel_id=1, source_target_pairs={{0,2},{1,3},{2,0},{3,1},{4,6},{5,7},{6,4},{7,5},{8,10},{9,11},{10,... | collective-permute-start | bytes 1572872 | tf_op jit(solution)/shard_map/ppermute | solution.py:103
  21.1 20.4 %collective-permute-start.7 = (bf16[4,128,512]{2,1,0:T(8,128)(2,1)S(1)}, bf16[4,128,512]{2,1,0:T(8,128)(2,1)S(1)}, u32[]{:S(2)}, u32[]{:S(2)}) collective-permute-start(bf16[4,128,512]{2,1,0:T(8,128)(2,1)S(1)} %pad_maximum_fusion.refs_0_), channel_id=1, source_target_pairs={{0,1},{1,0},{2,3},{3,2},{4,5},{5,4},{6,7},{7,6},{8,9},{9,8},{10,11... | collective-permute-start | bytes 1572872 | tf_op jit(solution)/shard_map/ppermute | solution.py:103
  31.1 12.0 %copy-start.2 = (bf16[4,128,512]{2,1,0:T(8,128)(2,1)}, bf16[4,128,512]{2,1,0:T(8,128)(2,1)S(1)}, u32[]{:S(2)}) copy-start(bf16[4,128,512]{2,1,0:T(8,128)(2,1)S(1)} %collective-permute-done.4.refs_2_) | copy-start | bytes 1572868
  31.1 6.8 %collective-permute-start.6 = (bf16[4,64,512]{2,1,0:T(8,128)(2,1)S(1)}, bf16[4,64,512]{2,1,0:T(8,128)(2,1)S(1)}, u32[]{:S(2)}, u32[]{:S(2)}) collective-permute-start(bf16[4,64,512]{2,1,0:T(8,128)(2,1)S(1)} %slice.9), channel_id=1, source_target_pairs={{0,2},{1,3},{2,0},{3,1},{4,6},{5,7},{6,4},{7,5},{8,10},{9,11},{10,... | collective-permute-start | bytes 786440 | tf_op jit(solution)/shard_map/ppermute | solution.py:103
  32.6 8.9 %collective-permute-start.9 = (bf16[4,128,512]{2,1,0:T(8,128)(2,1)S(1)}, bf16[4,128,512]{2,1,0:T(8,128)(2,1)S(1)}, u32[]{:S(2)}, u32[]{:S(2)}) collective-permute-start(bf16[4,128,512]{2,1,0:T(8,128)(2,1)S(1)} %collective-permute-done.4.refs_2_), channel_id=1, source_target_pairs={{0,1},{1,0},{2,3},{3,2},{4,5},{5,4},{6,7},{7,6},{8,9},{9,8},{10,11... | collective-permute-start | bytes 1572872 | tf_op jit(solution)/shard_map/ppermute | solution.py:103
  32.7 10.4 %copy-start.3 = (bf16[4,128,512]{2,1,0:T(8,128)(2,1)}, bf16[4,128,512]{2,1,0:T(8,128)(2,1)S(1)}, u32[]{:S(2)}) copy-start(bf16[4,128,512]{2,1,0:T(8,128)(2,1)S(1)} %collective-permute-done.3.refs_1_) | copy-start | bytes 1572868
  32.7 8.9 %collective-permute-start.8 = (bf16[4,128,512]{2,1,0:T(8,128)(2,1)S(1)}, bf16[4,128,512]{2,1,0:T(8,128)(2,1)S(1)}, u32[]{:S(2)}, u32[]{:S(2)}) collective-permute-start(bf16[4,128,512]{2,1,0:T(8,128)(2,1)S(1)} %collective-permute-done.3.refs_1_), channel_id=1, source_target_pairs={{0,1},{1,0},{2,3},{3,2},{4,5},{5,4},{6,7},{7,6},{8,9},{9,8},{10,11... | collective-permute-start | bytes 1572872 | tf_op jit(solution)/shard_map/ppermute | solution.py:103
  33.2 8.3 %collective-permute-start.5 = (bf16[4,64,512]{2,1,0:T(8,128)(2,1)S(1)}, bf16[4,64,512]{2,1,0:T(8,128)(2,1)S(1)}, u32[]{:S(2)}, u32[]{:S(2)}) collective-permute-start(bf16[4,64,512]{2,1,0:T(8,128)(2,1)S(1)} %slice.8), channel_id=1, source_target_pairs={{0,4},{4,0},{8,12},{12,8},{16,20},{20,16},{24,28},{28,24},{1,5},{5... | collective-permute-start | bytes 786440 | tf_op jit(solution)/shard_map/ppermute | solution.py:103
  37.9 5.2 %copy-start.18 = (bf16[4,64,512]{2,1,0:T(8,128)(2,1)}, bf16[4,64,512]{2,1,0:T(8,128)(2,1)S(1)}, u32[]{:S(2)}) copy-start(bf16[4,64,512]{2,1,0:T(8,128)(2,1)S(1)} %collective-permute-done.6.refs_4_) | copy-start | bytes 786436
  37.9 3.7 %collective-permute-start.11 = (bf16[4,64,512]{2,1,0:T(8,128)(2,1)S(1)}, bf16[4,64,512]{2,1,0:T(8,128)(2,1)S(1)}, u32[]{:S(2)}, u32[]{:S(2)}) collective-permute-start(bf16[4,64,512]{2,1,0:T(8,128)(2,1)S(1)} %collective-permute-done.6.refs_4_), channel_id=1, source_target_pairs={{0,1},{1,0},{2,3},{3,2},{4,5},{5,4},{6,7},{7,6},{8,9},{9,8},{10,11... | collective-permute-start | bytes 786440 | tf_op jit(solution)/shard_map/ppermute | solution.py:103
  41.5 1.6 copy-start.19
  41.5 1.5 collective-permute-start.10
  41.5 1.6 copy-start.11
  41.6 1.6 copy-start.12
  41.6 1.5 copy-start.13
  41.6 1.5 copy-start.20
  43.1 0.7 copy-start.21
  43.8 37.7 %copy-start.4 = (bf16[128,1,512]{2,0,1:T(8,128)(2,1)S(1)}, bf16[128,1,512]{2,0,1:T(8,128)(2,1)}, u32[]{:S(2)}) copy-start(bf16[128,1,512]{2,0,1:T(8,128)(2,1)} %param.7) | copy-start | bytes 393220
  56.0 25.5 %collective-permute-start.13 = (bf16[8,128,512]{2,1,0:T(8,128)(2,1)}, bf16[8,128,512]{2,1,0:T(8,128)(2,1)S(1)}, u32[]{:S(2)}, u32[]{:S(2)}) collective-permute-start(bf16[8,128,512]{2,1,0:T(8,128)(2,1)} %get-tuple-element.12.refs_0_), channel_id=1, source_target_pairs={{0,2},{1,3},{2,0},{3,1},{4,6},{5,7},{6,4},{7,5},{8,10},{9,11},{10,... | collective-permute-start | bytes 3145736 | tf_op jit(solution)/shard_map/ppermute | solution.py:103
  57.4 51.6 %collective-permute-start.12 = (bf16[8,128,512]{2,1,0:T(8,128)(2,1)}, bf16[8,128,512]{2,1,0:T(8,128)(2,1)S(1)}, u32[]{:S(2)}, u32[]{:S(2)}) collective-permute-start(bf16[8,128,512]{2,1,0:T(8,128)(2,1)} %get-tuple-element.12.refs_0_), channel_id=1, source_target_pairs={{0,1},{1,0},{2,3},{3,2},{4,5},{5,4},{6,7},{7,6},{8,9},{9,8},{10,11... | collective-permute-start | bytes 3145736 | tf_op jit(solution)/shard_map/ppermute | solution.py:103
  81.5 27.6 %copy-start.5 = (bf16[8,128,512]{2,1,0:T(8,128)(2,1)}, bf16[8,128,512]{2,1,0:T(8,128)(2,1)S(1)}, u32[]{:S(2)}) copy-start(bf16[8,128,512]{2,1,0:T(8,128)(2,1)S(1)} %collective-permute-done.13.refs_2_) | copy-start | bytes 3145732
  81.5 27.5 %collective-permute-start.14 = (bf16[8,128,512]{2,1,0:T(8,128)(2,1)S(1)}, bf16[8,128,512]{2,1,0:T(8,128)(2,1)S(1)}, u32[]{:S(2)}, u32[]{:S(2)}) collective-permute-start(bf16[8,128,512]{2,1,0:T(8,128)(2,1)S(1)} %collective-permute-done.13.refs_2_), channel_id=1, source_target_pairs={{0,1},{1,0},{2,3},{3,2},{4,5},{5,4},{6,7},{7,6},{8,9},{9,8},{10,11... | collective-permute-start | bytes 3145736 | tf_op jit(solution)/shard_map/ppermute | solution.py:103
  81.5 8.3 %collective-permute-start.17 = (bf16[1,128,512]{2,1,0:T(8,128)(2,1)S(1)}, bf16[1,128,512]{2,1,0:T(8,128)(2,1)S(1)}, u32[]{:S(2)}, u32[]{:S(2)}) collective-permute-start(bf16[1,128,512]{2,1,0:T(8,128)(2,1)S(1)} %bitcast.23), channel_id=1, source_target_pairs={{0,24},{4,28},{8,16},{12,20},{16,8},{20,12},{24,0},{28,4},{1,25},{... | collective-permute-start | bytes 393224 | tf_op jit(solution)/shard_map/ppermute | solution.py:103
  83.9 11.1 %collective-permute-start.16 = (bf16[1,128,512]{2,1,0:T(8,128)(2,1)S(1)}, bf16[1,128,512]{2,1,0:T(8,128)(2,1)S(1)}, u32[]{:S(2)}, u32[]{:S(2)}) collective-permute-start(bf16[1,128,512]{2,1,0:T(8,128)(2,1)S(1)} %bitcast.24), channel_id=1, source_target_pairs={{0,16},{4,20},{8,24},{12,28},{16,0},{20,4},{24,8},{28,12},{1,17},{... | collective-permute-start | bytes 393224 | tf_op jit(solution)/shard_map/ppermute | solution.py:103
  83.9 11.1 %collective-permute-start.15 = (bf16[1,128,512]{2,1,0:T(8,128)(2,1)S(1)}, bf16[1,128,512]{2,1,0:T(8,128)(2,1)S(1)}, u32[]{:S(2)}, u32[]{:S(2)}) collective-permute-start(bf16[1,128,512]{2,1,0:T(8,128)(2,1)S(1)} %bitcast.25), channel_id=1, source_target_pairs={{0,8},{4,12},{8,0},{12,4},{16,24},{20,28},{24,16},{28,20},{1,9},{5... | collective-permute-start | bytes 393224 | tf_op jit(solution)/shard_map/ppermute | solution.py:103
  95.0 14.1 %copy-start.1 = (bf16[4,128,512]{2,1,0:T(8,128)(2,1)}, bf16[4,128,512]{2,1,0:T(8,128)(2,1)S(1)}, u32[]{:S(2)}) copy-start(bf16[4,128,512]{2,1,0:T(8,128)(2,1)S(1)} %pad_maximum_fusion.1.refs_5_) | copy-start | bytes 1572868
  95.0 14.0 %collective-permute-start.18 = (bf16[4,128,512]{2,1,0:T(8,128)(2,1)S(1)}, bf16[4,128,512]{2,1,0:T(8,128)(2,1)S(1)}, u32[]{:S(2)}, u32[]{:S(2)}) collective-permute-start(bf16[4,128,512]{2,1,0:T(8,128)(2,1)S(1)} %pad_maximum_fusion.1.refs_5_), channel_id=1, source_target_pairs={{0,4},{4,0},{8,12},{12,8},{16,20},{20,16},{24,28},{28,24},{1,5},{5... | collective-permute-start | bytes 1572872 | tf_op jit(solution)/shard_map/ppermute | solution.py:103
  109.1 0.8 copy-start.14
  109.1 1.2 copy-start.6
  109.1 1.5 copy-start.7
  122.9 24.6 %collective-permute-start.20 = (bf16[8,128,512]{2,1,0:T(8,128)(2,1)}, bf16[8,128,512]{2,1,0:T(8,128)(2,1)S(1)}, u32[]{:S(2)}, u32[]{:S(2)}) collective-permute-start(bf16[8,128,512]{2,1,0:T(8,128)(2,1)} %get-tuple-element.15.refs_0_.refs_4_), channel_id=1, source_target_pairs={{0,2},{1,3},{2,0},{3,1},{4,6},{5,7},{6,4},{7,5},{8,10},{9,11},{10,... | collective-permute-start | bytes 3145736 | tf_op jit(solution)/shard_map/ppermute | solution.py:103
  124.4 44.4 %collective-permute-start.19 = (bf16[8,128,512]{2,1,0:T(8,128)(2,1)}, bf16[8,128,512]{2,1,0:T(8,128)(2,1)S(1)}, u32[]{:S(2)}, u32[]{:S(2)}) collective-permute-start(bf16[8,128,512]{2,1,0:T(8,128)(2,1)} %get-tuple-element.15.refs_0_.refs_4_), channel_id=1, source_target_pairs={{0,1},{1,0},{2,3},{3,2},{4,5},{5,4},{6,7},{7,6},{8,9},{9,8},{10,11... | collective-permute-start | bytes 3145736 | tf_op jit(solution)/shard_map/ppermute | solution.py:103
  147.6 21.1 %copy-start.8 = (bf16[8,128,512]{2,1,0:T(8,128)(2,1)}, bf16[8,128,512]{2,1,0:T(8,128)(2,1)S(1)}, u32[]{:S(2)}) copy-start(bf16[8,128,512]{2,1,0:T(8,128)(2,1)S(1)} %collective-permute-done.20.refs_2_) | copy-start | bytes 3145732
  147.6 21.2 %collective-permute-start.21 = (bf16[8,128,512]{2,1,0:T(8,128)(2,1)S(1)}, bf16[8,128,512]{2,1,0:T(8,128)(2,1)S(1)}, u32[]{:S(2)}, u32[]{:S(2)}) collective-permute-start(bf16[8,128,512]{2,1,0:T(8,128)(2,1)S(1)} %collective-permute-done.20.refs_2_), channel_id=1, source_target_pairs={{0,1},{1,0},{2,3},{3,2},{4,5},{5,4},{6,7},{7,6},{8,9},{9,8},{10,11... | collective-permute-start | bytes 3145736 | tf_op jit(solution)/shard_map/ppermute | solution.py:103
  150.4 18.3 %collective-permute-start.22 = (bf16[9,128,128]{2,1,0:T(8,128)(2,1)}, bf16[9,128,128]{2,1,0:T(8,128)(2,1)S(1)}, u32[]{:S(2)}, u32[]{:S(2)}) collective-permute-start(bf16[9,128,128]{2,1,0:T(8,128)(2,1)} %get-tuple-element.17), channel_id=1, source_target_pairs={{0,1},{1,0},{2,3},{3,2},{4,5},{5,4},{6,7},{7,6},{8,9},{9,8},{10,11... | collective-permute-start | bytes 884744 | tf_op jit(solution)/shard_map/ppermute | solution.py:103
  150.5 18.2 %collective-permute-start.23 = (bf16[9,128,128]{2,1,0:T(8,128)(2,1)}, bf16[9,128,128]{2,1,0:T(8,128)(2,1)S(1)}, u32[]{:S(2)}, u32[]{:S(2)}) collective-permute-start(bf16[9,128,128]{2,1,0:T(8,128)(2,1)} %get-tuple-element.18), channel_id=1, source_target_pairs={{0,2},{1,3},{2,0},{3,1},{4,6},{5,7},{6,4},{7,5},{8,10},{9,11},{10,... | collective-permute-start | bytes 884744 | tf_op jit(solution)/shard_map/ppermute | solution.py:103
  151.8 17.0 %collective-permute-start.24 = (bf16[9,128,128]{2,1,0:T(8,128)(2,1)}, bf16[9,128,128]{2,1,0:T(8,128)(2,1)S(1)}, u32[]{:S(2)}, u32[]{:S(2)}) collective-permute-start(bf16[9,128,128]{2,1,0:T(8,128)(2,1)} %get-tuple-element.19), channel_id=1, source_target_pairs={{0,3},{1,2},{2,1},{3,0},{4,7},{5,6},{6,5},{7,4},{8,11},{9,10},{10,... | collective-permute-start | bytes 884744 | tf_op jit(solution)/shard_map/ppermute | solution.py:103
  168.7 0.7 copy-start.15
  168.7 0.8 copy-start.16
  168.8 0.9 copy-start.17
  168.8 1.2 copy-start.9
  168.8 1.5 copy-start.10

commit v2 on v0

v2 whole, which is shorter than its diff:
```python
import functools

import jax
import jax.numpy as jnp
from jax import lax
from jax.experimental import pallas as pl
from jax.experimental.pallas import tpu as pltpu
from jax.sharding import PartitionSpec as P

BF = jnp.bfloat16
F32 = jnp.float32
VMEM_BYTES = 24 * 1024 * 1024


def extended(cells, sides, width):
    for axis, dim in sides:
        count = lax.axis_size(axis)
        ends = count - 1
        head = lax.slice_in_dim(cells, 0, width, axis=dim)
        tail = lax.slice_in_dim(cells, cells.shape[dim] - width, cells.shape[dim], axis=dim)
        cells = jnp.concatenate(
            [
                lax.ppermute(tail, axis, [(i, (i + 1) % count) for i in range(ends)]),
                cells,
                lax.ppermute(head, axis, [((i + 1) % count, i) for i in range(ends)]),
            ],
            axis=dim,
        )
    return cells


def shift_cols(value, offset):
    if offset == 0:
        return value
    if offset > 0:
        return jnp.pad(value[..., offset:], ((0, 0), (0, 0), (0, offset)))
    return jnp.pad(value[..., :offset], ((0, 0), (0, 0), (-offset, 0)))


def conv_forward(weight, padded, count):
    total = jnp.zeros((weight.shape[0], count, padded.shape[2]), F32)
    for a in range(3):
        for b in range(3):
            part = jnp.einsum(
                "oi,ihw->ohw", weight[:, a, b, :], padded[:, a : a + count, :], preferred_element_type=F32
            )
            total = total + shift_cols(part, b - 1)
    return total


def conv_backward(weight, padded, count):
    total = jnp.zeros((weight.shape[3], count, padded.shape[2]), F32)
    for a in range(3):
        for b in range(3):
            part = jnp.einsum(
                "oi,ohw->ihw", weight[:, a, b, :], padded[:, 2 - a : 2 - a + count, :], preferred_element_type=F32
            )
            total = total + shift_cols(part, 1 - b)
    return total


def weight_terms(grad, padded, count):
    rows_out = []
    for a in range(3):
        cols_out = []
        for b in range(3):
            moved = shift_cols(grad, 1 - b)
            cols_out.append(
                jnp.einsum("ohw,ihw->oi", moved, padded[:, a : a + count, :], preferred_element_type=F32)
            )
        rows_out.append(jnp.stack(cols_out, axis=1))
    return jnp.stack(rows_out, axis=1)


def with_rims(value):
    return extended(value, (("rows", 1),), 1)


def all_channels(value):
    return lax.all_gather(with_rims(value), "filt", axis=0, tiled=True)


def split_rows(features, first_weight, second_weight, out_grad):
    count = features.shape[1]
    padded_in = all_channels(features)
    pre_first = conv_forward(first_weight, padded_in, count)
    hidden = jnp.maximum(pre_first, 0.0).astype(BF)
    padded_hidden = all_channels(hidden)
    pre_second = conv_forward(second_weight, padded_hidden, count) + features.astype(F32)
    block_out = jnp.maximum(pre_second, 0.0).astype(BF)
    grad_second = jnp.where(pre_second > 0, out_grad.astype(F32), 0.0).astype(BF)
    rimmed_grad = with_rims(grad_second)
    terms = conv_backward(second_weight, rimmed_grad, count)
    hidden_grad = lax.psum_scatter(terms, "filt", scatter_dimension=0, tiled=True)
    grad_first = jnp.where(pre_first > 0, hidden_grad, 0.0).astype(BF)
    second_local = weight_terms(grad_second, padded_hidden, count)
    first_local = weight_terms(grad_first, padded_in, count)
    first_grad, second_grad = lax.psum((first_local, second_local), "rows")
    return (block_out, first_grad, second_grad)


def swap(value, axis, bits):
    return lax.ppermute(value, axis, [(i, i ^ bits) for i in range(lax.axis_size(axis))])


def block_at(index, size):
    return pl.ds(pl.multiple_of(index * size, size), size)


def join_cols(left, mid, right):
    w = mid.shape[1]
    col = lax.broadcasted_iota(jnp.int32, mid.shape, 1)
    out = mid + jnp.where(col == 0, 0.0, pltpu.roll(left, 1, 1))
    return out + jnp.where(col == w - 1, 0.0, pltpu.roll(right, w - 1, 1))


def window(weight, x, r, rows, lo):
    c, w = x.shape[1], x.shape[2]
    first, last = max(r - 1, 0), min(r + 1, rows - 1)
    lhs = weight[:, (first - r + 1) * c : (last - r + 2) * c]
    rhs = x[first - lo : last - lo + 1].reshape((last - first + 1) * c, w)
    return jnp.dot(lhs, rhs, preferred_element_type=F32)


def thirds(acc):
    own = acc.shape[0] // 3
    return acc[:own], acc[own : 2 * own], acc[2 * own :]


def widen(weight, wide):
    c = weight.shape[2]
    for a in range(3):
        wide[:, a * c : (a + 1) * c] = weight[a]


def gather_rows(full, places, pieces):
    own = pieces[0].shape[1]
    r0, f0 = lax.axis_index("rows"), lax.axis_index("filt")
    for piece, k, d, e, lo in places:
        size = pieces[piece].shape[1]
        at = pl.ds(pl.multiple_of((f0 ^ e) * own + lo, size), size)
        full[r0 ^ d, at] = pieces[piece][k]


def first_rows(part, full, wide, hidden, mask):
    for r in range(*part):
        pre = join_cols(*thirds(window(wide, full, r, full.shape[0], 0)))
        hidden[r - part[0]] = jnp.maximum(pre, 0.0).astype(BF)
        mask[r - part[0]] = jnp.where(pre > 0, 1.0, 0.0).astype(BF)


def store_early(early, value, n, y0):
    count = early.shape[0]

    @pl.when(y0 == n // count)
    def _():
        early[n % count] = value


def first_kernel(places, n_pieces, part, *refs):
    pieces, weight = refs[:n_pieces], refs[n_pieces]
    full, hidden, mask, wide = refs[n_pieces + 1 :]
    gather_rows(full, places, pieces)
    widen(weight, wide)
    first_rows(part, full, wide, hidden, mask)


def first_rest_kernel(part, full, weight, hidden, mask, wide):
    widen(weight, wide)
    first_rows(part, full, wide, hidden, mask)


def copy_pieces(layout, refs, put, lo, hi):
    y0, f0 = lax.axis_index("rows") & 1, lax.axis_index("filt")
    for (e, base, kind), ref in zip(layout, refs):
        count, own = ref.shape[:2]
        at = block_at(f0 ^ e, own)
        for n in range(count):
            if kind == "whole":
                if lo <= base + n < hi:
                    put(base + n, at, ref[n])
                continue
            half = y0 if kind == "own" else 1 - y0
            for y in (0, 1):
                if lo <= base + y * count + n < hi:

                    @pl.when(half == y)
                    def _(ref=ref, n=n, y=y, at=at):
                        put(base + y * count + n, at, ref[n])


def fill_rows(x, layout, refs, lo, hi):
    def put(r, at, value):
        x[r - lo, at] = value

    copy_pieces(layout, refs, put, lo, hi)


def second_kernel(grad_places, layout, n_grad, part, rows, *refs):
    pieces, refs = refs[: len(layout)], refs[len(layout) :]
    full, grads, weight, before = refs[0], refs[1 : 1 + n_grad], refs[1 + n_grad], refs[2 + n_grad]
    block_out, grad_second, *early, wide, x, grad = refs[3 + n_grad :]
    own = grad_second.shape[1]
    r0, f0 = lax.axis_index("rows"), lax.axis_index("filt")
    y0 = r0 & 1
    lo, hi = max(part[0] - 1, 0), min(part[1] + 1, rows)
    fill_rows(x, layout, pieces, lo, hi)
    for piece, k, d in grad_places:
        grad[r0 ^ d] = grads[piece][k]
    widen(weight, wide)
    block_out[...] = before[...]
    for r in range(*part):
        feat = full[r, block_at(f0, own)].astype(F32)
        pre = join_cols(*thirds(window(wide, x, r, rows, lo))) + feat
        value = jnp.where(pre > 0, grad[r].astype(F32), 0.0).astype(BF)
        grad_second[r - part[0]] = value
        if early:
            store_early(early[0], value, r - part[0], y0)

        @pl.when(r0 == r)
        def _(pre=pre):
            block_out[0] = jnp.maximum(pre, 0.0).astype(BF)


def turn_kernel(weight, mine, mate, over):
    taps, own = weight.shape[:2]
    f0, y0 = lax.axis_index("filt"), lax.axis_index("rows") & 1
    for t in range(taps):
        mine[t] = weight[t, :, block_at(f0, own)].T
        mate[t] = weight[t, :, block_at(f0 ^ 1, own)].T
        for e in (2, 3):
            block = weight[t, :, block_at(f0 ^ e, own)].T

            @pl.when(y0 == 0)
            def _(block=block, e=e, t=t):
                over[e - 2, t] = block[: own // 2]

            @pl.when(y0 == 1)
            def _(block=block, e=e, t=t):
                over[e - 2, t] = block[own // 2 :]


def back_kernel(layout, *refs):
    pieces = refs[: len(layout)]
    mine, mate, near2, far2, near3, far3, mask_a, mask_b, grad_first, wide, x = refs[len(layout) :]
    rows, own = grad_first.shape[:2]
    c = x.shape[1]
    f0, y0 = lax.axis_index("filt"), lax.axis_index("rows") & 1
    fill_rows(x, layout, pieces, 0, rows)
    for t in range(9):
        a, b = t // 3, t % 3

        def at(e, a=a):
            return pl.ds(pl.multiple_of((2 - a) * c + (f0 ^ e) * own, own), own)

        wide[b * own : (b + 1) * own, at(0)] = mine[t]
        wide[b * own : (b + 1) * own, at(1)] = mate[t]
        for e, near, far in ((2, near2, far2), (3, near3, far3)):
            for y, ref in ((y0, near), (1 - y0, far)):
                rows_at = pl.ds(pl.multiple_of(b * own + y * (own // 2), own // 2), own // 2)
                wide[rows_at, at(e)] = ref[0, t]
    cut = mask_a.shape[0]
    for r in range(rows):
        left, mid, right = thirds(window(wide, x, r, rows, 0))
        total = join_cols(right, mid, left)
        mask = mask_a[r] if r < cut else mask_b[r - cut]
        grad_first[r] = jnp.where(mask > 0, total, 0.0).astype(BF)


def fill_moved(grads, moved):
    own, w = grads[0].shape[1:]
    col = lax.broadcasted_iota(jnp.int32, (own, w), 1)
    for r, (grad, n) in enumerate((grad, n) for grad in grads for n in range(grad.shape[0])):
        g = grad[n].astype(F32)
        at = slice(r * w, (r + 1) * w)
        moved[0:own, at] = jnp.where(col == w - 1, 0.0, pltpu.roll(g, w - 1, 1)).astype(BF)
        moved[own : 2 * own, at] = grad[n]
        moved[2 * own :, at] = jnp.where(col == 0, 0.0, pltpu.roll(g, 1, 1)).astype(BF)


def sum_terms(moved, x, w, out):
    n = moved.shape[1]
    for a, (m, h) in enumerate([(slice(w, n), slice(0, n - w)), (slice(0, n),) * 2, (slice(0, n - w), slice(w, n))]):
        out[a] = lax.dot_general(moved[:, m], x[:, h], (((1,), (1,)), ((), ())), preferred_element_type=F32)


def second_terms_kernel(layout, *refs):
    pieces, (grad_a, grad_b, out, x, moved) = refs[: len(layout)], refs[len(layout) :]
    w = grad_a.shape[2]

    def put(r, at, value):
        x[at, r * w : (r + 1) * w] = value

    copy_pieces(layout, pieces, put, 0, moved.shape[1] // w)
    fill_moved([grad_a, grad_b], moved)
    sum_terms(moved, x, w, out)


def first_terms_kernel(n_grads, full, *refs):
    grads, (out, x, moved) = refs[:n_grads], refs[n_grads:]
    rows, _, w = full.shape
    for r in range(rows):
        x[:, r * w : (r + 1) * w] = full[r]
    fill_moved(grads, moved)
    sum_terms(moved, x, w, out)


VM = pl.BlockSpec(memory_space=pltpu.VMEM)


def call(kernel, ins, outs, scratch, flops, name):
    nbytes = sum(v.size * v.dtype.itemsize for v in ins) if flops else 0
    return pl.pallas_call(
        kernel,
        out_shape=[jax.ShapeDtypeStruct(s, d) for s, d in outs],
        in_specs=[VM] * len(ins),
        out_specs=[VM] * len(outs),
        scratch_shapes=scratch,
        compiler_params=pltpu.CompilerParams(vmem_limit_bytes=VMEM_BYTES),
        cost_estimate=pl.CostEstimate(flops=flops, bytes_accessed=nbytes, transcendentals=0),
        name=name,
    )(*ins)


def wave(values):
    return dict(zip(values, lax.optimization_barrier(tuple(values.values()))))


def over_x(value):
    return swap(value, "filt", 2)


def over_y(value):
    return swap(value, "rows", 1)


def to_mate(value):
    return swap(value, "filt", 1)


def all_rows(features, first_weight, second_weight, out_grad):
    c = first_weight.shape[3]
    own, _, w = features.shape
    rows = lax.axis_size("rows")
    half, cut = own // 2, rows // 2
    row_flops = 2 * 9 * own * c * w
    vm = pltpu.VMEM
    zs = tuple(range(2, rows, 2))
    wide = vm((3 * own, 3 * c), BF)
    w1 = jnp.transpose(first_weight, (1, 2, 0, 3)).reshape(3, 3 * own, c)
    w2 = jnp.transpose(second_weight, (1, 2, 0, 3))
    w2_wide = w2.reshape(3, 3 * own, c)
    feat = jnp.transpose(features, (1, 0, 2))
    ograd = jnp.transpose(out_grad, (1, 0, 2))

    def act(n):
        return ((n, own, w), BF)

    v = {f"z{d}": swap(feat, "rows", d) for d in zs}
    mine, mate, over = call(
        turn_kernel,
        [w2.reshape(9, own, c)],
        [((9, own, own), BF), ((9, own, own), BF), ((2, 9, half, own), BF)],
        [],
        row_flops * 2,
        "turn_weight",
    )
    v |= {"mine": mine, "mate": mate, "near": over_x(over)}
    v = wave(v)

    zs = (0, *zs)
    z4 = jnp.concatenate([feat] + [v[f"z{d}"] for d in zs[1:]], axis=0)
    v |= {f"g{d}": swap(ograd, "rows", d) for d in zs[1:]}
    v |= {"z4": z4, "x4": over_x(z4), "y4": over_y(z4)}
    v = wave(v)

    v |= {"lo": over_y(v["x4"][:, :half]), "hi": over_x(v["y4"][:, half:])}
    v |= {"m" + k: to_mate(v[k]) for k in ("z4", "x4", "y4")}
    v |= {"g4": jnp.concatenate([ograd] + [v[f"g{d}"] for d in zs[1:]], axis=0)}
    v = wave(v)
    v |= {"mlo": to_mate(v["lo"]), "mhi": to_mate(v["hi"])}
    v = wave(v)

    pieces, places = [], []
    for name, d, e, lo in (("z4", 0, 0, 0), ("x4", 0, 2, 0), ("y4", 1, 0, 0), ("lo", 1, 2, 0), ("hi", 1, 2, half)):
        for core in (0, 1):
            places += [(len(pieces), k, z ^ d, e ^ core, lo) for k, z in enumerate(zs)]
            pieces.append(v["m" * core + name])
    cut_a, cut = rows // 2 + 1, rows // 2
    full, h_a, mask_a = call(
        functools.partial(first_kernel, places, len(pieces), (0, cut_a)),
        pieces + [w1],
        [((rows, c, w), BF), act(cut_a), act(cut_a)],
        [wide],
        0,
        "first_conv_a",
    )
    h = {"a0": h_a, "a1": to_mate(h_a), "a2": over_x(h_a)}
    gy = over_y(v["g4"])
    h |= {"m1": to_mate(v["mate"]), "near3": to_mate(v["near"][1:])}
    h["b0"], mask_b = call(
        functools.partial(first_rest_kernel, (cut_a, rows)),
        [full, w1],
        [act(rows - cut_a)] * 2,
        [wide],
        0,
        "first_conv_b",
    )
    h = wave(h)
    h |= {"b2": over_x(h["b0"]), "b1": to_mate(h["b0"])}
    a3 = to_mate(h["a2"])
    layout_a = [(e, 0, "whole") for e in range(4)]
    spread_a = [h["a0"], h["a1"], h["a2"], a3]
    grads = [v["g4"], gy]
    grad_places = [(p, k, z ^ p) for p in (0, 1) for k, z in enumerate(zs)]

    def second(layout, spread, part, before, early, name):
        n = part[1] - part[0]
        return call(
            functools.partial(second_kernel, grad_places, layout, len(grads), part, rows),
            [*spread, full, *grads, w2_wide, before],
            [act(1), act(n)] + [act(n // 2)] * early,
            [wide, vm((min(part[1] + 1, rows) - max(part[0] - 1, 0), c, w), BF), vm((rows, own, w), BF)],
            0,
            name,
        )

    s = {"b0": h["b0"], "b1": h["b1"], "b2": h["b2"], "far": over_y(lax.optimization_barrier((v["near"], gy))[0])}
    s["out"], s["a0"], s["early"] = second(layout_a, spread_a, (0, cut), feat, 1, "second_conv_a")
    s = wave(s)
    layout_b = layout_a + [(e, cut_a, "whole") for e in range(4)]
    spread_b = spread_a + [s["b0"], s["b1"], s["b2"], to_mate(s["b2"])]
    t = {"a0": s["a0"], "s2": over_x(s["early"]), "a1": to_mate(s["a0"])}
    t["out"], t["b0"] = second(layout_b, spread_b, (cut, rows), s["out"], 0, "second_conv_b")
    t = wave(t)
    t |= {"b2": over_x(t["b0"]), "t2": over_y(t["s2"]), "b1": to_mate(t["b0"]), "s3": to_mate(t["s2"])}
    t |= {"far3": to_mate(s["far"][1:])}
    (t["grad"],) = call(
        functools.partial(second_terms_kernel, layout_b),
        [*spread_b, t["a0"], t["b0"]],
        [((3, 3 * own, c), F32)],
        [vm((c, rows * w), BF), vm((3 * own, rows * w), BF)],
        row_flops * rows,
        "second_terms",
    )
    t = wave(t)
    t |= {"b3": to_mate(t["b2"]), "t3": to_mate(t["t2"])}
    t = wave(t)
    layout = [(e, 0, "whole") for e in (0, 1)] + [(e, cut, "whole") for e in range(4)]
    layout += [(e, 0, kind) for kind in ("own", "other") for e in (2, 3)]
    turned = [v["mine"], h["m1"], v["near"][:1], s["far"][:1], h["near3"], t["far3"]]
    (grad_first,) = call(
        functools.partial(back_kernel, layout),
        [*(t[k] for k in ("a0", "a1", "b0", "b1", "b2", "b3", "s2", "s3", "t2", "t3")), *turned, mask_a, mask_b],
        [act(rows)],
        [wide, vm((rows, c, w), BF)],
        row_flops * rows,
        "hidden_grad",
    )
    (first_grad,) = call(
        functools.partial(first_terms_kernel, 1),
        [full, grad_first],
        [((3, 3 * own, c), F32)],
        [vm((c, rows * w), BF), vm((3 * own, rows * w), BF)],
        row_flops * rows,
        "first_terms",
    )

    def as_weight(value):
        return jnp.transpose(value.reshape(3, 3, own, c), (2, 0, 1, 3))

    return jnp.transpose(t["out"], (1, 0, 2)), as_weight(first_grad), as_weight(t["grad"])


def solution(mesh):
    in_specs = (
        P("filt", "rows", None),
        P("filt", None, None, None),
        P("filt", None, None, None),
        P("filt", "rows", None),
    )
    out_specs = (P("filt", "rows", None), P("filt", None, None, None), P("filt", None, None, None))

    def per_device(features, first_weight, second_weight, out_grad):
        rows, filt = mesh.shape["rows"], mesh.shape["filt"]
        small = rows == 8 and filt == 4 and features.shape[1] == 1 and features.shape[0] % 32 == 0
        plan = all_rows if small else split_rows
        return plan(features, first_weight, second_weight, out_grad)

    return jax.shard_map(per_device, mesh=mesh, in_specs=in_specs, out_specs=out_specs, check_vma=False)
```

time: 318 us -> 117 us (0.37)
  waiting for transfers between devices: 244 us -> 59 us
  Pallas kernels: 0 us -> 32.3 us
  matrix products: 27.1 us -> 0 us
  between operations: 14.2 us -> 0.8 us
  other arithmetic: 7.08 us -> 0.14 us
  local copies, waits for them, and re-layouts: 7.95 us -> 1.37 us
  starting transfers between devices: 16.9 us -> 23.2 us
    psum x1 -> x0, waiting for transfers between devices: 168 us -> none  [per_device(): first_grad, second_grad = lax.psum((first_local, second_local), 'rows')]
    ppermute x6 -> x35, waiting for transfers between devices: 14.8 us -> 59 us  [swap(): lax.ppermute(value, axis, [(i, i ^ bits) for i in range(lax.axis_size(axi...]
    all_gather x2 -> x0, waiting for transfers between devices: 39.9 us -> none  [all_channels(): return lax.all_gather(with_rims(value), 'filt', axis=0, tiled=True)]
    pallas_call x0 -> x8, Pallas kernels: none -> 32.3 us  [call(): pl.pallas_call(kernel, out_shape=[jax.ShapeDtypeStruct(s, d) for s, d in...]
    dot_general x45 -> x0, matrix products: 27.1 us -> none  [the longest x18 18.3 us: conv_forward(): jnp.einsum('oi,ihw->ohw', weight[:, a, b, :], padded[:, a:a + count, :],...]
    reduce_scatter x1 -> x0, waiting for transfers between devices: 21.2 us -> none  [per_device(): lax.psum_scatter(terms, 'filt', scatter_dimension=0, tiled=True)]
    ppermute x6 -> x35, starting transfers between devices: 16.7 us -> 23.2 us  [swap(): lax.ppermute(value, axis, [(i, i ^ bits) for i in range(lax.axis_size(axi...]
    unnamed x21 -> x10, local copies, waits for them, and re-layouts: 7.39 us -> 1.29 us
  transfers between devices with their start and end apart: 10 -> 35, of which waited for: 10 -> 17; matrix products, arithmetic and copies ran while one was open for 2% -> 0% of each run, Pallas kernels for 0% -> 14%
where the time goes in v2:
time: 117 us
  waiting for transfers between devices  59 us (50%)
  Pallas kernels  32.3 us (28%)
  starting transfers between devices  23.2 us (20%)
  local copies, waits for them, and re-layouts  1.37 us (1%)
    ppermute x35, waiting for transfers between devices, swap(): lax.ppermute(value, axis, [(i, i ^ bits) for i in range(lax.axis_size(axi...  59 us
    pallas_call x8, Pallas kernels, call(): pl.pallas_call(kernel, out_shape=[jax.ShapeDtypeStruct(s, d) for s, d in...  32.3 us
    ppermute x35, starting transfers between devices, swap(): lax.ppermute(value, axis, [(i, i ^ bits) for i in range(lax.axis_size(axi...  23.2 us
  transfers between devices with their start and end apart: 35, of which 17 were waited for; matrix products, arithmetic and copies ran while one was open for 0% of the time, Pallas kernels for 14%

profile of v2, /device:TPU:0, one launch (start us, length us, event | category | flops | bytes accessed | tf_op | source)
XLA Modules:
  0.0 116.7 jit_solution(17321832194333115202)
XLA Ops:
  0.6 0.0 copy-start
  0.6 1.3 %copy-done = bf16[128,3,3,512]{3,0,2,1:T(8,128)(2,1)S(1)} copy-done((bf16[128,3,3,512]{3,0,2,1:T(8,128)(2,1)S(1)}, bf16[128,3,3,512]{3,0,2,1:T(8,128)(2,1)}, u32[]{:S(2)}) %copy-start) | copy-done | bytes 1179672
  1.9 1.4 %turn_weight.1 = (bf16[9,128,128]{2,1,0:T(8,128)(2,1)S(1)}, bf16[9,128,128]{2,1,0:T(8,128)(2,1)S(1)}, bf16[2,9,64,128]{3,2,1,0:T(8,128)(2,1)S(1)}) custom-call(bf16[9,128,512]{2,1,0:T(8,128)(2,1)S(1)} %bitcast.17), custom_call_target="tpu_custom_call" | custom-call | flops 1207959552 | bytes 1179648 | tf_op jit(solution)/shard_map/turn_weight/pallas_call | solution.py:313
  3.3 0.0 copy-start.2
  3.3 3.0 %collective-permute-start.3 = (bf16[2,9,64,128]{3,2,1,0:T(8,128)(2,1)S(1)}, bf16[2,9,64,128]{3,2,1,0:T(8,128)(2,1)S(1)}, u32[]{:S(2)}, u32[]{:S(2)}) collective-permute-start(bf16[2,9,64,128]{3,2,1,0:T(8,128)(2,1)S(1)} %get-tuple-element.102), channel_id=1, source_target_pairs={{0,2},{1,3},{2,0},{3,1},{4,6},{5,7},{6,4},{7,5},{8,10},{9,11},{10,... | collective-permute-start | bytes 884744 | tf_op jit(solution)/shard_map/ppermute | solution.py:103
  6.3 3.6 %collective-permute-start.2 = (bf16[1,128,512]{2,1,0:T(8,128)(2,1)S(1)}, bf16[1,128,512]{2,1,0:T(8,128)(2,1)S(1)}, u32[]{:S(2)}, u32[]{:S(2)}) collective-permute-start(bf16[1,128,512]{2,1,0:T(8,128)(2,1)S(1)} %bitcast.22), channel_id=1, source_target_pairs={{0,24},{4,28},{8,16},{12,20},{16,8},{20,12},{24,0},{28,4},{1,25},{... | collective-permute-start | bytes 393224 | tf_op jit(solution)/shard_map/ppermute | solution.py:103
  9.9 0.0 collective-permute-start.1
  9.9 0.8 collective-permute-start
  10.7 3.9 %collective-permute-done.2 = bf16[1,128,512]{2,1,0:T(8,128)(2,1)S(1)} collective-permute-done((bf16[1,128,512]{2,1,0:T(8,128)(2,1)S(1)}, bf16[1,128,512]{2,1,0:T(8,128)(2,1)S(1)}, u32[]{:S(2)}, u32[]{:S(2)}) %collective-permute-start.2) | collective-permute-done | bytes 131104 | tf_op jit(solution)/shard_map/ppermute | solution.py:103
  14.6 6.1 %collective-permute-done.1 = bf16[1,128,512]{2,1,0:T(8,128)(2,1)S(1)} collective-permute-done((bf16[1,128,512]{2,1,0:T(8,128)(2,1)S(1)}, bf16[1,128,512]{2,1,0:T(8,128)(2,1)S(1)}, u32[]{:S(2)}, u32[]{:S(2)}) %collective-permute-start.1) | collective-permute-done | bytes 131104 | tf_op jit(solution)/shard_map/ppermute | solution.py:103
  20.7 0.0 collective-permute-done
  20.7 0.1 pad_maximum_fusion.refs_0_
  20.8 1.6 %collective-permute-start.8 = (bf16[4,128,512]{2,1,0:T(8,128)(2,1)S(1)}, bf16[4,128,512]{2,1,0:T(8,128)(2,1)S(1)}, u32[]{:S(2)}, u32[]{:S(2)}) collective-permute-start(bf16[4,128,512]{2,1,0:T(8,128)(2,1)S(1)} %pad_maximum_fusion.refs_0_), channel_id=1, source_target_pairs={{0,4},{4,0},{8,12},{12,8},{16,20},{20,16},{24,28},{28,24},{1,5},{5... | collective-permute-start | bytes 1572872 | tf_op jit(solution)/shard_map/ppermute | solution.py:103
  22.4 0.5 collective-permute-start.7
  23.0 2.5 %collective-permute-start.6 = (bf16[1,128,512]{2,1,0:T(8,128)(2,1)S(1)}, bf16[1,128,512]{2,1,0:T(8,128)(2,1)S(1)}, u32[]{:S(2)}, u32[]{:S(2)}) collective-permute-start(bf16[1,128,512]{2,1,0:T(8,128)(2,1)S(1)} %bitcast.27), channel_id=1, source_target_pairs={{0,24},{4,28},{8,16},{12,20},{16,8},{20,12},{24,0},{28,4},{1,25},{... | collective-permute-start | bytes 393224 | tf_op jit(solution)/shard_map/ppermute | solution.py:103
  25.4 1.9 %collective-permute-start.4 = (bf16[1,128,512]{2,1,0:T(8,128)(2,1)S(1)}, bf16[1,128,512]{2,1,0:T(8,128)(2,1)S(1)}, u32[]{:S(2)}, u32[]{:S(2)}) collective-permute-start(bf16[1,128,512]{2,1,0:T(8,128)(2,1)S(1)} %bitcast.29), channel_id=1, source_target_pairs={{0,8},{4,12},{8,0},{12,4},{16,24},{20,28},{24,16},{28,20},{1,9},{5... | collective-permute-start | bytes 393224 | tf_op jit(solution)/shard_map/ppermute | solution.py:103
  27.3 3.8 %collective-permute-done.6 = bf16[1,128,512]{2,1,0:T(8,128)(2,1)S(1)} collective-permute-done((bf16[1,128,512]{2,1,0:T(8,128)(2,1)S(1)}, bf16[1,128,512]{2,1,0:T(8,128)(2,1)S(1)}, u32[]{:S(2)}, u32[]{:S(2)}) %collective-permute-start.6) | collective-permute-done | bytes 131104 | tf_op jit(solution)/shard_map/ppermute | solution.py:103
  31.2 4.4 %collective-permute-done.5 = bf16[1,128,512]{2,1,0:T(8,128)(2,1)S(1)} collective-permute-done((bf16[1,128,512]{2,1,0:T(8,128)(2,1)S(1)}, bf16[1,128,512]{2,1,0:T(8,128)(2,1)S(1)}, u32[]{:S(2)}, u32[]{:S(2)}) %collective-permute-start.5) | collective-permute-done | bytes 131104 | tf_op jit(solution)/shard_map/ppermute | solution.py:103
  35.6 0.0 collective-permute-done.4
  35.6 0.0 collective-permute-done.8.refs_4_
  35.6 0.0 collective-permute-done.7.refs_2_
  35.6 0.1 collective-permute-start.11
  35.7 0.5 collective-permute-start.12
  36.2 0.1 collective-permute-start.13
  36.3 1.6 %collective-permute-start.10 = (bf16[4,64,512]{2,1,0:T(8,128)(2,1)S(1)}, bf16[4,64,512]{2,1,0:T(8,128)(2,1)S(1)}, u32[]{:S(2)}, u32[]{:S(2)}) collective-permute-start(bf16[4,64,512]{2,1,0:T(8,128)(2,1)S(1)} %slice.19), channel_id=1, source_target_pairs={{0,2},{1,3},{2,0},{3,1},{4,6},{5,7},{6,4},{7,5},{8,10},{9,11},{10,... | collective-permute-start | bytes 786440 | tf_op jit(solution)/shard_map/ppermute | solution.py:103
  37.9 0.5 collective-permute-start.9
  38.3 0.1 pad_maximum_fusion.1.refs_5_.refs_9_
  38.4 6.6 %collective-permute-done.10.refs_8_ = bf16[4,64,512]{2,1,0:T(8,128)(2,1)S(1)} collective-permute-done((bf16[4,64,512]{2,1,0:T(8,128)(2,1)S(1)}, bf16[4,64,512]{2,1,0:T(8,128)(2,1)S(1)}, u32[]{:S(2)}, u32[]{:S(2)}) %collective-permute-start.10) | collective-permute-done | bytes 262176 | tf_op jit(solution)/shard_map/ppermute | solution.py:103
  45.0 1.2 %collective-permute-done.9.refs_6_ = bf16[4,64,512]{2,1,0:T(8,128)(2,1)S(1)} collective-permute-done((bf16[4,64,512]{2,1,0:T(8,128)(2,1)S(1)}, bf16[4,64,512]{2,1,0:T(8,128)(2,1)S(1)}, u32[]{:S(2)}, u32[]{:S(2)}) %collective-permute-start.9) | collective-permute-done | bytes 262176 | tf_op jit(solution)/shard_map/ppermute | solution.py:103
  46.3 0.1 collective-permute-start.14
  46.3 0.5 collective-permute-start.15
  46.8 1.0 collective-permute-done.14.refs_7_
  47.9 0.4 collective-permute-done.15.refs_9_
  48.2 3.4 %first_conv_a.1 = (bf16[8,512,512]{2,1,0:T(8,128)(2,1)S(1)}, bf16[5,128,512]{2,1,0:T(8,128)(2,1)S(1)}, bf16[5,128,512]{2,1,0:T(8,128)(2,1)S(1)}) custom-call(bf16[4,128,512]{2,1,0:T(8,128)(2,1)S(1)} %pad_maximum_fusion.refs_0_, bf16[4,128,512]{2,1,0:T(8,128)(2,1)S(1)} %collective-permute-done.11.refs_1_, ...), custom_call_target="tpu_custom_call" | custom-call | tf_op jit(solution)/shard_map/first_conv_a/pallas_call | solution.py:313
  51.6 0.6 collective-permute-start.17
  52.2 0.5 collective-permute-start.18
  52.8 0.5 collective-permute-start.22
  53.2 0.1 collective-permute-start.19
  53.3 0.0 copy-start.1
  53.3 1.9 %first_conv_b.1 = (bf16[3,128,512]{2,1,0:T(8,128)(2,1)S(1)}, bf16[3,128,512]{2,1,0:T(8,128)(2,1)S(1)}) custom-call(bf16[8,512,512]{2,1,0:T(8,128)(2,1)S(1)} %get-tuple-element.143.full.refs_4_.refs_8_, bf16[3,384,512]{2,1,0:T(8,128)(2,1)S(1)} %bitcast.21), custom_call_target="tpu_custom_call" | custom-call | tf_op jit(solution)/shard_map/first_conv_b/pallas_call | solution.py:313
  55.3 13.2 %collective-permute-done.17.refs_2_ = bf16[5,128,512]{2,1,0:T(8,128)(2,1)S(1)} collective-permute-done((bf16[5,128,512]{2,1,0:T(8,128)(2,1)S(1)}, bf16[5,128,512]{2,1,0:T(8,128)(2,1)S(1)}, u32[]{:S(2)}, u32[]{:S(2)}) %collective-permute-start.17) | collective-permute-done | bytes 655392 | tf_op jit(solution)/shard_map/ppermute | solution.py:103
  68.5 0.5 collective-permute-start.21
  69.0 0.2 collective-permute-start.20
  69.3 0.5 collective-permute-start.23
  69.7 0.9 collective-permute-done.24.refs_3_
  70.6 3.6 %second_conv_a.1 = (bf16[1,128,512]{2,1,0:T(8,128)(2,1)S(1)}, bf16[4,128,512]{2,1,0:T(8,128)(2,1)S(1)}, bf16[2,128,512]{2,1,0:T(8,128)(2,1)S(1)}) custom-call(bf16[5,128,512]{2,1,0:T(8,128)(2,1)S(1)} %get-tuple-element.148.refs_0_, bf16[5,128,512]{2,1,0:T(8,128)(2,1)S(1)} %collective-permute-done.16.refs_1_, ...), custom_call_target="tpu_custom_call" | custom-call | tf_op jit(solution)/shard_map/second_conv_a/pallas_call | solution.py:313
  74.2 4.3 %collective-permute-done.23 = bf16[2,9,64,128]{3,2,1,0:T(8,128)(2,1)S(1)} collective-permute-done((bf16[2,9,64,128]{3,2,1,0:T(8,128)(2,1)S(1)}, bf16[2,9,64,128]{3,2,1,0:T(8,128)(2,1)S(1)}, u32[]{:S(2)}, u32[]{:S(2)}) %collective-permute-start.23) | collective-permute-done | bytes 294944 | tf_op jit(solution)/shard_map/ppermute | solution.py:103
  78.5 1.6 %collective-permute-done.21.refs_6_ = bf16[3,128,512]{2,1,0:T(8,128)(2,1)S(1)} collective-permute-done((bf16[3,128,512]{2,1,0:T(8,128)(2,1)S(1)}, bf16[3,128,512]{2,1,0:T(8,128)(2,1)S(1)}, u32[]{:S(2)}, u32[]{:S(2)}) %collective-permute-start.21) | collective-permute-done | bytes 393248 | tf_op jit(solution)/shard_map/ppermute | solution.py:103
  80.0 0.5 collective-permute-start.27
  80.5 0.5 collective-permute-start.25
  81.1 1.4 %collective-permute-done.27.refs_7_ = bf16[3,128,512]{2,1,0:T(8,128)(2,1)S(1)} collective-permute-done((bf16[3,128,512]{2,1,0:T(8,128)(2,1)S(1)}, bf16[3,128,512]{2,1,0:T(8,128)(2,1)S(1)}, u32[]{:S(2)}, u32[]{:S(2)}) %collective-permute-start.27) | collective-permute-done | bytes 393248 | tf_op jit(solution)/shard_map/ppermute | solution.py:103
  82.5 4.4 %second_conv_b.1 = (bf16[1,128,512]{2,1,0:T(8,128)(2,1)}, bf16[4,128,512]{2,1,0:T(8,128)(2,1)S(1)}) custom-call(bf16[5,128,512]{2,1,0:T(8,128)(2,1)S(1)} %get-tuple-element.148.refs_0_, bf16[5,128,512]{2,1,0:T(8,128)(2,1)S(1)} %collective-permute-done.16.refs_1_, bf16[5,128,512]{2,1,0:T(8,128)(2,1)S(1)} %collective-permute-done.17.refs_2_, ...), custom_call_target="tpu_custom_call" | custom-call | tf_op jit(solution)/shard_map/second_conv_b/pallas_call | solution.py:313
  86.9 1.9 %collective-permute-done.25.refs_6_ = bf16[2,128,512]{2,1,0:T(8,128)(2,1)S(1)} collective-permute-done((bf16[2,128,512]{2,1,0:T(8,128)(2,1)S(1)}, bf16[2,128,512]{2,1,0:T(8,128)(2,1)S(1)}, u32[]{:S(2)}, u32[]{:S(2)}) %collective-permute-start.25) | collective-permute-done | bytes 262176 | tf_op jit(solution)/shard_map/ppermute | solution.py:103
  88.8 0.5 collective-permute-start.28
  89.3 0.3 collective-permute-start.32
  89.6 0.3 collective-permute-start.31
  89.9 0.5 collective-permute-start.29
  90.4 6.4 %second_terms.1 = f32[3,384,512]{2,1,0:T(8,128)} custom-call(bf16[5,128,512]{2,1,0:T(8,128)(2,1)S(1)} %get-tuple-element.148.refs_0_, bf16[5,128,512]{2,1,0:T(8,128)(2,1)S(1)} %collective-permute-done.16.refs_1_, bf16[5,128,512]{2,1,0:T(8,128)(2,1)S(1)} %collective-permute-done.17.refs_2_, bf16[5,128,512]{2,1,0:T(8,128)(2,1)S(1)} %collective-permute-done.24.refs_3_, ...), custom_call_target="tpu_custom_call" | custom-call | flops 4831838208 | bytes 5242880 | tf_op jit(solution)/shard_map/second_terms/pallas_call | solution.py:313
  96.7 1.6 %collective-permute-done.29.refs_8_ = bf16[2,128,512]{2,1,0:T(8,128)(2,1)S(1)} collective-permute-done((bf16[2,128,512]{2,1,0:T(8,128)(2,1)S(1)}, bf16[2,128,512]{2,1,0:T(8,128)(2,1)S(1)}, u32[]{:S(2)}, u32[]{:S(2)}) %collective-permute-start.29) | collective-permute-done | bytes 262176 | tf_op jit(solution)/shard_map/ppermute | solution.py:103
  98.3 4.8 %collective-permute-done.28.refs_4_ = bf16[4,128,512]{2,1,0:T(8,128)(2,1)S(1)} collective-permute-done((bf16[4,128,512]{2,1,0:T(8,128)(2,1)S(1)}, bf16[4,128,512]{2,1,0:T(8,128)(2,1)S(1)}, u32[]{:S(2)}, u32[]{:S(2)}) %collective-permute-start.28) | collective-permute-done | bytes 524320 | tf_op jit(solution)/shard_map/ppermute | solution.py:103
  103.1 0.5 collective-permute-start.34
  103.6 1.8 %collective-permute-done.34.refs_9_ = bf16[2,128,512]{2,1,0:T(8,128)(2,1)S(1)} collective-permute-done((bf16[2,128,512]{2,1,0:T(8,128)(2,1)S(1)}, bf16[2,128,512]{2,1,0:T(8,128)(2,1)S(1)}, u32[]{:S(2)}, u32[]{:S(2)}) %collective-permute-start.34) | collective-permute-done | bytes 262176 | tf_op jit(solution)/shard_map/ppermute | solution.py:103
  105.4 5.3 %hidden_grad.1.refs_0_ = bf16[8,128,512]{2,1,0:T(8,128)(2,1)S(1)} custom-call(bf16[4,128,512]{2,1,0:T(8,128)(2,1)S(1)} %get-tuple-element.180.refs_8_.refs_0_, bf16[4,128,512]{2,1,0:T(8,128)(2,1)S(1)} %collective-permute-done.26.refs_1_, bf16[4,128,512]{2,1,0:T(8,128)(2,1)S(1)} %get-tuple-element.182.refs_9_.refs_2_, ...), custom_call_target="tpu_custom_call" | custom-call | flops 4831838208 | bytes 6422528 | tf_op jit(solution)/shard_map/hidden_grad/pallas_call | solution.py:313
  110.7 6.1 %first_terms.1 = f32[3,384,512]{2,1,0:T(8,128)} custom-call(bf16[8,512,512]{2,1,0:T(8,128)(2,1)S(1)} %get-tuple-element.143.full.refs_4_.refs_8_, bf16[8,128,512]{2,1,0:T(8,128)(2,1)S(1)} %hidden_grad.1.refs_0_), custom_call_target="tpu_custom_call" | custom-call | flops 4831838208 | bytes 5242880 | tf_op jit(solution)/shard_map/first_terms/pallas_call | solution.py:313
  (30 shorter events, 0.1 us)
Async XLA Ops:
  0.6 1.3 %copy-start = (bf16[128,3,3,512]{3,0,2,1:T(8,128)(2,1)S(1)}, bf16[128,3,3,512]{3,0,2,1:T(8,128)(2,1)}, u32[]{:S(2)}) copy-start(bf16[128,3,3,512]{3,0,2,1:T(8,128)(2,1)} %param.6) | copy-start | bytes 3538948
  1.9 4.4 %copy-start.3 = (bf16[128,1,512]{2,0,1:T(8,128)(2,1)S(1)}, bf16[128,1,512]{2,0,1:T(8,128)(2,1)}, u32[]{:S(2)}) copy-start(bf16[128,1,512]{2,0,1:T(8,128)(2,1)} %param.4) | copy-start | bytes 393220
  1.9 21.0 %copy-start.4 = (bf16[128,1,512]{2,0,1:T(8,128)(2,1)S(1)}, bf16[128,1,512]{2,0,1:T(8,128)(2,1)}, u32[]{:S(2)}) copy-start(bf16[128,1,512]{2,0,1:T(8,128)(2,1)} %param.7) | copy-start | bytes 393220
  3.3 45.0 %copy-start.2 = (bf16[128,3,3,512]{3,0,2,1:T(8,128)(2,1)S(1)}, bf16[128,3,3,512]{3,0,2,1:T(8,128)(2,1)}, u32[]{:S(2)}) copy-start(bf16[128,3,3,512]{3,0,2,1:T(8,128)(2,1)} %param.5) | copy-start | bytes 3538948
  3.3 17.4 %collective-permute-start.3 = (bf16[2,9,64,128]{3,2,1,0:T(8,128)(2,1)S(1)}, bf16[2,9,64,128]{3,2,1,0:T(8,128)(2,1)S(1)}, u32[]{:S(2)}, u32[]{:S(2)}) collective-permute-start(bf16[2,9,64,128]{3,2,1,0:T(8,128)(2,1)S(1)} %get-tuple-element.102), channel_id=1, source_target_pairs={{0,2},{1,3},{2,0},{3,1},{4,6},{5,7},{6,4},{7,5},{8,10},{9,11},{10,... | collective-permute-start | bytes 884744 | tf_op jit(solution)/shard_map/ppermute | solution.py:103
  6.3 8.3 %collective-permute-start.2 = (bf16[1,128,512]{2,1,0:T(8,128)(2,1)S(1)}, bf16[1,128,512]{2,1,0:T(8,128)(2,1)S(1)}, u32[]{:S(2)}, u32[]{:S(2)}) collective-permute-start(bf16[1,128,512]{2,1,0:T(8,128)(2,1)S(1)} %bitcast.22), channel_id=1, source_target_pairs={{0,24},{4,28},{8,16},{12,20},{16,8},{20,12},{24,0},{28,4},{1,25},{... | collective-permute-start | bytes 393224 | tf_op jit(solution)/shard_map/ppermute | solution.py:103
  9.9 10.8 %collective-permute-start.1 = (bf16[1,128,512]{2,1,0:T(8,128)(2,1)S(1)}, bf16[1,128,512]{2,1,0:T(8,128)(2,1)S(1)}, u32[]{:S(2)}, u32[]{:S(2)}) collective-permute-start(bf16[1,128,512]{2,1,0:T(8,128)(2,1)S(1)} %bitcast.23), channel_id=1, source_target_pairs={{0,16},{4,20},{8,24},{12,28},{16,0},{20,4},{24,8},{28,12},{1,17},{... | collective-permute-start | bytes 393224 | tf_op jit(solution)/shard_map/ppermute | solution.py:103
  9.9 10.8 %collective-permute-start = (bf16[1,128,512]{2,1,0:T(8,128)(2,1)S(1)}, bf16[1,128,512]{2,1,0:T(8,128)(2,1)S(1)}, u32[]{:S(2)}, u32[]{:S(2)}) collective-permute-start(bf16[1,128,512]{2,1,0:T(8,128)(2,1)S(1)} %bitcast.24), channel_id=1, source_target_pairs={{0,8},{4,12},{8,0},{12,4},{16,24},{20,28},{24,16},{28,20},{1,9},{5... | collective-permute-start | bytes 393224 | tf_op jit(solution)/shard_map/ppermute | solution.py:103
  20.8 14.8 %collective-permute-start.8 = (bf16[4,128,512]{2,1,0:T(8,128)(2,1)S(1)}, bf16[4,128,512]{2,1,0:T(8,128)(2,1)S(1)}, u32[]{:S(2)}, u32[]{:S(2)}) collective-permute-start(bf16[4,128,512]{2,1,0:T(8,128)(2,1)S(1)} %pad_maximum_fusion.refs_0_), channel_id=1, source_target_pairs={{0,4},{4,0},{8,12},{12,8},{16,20},{20,16},{24,28},{28,24},{1,5},{5... | collective-permute-start | bytes 1572872 | tf_op jit(solution)/shard_map/ppermute | solution.py:103
  22.4 13.2 %collective-permute-start.7 = (bf16[4,128,512]{2,1,0:T(8,128)(2,1)S(1)}, bf16[4,128,512]{2,1,0:T(8,128)(2,1)S(1)}, u32[]{:S(2)}, u32[]{:S(2)}) collective-permute-start(bf16[4,128,512]{2,1,0:T(8,128)(2,1)S(1)} %pad_maximum_fusion.refs_0_), channel_id=1, source_target_pairs={{0,2},{1,3},{2,0},{3,1},{4,6},{5,7},{6,4},{7,5},{8,10},{9,11},{10,... | collective-permute-start | bytes 1572872 | tf_op jit(solution)/shard_map/ppermute | solution.py:103
  23.0 8.2 %collective-permute-start.6 = (bf16[1,128,512]{2,1,0:T(8,128)(2,1)S(1)}, bf16[1,128,512]{2,1,0:T(8,128)(2,1)S(1)}, u32[]{:S(2)}, u32[]{:S(2)}) collective-permute-start(bf16[1,128,512]{2,1,0:T(8,128)(2,1)S(1)} %bitcast.27), channel_id=1, source_target_pairs={{0,24},{4,28},{8,16},{12,20},{16,8},{20,12},{24,0},{28,4},{1,25},{... | collective-permute-start | bytes 393224 | tf_op jit(solution)/shard_map/ppermute | solution.py:103
  25.4 10.2 %collective-permute-start.5 = (bf16[1,128,512]{2,1,0:T(8,128)(2,1)S(1)}, bf16[1,128,512]{2,1,0:T(8,128)(2,1)S(1)}, u32[]{:S(2)}, u32[]{:S(2)}) collective-permute-start(bf16[1,128,512]{2,1,0:T(8,128)(2,1)S(1)} %bitcast.28), channel_id=1, source_target_pairs={{0,16},{4,20},{8,24},{12,28},{16,0},{20,4},{24,8},{28,12},{1,17},{... | collective-permute-start | bytes 393224 | tf_op jit(solution)/shard_map/ppermute | solution.py:103
  25.4 10.2 %collective-permute-start.4 = (bf16[1,128,512]{2,1,0:T(8,128)(2,1)S(1)}, bf16[1,128,512]{2,1,0:T(8,128)(2,1)S(1)}, u32[]{:S(2)}, u32[]{:S(2)}) collective-permute-start(bf16[1,128,512]{2,1,0:T(8,128)(2,1)S(1)} %bitcast.29), channel_id=1, source_target_pairs={{0,8},{4,12},{8,0},{12,4},{16,24},{20,28},{24,16},{28,20},{1,9},{5... | collective-permute-start | bytes 393224 | tf_op jit(solution)/shard_map/ppermute | solution.py:103
  35.6 10.6 %collective-permute-start.11 = (bf16[4,128,512]{2,1,0:T(8,128)(2,1)S(1)}, bf16[4,128,512]{2,1,0:T(8,128)(2,1)S(1)}, u32[]{:S(2)}, u32[]{:S(2)}) collective-permute-start(bf16[4,128,512]{2,1,0:T(8,128)(2,1)S(1)} %pad_maximum_fusion.refs_0_), channel_id=1, source_target_pairs={{0,1},{1,0},{2,3},{3,2},{4,5},{5,4},{6,7},{7,6},{8,9},{9,8},{10,11... | collective-permute-start | bytes 1572872 | tf_op jit(solution)/shard_map/ppermute | solution.py:103
  35.7 10.6 %collective-permute-start.12 = (bf16[4,128,512]{2,1,0:T(8,128)(2,1)S(1)}, bf16[4,128,512]{2,1,0:T(8,128)(2,1)S(1)}, u32[]{:S(2)}, u32[]{:S(2)}) collective-permute-start(bf16[4,128,512]{2,1,0:T(8,128)(2,1)S(1)} %collective-permute-done.7.refs_2_), channel_id=1, source_target_pairs={{0,1},{1,0},{2,3},{3,2},{4,5},{5,4},{6,7},{7,6},{8,9},{9,8},{10,11... | collective-permute-start | bytes 1572872 | tf_op jit(solution)/shard_map/ppermute | solution.py:103
  36.2 10.1 %collective-permute-start.13 = (bf16[4,128,512]{2,1,0:T(8,128)(2,1)S(1)}, bf16[4,128,512]{2,1,0:T(8,128)(2,1)S(1)}, u32[]{:S(2)}, u32[]{:S(2)}) collective-permute-start(bf16[4,128,512]{2,1,0:T(8,128)(2,1)S(1)} %collective-permute-done.8.refs_4_), channel_id=1, source_target_pairs={{0,1},{1,0},{2,3},{3,2},{4,5},{5,4},{6,7},{7,6},{8,9},{9,8},{10,11... | collective-permute-start | bytes 1572872 | tf_op jit(solution)/shard_map/ppermute | solution.py:103
  36.3 8.7 %collective-permute-start.10 = (bf16[4,64,512]{2,1,0:T(8,128)(2,1)S(1)}, bf16[4,64,512]{2,1,0:T(8,128)(2,1)S(1)}, u32[]{:S(2)}, u32[]{:S(2)}) collective-permute-start(bf16[4,64,512]{2,1,0:T(8,128)(2,1)S(1)} %slice.19), channel_id=1, source_target_pairs={{0,2},{1,3},{2,0},{3,1},{4,6},{5,7},{6,4},{7,5},{8,10},{9,11},{10,... | collective-permute-start | bytes 786440 | tf_op jit(solution)/shard_map/ppermute | solution.py:103
  37.9 8.4 %collective-permute-start.9 = (bf16[4,64,512]{2,1,0:T(8,128)(2,1)S(1)}, bf16[4,64,512]{2,1,0:T(8,128)(2,1)S(1)}, u32[]{:S(2)}, u32[]{:S(2)}) collective-permute-start(bf16[4,64,512]{2,1,0:T(8,128)(2,1)S(1)} %slice.18), channel_id=1, source_target_pairs={{0,4},{4,0},{8,12},{12,8},{16,20},{20,16},{24,28},{28,24},{1,5},{5... | collective-permute-start | bytes 786440 | tf_op jit(solution)/shard_map/ppermute | solution.py:103
  46.3 1.6 %collective-permute-start.14 = (bf16[4,64,512]{2,1,0:T(8,128)(2,1)S(1)}, bf16[4,64,512]{2,1,0:T(8,128)(2,1)S(1)}, u32[]{:S(2)}, u32[]{:S(2)}) collective-permute-start(bf16[4,64,512]{2,1,0:T(8,128)(2,1)S(1)} %collective-permute-done.9.refs_6_), channel_id=1, source_target_pairs={{0,1},{1,0},{2,3},{3,2},{4,5},{5,4},{6,7},{7,6},{8,9},{9,8},{10,11... | collective-permute-start | bytes 786440 | tf_op jit(solution)/shard_map/ppermute | solution.py:103
  46.3 1.9 %collective-permute-start.15 = (bf16[4,64,512]{2,1,0:T(8,128)(2,1)S(1)}, bf16[4,64,512]{2,1,0:T(8,128)(2,1)S(1)}, u32[]{:S(2)}, u32[]{:S(2)}) collective-permute-start(bf16[4,64,512]{2,1,0:T(8,128)(2,1)S(1)} %collective-permute-done.10.refs_8_), channel_id=1, source_target_pairs={{0,1},{1,0},{2,3},{3,2},{4,5},{5,4},{6,7},{7,6},{8,9},{9,8},{10,11... | collective-permute-start | bytes 786440 | tf_op jit(solution)/shard_map/ppermute | solution.py:103
  51.6 16.8 %collective-permute-start.17 = (bf16[5,128,512]{2,1,0:T(8,128)(2,1)S(1)}, bf16[5,128,512]{2,1,0:T(8,128)(2,1)S(1)}, u32[]{:S(2)}, u32[]{:S(2)}) collective-permute-start(bf16[5,128,512]{2,1,0:T(8,128)(2,1)S(1)} %get-tuple-element.148.refs_0_), channel_id=1, source_target_pairs={{0,2},{1,3},{2,0},{3,1},{4,6},{5,7},{6,4},{7,5},{8,10},{9,11},{10,... | collective-permute-start | bytes 1966088 | tf_op jit(solution)/shard_map/ppermute | solution.py:103
  52.2 16.2 %collective-permute-start.16 = (bf16[5,128,512]{2,1,0:T(8,128)(2,1)S(1)}, bf16[5,128,512]{2,1,0:T(8,128)(2,1)S(1)}, u32[]{:S(2)}, u32[]{:S(2)}) collective-permute-start(bf16[5,128,512]{2,1,0:T(8,128)(2,1)S(1)} %get-tuple-element.148.refs_0_), channel_id=1, source_target_pairs={{0,1},{1,0},{2,3},{3,2},{4,5},{5,4},{6,7},{7,6},{8,9},{9,8},{10,11... | collective-permute-start | bytes 1966088 | tf_op jit(solution)/shard_map/ppermute | solution.py:103
  52.2 3.0 %collective-permute-start.18 = (bf16[9,128,128]{2,1,0:T(8,128)(2,1)S(1)}, bf16[9,128,128]{2,1,0:T(8,128)(2,1)S(1)}, u32[]{:S(2)}, u32[]{:S(2)}) collective-permute-start(bf16[9,128,128]{2,1,0:T(8,128)(2,1)S(1)} %get-tuple-element.141), channel_id=1, source_target_pairs={{0,1},{1,0},{2,3},{3,2},{4,5},{5,4},{6,7},{7,6},{8,9},{9,8},{10,11... | collective-permute-start | bytes 884744 | tf_op jit(solution)/shard_map/ppermute | solution.py:103
  52.8 16.5 %collective-permute-start.22 = (bf16[4,128,512]{2,1,0:T(8,128)(2,1)S(1)}, bf16[4,128,512]{2,1,0:T(8,128)(2,1)S(1)}, u32[]{:S(2)}, u32[]{:S(2)}) collective-permute-start(bf16[4,128,512]{2,1,0:T(8,128)(2,1)S(1)} %pad_maximum_fusion.1.refs_5_.refs_9_), channel_id=1, source_target_pairs={{0,4},{4,0},{8,12},{12,8},{16,20},{20,16},{24,28},{28,24},{1,5},{5... | collective-permute-start | bytes 1572872 | tf_op jit(solution)/shard_map/ppermute | solution.py:103
  53.2 2.0 %collective-permute-start.19 = (bf16[1,9,64,128]{3,2,1,0:T(8,128)(2,1)S(1)}, bf16[1,9,64,128]{3,2,1,0:T(8,128)(2,1)S(1)}, u32[]{:S(2)}, u32[]{:S(2)}) collective-permute-start(bf16[1,9,64,128]{3,2,1,0:T(8,128)(2,1)S(1)} %get-tuple-element.200), channel_id=1, source_target_pairs={{0,1},{1,0},{2,3},{3,2},{4,5},{5,4},{6,7},{7,6},{8,9},{9,8},{10,11... | collective-permute-start | bytes 442376 | tf_op jit(solution)/shard_map/ppermute | solution.py:103
  53.3 17.3 %copy-start.1 = (bf16[128,3,3,512]{3,0,2,1:T(8,128)(2,1)S(1)}, bf16[128,3,3,512]{3,0,2,1:T(8,128)(2,1)}, u32[]{:S(2)}) copy-start(bf16[128,3,3,512]{3,0,2,1:T(8,128)(2,1)} %param.6) | copy-start | bytes 3538948
  68.5 2.1 %collective-permute-start.24 = (bf16[5,128,512]{2,1,0:T(8,128)(2,1)S(1)}, bf16[5,128,512]{2,1,0:T(8,128)(2,1)S(1)}, u32[]{:S(2)}, u32[]{:S(2)}) collective-permute-start(bf16[5,128,512]{2,1,0:T(8,128)(2,1)S(1)} %collective-permute-done.17.refs_2_), channel_id=1, source_target_pairs={{0,1},{1,0},{2,3},{3,2},{4,5},{5,4},{6,7},{7,6},{8,9},{9,8},{10,11... | collective-permute-start | bytes 1966088 | tf_op jit(solution)/shard_map/ppermute | solution.py:103
  68.5 11.5 %collective-permute-start.21 = (bf16[3,128,512]{2,1,0:T(8,128)(2,1)S(1)}, bf16[3,128,512]{2,1,0:T(8,128)(2,1)S(1)}, u32[]{:S(2)}, u32[]{:S(2)}) collective-permute-start(bf16[3,128,512]{2,1,0:T(8,128)(2,1)S(1)} %get-tuple-element.156.refs_4_), channel_id=1, source_target_pairs={{0,2},{1,3},{2,0},{3,1},{4,6},{5,7},{6,4},{7,5},{8,10},{9,11},{10,... | collective-permute-start | bytes 1179656 | tf_op jit(solution)/shard_map/ppermute | solution.py:103
  69.0 11.0 %collective-permute-start.20 = (bf16[3,128,512]{2,1,0:T(8,128)(2,1)S(1)}, bf16[3,128,512]{2,1,0:T(8,128)(2,1)S(1)}, u32[]{:S(2)}, u32[]{:S(2)}) collective-permute-start(bf16[3,128,512]{2,1,0:T(8,128)(2,1)S(1)} %get-tuple-element.156.refs_4_), channel_id=1, source_target_pairs={{0,1},{1,0},{2,3},{3,2},{4,5},{5,4},{6,7},{7,6},{8,9},{9,8},{10,11... | collective-permute-start | bytes 1179656 | tf_op jit(solution)/shard_map/ppermute | solution.py:103
  69.3 9.2 %collective-permute-start.23 = (bf16[2,9,64,128]{3,2,1,0:T(8,128)(2,1)S(1)}, bf16[2,9,64,128]{3,2,1,0:T(8,128)(2,1)S(1)}, u32[]{:S(2)}, u32[]{:S(2)}) collective-permute-start(bf16[2,9,64,128]{3,2,1,0:T(8,128)(2,1)S(1)} %collective-permute-done.3), channel_id=1, source_target_pairs={{0,4},{4,0},{8,12},{12,8},{16,20},{20,16},{24,28},{28,24},{1,5},{5... | collective-permute-start | bytes 884744 | tf_op jit(solution)/shard_map/ppermute | solution.py:103
  80.0 8.7 %collective-permute-start.26 = (bf16[4,128,512]{2,1,0:T(8,128)(2,1)S(1)}, bf16[4,128,512]{2,1,0:T(8,128)(2,1)S(1)}, u32[]{:S(2)}, u32[]{:S(2)}) collective-permute-start(bf16[4,128,512]{2,1,0:T(8,128)(2,1)S(1)} %get-tuple-element.180.refs_8_.refs_0_), channel_id=1, source_target_pairs={{0,1},{1,0},{2,3},{3,2},{4,5},{5,4},{6,7},{7,6},{8,9},{9,8},{10,11... | collective-permute-start | bytes 1572872 | tf_op jit(solution)/shard_map/ppermute | solution.py:103
  80.0 2.5 %collective-permute-start.27 = (bf16[3,128,512]{2,1,0:T(8,128)(2,1)S(1)}, bf16[3,128,512]{2,1,0:T(8,128)(2,1)S(1)}, u32[]{:S(2)}, u32[]{:S(2)}) collective-permute-start(bf16[3,128,512]{2,1,0:T(8,128)(2,1)S(1)} %collective-permute-done.21.refs_6_), channel_id=1, source_target_pairs={{0,1},{1,0},{2,3},{3,2},{4,5},{5,4},{6,7},{7,6},{8,9},{9,8},{10,11... | collective-permute-start | bytes 1179656 | tf_op jit(solution)/shard_map/ppermute | solution.py:103
  80.5 8.2 %collective-permute-start.25 = (bf16[2,128,512]{2,1,0:T(8,128)(2,1)S(1)}, bf16[2,128,512]{2,1,0:T(8,128)(2,1)S(1)}, u32[]{:S(2)}, u32[]{:S(2)}) collective-permute-start(bf16[2,128,512]{2,1,0:T(8,128)(2,1)S(1)} %get-tuple-element.155), channel_id=1, source_target_pairs={{0,2},{1,3},{2,0},{3,1},{4,6},{5,7},{6,4},{7,5},{8,10},{9,11},{10,... | collective-permute-start | bytes 786440 | tf_op jit(solution)/shard_map/ppermute | solution.py:103
  88.8 9.6 %collective-permute-start.30 = (bf16[4,128,512]{2,1,0:T(8,128)(2,1)S(1)}, bf16[4,128,512]{2,1,0:T(8,128)(2,1)S(1)}, u32[]{:S(2)}, u32[]{:S(2)}) collective-permute-start(bf16[4,128,512]{2,1,0:T(8,128)(2,1)S(1)} %get-tuple-element.182.refs_9_.refs_2_), channel_id=1, source_target_pairs={{0,1},{1,0},{2,3},{3,2},{4,5},{5,4},{6,7},{7,6},{8,9},{9,8},{10,11... | collective-permute-start | bytes 1572872 | tf_op jit(solution)/shard_map/ppermute | solution.py:103
  88.8 14.3 %collective-permute-start.28 = (bf16[4,128,512]{2,1,0:T(8,128)(2,1)S(1)}, bf16[4,128,512]{2,1,0:T(8,128)(2,1)S(1)}, u32[]{:S(2)}, u32[]{:S(2)}) collective-permute-start(bf16[4,128,512]{2,1,0:T(8,128)(2,1)S(1)} %get-tuple-element.182.refs_9_.refs_2_), channel_id=1, source_target_pairs={{0,2},{1,3},{2,0},{3,1},{4,6},{5,7},{6,4},{7,5},{8,10},{9,11},{10,... | collective-permute-start | bytes 1572872 | tf_op jit(solution)/shard_map/ppermute | solution.py:103
  89.3 7.4 %collective-permute-start.32 = (bf16[1,9,64,128]{3,2,1,0:T(8,128)(2,1)S(1)}, bf16[1,9,64,128]{3,2,1,0:T(8,128)(2,1)S(1)}, u32[]{:S(2)}, u32[]{:S(2)}) collective-permute-start(bf16[1,9,64,128]{3,2,1,0:T(8,128)(2,1)S(1)} %get-tuple-element.198), channel_id=1, source_target_pairs={{0,1},{1,0},{2,3},{3,2},{4,5},{5,4},{6,7},{7,6},{8,9},{9,8},{10,11... | collective-permute-start | bytes 442376 | tf_op jit(solution)/shard_map/ppermute | solution.py:103
  89.6 7.1 %collective-permute-start.31 = (bf16[2,128,512]{2,1,0:T(8,128)(2,1)S(1)}, bf16[2,128,512]{2,1,0:T(8,128)(2,1)S(1)}, u32[]{:S(2)}, u32[]{:S(2)}) collective-permute-start(bf16[2,128,512]{2,1,0:T(8,128)(2,1)S(1)} %collective-permute-done.25.refs_6_), channel_id=1, source_target_pairs={{0,1},{1,0},{2,3},{3,2},{4,5},{5,4},{6,7},{7,6},{8,9},{9,8},{10,11... | collective-permute-start | bytes 786440 | tf_op jit(solution)/shard_map/ppermute | solution.py:103
  89.9 8.4 %collective-permute-start.29 = (bf16[2,128,512]{2,1,0:T(8,128)(2,1)S(1)}, bf16[2,128,512]{2,1,0:T(8,128)(2,1)S(1)}, u32[]{:S(2)}, u32[]{:S(2)}) collective-permute-start(bf16[2,128,512]{2,1,0:T(8,128)(2,1)S(1)} %collective-permute-done.25.refs_6_), channel_id=1, source_target_pairs={{0,4},{4,0},{8,12},{12,8},{16,20},{20,16},{24,28},{28,24},{1,5},{5... | collective-permute-start | bytes 786440 | tf_op jit(solution)/shard_map/ppermute | solution.py:103
  103.1 2.3 %collective-permute-start.33 = (bf16[4,128,512]{2,1,0:T(8,128)(2,1)S(1)}, bf16[4,128,512]{2,1,0:T(8,128)(2,1)S(1)}, u32[]{:S(2)}, u32[]{:S(2)}) collective-permute-start(bf16[4,128,512]{2,1,0:T(8,128)(2,1)S(1)} %collective-permute-done.28.refs_4_), channel_id=1, source_target_pairs={{0,1},{1,0},{2,3},{3,2},{4,5},{5,4},{6,7},{7,6},{8,9},{9,8},{10,11... | collective-permute-start | bytes 1572872 | tf_op jit(solution)/shard_map/ppermute | solution.py:103
  103.1 2.3 %collective-permute-start.34 = (bf16[2,128,512]{2,1,0:T(8,128)(2,1)S(1)}, bf16[2,128,512]{2,1,0:T(8,128)(2,1)S(1)}, u32[]{:S(2)}, u32[]{:S(2)}) collective-permute-start(bf16[2,128,512]{2,1,0:T(8,128)(2,1)S(1)} %collective-permute-done.29.refs_8_), channel_id=1, source_target_pairs={{0,1},{1,0},{2,3},{3,2},{4,5},{5,4},{6,7},{7,6},{8,9},{9,8},{10,11... | collective-permute-start | bytes 786440 | tf_op jit(solution)/shard_map/ppermute | solution.py:103

commit v3 on v2

--- a/solution.py
+++ b/solution.py
@@ -165,9 +165,12 @@
     first_rows(part, full, wide, hidden, mask)
 
 
-def first_rest_kernel(part, full, weight, hidden, mask, wide):
+def first_rest_kernel(part, full, weight, hidden, mask, flat, wide):
     widen(weight, wide)
     first_rows(part, full, wide, hidden, mask)
+    rows, _, w = full.shape
+    for r in range(rows):
+        flat[:, r * w : (r + 1) * w] = full[r]
 
 
 def copy_pieces(layout, refs, put, lo, hi):
@@ -240,13 +243,21 @@
                 over[e - 2, t] = block[own // 2 :]
 
 
-def back_kernel(layout, *refs):
+def back_rows(part, rows, lo, x, wide, masks, grad_first):
+    for r in range(*part):
+        left, mid, right = thirds(window(wide, x, r, rows, lo))
+        total = join_cols(right, mid, left)
+        (mask,) = [ref[r - base] for base, ref in masks if 0 <= r - base < ref.shape[0]]
+        grad_first[r - part[0]] = jnp.where(mask > 0, total, 0.0).astype(BF)
+
+
+def back_kernel(layout, part, rows, *refs):
     pieces = refs[: len(layout)]
-    mine, mate, near2, far2, near3, far3, mask_a, mask_b, grad_first, wide, x = refs[len(layout) :]
-    rows, own = grad_first.shape[:2]
-    c = x.shape[1]
+    mine, mate, near2, far2, near3, far3, mask, grad_first, wide, x = refs[len(layout) :]
+    own, c = grad_first.shape[1], x.shape[1]
     f0, y0 = lax.axis_index("filt"), lax.axis_index("rows") & 1
-    fill_rows(x, layout, pieces, 0, rows)
+    lo, hi = max(part[0] - 1, 0), min(part[1] + 1, rows)
+    fill_rows(x, layout, pieces, lo, hi)
     for t in range(9):
         a, b = t // 3, t % 3
 
@@ -259,12 +270,14 @@
             for y, ref in ((y0, near), (1 - y0, far)):
                 rows_at = pl.ds(pl.multiple_of(b * own + y * (own // 2), own // 2), own // 2)
                 wide[rows_at, at(e)] = ref[0, t]
-    cut = mask_a.shape[0]
-    for r in range(rows):
-        left, mid, right = thirds(window(wide, x, r, rows, 0))
-        total = join_cols(right, mid, left)
-        mask = mask_a[r] if r < cut else mask_b[r - cut]
-        grad_first[r] = jnp.where(mask > 0, total, 0.0).astype(BF)
+    back_rows(part, rows, lo, x, wide, [(0, mask)], grad_first)
+
+
+def back_rest_kernel(layout, part, rows, cut, *refs):
+    pieces, (wide, mask_a, mask_b, grad_first, x) = refs[: len(layout)], refs[len(layout) :]
+    lo, hi = max(part[0] - 1, 0), min(part[1] + 1, rows)
+    fill_rows(x, layout, pieces, lo, hi)
+    back_rows(part, rows, lo, x, wide, [(0, mask_a), (cut, mask_b)], grad_first)
 
 
 def fill_moved(grads, moved):
@@ -278,43 +291,54 @@
         moved[2 * own :, at] = jnp.where(col == 0, 0.0, pltpu.roll(g, 1, 1)).astype(BF)
 
 
-def sum_terms(moved, x, w, out):
-    n = moved.shape[1]
-    for a, (m, h) in enumerate([(slice(w, n), slice(0, n - w)), (slice(0, n),) * 2, (slice(0, n - w), slice(w, n))]):
-        out[a] = lax.dot_general(moved[:, m], x[:, h], (((1,), (1,)), ((), ())), preferred_element_type=F32)
+def sum_terms(moved, x, w, a, part):
+    rows = x.shape[1] // w
+    lo, hi = max(part[0], 1 - a), min(part[1], rows + 1 - a)
+    left, right = moved[:, (lo - part[0]) * w : (hi - part[0]) * w], x[:, (lo + a - 1) * w : (hi + a - 1) * w]
+    return lax.dot_general(left, right, (((1,), (1,)), ((), ())), preferred_element_type=F32)
 
 
 def second_terms_kernel(layout, *refs):
     pieces, (grad_a, grad_b, out, x, moved) = refs[: len(layout)], refs[len(layout) :]
     w = grad_a.shape[2]
+    rows = moved.shape[1] // w
 
     def put(r, at, value):
         x[at, r * w : (r + 1) * w] = value
 
-    copy_pieces(layout, pieces, put, 0, moved.shape[1] // w)
+    copy_pieces(layout, pieces, put, 0, rows)
     fill_moved([grad_a, grad_b], moved)
-    sum_terms(moved, x, w, out)
-
-
-def first_terms_kernel(n_grads, full, *refs):
-    grads, (out, x, moved) = refs[:n_grads], refs[n_grads:]
-    rows, _, w = full.shape
-    for r in range(rows):
-        x[:, r * w : (r + 1) * w] = full[r]
-    fill_moved(grads, moved)
-    sum_terms(moved, x, w, out)
+    for a in range(3):
+        out[a] = sum_terms(moved, x, w, a, (0, rows))
+
+
+def first_terms_kernel(part, flat, grad, out, moved):
+    fill_moved([grad], moved)
+    for a in range(3):
+        out[a] = sum_terms(moved, flat, grad.shape[2], a, part)
+
+
+def first_terms_rest_kernel(part, flat, grad, before, out, moved, total, sems):
+    fill_moved([grad], moved)
+    copies = []
+    for a in range(3):
+        total[a] = before[a] + sum_terms(moved, flat, grad.shape[2], a, part)
+        copies.append(pltpu.make_async_copy(total.at[a], out.at[a], sems.at[a]))
+        copies[-1].start()
+    for copy in copies:
+        copy.wait()
 
 
 VM = pl.BlockSpec(memory_space=pltpu.VMEM)
 
 
-def call(kernel, ins, outs, scratch, flops, name):
+def call(kernel, ins, outs, scratch, flops, name, out_spec=VM):
     nbytes = sum(v.size * v.dtype.itemsize for v in ins) if flops else 0
     return pl.pallas_call(
         kernel,
         out_shape=[jax.ShapeDtypeStruct(s, d) for s, d in outs],
         in_specs=[VM] * len(ins),
-        out_specs=[VM] * len(outs),
+        out_specs=[out_spec] * len(outs),
         scratch_shapes=scratch,
         compiler_params=pltpu.CompilerParams(vmem_limit_bytes=VMEM_BYTES),
         cost_estimate=pl.CostEstimate(flops=flops, bytes_accessed=nbytes, transcendentals=0),
@@ -398,10 +422,10 @@
     h = {"a0": h_a, "a1": to_mate(h_a), "a2": over_x(h_a)}
     gy = over_y(v["g4"])
     h |= {"m1": to_mate(v["mate"]), "near3": to_mate(v["near"][1:])}
-    h["b0"], mask_b = call(
+    h["b0"], mask_b, flat = call(
         functools.partial(first_rest_kernel, (cut_a, rows)),
         [full, w1],
-        [act(rows - cut_a)] * 2,
+        [act(rows - cut_a)] * 2 + [((c, rows * w), BF)],
         [wide],
         0,
         "first_conv_b",
@@ -430,40 +454,61 @@
     s = wave(s)
     layout_b = layout_a + [(e, cut_a, "whole") for e in range(4)]
     spread_b = spread_a + [s["b0"], s["b1"], s["b2"], to_mate(s["b2"])]
-    t = {"a0": s["a0"], "s2": over_x(s["early"]), "a1": to_mate(s["a0"])}
+    t = {"a0": s["a0"], "s2": over_x(s["early"]), "a1": to_mate(s["a0"]), "far3": to_mate(s["far"][1:])}
     t["out"], t["b0"] = second(layout_b, spread_b, (cut, rows), s["out"], 0, "second_conv_b")
     t = wave(t)
-    t |= {"b2": over_x(t["b0"]), "t2": over_y(t["s2"]), "b1": to_mate(t["b0"]), "s3": to_mate(t["s2"])}
-    t |= {"far3": to_mate(s["far"][1:])}
-    (t["grad"],) = call(
+    b2 = over_x(t["b0"])
+    t |= {"b1": to_mate(t["b0"]), "t2": over_y(t["s2"]), "s3": to_mate(t["s2"])}
+
+    (second_grad,) = call(
         functools.partial(second_terms_kernel, layout_b),
         [*spread_b, t["a0"], t["b0"]],
         [((3, 3 * own, c), F32)],
         [vm((c, rows * w), BF), vm((3 * own, rows * w), BF)],
-        row_flops * rows,
+        0,
         "second_terms",
     )
+    t["t2"], second_grad = lax.optimization_barrier((t["t2"], second_grad))
+    t["t3"] = to_mate(t["t2"])
+    last = cut - 1
+    layout = [(e, 0, "whole") for e in (0, 1)] + [(e, 0, kind) for kind in ("own", "other") for e in (2, 3)]
+    names = ["a0", "a1", "s2", "s3", "t2", "t3"]
+    turned = [v["mine"], h["m1"], v["near"][:1], s["far"][:1], h["near3"], t["far3"]]
+    grad_first, wide_back = call(
+        functools.partial(back_kernel, layout, (0, last), rows),
+        [*(t[k] for k in names), *turned, mask_a],
+        [act(last), ((3 * own, 3 * c), BF)],
+        [vm((cut, c, w), BF)],
+        0,
+        "hidden_grad_a",
+    )
+    (terms,) = call(
+        functools.partial(first_terms_kernel, (0, last)),
+        [flat, grad_first],
+        [((3, 3 * own, c), F32)],
+        [vm((3 * own, last * w), BF)],
+        0,
+        "first_terms_a",
+    )
+    t |= {"b2": b2, "terms": terms, "wide": wide_back, "grad": second_grad}
     t = wave(t)
-    t |= {"b3": to_mate(t["b2"]), "t3": to_mate(t["t2"])}
-    t = wave(t)
-    layout = [(e, 0, "whole") for e in (0, 1)] + [(e, cut, "whole") for e in range(4)]
-    layout += [(e, 0, kind) for kind in ("own", "other") for e in (2, 3)]
-    turned = [v["mine"], h["m1"], v["near"][:1], s["far"][:1], h["near3"], t["far3"]]
+    layout += [(e, cut, "whole") for e in range(4)]
     (grad_first,) = call(
-        functools.partial(back_kernel, layout),
-        [*(t[k] for k in ("a0", "a1", "b0", "b1", "b2", "b3", "s2", "s3", "t2", "t3")), *turned, mask_a, mask_b],
-        [act(rows)],
-        [wide, vm((rows, c, w), BF)],
-        row_flops * rows,
-        "hidden_grad",
+        functools.partial(back_rest_kernel, layout, (last, rows), rows, cut_a),
+        [*(t[k] for k in names), t["b0"], t["b1"], t["b2"], to_mate(t["b2"]), t["wide"], mask_a, mask_b],
+        [act(rows - last)],
+        [vm((rows - last + 1, c, w), BF)],
+        row_flops * (rows - last),
+        "hidden_grad_b",
     )
     (first_grad,) = call(
-        functools.partial(first_terms_kernel, 1),
-        [full, grad_first],
+        functools.partial(first_terms_rest_kernel, (last, rows)),
+        [flat, grad_first, t["terms"]],
         [((3, 3 * own, c), F32)],
-        [vm((c, rows * w), BF), vm((3 * own, rows * w), BF)],
-        row_flops * rows,
-        "first_terms",
+        [vm((3 * own, (rows - last) * w), BF), vm((3, 3 * own, c), F32), pltpu.SemaphoreType.DMA((3,))],
+        row_flops * (rows - last),
+        "first_terms_b",
+        pl.BlockSpec(memory_space=pl.ANY),
     )
 
     def as_weight(value):

time: 117 us -> 112 us (0.957)
  waiting for transfers between devices: 59 us -> 53.8 us
    ppermute x35, waiting for transfers between devices: 59 us -> 53.8 us  [swap(): lax.ppermute(value, axis, [(i, i ^ bits) for i in range(lax.axis_size(axi...]
    pallas_call x8 -> x10, Pallas kernels: 32.3 us -> 32.8 us  [call(): pl.pallas_call(kernel, out_shape=[jax.ShapeDtypeStruct(s, d) for s, d in...]
  transfers between devices with their start and end apart: 35 -> 35, of which waited for: 17 -> 16; matrix products, arithmetic and copies ran while one was open for 0% -> 0% of each run, Pallas kernels for 14% -> 18%
where the time goes in v3:
time: 112 us
  waiting for transfers between devices  53.8 us (48%)
  Pallas kernels  32.8 us (29%)
  starting transfers between devices  22.9 us (20%)
  local copies, waits for them, and re-layouts  1.37 us (1%)
    ppermute x35, waiting for transfers between devices, swap(): lax.ppermute(value, axis, [(i, i ^ bits) for i in range(lax.axis_size(axi...  53.8 us
    pallas_call x10, Pallas kernels, call(): pl.pallas_call(kernel, out_shape=[jax.ShapeDtypeStruct(s, d) for s, d in...  32.8 us
    ppermute x35, starting transfers between devices, swap(): lax.ppermute(value, axis, [(i, i ^ bits) for i in range(lax.axis_size(axi...  22.9 us
  transfers between devices with their start and end apart: 35, of which 16 were waited for; matrix products, arithmetic and copies ran while one was open for 0% of the time, Pallas kernels for 18%

profile of v3, /device:TPU:0, one launch (start us, length us, event | category | flops | bytes accessed | tf_op | source)
XLA Modules:
  0.0 112.0 jit_solution(3770033180246034777)
XLA Ops:
  0.6 0.0 copy-start
  0.6 1.3 %copy-done = bf16[128,3,3,512]{3,0,2,1:T(8,128)(2,1)S(1)} copy-done((bf16[128,3,3,512]{3,0,2,1:T(8,128)(2,1)S(1)}, bf16[128,3,3,512]{3,0,2,1:T(8,128)(2,1)}, u32[]{:S(2)}) %copy-start) | copy-done | bytes 1179672
  1.9 1.4 %turn_weight.1 = (bf16[9,128,128]{2,1,0:T(8,128)(2,1)S(1)}, bf16[9,128,128]{2,1,0:T(8,128)(2,1)S(1)}, bf16[2,9,64,128]{3,2,1,0:T(8,128)(2,1)S(1)}) custom-call(bf16[9,128,512]{2,1,0:T(8,128)(2,1)S(1)} %bitcast.17), custom_call_target="tpu_custom_call" | custom-call | flops 1207959552 | bytes 1179648 | tf_op jit(solution)/shard_map/turn_weight/pallas_call | solution.py:337
  3.3 0.0 copy-start.2
  3.3 3.0 %collective-permute-start.3 = (bf16[2,9,64,128]{3,2,1,0:T(8,128)(2,1)S(1)}, bf16[2,9,64,128]{3,2,1,0:T(8,128)(2,1)S(1)}, u32[]{:S(2)}, u32[]{:S(2)}) collective-permute-start(bf16[2,9,64,128]{3,2,1,0:T(8,128)(2,1)S(1)} %get-tuple-element.97), channel_id=1, source_target_pairs={{0,2},{1,3},{2,0},{3,1},{4,6},{5,7},{6,4},{7,5},{8,10},{9,11},{10,... | collective-permute-start | bytes 884744 | tf_op jit(solution)/shard_map/ppermute | solution.py:103
  6.3 3.6 %collective-permute-start.2 = (bf16[1,128,512]{2,1,0:T(8,128)(2,1)S(1)}, bf16[1,128,512]{2,1,0:T(8,128)(2,1)S(1)}, u32[]{:S(2)}, u32[]{:S(2)}) collective-permute-start(bf16[1,128,512]{2,1,0:T(8,128)(2,1)S(1)} %bitcast.22), channel_id=1, source_target_pairs={{0,24},{4,28},{8,16},{12,20},{16,8},{20,12},{24,0},{28,4},{1,25},{... | collective-permute-start | bytes 393224 | tf_op jit(solution)/shard_map/ppermute | solution.py:103
  9.9 0.8 collective-permute-start
  10.7 3.9 %collective-permute-done.2 = bf16[1,128,512]{2,1,0:T(8,128)(2,1)S(1)} collective-permute-done((bf16[1,128,512]{2,1,0:T(8,128)(2,1)S(1)}, bf16[1,128,512]{2,1,0:T(8,128)(2,1)S(1)}, u32[]{:S(2)}, u32[]{:S(2)}) %collective-permute-start.2) | collective-permute-done | bytes 131104 | tf_op jit(solution)/shard_map/ppermute | solution.py:103
  14.6 6.1 %collective-permute-done.1 = bf16[1,128,512]{2,1,0:T(8,128)(2,1)S(1)} collective-permute-done((bf16[1,128,512]{2,1,0:T(8,128)(2,1)S(1)}, bf16[1,128,512]{2,1,0:T(8,128)(2,1)S(1)}, u32[]{:S(2)}, u32[]{:S(2)}) %collective-permute-start.1) | collective-permute-done | bytes 131104 | tf_op jit(solution)/shard_map/ppermute | solution.py:103
  20.7 0.0 collective-permute-done
  20.7 0.0 collective-permute-done.3
  20.7 0.1 pad_maximum_fusion.refs_0_
  20.8 1.6 %collective-permute-start.8 = (bf16[4,128,512]{2,1,0:T(8,128)(2,1)S(1)}, bf16[4,128,512]{2,1,0:T(8,128)(2,1)S(1)}, u32[]{:S(2)}, u32[]{:S(2)}) collective-permute-start(bf16[4,128,512]{2,1,0:T(8,128)(2,1)S(1)} %pad_maximum_fusion.refs_0_), channel_id=1, source_target_pairs={{0,4},{4,0},{8,12},{12,8},{16,20},{20,16},{24,28},{28,24},{1,5},{5... | collective-permute-start | bytes 1572872 | tf_op jit(solution)/shard_map/ppermute | solution.py:103
  22.4 0.5 collective-permute-start.7
  23.0 2.5 %collective-permute-start.6 = (bf16[1,128,512]{2,1,0:T(8,128)(2,1)S(1)}, bf16[1,128,512]{2,1,0:T(8,128)(2,1)S(1)}, u32[]{:S(2)}, u32[]{:S(2)}) collective-permute-start(bf16[1,128,512]{2,1,0:T(8,128)(2,1)S(1)} %bitcast.28), channel_id=1, source_target_pairs={{0,24},{4,28},{8,16},{12,20},{16,8},{20,12},{24,0},{28,4},{1,25},{... | collective-permute-start | bytes 393224 | tf_op jit(solution)/shard_map/ppermute | solution.py:103
  25.4 0.0 collective-permute-start.5
  25.4 1.9 %collective-permute-start.4 = (bf16[1,128,512]{2,1,0:T(8,128)(2,1)S(1)}, bf16[1,128,512]{2,1,0:T(8,128)(2,1)S(1)}, u32[]{:S(2)}, u32[]{:S(2)}) collective-permute-start(bf16[1,128,512]{2,1,0:T(8,128)(2,1)S(1)} %bitcast.30), channel_id=1, source_target_pairs={{0,8},{4,12},{8,0},{12,4},{16,24},{20,28},{24,16},{28,20},{1,9},{5... | collective-permute-start | bytes 393224 | tf_op jit(solution)/shard_map/ppermute | solution.py:103
  27.3 3.8 %collective-permute-done.6 = bf16[1,128,512]{2,1,0:T(8,128)(2,1)S(1)} collective-permute-done((bf16[1,128,512]{2,1,0:T(8,128)(2,1)S(1)}, bf16[1,128,512]{2,1,0:T(8,128)(2,1)S(1)}, u32[]{:S(2)}, u32[]{:S(2)}) %collective-permute-start.6) | collective-permute-done | bytes 131104 | tf_op jit(solution)/shard_map/ppermute | solution.py:103
  31.2 4.4 %collective-permute-done.5 = bf16[1,128,512]{2,1,0:T(8,128)(2,1)S(1)} collective-permute-done((bf16[1,128,512]{2,1,0:T(8,128)(2,1)S(1)}, bf16[1,128,512]{2,1,0:T(8,128)(2,1)S(1)}, u32[]{:S(2)}, u32[]{:S(2)}) %collective-permute-start.5) | collective-permute-done | bytes 131104 | tf_op jit(solution)/shard_map/ppermute | solution.py:103
  35.6 0.1 collective-permute-start.11
  35.7 0.5 collective-permute-start.12
  36.2 0.1 collective-permute-start.13
  36.3 1.6 %collective-permute-start.10 = (bf16[4,64,512]{2,1,0:T(8,128)(2,1)S(1)}, bf16[4,64,512]{2,1,0:T(8,128)(2,1)S(1)}, u32[]{:S(2)}, u32[]{:S(2)}) collective-permute-start(bf16[4,64,512]{2,1,0:T(8,128)(2,1)S(1)} %slice.19), channel_id=1, source_target_pairs={{0,2},{1,3},{2,0},{3,1},{4,6},{5,7},{6,4},{7,5},{8,10},{9,11},{10,... | collective-permute-start | bytes 786440 | tf_op jit(solution)/shard_map/ppermute | solution.py:103
  37.9 0.5 collective-permute-start.9
  38.3 0.1 pad_maximum_fusion.1.refs_5_.refs_9_
  38.4 6.6 %collective-permute-done.10.refs_8_ = bf16[4,64,512]{2,1,0:T(8,128)(2,1)S(1)} collective-permute-done((bf16[4,64,512]{2,1,0:T(8,128)(2,1)S(1)}, bf16[4,64,512]{2,1,0:T(8,128)(2,1)S(1)}, u32[]{:S(2)}, u32[]{:S(2)}) %collective-permute-start.10) | collective-permute-done | bytes 262176 | tf_op jit(solution)/shard_map/ppermute | solution.py:103
  45.0 1.2 %collective-permute-done.9.refs_6_ = bf16[4,64,512]{2,1,0:T(8,128)(2,1)S(1)} collective-permute-done((bf16[4,64,512]{2,1,0:T(8,128)(2,1)S(1)}, bf16[4,64,512]{2,1,0:T(8,128)(2,1)S(1)}, u32[]{:S(2)}, u32[]{:S(2)}) %collective-permute-start.9) | collective-permute-done | bytes 262176 | tf_op jit(solution)/shard_map/ppermute | solution.py:103
  46.3 0.1 collective-permute-start.14
  46.3 0.5 collective-permute-start.15
  46.8 1.0 collective-permute-done.14.refs_7_
  47.9 0.4 collective-permute-done.15.refs_9_
  48.2 3.4 %first_conv_a.1 = (bf16[8,512,512]{2,1,0:T(8,128)(2,1)S(1)}, bf16[5,128,512]{2,1,0:T(8,128)(2,1)S(1)}, bf16[5,128,512]{2,1,0:T(8,128)(2,1)S(1)}) custom-call(bf16[4,128,512]{2,1,0:T(8,128)(2,1)S(1)} %pad_maximum_fusion.refs_0_, bf16[4,128,512]{2,1,0:T(8,128)(2,1)S(1)} %collective-permute-done.11.refs_1_, ...), custom_call_target="tpu_custom_call" | custom-call | tf_op jit(solution)/shard_map/first_conv_a/pallas_call | solution.py:337
  51.6 0.6 collective-permute-start.17
  52.2 0.5 collective-permute-start.18
  52.8 0.5 collective-permute-start.22
  53.2 0.1 collective-permute-start.19
  53.3 0.0 copy-start.1
  53.3 2.2 %first_conv_b.1 = (bf16[3,128,512]{2,1,0:T(8,128)(2,1)S(1)}, bf16[3,128,512]{2,1,0:T(8,128)(2,1)S(1)}, bf16[512,4096]{1,0:T(8,128)(2,1)S(1)}) custom-call(bf16[8,512,512]{2,1,0:T(8,128)(2,1)S(1)} %get-tuple-element.138.full.refs_4_.refs_8_, bf16[3,384,512]{2,1,0:T(8,128)(2,1)S(1)} %bitcast.21), custom_call_target="tpu_custom_call" | custom-call | tf_op jit(solution)/shard_map/first_conv_b/pallas_call | solution.py:337
  55.5 13.0 %collective-permute-done.17.refs_2_ = bf16[5,128,512]{2,1,0:T(8,128)(2,1)S(1)} collective-permute-done((bf16[5,128,512]{2,1,0:T(8,128)(2,1)S(1)}, bf16[5,128,512]{2,1,0:T(8,128)(2,1)S(1)}, u32[]{:S(2)}, u32[]{:S(2)}) %collective-permute-start.17) | collective-permute-done | bytes 655392 | tf_op jit(solution)/shard_map/ppermute | solution.py:103
  68.5 0.5 collective-permute-start.21
  69.0 0.2 collective-permute-start.20
  69.3 0.5 collective-permute-start.23
  69.7 0.9 collective-permute-done.24.refs_3_
  70.6 3.6 %second_conv_a.1 = (bf16[1,128,512]{2,1,0:T(8,128)(2,1)S(1)}, bf16[4,128,512]{2,1,0:T(8,128)(2,1)S(1)}, bf16[2,128,512]{2,1,0:T(8,128)(2,1)S(1)}) custom-call(bf16[5,128,512]{2,1,0:T(8,128)(2,1)S(1)} %get-tuple-element.143.refs_0_, bf16[5,128,512]{2,1,0:T(8,128)(2,1)S(1)} %collective-permute-done.16.refs_1_, ...), custom_call_target="tpu_custom_call" | custom-call | tf_op jit(solution)/shard_map/second_conv_a/pallas_call | solution.py:337
  74.2 4.3 %collective-permute-done.23 = bf16[2,9,64,128]{3,2,1,0:T(8,128)(2,1)S(1)} collective-permute-done((bf16[2,9,64,128]{3,2,1,0:T(8,128)(2,1)S(1)}, bf16[2,9,64,128]{3,2,1,0:T(8,128)(2,1)S(1)}, u32[]{:S(2)}, u32[]{:S(2)}) %collective-permute-start.23) | collective-permute-done | bytes 294944 | tf_op jit(solution)/shard_map/ppermute | solution.py:103
  78.5 1.6 %collective-permute-done.21.refs_6_ = bf16[3,128,512]{2,1,0:T(8,128)(2,1)S(1)} collective-permute-done((bf16[3,128,512]{2,1,0:T(8,128)(2,1)S(1)}, bf16[3,128,512]{2,1,0:T(8,128)(2,1)S(1)}, u32[]{:S(2)}, u32[]{:S(2)}) %collective-permute-start.21) | collective-permute-done | bytes 393248 | tf_op jit(solution)/shard_map/ppermute | solution.py:103
  80.0 0.5 collective-permute-start.28
  80.5 0.5 collective-permute-start.25
  81.1 0.1 collective-permute-start.27
  81.2 1.3 %collective-permute-done.28.refs_7_ = bf16[3,128,512]{2,1,0:T(8,128)(2,1)S(1)} collective-permute-done((bf16[3,128,512]{2,1,0:T(8,128)(2,1)S(1)}, bf16[3,128,512]{2,1,0:T(8,128)(2,1)S(1)}, u32[]{:S(2)}, u32[]{:S(2)}) %collective-permute-start.28) | collective-permute-done | bytes 393248 | tf_op jit(solution)/shard_map/ppermute | solution.py:103
  82.5 4.4 %second_conv_b.1 = (bf16[1,128,512]{2,1,0:T(8,128)(2,1)}, bf16[4,128,512]{2,1,0:T(8,128)(2,1)S(1)}) custom-call(bf16[5,128,512]{2,1,0:T(8,128)(2,1)S(1)} %get-tuple-element.143.refs_0_, bf16[5,128,512]{2,1,0:T(8,128)(2,1)S(1)} %collective-permute-done.16.refs_1_, bf16[5,128,512]{2,1,0:T(8,128)(2,1)S(1)} %collective-permute-done.17.refs_2_, ...), custom_call_target="tpu_custom_call" | custom-call | tf_op jit(solution)/shard_map/second_conv_b/pallas_call | solution.py:337
  86.9 1.9 %collective-permute-done.25.refs_2_ = bf16[2,128,512]{2,1,0:T(8,128)(2,1)S(1)} collective-permute-done((bf16[2,128,512]{2,1,0:T(8,128)(2,1)S(1)}, bf16[2,128,512]{2,1,0:T(8,128)(2,1)S(1)}, u32[]{:S(2)}, u32[]{:S(2)}) %collective-permute-start.25) | collective-permute-done | bytes 262176 | tf_op jit(solution)/shard_map/ppermute | solution.py:103
  88.8 0.5 collective-permute-start.30
  89.2 0.5 collective-permute-start.33
  89.8 0.5 collective-permute-start.31
  90.3 6.4 %second_terms.1 = f32[3,384,512]{2,1,0:T(8,128)} custom-call(bf16[5,128,512]{2,1,0:T(8,128)(2,1)S(1)} %get-tuple-element.143.refs_0_, bf16[5,128,512]{2,1,0:T(8,128)(2,1)S(1)} %collective-permute-done.16.refs_1_, bf16[5,128,512]{2,1,0:T(8,128)(2,1)S(1)} %collective-permute-done.17.refs_2_, bf16[5,128,512]{2,1,0:T(8,128)(2,1)S(1)} %collective-permute-done.24.refs_3_, ...), custom_call_target="tpu_custom_call" | custom-call | tf_op jit(solution)/shard_map/second_terms/pallas_call | solution.py:337
  96.6 0.0 collective-permute-start.32
  96.6 1.5 %collective-permute-done.32.refs_5_ = bf16[2,128,512]{2,1,0:T(8,128)(2,1)S(1)} collective-permute-done((bf16[2,128,512]{2,1,0:T(8,128)(2,1)S(1)}, bf16[2,128,512]{2,1,0:T(8,128)(2,1)S(1)}, u32[]{:S(2)}, u32[]{:S(2)}) %collective-permute-start.32) | collective-permute-done | bytes 262176 | tf_op jit(solution)/shard_map/ppermute | solution.py:103
  98.2 2.3 %hidden_grad_a.1 = (bf16[3,128,512]{2,1,0:T(8,128)(2,1)S(1)}, bf16[384,1536]{1,0:T(8,128)(2,1)S(1)}) custom-call(bf16[4,128,512]{2,1,0:T(8,128)(2,1)S(1)} %get-tuple-element.174.refs_8_.refs_0_, bf16[4,128,512]{2,1,0:T(8,128)(2,1)S(1)} %collective-permute-done.26.refs_1_, bf16[2,128,512]{2,1,0:T(8,128)(2,1)S(1)} %collective-permute-done.25.refs_2_, ...), custom_call_target="tpu_custom_call" | custom-call | tf_op jit(solution)/shard_map/hidden_grad_a/pallas_call | solution.py:337
  100.4 1.8 %first_terms_a.1.before = f32[3,384,512]{2,1,0:T(8,128)S(1)} custom-call(bf16[512,4096]{1,0:T(8,128)(2,1)S(1)} %get-tuple-element.165.flat, bf16[3,128,512]{2,1,0:T(8,128)(2,1)S(1)} %get-tuple-element.170.grad), custom_call_target="tpu_custom_call" | custom-call | tf_op jit(solution)/shard_map/first_terms_a/pallas_call | solution.py:337
  102.3 0.2 collective-permute-start.34
  102.5 1.8 %collective-permute-done.34.refs_9_ = bf16[4,128,512]{2,1,0:T(8,128)(2,1)S(1)} collective-permute-done((bf16[4,128,512]{2,1,0:T(8,128)(2,1)S(1)}, bf16[4,128,512]{2,1,0:T(8,128)(2,1)S(1)}, u32[]{:S(2)}, u32[]{:S(2)}) %collective-permute-start.34) | collective-permute-done | bytes 524320 | tf_op jit(solution)/shard_map/ppermute | solution.py:103
  104.3 3.6 %hidden_grad_b.1.grad = bf16[5,128,512]{2,1,0:T(8,128)(2,1)S(1)} custom-call(bf16[4,128,512]{2,1,0:T(8,128)(2,1)S(1)} %get-tuple-element.174.refs_8_.refs_0_, bf16[4,128,512]{2,1,0:T(8,128)(2,1)S(1)} %collective-permute-done.26.refs_1_, bf16[2,128,512]{2,1,0:T(8,128)(2,1)S(1)} %collective-permute-done.25.refs_2_, ...), custom_call_target="tpu_custom_call" | custom-call | flops 3019898880 | bytes 6422528 | tf_op jit(solution)/shard_map/hidden_grad_b/pallas_call | solution.py:337
  107.8 4.0 %first_terms_b.1 = f32[3,384,512]{2,1,0:T(8,128)} custom-call(bf16[512,4096]{1,0:T(8,128)(2,1)S(1)} %get-tuple-element.165.flat, bf16[5,128,512]{2,1,0:T(8,128)(2,1)S(1)} %hidden_grad_b.1.grad, f32[3,384,512]{2,1,0:T(8,128)S(1)} %first_terms_a.1.before), custom_call_target="tpu_custom_call" | custom-call | flops 3019898880 | bytes 7208960 | tf_op jit(solution)/shard_map/first_terms_b/pallas_call | solution.py:337
  (32 shorter events, 0.1 us)
Async XLA Ops:
  0.6 1.3 %copy-start = (bf16[128,3,3,512]{3,0,2,1:T(8,128)(2,1)S(1)}, bf16[128,3,3,512]{3,0,2,1:T(8,128)(2,1)}, u32[]{:S(2)}) copy-start(bf16[128,3,3,512]{3,0,2,1:T(8,128)(2,1)} %param.6) | copy-start | bytes 3538948
  1.9 4.4 %copy-start.3 = (bf16[128,1,512]{2,0,1:T(8,128)(2,1)S(1)}, bf16[128,1,512]{2,0,1:T(8,128)(2,1)}, u32[]{:S(2)}) copy-start(bf16[128,1,512]{2,0,1:T(8,128)(2,1)} %param.4) | copy-start | bytes 393220
  1.9 21.0 %copy-start.4 = (bf16[128,1,512]{2,0,1:T(8,128)(2,1)S(1)}, bf16[128,1,512]{2,0,1:T(8,128)(2,1)}, u32[]{:S(2)}) copy-start(bf16[128,1,512]{2,0,1:T(8,128)(2,1)} %param.7) | copy-start | bytes 393220
  3.3 45.0 %copy-start.2 = (bf16[128,3,3,512]{3,0,2,1:T(8,128)(2,1)S(1)}, bf16[128,3,3,512]{3,0,2,1:T(8,128)(2,1)}, u32[]{:S(2)}) copy-start(bf16[128,3,3,512]{3,0,2,1:T(8,128)(2,1)} %param.5) | copy-start | bytes 3538948
  3.3 17.4 %collective-permute-start.3 = (bf16[2,9,64,128]{3,2,1,0:T(8,128)(2,1)S(1)}, bf16[2,9,64,128]{3,2,1,0:T(8,128)(2,1)S(1)}, u32[]{:S(2)}, u32[]{:S(2)}) collective-permute-start(bf16[2,9,64,128]{3,2,1,0:T(8,128)(2,1)S(1)} %get-tuple-element.97), channel_id=1, source_target_pairs={{0,2},{1,3},{2,0},{3,1},{4,6},{5,7},{6,4},{7,5},{8,10},{9,11},{10,... | collective-permute-start | bytes 884744 | tf_op jit(solution)/shard_map/ppermute | solution.py:103
  6.3 8.3 %collective-permute-start.2 = (bf16[1,128,512]{2,1,0:T(8,128)(2,1)S(1)}, bf16[1,128,512]{2,1,0:T(8,128)(2,1)S(1)}, u32[]{:S(2)}, u32[]{:S(2)}) collective-permute-start(bf16[1,128,512]{2,1,0:T(8,128)(2,1)S(1)} %bitcast.22), channel_id=1, source_target_pairs={{0,24},{4,28},{8,16},{12,20},{16,8},{20,12},{24,0},{28,4},{1,25},{... | collective-permute-start | bytes 393224 | tf_op jit(solution)/shard_map/ppermute | solution.py:103
  9.9 10.8 %collective-permute-start.1 = (bf16[1,128,512]{2,1,0:T(8,128)(2,1)S(1)}, bf16[1,128,512]{2,1,0:T(8,128)(2,1)S(1)}, u32[]{:S(2)}, u32[]{:S(2)}) collective-permute-start(bf16[1,128,512]{2,1,0:T(8,128)(2,1)S(1)} %bitcast.23), channel_id=1, source_target_pairs={{0,16},{4,20},{8,24},{12,28},{16,0},{20,4},{24,8},{28,12},{1,17},{... | collective-permute-start | bytes 393224 | tf_op jit(solution)/shard_map/ppermute | solution.py:103
  9.9 10.8 %collective-permute-start = (bf16[1,128,512]{2,1,0:T(8,128)(2,1)S(1)}, bf16[1,128,512]{2,1,0:T(8,128)(2,1)S(1)}, u32[]{:S(2)}, u32[]{:S(2)}) collective-permute-start(bf16[1,128,512]{2,1,0:T(8,128)(2,1)S(1)} %bitcast.24), channel_id=1, source_target_pairs={{0,8},{4,12},{8,0},{12,4},{16,24},{20,28},{24,16},{28,20},{1,9},{5... | collective-permute-start | bytes 393224 | tf_op jit(solution)/shard_map/ppermute | solution.py:103
  20.8 14.8 %collective-permute-start.8 = (bf16[4,128,512]{2,1,0:T(8,128)(2,1)S(1)}, bf16[4,128,512]{2,1,0:T(8,128)(2,1)S(1)}, u32[]{:S(2)}, u32[]{:S(2)}) collective-permute-start(bf16[4,128,512]{2,1,0:T(8,128)(2,1)S(1)} %pad_maximum_fusion.refs_0_), channel_id=1, source_target_pairs={{0,4},{4,0},{8,12},{12,8},{16,20},{20,16},{24,28},{28,24},{1,5},{5... | collective-permute-start | bytes 1572872 | tf_op jit(solution)/shard_map/ppermute | solution.py:103
  22.4 13.2 %collective-permute-start.7 = (bf16[4,128,512]{2,1,0:T(8,128)(2,1)S(1)}, bf16[4,128,512]{2,1,0:T(8,128)(2,1)S(1)}, u32[]{:S(2)}, u32[]{:S(2)}) collective-permute-start(bf16[4,128,512]{2,1,0:T(8,128)(2,1)S(1)} %pad_maximum_fusion.refs_0_), channel_id=1, source_target_pairs={{0,2},{1,3},{2,0},{3,1},{4,6},{5,7},{6,4},{7,5},{8,10},{9,11},{10,... | collective-permute-start | bytes 1572872 | tf_op jit(solution)/shard_map/ppermute | solution.py:103
  23.0 8.2 %collective-permute-start.6 = (bf16[1,128,512]{2,1,0:T(8,128)(2,1)S(1)}, bf16[1,128,512]{2,1,0:T(8,128)(2,1)S(1)}, u32[]{:S(2)}, u32[]{:S(2)}) collective-permute-start(bf16[1,128,512]{2,1,0:T(8,128)(2,1)S(1)} %bitcast.28), channel_id=1, source_target_pairs={{0,24},{4,28},{8,16},{12,20},{16,8},{20,12},{24,0},{28,4},{1,25},{... | collective-permute-start | bytes 393224 | tf_op jit(solution)/shard_map/ppermute | solution.py:103
  25.4 10.2 %collective-permute-start.5 = (bf16[1,128,512]{2,1,0:T(8,128)(2,1)S(1)}, bf16[1,128,512]{2,1,0:T(8,128)(2,1)S(1)}, u32[]{:S(2)}, u32[]{:S(2)}) collective-permute-start(bf16[1,128,512]{2,1,0:T(8,128)(2,1)S(1)} %bitcast.29), channel_id=1, source_target_pairs={{0,16},{4,20},{8,24},{12,28},{16,0},{20,4},{24,8},{28,12},{1,17},{... | collective-permute-start | bytes 393224 | tf_op jit(solution)/shard_map/ppermute | solution.py:103
  25.4 10.2 %collective-permute-start.4 = (bf16[1,128,512]{2,1,0:T(8,128)(2,1)S(1)}, bf16[1,128,512]{2,1,0:T(8,128)(2,1)S(1)}, u32[]{:S(2)}, u32[]{:S(2)}) collective-permute-start(bf16[1,128,512]{2,1,0:T(8,128)(2,1)S(1)} %bitcast.30), channel_id=1, source_target_pairs={{0,8},{4,12},{8,0},{12,4},{16,24},{20,28},{24,16},{28,20},{1,9},{5... | collective-permute-start | bytes 393224 | tf_op jit(solution)/shard_map/ppermute | solution.py:103
  35.6 10.6 %collective-permute-start.11 = (bf16[4,128,512]{2,1,0:T(8,128)(2,1)S(1)}, bf16[4,128,512]{2,1,0:T(8,128)(2,1)S(1)}, u32[]{:S(2)}, u32[]{:S(2)}) collective-permute-start(bf16[4,128,512]{2,1,0:T(8,128)(2,1)S(1)} %pad_maximum_fusion.refs_0_), channel_id=1, source_target_pairs={{0,1},{1,0},{2,3},{3,2},{4,5},{5,4},{6,7},{7,6},{8,9},{9,8},{10,11... | collective-permute-start | bytes 1572872 | tf_op jit(solution)/shard_map/ppermute | solution.py:103
  35.7 10.6 %collective-permute-start.12 = (bf16[4,128,512]{2,1,0:T(8,128)(2,1)S(1)}, bf16[4,128,512]{2,1,0:T(8,128)(2,1)S(1)}, u32[]{:S(2)}, u32[]{:S(2)}) collective-permute-start(bf16[4,128,512]{2,1,0:T(8,128)(2,1)S(1)} %collective-permute-done.7.refs_2_), channel_id=1, source_target_pairs={{0,1},{1,0},{2,3},{3,2},{4,5},{5,4},{6,7},{7,6},{8,9},{9,8},{10,11... | collective-permute-start | bytes 1572872 | tf_op jit(solution)/shard_map/ppermute | solution.py:103
  36.2 10.1 %collective-permute-start.13 = (bf16[4,128,512]{2,1,0:T(8,128)(2,1)S(1)}, bf16[4,128,512]{2,1,0:T(8,128)(2,1)S(1)}, u32[]{:S(2)}, u32[]{:S(2)}) collective-permute-start(bf16[4,128,512]{2,1,0:T(8,128)(2,1)S(1)} %collective-permute-done.8.refs_4_), channel_id=1, source_target_pairs={{0,1},{1,0},{2,3},{3,2},{4,5},{5,4},{6,7},{7,6},{8,9},{9,8},{10,11... | collective-permute-start | bytes 1572872 | tf_op jit(solution)/shard_map/ppermute | solution.py:103
  36.3 8.7 %collective-permute-start.10 = (bf16[4,64,512]{2,1,0:T(8,128)(2,1)S(1)}, bf16[4,64,512]{2,1,0:T(8,128)(2,1)S(1)}, u32[]{:S(2)}, u32[]{:S(2)}) collective-permute-start(bf16[4,64,512]{2,1,0:T(8,128)(2,1)S(1)} %slice.19), channel_id=1, source_target_pairs={{0,2},{1,3},{2,0},{3,1},{4,6},{5,7},{6,4},{7,5},{8,10},{9,11},{10,... | collective-permute-start | bytes 786440 | tf_op jit(solution)/shard_map/ppermute | solution.py:103
  37.9 8.4 %collective-permute-start.9 = (bf16[4,64,512]{2,1,0:T(8,128)(2,1)S(1)}, bf16[4,64,512]{2,1,0:T(8,128)(2,1)S(1)}, u32[]{:S(2)}, u32[]{:S(2)}) collective-permute-start(bf16[4,64,512]{2,1,0:T(8,128)(2,1)S(1)} %slice.18), channel_id=1, source_target_pairs={{0,4},{4,0},{8,12},{12,8},{16,20},{20,16},{24,28},{28,24},{1,5},{5... | collective-permute-start | bytes 786440 | tf_op jit(solution)/shard_map/ppermute | solution.py:103
  46.3 1.6 %collective-permute-start.14 = (bf16[4,64,512]{2,1,0:T(8,128)(2,1)S(1)}, bf16[4,64,512]{2,1,0:T(8,128)(2,1)S(1)}, u32[]{:S(2)}, u32[]{:S(2)}) collective-permute-start(bf16[4,64,512]{2,1,0:T(8,128)(2,1)S(1)} %collective-permute-done.9.refs_6_), channel_id=1, source_target_pairs={{0,1},{1,0},{2,3},{3,2},{4,5},{5,4},{6,7},{7,6},{8,9},{9,8},{10,11... | collective-permute-start | bytes 786440 | tf_op jit(solution)/shard_map/ppermute | solution.py:103
  46.3 1.9 %collective-permute-start.15 = (bf16[4,64,512]{2,1,0:T(8,128)(2,1)S(1)}, bf16[4,64,512]{2,1,0:T(8,128)(2,1)S(1)}, u32[]{:S(2)}, u32[]{:S(2)}) collective-permute-start(bf16[4,64,512]{2,1,0:T(8,128)(2,1)S(1)} %collective-permute-done.10.refs_8_), channel_id=1, source_target_pairs={{0,1},{1,0},{2,3},{3,2},{4,5},{5,4},{6,7},{7,6},{8,9},{9,8},{10,11... | collective-permute-start | bytes 786440 | tf_op jit(solution)/shard_map/ppermute | solution.py:103
  51.6 16.8 %collective-permute-start.17 = (bf16[5,128,512]{2,1,0:T(8,128)(2,1)S(1)}, bf16[5,128,512]{2,1,0:T(8,128)(2,1)S(1)}, u32[]{:S(2)}, u32[]{:S(2)}) collective-permute-start(bf16[5,128,512]{2,1,0:T(8,128)(2,1)S(1)} %get-tuple-element.143.refs_0_), channel_id=1, source_target_pairs={{0,2},{1,3},{2,0},{3,1},{4,6},{5,7},{6,4},{7,5},{8,10},{9,11},{10,... | collective-permute-start | bytes 1966088 | tf_op jit(solution)/shard_map/ppermute | solution.py:103
  52.2 16.2 %collective-permute-start.16 = (bf16[5,128,512]{2,1,0:T(8,128)(2,1)S(1)}, bf16[5,128,512]{2,1,0:T(8,128)(2,1)S(1)}, u32[]{:S(2)}, u32[]{:S(2)}) collective-permute-start(bf16[5,128,512]{2,1,0:T(8,128)(2,1)S(1)} %get-tuple-element.143.refs_0_), channel_id=1, source_target_pairs={{0,1},{1,0},{2,3},{3,2},{4,5},{5,4},{6,7},{7,6},{8,9},{9,8},{10,11... | collective-permute-start | bytes 1966088 | tf_op jit(solution)/shard_map/ppermute | solution.py:103
  52.2 3.3 %collective-permute-start.18 = (bf16[9,128,128]{2,1,0:T(8,128)(2,1)S(1)}, bf16[9,128,128]{2,1,0:T(8,128)(2,1)S(1)}, u32[]{:S(2)}, u32[]{:S(2)}) collective-permute-start(bf16[9,128,128]{2,1,0:T(8,128)(2,1)S(1)} %get-tuple-element.136), channel_id=1, source_target_pairs={{0,1},{1,0},{2,3},{3,2},{4,5},{5,4},{6,7},{7,6},{8,9},{9,8},{10,11... | collective-permute-start | bytes 884744 | tf_op jit(solution)/shard_map/ppermute | solution.py:103
  52.8 16.5 %collective-permute-start.22 = (bf16[4,128,512]{2,1,0:T(8,128)(2,1)S(1)}, bf16[4,128,512]{2,1,0:T(8,128)(2,1)S(1)}, u32[]{:S(2)}, u32[]{:S(2)}) collective-permute-start(bf16[4,128,512]{2,1,0:T(8,128)(2,1)S(1)} %pad_maximum_fusion.1.refs_5_.refs_9_), channel_id=1, source_target_pairs={{0,4},{4,0},{8,12},{12,8},{16,20},{20,16},{24,28},{28,24},{1,5},{5... | collective-permute-start | bytes 1572872 | tf_op jit(solution)/shard_map/ppermute | solution.py:103
  53.2 2.3 %collective-permute-start.19 = (bf16[1,9,64,128]{3,2,1,0:T(8,128)(2,1)S(1)}, bf16[1,9,64,128]{3,2,1,0:T(8,128)(2,1)S(1)}, u32[]{:S(2)}, u32[]{:S(2)}) collective-permute-start(bf16[1,9,64,128]{3,2,1,0:T(8,128)(2,1)S(1)} %get-tuple-element.190), channel_id=1, source_target_pairs={{0,1},{1,0},{2,3},{3,2},{4,5},{5,4},{6,7},{7,6},{8,9},{9,8},{10,11... | collective-permute-start | bytes 442376 | tf_op jit(solution)/shard_map/ppermute | solution.py:103
  53.3 17.3 %copy-start.1 = (bf16[128,3,3,512]{3,0,2,1:T(8,128)(2,1)S(1)}, bf16[128,3,3,512]{3,0,2,1:T(8,128)(2,1)}, u32[]{:S(2)}) copy-start(bf16[128,3,3,512]{3,0,2,1:T(8,128)(2,1)} %param.6) | copy-start | bytes 3538948
  68.5 2.1 %collective-permute-start.24 = (bf16[5,128,512]{2,1,0:T(8,128)(2,1)S(1)}, bf16[5,128,512]{2,1,0:T(8,128)(2,1)S(1)}, u32[]{:S(2)}, u32[]{:S(2)}) collective-permute-start(bf16[5,128,512]{2,1,0:T(8,128)(2,1)S(1)} %collective-permute-done.17.refs_2_), channel_id=1, source_target_pairs={{0,1},{1,0},{2,3},{3,2},{4,5},{5,4},{6,7},{7,6},{8,9},{9,8},{10,11... | collective-permute-start | bytes 1966088 | tf_op jit(solution)/shard_map/ppermute | solution.py:103
  68.5 11.5 %collective-permute-start.21 = (bf16[3,128,512]{2,1,0:T(8,128)(2,1)S(1)}, bf16[3,128,512]{2,1,0:T(8,128)(2,1)S(1)}, u32[]{:S(2)}, u32[]{:S(2)}) collective-permute-start(bf16[3,128,512]{2,1,0:T(8,128)(2,1)S(1)} %get-tuple-element.152.refs_4_), channel_id=1, source_target_pairs={{0,2},{1,3},{2,0},{3,1},{4,6},{5,7},{6,4},{7,5},{8,10},{9,11},{10,... | collective-permute-start | bytes 1179656 | tf_op jit(solution)/shard_map/ppermute | solution.py:103
  69.0 11.0 %collective-permute-start.20 = (bf16[3,128,512]{2,1,0:T(8,128)(2,1)S(1)}, bf16[3,128,512]{2,1,0:T(8,128)(2,1)S(1)}, u32[]{:S(2)}, u32[]{:S(2)}) collective-permute-start(bf16[3,128,512]{2,1,0:T(8,128)(2,1)S(1)} %get-tuple-element.152.refs_4_), channel_id=1, source_target_pairs={{0,1},{1,0},{2,3},{3,2},{4,5},{5,4},{6,7},{7,6},{8,9},{9,8},{10,11... | collective-permute-start | bytes 1179656 | tf_op jit(solution)/shard_map/ppermute | solution.py:103
  69.3 9.2 %collective-permute-start.23 = (bf16[2,9,64,128]{3,2,1,0:T(8,128)(2,1)S(1)}, bf16[2,9,64,128]{3,2,1,0:T(8,128)(2,1)S(1)}, u32[]{:S(2)}, u32[]{:S(2)}) collective-permute-start(bf16[2,9,64,128]{3,2,1,0:T(8,128)(2,1)S(1)} %collective-permute-done.3), channel_id=1, source_target_pairs={{0,4},{4,0},{8,12},{12,8},{16,20},{20,16},{24,28},{28,24},{1,5},{5... | collective-permute-start | bytes 884744 | tf_op jit(solution)/shard_map/ppermute | solution.py:103
  80.0 8.7 %collective-permute-start.26 = (bf16[4,128,512]{2,1,0:T(8,128)(2,1)S(1)}, bf16[4,128,512]{2,1,0:T(8,128)(2,1)S(1)}, u32[]{:S(2)}, u32[]{:S(2)}) collective-permute-start(bf16[4,128,512]{2,1,0:T(8,128)(2,1)S(1)} %get-tuple-element.174.refs_8_.refs_0_), channel_id=1, source_target_pairs={{0,1},{1,0},{2,3},{3,2},{4,5},{5,4},{6,7},{7,6},{8,9},{9,8},{10,11... | collective-permute-start | bytes 1572872 | tf_op jit(solution)/shard_map/ppermute | solution.py:103
  80.0 2.5 %collective-permute-start.28 = (bf16[3,128,512]{2,1,0:T(8,128)(2,1)S(1)}, bf16[3,128,512]{2,1,0:T(8,128)(2,1)S(1)}, u32[]{:S(2)}, u32[]{:S(2)}) collective-permute-start(bf16[3,128,512]{2,1,0:T(8,128)(2,1)S(1)} %collective-permute-done.21.refs_6_), channel_id=1, source_target_pairs={{0,1},{1,0},{2,3},{3,2},{4,5},{5,4},{6,7},{7,6},{8,9},{9,8},{10,11... | collective-permute-start | bytes 1179656 | tf_op jit(solution)/shard_map/ppermute | solution.py:103
  80.5 8.2 %collective-permute-start.25 = (bf16[2,128,512]{2,1,0:T(8,128)(2,1)S(1)}, bf16[2,128,512]{2,1,0:T(8,128)(2,1)S(1)}, u32[]{:S(2)}, u32[]{:S(2)}) collective-permute-start(bf16[2,128,512]{2,1,0:T(8,128)(2,1)S(1)} %get-tuple-element.150), channel_id=1, source_target_pairs={{0,2},{1,3},{2,0},{3,1},{4,6},{5,7},{6,4},{7,5},{8,10},{9,11},{10,... | collective-permute-start | bytes 786440 | tf_op jit(solution)/shard_map/ppermute | solution.py:103
  81.1 5.8 %collective-permute-start.27 = (bf16[1,9,64,128]{3,2,1,0:T(8,128)(2,1)S(1)}, bf16[1,9,64,128]{3,2,1,0:T(8,128)(2,1)S(1)}, u32[]{:S(2)}, u32[]{:S(2)}) collective-permute-start(bf16[1,9,64,128]{3,2,1,0:T(8,128)(2,1)S(1)} %get-tuple-element.188), channel_id=1, source_target_pairs={{0,1},{1,0},{2,3},{3,2},{4,5},{5,4},{6,7},{7,6},{8,9},{9,8},{10,11... | collective-permute-start | bytes 442376 | tf_op jit(solution)/shard_map/ppermute | solution.py:103
  88.8 7.9 %collective-permute-start.30 = (bf16[2,128,512]{2,1,0:T(8,128)(2,1)S(1)}, bf16[2,128,512]{2,1,0:T(8,128)(2,1)S(1)}, u32[]{:S(2)}, u32[]{:S(2)}) collective-permute-start(bf16[2,128,512]{2,1,0:T(8,128)(2,1)S(1)} %collective-permute-done.25.refs_2_), channel_id=1, source_target_pairs={{0,4},{4,0},{8,12},{12,8},{16,20},{20,16},{24,28},{28,24},{1,5},{5... | collective-permute-start | bytes 786440 | tf_op jit(solution)/shard_map/ppermute | solution.py:103
  89.2 13.1 %collective-permute-start.33 = (bf16[4,128,512]{2,1,0:T(8,128)(2,1)S(1)}, bf16[4,128,512]{2,1,0:T(8,128)(2,1)S(1)}, u32[]{:S(2)}, u32[]{:S(2)}) collective-permute-start(bf16[4,128,512]{2,1,0:T(8,128)(2,1)S(1)} %get-tuple-element.180.refs_9_.refs_6_), channel_id=1, source_target_pairs={{0,2},{1,3},{2,0},{3,1},{4,6},{5,7},{6,4},{7,5},{8,10},{9,11},{10,... | collective-permute-start | bytes 1572872 | tf_op jit(solution)/shard_map/ppermute | solution.py:103
  89.8 12.5 %collective-permute-start.29 = (bf16[4,128,512]{2,1,0:T(8,128)(2,1)S(1)}, bf16[4,128,512]{2,1,0:T(8,128)(2,1)S(1)}, u32[]{:S(2)}, u32[]{:S(2)}) collective-permute-start(bf16[4,128,512]{2,1,0:T(8,128)(2,1)S(1)} %get-tuple-element.180.refs_9_.refs_6_), channel_id=1, source_target_pairs={{0,1},{1,0},{2,3},{3,2},{4,5},{5,4},{6,7},{7,6},{8,9},{9,8},{10,11... | collective-permute-start | bytes 1572872 | tf_op jit(solution)/shard_map/ppermute | solution.py:103
  89.8 6.9 %collective-permute-start.31 = (bf16[2,128,512]{2,1,0:T(8,128)(2,1)S(1)}, bf16[2,128,512]{2,1,0:T(8,128)(2,1)S(1)}, u32[]{:S(2)}, u32[]{:S(2)}) collective-permute-start(bf16[2,128,512]{2,1,0:T(8,128)(2,1)S(1)} %collective-permute-done.25.refs_2_), channel_id=1, source_target_pairs={{0,1},{1,0},{2,3},{3,2},{4,5},{5,4},{6,7},{7,6},{8,9},{9,8},{10,11... | collective-permute-start | bytes 786440 | tf_op jit(solution)/shard_map/ppermute | solution.py:103
  96.6 1.5 %collective-permute-start.32 = (bf16[2,128,512]{2,1,0:T(8,128)(2,1)S(1)}, bf16[2,128,512]{2,1,0:T(8,128)(2,1)S(1)}, u32[]{:S(2)}, u32[]{:S(2)}) collective-permute-start(bf16[2,128,512]{2,1,0:T(8,128)(2,1)S(1)} %collective-permute-done.30.refs_4_), channel_id=1, source_target_pairs={{0,1},{1,0},{2,3},{3,2},{4,5},{5,4},{6,7},{7,6},{8,9},{9,8},{10,11... | collective-permute-start | bytes 786440 | tf_op jit(solution)/shard_map/ppermute | solution.py:103
  102.3 2.0 %collective-permute-start.34 = (bf16[4,128,512]{2,1,0:T(8,128)(2,1)S(1)}, bf16[4,128,512]{2,1,0:T(8,128)(2,1)S(1)}, u32[]{:S(2)}, u32[]{:S(2)}) collective-permute-start(bf16[4,128,512]{2,1,0:T(8,128)(2,1)S(1)} %collective-permute-done.33.refs_8_), channel_id=1, source_target_pairs={{0,1},{1,0},{2,3},{3,2},{4,5},{5,4},{6,7},{7,6},{8,9},{9,8},{10,11... | collective-permute-start | bytes 1572872 | tf_op jit(solution)/shard_map/ppermute | solution.py:103

commit v4 on v3

--- a/solution.py
+++ b/solution.py
@@ -100,7 +100,12 @@
 
 
 def swap(value, axis, bits):
-    return lax.ppermute(value, axis, [(i, i ^ bits) for i in range(lax.axis_size(axis))])
+    if axis == "filt":
+        way = "mate" if bits == 1 else "over_x"
+    else:
+        way = "over_y" if bits == 1 else "along_z"
+    with jax.named_scope(way):
+        return lax.ppermute(value, axis, [(i, i ^ bits) for i in range(lax.axis_size(axis))])
 
 
 def block_at(index, size):
@@ -225,22 +230,32 @@
             block_out[0] = jnp.maximum(pre, 0.0).astype(BF)
 
 
-def turn_kernel(weight, mine, mate, over):
-    taps, own = weight.shape[:2]
+def pick_kernel(weight, mate, over, sems):
+    own, half = mate.shape[1], over.shape[2]
     f0, y0 = lax.axis_index("filt"), lax.axis_index("rows") & 1
-    for t in range(taps):
-        mine[t] = weight[t, :, block_at(f0, own)].T
-        mate[t] = weight[t, :, block_at(f0 ^ 1, own)].T
-        for e in (2, 3):
-            block = weight[t, :, block_at(f0 ^ e, own)].T
-
-            @pl.when(y0 == 0)
-            def _(block=block, e=e, t=t):
-                over[e - 2, t] = block[: own // 2]
-
-            @pl.when(y0 == 1)
-            def _(block=block, e=e, t=t):
-                over[e - 2, t] = block[own // 2 :]
+    copies = [pltpu.make_async_copy(weight.at[:, :, block_at(f0 ^ 1, own)], mate, sems.at[0])]
+    for e in (2, 3):
+        part = weight.at[:, block_at(y0, half), block_at(f0 ^ e, own)]
+        copies.append(pltpu.make_async_copy(part, over.at[e - 2], sems.at[e - 1]))
+    for copy in copies:
+        copy.start()
+    for copy in copies:
+        copy.wait()
+
+
+def turn_kernel(weight, mate, near2, near3, far2, far3, wide):
+    own, half = mate.shape[1], near2.shape[2]
+    c = wide.shape[1] // 3
+    f0, y0 = lax.axis_index("filt"), lax.axis_index("rows") & 1
+    for t in range(weight.shape[0]):
+        a, b = t // 3, t % 3
+        left = jnp.concatenate([near2[0, t], far2[0, t]], axis=0), jnp.concatenate([near3[0, t], far3[0, t]], axis=0)
+        right = jnp.concatenate([far2[0, t], near2[0, t]], axis=0), jnp.concatenate([far3[0, t], near3[0, t]], axis=0)
+        blocks = [weight[t, :, block_at(f0, own)], mate[t]]
+        blocks += [jnp.where(y0 == 0, x, y) for x, y in zip(left, right)]
+        for e, block in enumerate(blocks):
+            at = pl.ds(pl.multiple_of((2 - a) * c + (f0 ^ e) * own, own), own)
+            wide[b * own : (b + 1) * own, at] = block.T
 
 
 def back_rows(part, rows, lo, x, wide, masks, grad_first):
@@ -251,33 +266,11 @@
         grad_first[r - part[0]] = jnp.where(mask > 0, total, 0.0).astype(BF)
 
 
-def back_kernel(layout, part, rows, *refs):
-    pieces = refs[: len(layout)]
-    mine, mate, near2, far2, near3, far3, mask, grad_first, wide, x = refs[len(layout) :]
-    own, c = grad_first.shape[1], x.shape[1]
-    f0, y0 = lax.axis_index("filt"), lax.axis_index("rows") & 1
+def back_kernel(layout, part, rows, bases, *refs):
+    pieces, (wide, *masks, grad_first, x) = refs[: len(layout)], refs[len(layout) :]
     lo, hi = max(part[0] - 1, 0), min(part[1] + 1, rows)
     fill_rows(x, layout, pieces, lo, hi)
-    for t in range(9):
-        a, b = t // 3, t % 3
-
-        def at(e, a=a):
-            return pl.ds(pl.multiple_of((2 - a) * c + (f0 ^ e) * own, own), own)
-
-        wide[b * own : (b + 1) * own, at(0)] = mine[t]
-        wide[b * own : (b + 1) * own, at(1)] = mate[t]
-        for e, near, far in ((2, near2, far2), (3, near3, far3)):
-            for y, ref in ((y0, near), (1 - y0, far)):
-                rows_at = pl.ds(pl.multiple_of(b * own + y * (own // 2), own // 2), own // 2)
-                wide[rows_at, at(e)] = ref[0, t]
-    back_rows(part, rows, lo, x, wide, [(0, mask)], grad_first)
-
-
-def back_rest_kernel(layout, part, rows, cut, *refs):
-    pieces, (wide, mask_a, mask_b, grad_first, x) = refs[: len(layout)], refs[len(layout) :]
-    lo, hi = max(part[0] - 1, 0), min(part[1] + 1, rows)
-    fill_rows(x, layout, pieces, lo, hi)
-    back_rows(part, rows, lo, x, wide, [(0, mask_a), (cut, mask_b)], grad_first)
+    back_rows(part, rows, lo, x, wide, list(zip(bases, masks)), grad_first)
 
 
 def fill_moved(grads, moved):
@@ -298,18 +291,19 @@
     return lax.dot_general(left, right, (((1,), (1,)), ((), ())), preferred_element_type=F32)
 
 
-def second_terms_kernel(layout, *refs):
-    pieces, (grad_a, grad_b, out, x, moved) = refs[: len(layout)], refs[len(layout) :]
-    w = grad_a.shape[2]
-    rows = moved.shape[1] // w
+def second_terms_kernel(layout, part, with_before, *refs):
+    pieces, (grad, *refs) = refs[: len(layout)], refs[len(layout) :]
+    out, x, moved = refs[with_before:]
+    w = grad.shape[2]
 
     def put(r, at, value):
         x[at, r * w : (r + 1) * w] = value
 
-    copy_pieces(layout, pieces, put, 0, rows)
-    fill_moved([grad_a, grad_b], moved)
-    for a in range(3):
-        out[a] = sum_terms(moved, x, w, a, (0, rows))
+    copy_pieces(layout, pieces, put, max(part[0] - 1, 0), min(part[1] + 1, x.shape[1] // w))
+    fill_moved([grad], moved)
+    for a in range(3):
+        terms = sum_terms(moved, x, w, a, part)
+        out[a] = refs[0][a] + terms if with_before else terms
 
 
 def first_terms_kernel(part, flat, grad, out, moved):
@@ -330,14 +324,16 @@
 
 
 VM = pl.BlockSpec(memory_space=pltpu.VMEM)
-
-
-def call(kernel, ins, outs, scratch, flops, name, out_spec=VM):
+ANY = pl.BlockSpec(memory_space=pl.ANY)
+DMA = pltpu.SemaphoreType.DMA
+
+
+def call(kernel, ins, outs, scratch, flops, name, in_spec=VM, out_spec=VM):
     nbytes = sum(v.size * v.dtype.itemsize for v in ins) if flops else 0
     return pl.pallas_call(
         kernel,
         out_shape=[jax.ShapeDtypeStruct(s, d) for s, d in outs],
-        in_specs=[VM] * len(ins),
+        in_specs=[in_spec] * len(ins),
         out_specs=[out_spec] * len(outs),
         scratch_shapes=scratch,
         compiler_params=pltpu.CompilerParams(vmem_limit_bytes=VMEM_BYTES),
@@ -380,21 +376,23 @@
     def act(n):
         return ((n, own, w), BF)
 
-    v = {f"z{d}": swap(feat, "rows", d) for d in zs}
-    mine, mate, over = call(
-        turn_kernel,
-        [w2.reshape(9, own, c)],
-        [((9, own, own), BF), ((9, own, own), BF), ((2, 9, half, own), BF)],
-        [],
-        row_flops * 2,
-        "turn_weight",
-    )
-    v |= {"mine": mine, "mate": mate, "near": over_x(over)}
+    v = {f"z{d}": swap(feat, "rows", d) for d in zs[::-1]}
+    w2_taps = w2.reshape(9, own, c)
+    mate, over = call(
+        pick_kernel,
+        [w2_taps],
+        [((9, own, own), BF), ((2, 9, half, own), BF)],
+        [DMA((3,))],
+        0,
+        "pick_weight",
+        in_spec=ANY,
+    )
+    v |= {"mate": mate, "near": over_x(over)}
     v = wave(v)
 
     zs = (0, *zs)
     z4 = jnp.concatenate([feat] + [v[f"z{d}"] for d in zs[1:]], axis=0)
-    v |= {f"g{d}": swap(ograd, "rows", d) for d in zs[1:]}
+    v |= {f"g{d}": swap(ograd, "rows", d) for d in zs[:0:-1]}
     v |= {"z4": z4, "x4": over_x(z4), "y4": over_y(z4)}
     v = wave(v)
 
@@ -422,7 +420,8 @@
     h = {"a0": h_a, "a1": to_mate(h_a), "a2": over_x(h_a)}
     gy = over_y(v["g4"])
     h |= {"m1": to_mate(v["mate"]), "near3": to_mate(v["near"][1:])}
-    h["b0"], mask_b, flat = call(
+    h["gy"] = gy
+    h_b, mask_b, flat = call(
         functools.partial(first_rest_kernel, (cut_a, rows)),
         [full, w1],
         [act(rows - cut_a)] * 2 + [((c, rows * w), BF)],
@@ -430,12 +429,14 @@
         0,
         "first_conv_b",
     )
+    b1, b2 = to_mate(h_b), over_x(h_b)
+    h |= {"b0": h_b}
     h = wave(h)
-    h |= {"b2": over_x(h["b0"]), "b1": to_mate(h["b0"])}
-    a3 = to_mate(h["a2"])
-    layout_a = [(e, 0, "whole") for e in range(4)]
-    spread_a = [h["a0"], h["a1"], h["a2"], a3]
-    grads = [v["g4"], gy]
+    h |= {"b2": b2, "b1": b1}
+    cuts = [(n, min(n + 2, cut_a)) for n in range(0, cut_a, 2)]
+    layout_a = [(e, 0, "whole") for e in range(3)] + [(3, n, "whole") for n, _ in cuts]
+    spread_a = [h["a0"], h["a1"], h["a2"]] + [to_mate(h["a2"][n:m]) for n, m in cuts]
+    grads = [v["g4"], h["gy"]]
     grad_places = [(p, k, z ^ p) for p in (0, 1) for k, z in enumerate(zs)]
 
     def second(layout, spread, part, before, early, name):
@@ -450,34 +451,44 @@
         )
 
     s = {"b0": h["b0"], "b1": h["b1"], "b2": h["b2"], "far": over_y(lax.optimization_barrier((v["near"], gy))[0])}
-    s["out"], s["a0"], s["early"] = second(layout_a, spread_a, (0, cut), feat, 1, "second_conv_a")
+    s["out"], gs_a, early = second(layout_a, spread_a, (0, cut), feat, 1, "second_conv_a")
+    (s["terms"],) = call(
+        functools.partial(second_terms_kernel, layout_a, (0, cut), 0),
+        [*spread_a, gs_a],
+        [((3, 3 * own, c), F32)],
+        [vm((c, cut_a * w), BF), vm((3 * own, cut * w), BF)],
+        0,
+        "second_terms_a",
+    )
     s = wave(s)
-    layout_b = layout_a + [(e, cut_a, "whole") for e in range(4)]
-    spread_b = spread_a + [s["b0"], s["b1"], s["b2"], to_mate(s["b2"])]
-    t = {"a0": s["a0"], "s2": over_x(s["early"]), "a1": to_mate(s["a0"]), "far3": to_mate(s["far"][1:])}
+    n_b = rows - cut_a
+    layout_b = layout_a + [(e, cut_a, "whole") for e in range(3)] + [(3, cut_a + n, "whole") for n in range(n_b)]
+    spread_b = spread_a + [s["b0"], s["b1"], s["b2"]] + [to_mate(s["b2"][n : n + 1]) for n in range(n_b)]
+    t = {"a0": gs_a, "s2": over_x(early), "a1": to_mate(gs_a), "far3": to_mate(s["far"][1:])}
     t["out"], t["b0"] = second(layout_b, spread_b, (cut, rows), s["out"], 0, "second_conv_b")
+    b2 = over_x(t["b0"])
     t = wave(t)
-    b2 = over_x(t["b0"])
     t |= {"b1": to_mate(t["b0"]), "t2": over_y(t["s2"]), "s3": to_mate(t["s2"])}
 
     (second_grad,) = call(
-        functools.partial(second_terms_kernel, layout_b),
-        [*spread_b, t["a0"], t["b0"]],
+        functools.partial(second_terms_kernel, layout_b, (cut, rows), 1),
+        [*spread_b, t["b0"], s["terms"]],
         [((3, 3 * own, c), F32)],
-        [vm((c, rows * w), BF), vm((3 * own, rows * w), BF)],
-        0,
-        "second_terms",
+        [vm((c, rows * w), BF), vm((3 * own, (rows - cut) * w), BF)],
+        0,
+        "second_terms_b",
     )
     t["t2"], second_grad = lax.optimization_barrier((t["t2"], second_grad))
     t["t3"] = to_mate(t["t2"])
     last = cut - 1
     layout = [(e, 0, "whole") for e in (0, 1)] + [(e, 0, kind) for kind in ("own", "other") for e in (2, 3)]
     names = ["a0", "a1", "s2", "s3", "t2", "t3"]
-    turned = [v["mine"], h["m1"], v["near"][:1], s["far"][:1], h["near3"], t["far3"]]
-    grad_first, wide_back = call(
-        functools.partial(back_kernel, layout, (0, last), rows),
-        [*(t[k] for k in names), *turned, mask_a],
-        [act(last), ((3 * own, 3 * c), BF)],
+    turned = [w2_taps, h["m1"], v["near"][:1], h["near3"], s["far"][:1], t["far3"]]
+    (wide_back,) = call(turn_kernel, turned, [((3 * own, 3 * c), BF)], [], 0, "turn_weight")
+    (grad_first,) = call(
+        functools.partial(back_kernel, layout, (0, last), rows, (0,)),
+        [*(t[k] for k in names), wide_back, mask_a],
+        [act(last)],
         [vm((cut, c, w), BF)],
         0,
         "hidden_grad_a",
@@ -494,7 +505,7 @@
     t = wave(t)
     layout += [(e, cut, "whole") for e in range(4)]
     (grad_first,) = call(
-        functools.partial(back_rest_kernel, layout, (last, rows), rows, cut_a),
+        functools.partial(back_kernel, layout, (last, rows), rows, (0, cut_a)),
         [*(t[k] for k in names), t["b0"], t["b1"], t["b2"], to_mate(t["b2"]), t["wide"], mask_a, mask_b],
         [act(rows - last)],
         [vm((rows - last + 1, c, w), BF)],
@@ -505,10 +516,10 @@
         functools.partial(first_terms_rest_kernel, (last, rows)),
         [flat, grad_first, t["terms"]],
         [((3, 3 * own, c), F32)],
-        [vm((3 * own, (rows - last) * w), BF), vm((3, 3 * own, c), F32), pltpu.SemaphoreType.DMA((3,))],
+        [vm((3 * own, (rows - last) * w), BF), vm((3, 3 * own, c), F32), DMA((3,))],
         row_flops * (rows - last),
         "first_terms_b",
-        pl.BlockSpec(memory_space=pl.ANY),
+        out_spec=ANY,
     )
 
     def as_weight(value):

time: 112 us -> 111 us (level)
  waiting for transfers between devices: 53.8 us -> 49 us
  starting transfers between devices: 22.9 us -> 26.1 us
    ppermute x35 -> x39, waiting for transfers between devices: 53.8 us -> 49 us  [swap(): lax.ppermute(value, axis, [(i, i ^ bits) for i in range(lax.axis_size(axi...]
    ppermute x35 -> x39, starting transfers between devices: 22.9 us -> 26.1 us  [swap(): lax.ppermute(value, axis, [(i, i ^ bits) for i in range(lax.axis_size(axi...]
    pallas_call x10 -> x12, Pallas kernels: 32.8 us -> 32 us  [call(): pl.pallas_call(kernel, out_shape=[jax.ShapeDtypeStruct(s, d) for s, d in...]
  transfers between devices with their start and end apart: 35 -> 39, of which waited for: 16 -> 20; matrix products, arithmetic and copies ran while one was open for 0% -> 0% of each run, Pallas kernels for 18% -> 19%
where the time goes in v4:
time: 111 us
  waiting for transfers between devices  49 us (44%)
  Pallas kernels  32 us (29%)
  starting transfers between devices  26.1 us (24%)
  local copies, waits for them, and re-layouts  1.43 us (1%)
    ppermute x39, waiting for transfers between devices, swap(): lax.ppermute(value, axis, [(i, i ^ bits) for i in range(lax.axis_size(axi...  49 us
    pallas_call x12, Pallas kernels, call(): pl.pallas_call(kernel, out_shape=[jax.ShapeDtypeStruct(s, d) for s, d in...  32 us
    ppermute x39, starting transfers between devices, swap(): lax.ppermute(value, axis, [(i, i ^ bits) for i in range(lax.axis_size(axi...  26.1 us
  transfers between devices with their start and end apart: 39, of which 20 were waited for; matrix products, arithmetic and copies ran while one was open for 0% of the time, Pallas kernels for 19%

profile of v4, /device:TPU:0, one launch (start us, length us, event | category | flops | bytes accessed | tf_op | source)
XLA Modules:
  0.0 110.6 jit_solution(5384050229260392299)
XLA Ops:
  0.6 1.3 %copy-done = bf16[128,3,3,512]{3,0,2,1:T(8,128)(2,1)S(1)} copy-done((bf16[128,3,3,512]{3,0,2,1:T(8,128)(2,1)S(1)}, bf16[128,3,3,512]{3,0,2,1:T(8,128)(2,1)}, u32[]{:S(2)}) %copy-start) | copy-done | bytes 1179672
  1.9 0.1 pick_weight.1
  2.1 3.0 %collective-permute-start.3 = (bf16[2,9,64,128]{3,2,1,0:T(8,128)(2,1)S(1)}, bf16[2,9,64,128]{3,2,1,0:T(8,128)(2,1)S(1)}, u32[]{:S(2)}, u32[]{:S(2)}) collective-permute-start(bf16[2,9,64,128]{3,2,1,0:T(8,128)(2,1)S(1)} %get-tuple-element.89), channel_id=1, source_target_pairs={{0,2},{1,3},{2,0},{3,1},{4,6},{5,7},{6,4},{7,5},{8,10},{9,11},{10,... | collective-permute-start | bytes 884744 | tf_op jit(solution)/shard_map/over_x/ppermute | solution.py:108
  5.1 3.6 %collective-permute-start = (bf16[1,128,512]{2,1,0:T(8,128)(2,1)}, bf16[1,128,512]{2,1,0:T(8,128)(2,1)S(1)}, u32[]{:S(2)}, u32[]{:S(2)}) collective-permute-start(bf16[1,128,512]{2,1,0:T(8,128)(2,1)} %bitcast.23), channel_id=1, source_target_pairs={{0,24},{4,28},{8,16},{12,20},{16,8},{20,12},{24,0},{28,4},{1,25},{... | collective-permute-start | bytes 393224 | tf_op jit(solution)/shard_map/along_z/ppermute | solution.py:108
  8.7 0.8 collective-permute-start.2
  9.4 4.1 %collective-permute-done = bf16[1,128,512]{2,1,0:T(8,128)(2,1)S(1)} collective-permute-done((bf16[1,128,512]{2,1,0:T(8,128)(2,1)}, bf16[1,128,512]{2,1,0:T(8,128)(2,1)S(1)}, u32[]{:S(2)}, u32[]{:S(2)}) %collective-permute-start) | collective-permute-done | bytes 131104 | tf_op jit(solution)/shard_map/along_z/ppermute | solution.py:108
  13.5 6.1 %collective-permute-done.1 = bf16[1,128,512]{2,1,0:T(8,128)(2,1)S(1)} collective-permute-done((bf16[1,128,512]{2,1,0:T(8,128)(2,1)}, bf16[1,128,512]{2,1,0:T(8,128)(2,1)S(1)}, u32[]{:S(2)}, u32[]{:S(2)}) %collective-permute-start.1) | collective-permute-done | bytes 131104 | tf_op jit(solution)/shard_map/along_z/ppermute | solution.py:108
  19.7 1.0 pad_maximum_fusion.refs_0_
  20.6 0.6 collective-permute-start.7
  21.2 1.5 %collective-permute-start.8 = (bf16[4,128,512]{2,1,0:T(8,128)(2,1)S(1)}, bf16[4,128,512]{2,1,0:T(8,128)(2,1)S(1)}, u32[]{:S(2)}, u32[]{:S(2)}) collective-permute-start(bf16[4,128,512]{2,1,0:T(8,128)(2,1)S(1)} %pad_maximum_fusion.refs_0_), channel_id=1, source_target_pairs={{0,4},{4,0},{8,12},{12,8},{16,20},{20,16},{24,28},{28,24},{1,5},{5... | collective-permute-start | bytes 1572872 | tf_op jit(solution)/shard_map/over_y/ppermute | solution.py:108
  22.8 2.5 %collective-permute-start.4 = (bf16[1,128,512]{2,1,0:T(8,128)(2,1)}, bf16[1,128,512]{2,1,0:T(8,128)(2,1)S(1)}, u32[]{:S(2)}, u32[]{:S(2)}) collective-permute-start(bf16[1,128,512]{2,1,0:T(8,128)(2,1)} %bitcast.29), channel_id=1, source_target_pairs={{0,24},{4,28},{8,16},{12,20},{16,8},{20,12},{24,0},{28,4},{1,25},{... | collective-permute-start | bytes 393224 | tf_op jit(solution)/shard_map/along_z/ppermute | solution.py:108
  25.2 1.9 %collective-permute-start.6 = (bf16[1,128,512]{2,1,0:T(8,128)(2,1)}, bf16[1,128,512]{2,1,0:T(8,128)(2,1)S(1)}, u32[]{:S(2)}, u32[]{:S(2)}) collective-permute-start(bf16[1,128,512]{2,1,0:T(8,128)(2,1)} %bitcast.31), channel_id=1, source_target_pairs={{0,8},{4,12},{8,0},{12,4},{16,24},{20,28},{24,16},{28,20},{1,9},{5... | collective-permute-start | bytes 393224 | tf_op jit(solution)/shard_map/along_z/ppermute | solution.py:108
  27.2 4.1 %collective-permute-done.4 = bf16[1,128,512]{2,1,0:T(8,128)(2,1)S(1)} collective-permute-done((bf16[1,128,512]{2,1,0:T(8,128)(2,1)}, bf16[1,128,512]{2,1,0:T(8,128)(2,1)S(1)}, u32[]{:S(2)}, u32[]{:S(2)}) %collective-permute-start.4) | collective-permute-done | bytes 131104 | tf_op jit(solution)/shard_map/along_z/ppermute | solution.py:108
  31.2 4.4 %collective-permute-done.5 = bf16[1,128,512]{2,1,0:T(8,128)(2,1)S(1)} collective-permute-done((bf16[1,128,512]{2,1,0:T(8,128)(2,1)}, bf16[1,128,512]{2,1,0:T(8,128)(2,1)S(1)}, u32[]{:S(2)}, u32[]{:S(2)}) %collective-permute-start.5) | collective-permute-done | bytes 131104 | tf_op jit(solution)/shard_map/along_z/ppermute | solution.py:108
  35.7 0.5 collective-permute-start.12
  36.2 0.1 collective-permute-start.13
  36.3 1.6 %collective-permute-start.10 = (bf16[4,64,512]{2,1,0:T(8,128)(2,1)S(1)}, bf16[4,64,512]{2,1,0:T(8,128)(2,1)S(1)}, u32[]{:S(2)}, u32[]{:S(2)}) collective-permute-start(bf16[4,64,512]{2,1,0:T(8,128)(2,1)S(1)} %slice.37), channel_id=1, source_target_pairs={{0,2},{1,3},{2,0},{3,1},{4,6},{5,7},{6,4},{7,5},{8,10},{9,11},{10,... | collective-permute-start | bytes 786440 | tf_op jit(solution)/shard_map/over_x/ppermute | solution.py:108
  37.9 0.5 collective-permute-start.9
  38.5 6.6 %collective-permute-done.10.refs_8_ = bf16[4,64,512]{2,1,0:T(8,128)(2,1)S(1)} collective-permute-done((bf16[4,64,512]{2,1,0:T(8,128)(2,1)S(1)}, bf16[4,64,512]{2,1,0:T(8,128)(2,1)S(1)}, u32[]{:S(2)}, u32[]{:S(2)}) %collective-permute-start.10) | collective-permute-done | bytes 262176 | tf_op jit(solution)/shard_map/over_x/ppermute | solution.py:108
  45.1 1.2 %collective-permute-done.9.refs_6_ = bf16[4,64,512]{2,1,0:T(8,128)(2,1)S(1)} collective-permute-done((bf16[4,64,512]{2,1,0:T(8,128)(2,1)S(1)}, bf16[4,64,512]{2,1,0:T(8,128)(2,1)S(1)}, u32[]{:S(2)}, u32[]{:S(2)}) %collective-permute-start.9) | collective-permute-done | bytes 262176 | tf_op jit(solution)/shard_map/over_y/ppermute | solution.py:108
  46.4 0.5 collective-permute-start.15
  46.9 1.0 collective-permute-done.14.refs_7_
  47.9 0.4 collective-permute-done.15.refs_9_
  48.3 3.4 %first_conv_a.1 = (bf16[8,512,512]{2,1,0:T(8,128)(2,1)S(1)}, bf16[5,128,512]{2,1,0:T(8,128)(2,1)S(1)}, bf16[5,128,512]{2,1,0:T(8,128)(2,1)S(1)}) custom-call(bf16[4,128,512]{2,1,0:T(8,128)(2,1)S(1)} %pad_maximum_fusion.refs_0_, bf16[4,128,512]{2,1,0:T(8,128)(2,1)S(1)} %collective-permute-done.11.refs_1_, ...), custom_call_target="tpu_custom_call" | custom-call | tf_op jit(solution)/shard_map/first_conv_a/pallas_call | solution.py:333
  51.7 0.2 collective-permute-start.16
  51.9 0.5 collective-permute-start.17
  52.4 0.5 collective-permute-start.20
  53.0 0.6 collective-permute-start.19
  53.5 2.2 %first_conv_b.1 = (bf16[3,128,512]{2,1,0:T(8,128)(2,1)S(1)}, bf16[3,128,512]{2,1,0:T(8,128)(2,1)S(1)}, bf16[512,4096]{1,0:T(8,128)(2,1)S(1)}) custom-call(bf16[8,512,512]{2,1,0:T(8,128)(2,1)S(1)} %get-tuple-element.128.full.refs_6_.refs_12_, bf16[3,384,512]{2,1,0:T(8,128)(2,1)S(1)} %bitcast.22), custom_call_target="tpu_custom_call" | custom-call | tf_op jit(solution)/shard_map/first_conv_b/pallas_call | solution.py:333
  55.7 10.6 %collective-permute-done.20.refs_8_.refs_14_ = bf16[4,128,512]{2,1,0:T(8,128)(2,1)S(1)} collective-permute-done((bf16[4,128,512]{2,1,0:T(8,128)(2,1)S(1)}, bf16[4,128,512]{2,1,0:T(8,128)(2,1)S(1)}, u32[]{:S(2)}, u32[]{:S(2)}) %collective-permute-start.20) | collective-permute-done | bytes 524320 | tf_op jit(solution)/shard_map/over_y/ppermute | solution.py:108
  66.3 1.5 %collective-permute-start.27 = (bf16[3,128,512]{2,1,0:T(8,128)(2,1)S(1)}, bf16[3,128,512]{2,1,0:T(8,128)(2,1)S(1)}, u32[]{:S(2)}, u32[]{:S(2)}) collective-permute-start(bf16[3,128,512]{2,1,0:T(8,128)(2,1)S(1)} %get-tuple-element.140.refs_6_), channel_id=1, source_target_pairs={{0,2},{1,3},{2,0},{3,1},{4,6},{5,7},{6,4},{7,5},{8,10},{9,11},{10,... | collective-permute-start | bytes 1179656 | tf_op jit(solution)/shard_map/over_x/ppermute | solution.py:108
  67.8 0.5 collective-permute-start.28
  68.3 0.5 collective-permute-done.17.refs_2_
  68.9 0.1 collective-permute-start.23
  69.0 0.6 collective-permute-start.21
  69.6 0.7 collective-permute-done.23.refs_5_
  70.3 0.1 collective-permute-start.22
  70.5 0.3 collective-permute-done.21.refs_3_
  70.7 1.1 collective-permute-done.22.refs_4_
  71.9 3.6 %second_conv_a.1 = (bf16[1,128,512]{2,1,0:T(8,128)(2,1)S(1)}, bf16[4,128,512]{2,1,0:T(8,128)(2,1)S(1)}, bf16[2,128,512]{2,1,0:T(8,128)(2,1)S(1)}) custom-call(bf16[5,128,512]{2,1,0:T(8,128)(2,1)S(1)} %get-tuple-element.130.refs_0_, bf16[5,128,512]{2,1,0:T(8,128)(2,1)S(1)} %collective-permute-done.16.refs_1_, ...), custom_call_target="tpu_custom_call" | custom-call | tf_op jit(solution)/shard_map/second_conv_a/pallas_call | solution.py:333
  75.4 0.2 collective-permute-start.25
  75.6 2.6 %second_terms_a.1.refs_13_ = f32[3,384,512]{2,1,0:T(8,128)S(1)} custom-call(bf16[5,128,512]{2,1,0:T(8,128)(2,1)S(1)} %get-tuple-element.130.refs_0_, bf16[5,128,512]{2,1,0:T(8,128)(2,1)S(1)} %collective-permute-done.16.refs_1_, bf16[5,128,512]{2,1,0:T(8,128)(2,1)S(1)} %collective-permute-done.17.refs_2_, ...), custom_call_target="tpu_custom_call" | custom-call | tf_op jit(solution)/shard_map/second_terms_a/pallas_call | solution.py:333
  78.3 0.4 collective-permute-start.30
  78.7 0.8 collective-permute-start.24
  79.6 0.2 collective-permute-start.29
  79.8 0.3 collective-permute-start.31
  80.1 0.2 collective-permute-start.32
  80.3 0.9 collective-permute-done.31.refs_10_
  81.2 0.3 collective-permute-done.32.refs_11_
  81.5 4.4 %second_conv_b.1 = (bf16[1,128,512]{2,1,0:T(8,128)(2,1)}, bf16[4,128,512]{2,1,0:T(8,128)(2,1)S(1)}) custom-call(bf16[5,128,512]{2,1,0:T(8,128)(2,1)S(1)} %get-tuple-element.130.refs_0_, bf16[5,128,512]{2,1,0:T(8,128)(2,1)S(1)} %collective-permute-done.16.refs_1_, bf16[5,128,512]{2,1,0:T(8,128)(2,1)S(1)} %collective-permute-done.17.refs_2_, ...), custom_call_target="tpu_custom_call" | custom-call | tf_op jit(solution)/shard_map/second_conv_b/pallas_call | solution.py:333
  85.9 1.3 %collective-permute-done.24.refs_2_ = bf16[2,128,512]{2,1,0:T(8,128)(2,1)S(1)} collective-permute-done((bf16[2,128,512]{2,1,0:T(8,128)(2,1)S(1)}, bf16[2,128,512]{2,1,0:T(8,128)(2,1)S(1)}, u32[]{:S(2)}, u32[]{:S(2)}) %collective-permute-start.24) | collective-permute-done | bytes 262176 | tf_op jit(solution)/shard_map/over_x/ppermute | solution.py:108
  87.1 1.0 collective-permute-start.34
  88.1 0.6 collective-permute-start.37
  88.7 0.5 collective-permute-start.35
  89.2 4.0 %second_terms_b.1 = f32[3,384,512]{2,1,0:T(8,128)} custom-call(bf16[5,128,512]{2,1,0:T(8,128)(2,1)S(1)} %get-tuple-element.130.refs_0_, bf16[5,128,512]{2,1,0:T(8,128)(2,1)S(1)} %collective-permute-done.16.refs_1_, bf16[5,128,512]{2,1,0:T(8,128)(2,1)S(1)} %collective-permute-done.17.refs_2_, bf16[2,128,512]{2,1,0:T(8,128)(2,1)S(1)} %collective-permute-done.21.refs_3_, ...), custom_call_target="tpu_custom_call" | custom-call | tf_op jit(solution)/shard_map/second_terms_b/pallas_call | solution.py:333
  93.2 1.4 %collective-permute-done.34.refs_4_ = bf16[2,128,512]{2,1,0:T(8,128)(2,1)S(1)} collective-permute-done((bf16[2,128,512]{2,1,0:T(8,128)(2,1)S(1)}, bf16[2,128,512]{2,1,0:T(8,128)(2,1)S(1)}, u32[]{:S(2)}, u32[]{:S(2)}) %collective-permute-start.34) | collective-permute-done | bytes 262176 | tf_op jit(solution)/shard_map/over_y/ppermute | solution.py:108
  94.6 0.4 turn_weight.1.refs_6_.refs_10_
  95.0 1.1 %collective-permute-done.36.refs_5_ = bf16[2,128,512]{2,1,0:T(8,128)(2,1)S(1)} collective-permute-done((bf16[2,128,512]{2,1,0:T(8,128)(2,1)S(1)}, bf16[2,128,512]{2,1,0:T(8,128)(2,1)S(1)}, u32[]{:S(2)}, u32[]{:S(2)}) %collective-permute-start.36) | collective-permute-done | bytes 262176 | tf_op jit(solution)/shard_map/mate/ppermute | solution.py:108
  96.2 2.1 %hidden_grad_a.1.grad = bf16[3,128,512]{2,1,0:T(8,128)(2,1)S(1)} custom-call(bf16[4,128,512]{2,1,0:T(8,128)(2,1)S(1)} %get-tuple-element.160.refs_6_.refs_0_, bf16[4,128,512]{2,1,0:T(8,128)(2,1)S(1)} %collective-permute-done.25.refs_1_, bf16[2,128,512]{2,1,0:T(8,128)(2,1)S(1)} %collective-permute-done.24.refs_2_, ...), custom_call_target="tpu_custom_call" | custom-call | tf_op jit(solution)/shard_map/hidden_grad_a/pallas_call | solution.py:333
  98.3 1.8 %first_terms_a.1.before = f32[3,384,512]{2,1,0:T(8,128)S(1)} custom-call(bf16[512,4096]{1,0:T(8,128)(2,1)S(1)} %get-tuple-element.154.flat, bf16[3,128,512]{2,1,0:T(8,128)(2,1)S(1)} %hidden_grad_a.1.grad), custom_call_target="tpu_custom_call" | custom-call | tf_op jit(solution)/shard_map/first_terms_a/pallas_call | solution.py:333
  100.1 0.9 collective-permute-done.37.refs_8_
  101.0 1.9 %collective-permute-done.38.refs_9_ = bf16[4,128,512]{2,1,0:T(8,128)(2,1)S(1)} collective-permute-done((bf16[4,128,512]{2,1,0:T(8,128)(2,1)S(1)}, bf16[4,128,512]{2,1,0:T(8,128)(2,1)S(1)}, u32[]{:S(2)}, u32[]{:S(2)}) %collective-permute-start.38) | collective-permute-done | bytes 524320 | tf_op jit(solution)/shard_map/mate/ppermute | solution.py:108
  102.9 3.6 %hidden_grad_b.1.grad = bf16[5,128,512]{2,1,0:T(8,128)(2,1)S(1)} custom-call(bf16[4,128,512]{2,1,0:T(8,128)(2,1)S(1)} %get-tuple-element.160.refs_6_.refs_0_, bf16[4,128,512]{2,1,0:T(8,128)(2,1)S(1)} %collective-permute-done.25.refs_1_, bf16[2,128,512]{2,1,0:T(8,128)(2,1)S(1)} %collective-permute-done.24.refs_2_, ...), custom_call_target="tpu_custom_call" | custom-call | flops 3019898880 | bytes 6422528 | tf_op jit(solution)/shard_map/hidden_grad_b/pallas_call | solution.py:333
  106.4 4.0 %first_terms_b.1 = f32[3,384,512]{2,1,0:T(8,128)} custom-call(bf16[512,4096]{1,0:T(8,128)(2,1)S(1)} %get-tuple-element.154.flat, bf16[5,128,512]{2,1,0:T(8,128)(2,1)S(1)} %hidden_grad_b.1.grad, f32[3,384,512]{2,1,0:T(8,128)S(1)} %first_terms_a.1.before), custom_call_target="tpu_custom_call" | custom-call | flops 3019898880 | bytes 7208960 | tf_op jit(solution)/shard_map/first_terms_b/pallas_call | solution.py:333
  (45 shorter events, 0.4 us)
Async XLA Ops:
  0.6 1.3 %copy-start = (bf16[128,3,3,512]{3,0,2,1:T(8,128)(2,1)S(1)}, bf16[128,3,3,512]{3,0,2,1:T(8,128)(2,1)}, u32[]{:S(2)}) copy-start(bf16[128,3,3,512]{3,0,2,1:T(8,128)(2,1)} %param.6) | copy-start | bytes 3538948
  1.9 36.5 %copy-start.4 = (bf16[128,1,512]{2,0,1:T(8,128)(2,1)S(1)}, bf16[128,1,512]{2,0,1:T(8,128)(2,1)}, u32[]{:S(2)}) copy-start(bf16[128,1,512]{2,0,1:T(8,128)(2,1)} %param.7) | copy-start | bytes 393220
  1.9 46.4 %copy-start.2 = (bf16[128,3,3,512]{3,0,2,1:T(8,128)(2,1)S(1)}, bf16[128,3,3,512]{3,0,2,1:T(8,128)(2,1)}, u32[]{:S(2)}) copy-start(bf16[128,3,3,512]{3,0,2,1:T(8,128)(2,1)} %param.5) | copy-start | bytes 3538948
  2.1 17.6 %collective-permute-start.3 = (bf16[2,9,64,128]{3,2,1,0:T(8,128)(2,1)S(1)}, bf16[2,9,64,128]{3,2,1,0:T(8,128)(2,1)S(1)}, u32[]{:S(2)}, u32[]{:S(2)}) collective-permute-start(bf16[2,9,64,128]{3,2,1,0:T(8,128)(2,1)S(1)} %get-tuple-element.89), channel_id=1, source_target_pairs={{0,2},{1,3},{2,0},{3,1},{4,6},{5,7},{6,4},{7,5},{8,10},{9,11},{10,... | collective-permute-start | bytes 884744 | tf_op jit(solution)/shard_map/over_x/ppermute | solution.py:108
  5.1 8.5 %collective-permute-start = (bf16[1,128,512]{2,1,0:T(8,128)(2,1)}, bf16[1,128,512]{2,1,0:T(8,128)(2,1)S(1)}, u32[]{:S(2)}, u32[]{:S(2)}) collective-permute-start(bf16[1,128,512]{2,1,0:T(8,128)(2,1)} %bitcast.23), channel_id=1, source_target_pairs={{0,24},{4,28},{8,16},{12,20},{16,8},{20,12},{24,0},{28,4},{1,25},{... | collective-permute-start | bytes 393224 | tf_op jit(solution)/shard_map/along_z/ppermute | solution.py:108
  8.7 11.0 %collective-permute-start.1 = (bf16[1,128,512]{2,1,0:T(8,128)(2,1)}, bf16[1,128,512]{2,1,0:T(8,128)(2,1)S(1)}, u32[]{:S(2)}, u32[]{:S(2)}) collective-permute-start(bf16[1,128,512]{2,1,0:T(8,128)(2,1)} %bitcast.24), channel_id=1, source_target_pairs={{0,16},{4,20},{8,24},{12,28},{16,0},{20,4},{24,8},{28,12},{1,17},{... | collective-permute-start | bytes 393224 | tf_op jit(solution)/shard_map/along_z/ppermute | solution.py:108
  8.7 11.0 %collective-permute-start.2 = (bf16[1,128,512]{2,1,0:T(8,128)(2,1)}, bf16[1,128,512]{2,1,0:T(8,128)(2,1)S(1)}, u32[]{:S(2)}, u32[]{:S(2)}) collective-permute-start(bf16[1,128,512]{2,1,0:T(8,128)(2,1)} %bitcast.25), channel_id=1, source_target_pairs={{0,8},{4,12},{8,0},{12,4},{16,24},{20,28},{24,16},{28,20},{1,9},{5... | collective-permute-start | bytes 393224 | tf_op jit(solution)/shard_map/along_z/ppermute | solution.py:108
  20.6 15.0 %collective-permute-start.7 = (bf16[4,128,512]{2,1,0:T(8,128)(2,1)S(1)}, bf16[4,128,512]{2,1,0:T(8,128)(2,1)S(1)}, u32[]{:S(2)}, u32[]{:S(2)}) collective-permute-start(bf16[4,128,512]{2,1,0:T(8,128)(2,1)S(1)} %pad_maximum_fusion.refs_0_), channel_id=1, source_target_pairs={{0,2},{1,3},{2,0},{3,1},{4,6},{5,7},{6,4},{7,5},{8,10},{9,11},{10,... | collective-permute-start | bytes 1572872 | tf_op jit(solution)/shard_map/over_x/ppermute | solution.py:108
  21.2 14.4 %collective-permute-start.8 = (bf16[4,128,512]{2,1,0:T(8,128)(2,1)S(1)}, bf16[4,128,512]{2,1,0:T(8,128)(2,1)S(1)}, u32[]{:S(2)}, u32[]{:S(2)}) collective-permute-start(bf16[4,128,512]{2,1,0:T(8,128)(2,1)S(1)} %pad_maximum_fusion.refs_0_), channel_id=1, source_target_pairs={{0,4},{4,0},{8,12},{12,8},{16,20},{20,16},{24,28},{28,24},{1,5},{5... | collective-permute-start | bytes 1572872 | tf_op jit(solution)/shard_map/over_y/ppermute | solution.py:108
  22.8 8.4 %collective-permute-start.4 = (bf16[1,128,512]{2,1,0:T(8,128)(2,1)}, bf16[1,128,512]{2,1,0:T(8,128)(2,1)S(1)}, u32[]{:S(2)}, u32[]{:S(2)}) collective-permute-start(bf16[1,128,512]{2,1,0:T(8,128)(2,1)} %bitcast.29), channel_id=1, source_target_pairs={{0,24},{4,28},{8,16},{12,20},{16,8},{20,12},{24,0},{28,4},{1,25},{... | collective-permute-start | bytes 393224 | tf_op jit(solution)/shard_map/along_z/ppermute | solution.py:108
  25.2 10.4 %collective-permute-start.5 = (bf16[1,128,512]{2,1,0:T(8,128)(2,1)}, bf16[1,128,512]{2,1,0:T(8,128)(2,1)S(1)}, u32[]{:S(2)}, u32[]{:S(2)}) collective-permute-start(bf16[1,128,512]{2,1,0:T(8,128)(2,1)} %bitcast.30), channel_id=1, source_target_pairs={{0,16},{4,20},{8,24},{12,28},{16,0},{20,4},{24,8},{28,12},{1,17},{... | collective-permute-start | bytes 393224 | tf_op jit(solution)/shard_map/along_z/ppermute | solution.py:108
  25.2 10.4 %collective-permute-start.6 = (bf16[1,128,512]{2,1,0:T(8,128)(2,1)}, bf16[1,128,512]{2,1,0:T(8,128)(2,1)S(1)}, u32[]{:S(2)}, u32[]{:S(2)}) collective-permute-start(bf16[1,128,512]{2,1,0:T(8,128)(2,1)} %bitcast.31), channel_id=1, source_target_pairs={{0,8},{4,12},{8,0},{12,4},{16,24},{20,28},{24,16},{28,20},{1,9},{5... | collective-permute-start | bytes 393224 | tf_op jit(solution)/shard_map/along_z/ppermute | solution.py:108
  35.6 10.6 %collective-permute-start.11 = (bf16[4,128,512]{2,1,0:T(8,128)(2,1)S(1)}, bf16[4,128,512]{2,1,0:T(8,128)(2,1)S(1)}, u32[]{:S(2)}, u32[]{:S(2)}) collective-permute-start(bf16[4,128,512]{2,1,0:T(8,128)(2,1)S(1)} %pad_maximum_fusion.refs_0_), channel_id=1, source_target_pairs={{0,1},{1,0},{2,3},{3,2},{4,5},{5,4},{6,7},{7,6},{8,9},{9,8},{10,11... | collective-permute-start | bytes 1572872 | tf_op jit(solution)/shard_map/mate/ppermute | solution.py:108
  35.7 10.6 %collective-permute-start.12 = (bf16[4,128,512]{2,1,0:T(8,128)(2,1)S(1)}, bf16[4,128,512]{2,1,0:T(8,128)(2,1)S(1)}, u32[]{:S(2)}, u32[]{:S(2)}) collective-permute-start(bf16[4,128,512]{2,1,0:T(8,128)(2,1)S(1)} %collective-permute-done.7.refs_2_), channel_id=1, source_target_pairs={{0,1},{1,0},{2,3},{3,2},{4,5},{5,4},{6,7},{7,6},{8,9},{9,8},{10,11... | collective-permute-start | bytes 1572872 | tf_op jit(solution)/shard_map/mate/ppermute | solution.py:108
  36.2 10.1 %collective-permute-start.13 = (bf16[4,128,512]{2,1,0:T(8,128)(2,1)S(1)}, bf16[4,128,512]{2,1,0:T(8,128)(2,1)S(1)}, u32[]{:S(2)}, u32[]{:S(2)}) collective-permute-start(bf16[4,128,512]{2,1,0:T(8,128)(2,1)S(1)} %collective-permute-done.8.refs_4_), channel_id=1, source_target_pairs={{0,1},{1,0},{2,3},{3,2},{4,5},{5,4},{6,7},{7,6},{8,9},{9,8},{10,11... | collective-permute-start | bytes 1572872 | tf_op jit(solution)/shard_map/mate/ppermute | solution.py:108
  36.3 8.7 %collective-permute-start.10 = (bf16[4,64,512]{2,1,0:T(8,128)(2,1)S(1)}, bf16[4,64,512]{2,1,0:T(8,128)(2,1)S(1)}, u32[]{:S(2)}, u32[]{:S(2)}) collective-permute-start(bf16[4,64,512]{2,1,0:T(8,128)(2,1)S(1)} %slice.37), channel_id=1, source_target_pairs={{0,2},{1,3},{2,0},{3,1},{4,6},{5,7},{6,4},{7,5},{8,10},{9,11},{10,... | collective-permute-start | bytes 786440 | tf_op jit(solution)/shard_map/over_x/ppermute | solution.py:108
  37.9 8.4 %collective-permute-start.9 = (bf16[4,64,512]{2,1,0:T(8,128)(2,1)S(1)}, bf16[4,64,512]{2,1,0:T(8,128)(2,1)S(1)}, u32[]{:S(2)}, u32[]{:S(2)}) collective-permute-start(bf16[4,64,512]{2,1,0:T(8,128)(2,1)S(1)} %slice.36), channel_id=1, source_target_pairs={{0,4},{4,0},{8,12},{12,8},{16,20},{20,16},{24,28},{28,24},{1,5},{5... | collective-permute-start | bytes 786440 | tf_op jit(solution)/shard_map/over_y/ppermute | solution.py:108
  46.3 1.6 %collective-permute-start.14 = (bf16[4,64,512]{2,1,0:T(8,128)(2,1)S(1)}, bf16[4,64,512]{2,1,0:T(8,128)(2,1)S(1)}, u32[]{:S(2)}, u32[]{:S(2)}) collective-permute-start(bf16[4,64,512]{2,1,0:T(8,128)(2,1)S(1)} %collective-permute-done.9.refs_6_), channel_id=1, source_target_pairs={{0,1},{1,0},{2,3},{3,2},{4,5},{5,4},{6,7},{7,6},{8,9},{9,8},{10,11... | collective-permute-start | bytes 786440 | tf_op jit(solution)/shard_map/mate/ppermute | solution.py:108
  46.4 1.9 %collective-permute-start.15 = (bf16[4,64,512]{2,1,0:T(8,128)(2,1)S(1)}, bf16[4,64,512]{2,1,0:T(8,128)(2,1)S(1)}, u32[]{:S(2)}, u32[]{:S(2)}) collective-permute-start(bf16[4,64,512]{2,1,0:T(8,128)(2,1)S(1)} %collective-permute-done.10.refs_8_), channel_id=1, source_target_pairs={{0,1},{1,0},{2,3},{3,2},{4,5},{5,4},{6,7},{7,6},{8,9},{9,8},{10,11... | collective-permute-start | bytes 786440 | tf_op jit(solution)/shard_map/mate/ppermute | solution.py:108
  51.7 16.7 %collective-permute-start.16 = (bf16[5,128,512]{2,1,0:T(8,128)(2,1)S(1)}, bf16[5,128,512]{2,1,0:T(8,128)(2,1)S(1)}, u32[]{:S(2)}, u32[]{:S(2)}) collective-permute-start(bf16[5,128,512]{2,1,0:T(8,128)(2,1)S(1)} %get-tuple-element.130.refs_0_), channel_id=1, source_target_pairs={{0,1},{1,0},{2,3},{3,2},{4,5},{5,4},{6,7},{7,6},{8,9},{9,8},{10,11... | collective-permute-start | bytes 1966088 | tf_op jit(solution)/shard_map/mate/ppermute | solution.py:108
  51.9 17.0 %collective-permute-start.17 = (bf16[5,128,512]{2,1,0:T(8,128)(2,1)S(1)}, bf16[5,128,512]{2,1,0:T(8,128)(2,1)S(1)}, u32[]{:S(2)}, u32[]{:S(2)}) collective-permute-start(bf16[5,128,512]{2,1,0:T(8,128)(2,1)S(1)} %get-tuple-element.130.refs_0_), channel_id=1, source_target_pairs={{0,2},{1,3},{2,0},{3,1},{4,6},{5,7},{6,4},{7,5},{8,10},{9,11},{10,... | collective-permute-start | bytes 1966088 | tf_op jit(solution)/shard_map/over_x/ppermute | solution.py:108
  52.4 13.9 %collective-permute-start.20 = (bf16[4,128,512]{2,1,0:T(8,128)(2,1)S(1)}, bf16[4,128,512]{2,1,0:T(8,128)(2,1)S(1)}, u32[]{:S(2)}, u32[]{:S(2)}) collective-permute-start(bf16[4,128,512]{2,1,0:T(8,128)(2,1)S(1)} %pad_maximum_fusion.1.refs_7_.refs_13_), channel_id=1, source_target_pairs={{0,4},{4,0},{8,12},{12,8},{16,20},{20,16},{24,28},{28,24},{1,5},{5... | collective-permute-start | bytes 1572872 | tf_op jit(solution)/shard_map/over_y/ppermute | solution.py:108
  52.9 14.9 %collective-permute-start.18 = (bf16[9,128,128]{2,1,0:T(8,128)(2,1)S(1)}, bf16[9,128,128]{2,1,0:T(8,128)(2,1)S(1)}, u32[]{:S(2)}, u32[]{:S(2)}) collective-permute-start(bf16[9,128,128]{2,1,0:T(8,128)(2,1)S(1)} %get-tuple-element.125), channel_id=1, source_target_pairs={{0,1},{1,0},{2,3},{3,2},{4,5},{5,4},{6,7},{7,6},{8,9},{9,8},{10,11... | collective-permute-start | bytes 884744 | tf_op jit(solution)/shard_map/mate/ppermute | solution.py:108
  53.0 13.4 %collective-permute-start.19 = (bf16[1,9,64,128]{3,2,1,0:T(8,128)(2,1)S(1)}, bf16[1,9,64,128]{3,2,1,0:T(8,128)(2,1)S(1)}, u32[]{:S(2)}, u32[]{:S(2)}) collective-permute-start(bf16[1,9,64,128]{3,2,1,0:T(8,128)(2,1)S(1)} %get-tuple-element.181), channel_id=1, source_target_pairs={{0,1},{1,0},{2,3},{3,2},{4,5},{5,4},{6,7},{7,6},{8,9},{9,8},{10,11... | collective-permute-start | bytes 442376 | tf_op jit(solution)/shard_map/mate/ppermute | solution.py:108
  53.5 18.3 %copy-start.1 = (bf16[128,3,3,512]{3,0,2,1:T(8,128)(2,1)S(1)}, bf16[128,3,3,512]{3,0,2,1:T(8,128)(2,1)}, u32[]{:S(2)}) copy-start(bf16[128,3,3,512]{3,0,2,1:T(8,128)(2,1)} %param.6) | copy-start | bytes 3538948
  53.5 18.3 %copy-start.3 = (bf16[128,1,512]{2,0,1:T(8,128)(2,1)S(1)}, bf16[128,1,512]{2,0,1:T(8,128)(2,1)}, u32[]{:S(2)}) copy-start(bf16[128,1,512]{2,0,1:T(8,128)(2,1)} %param.4) | copy-start | bytes 393220
  66.3 11.9 %collective-permute-start.26 = (bf16[3,128,512]{2,1,0:T(8,128)(2,1)S(1)}, bf16[3,128,512]{2,1,0:T(8,128)(2,1)S(1)}, u32[]{:S(2)}, u32[]{:S(2)}) collective-permute-start(bf16[3,128,512]{2,1,0:T(8,128)(2,1)S(1)} %get-tuple-element.140.refs_6_), channel_id=1, source_target_pairs={{0,1},{1,0},{2,3},{3,2},{4,5},{5,4},{6,7},{7,6},{8,9},{9,8},{10,11... | collective-permute-start | bytes 1179656 | tf_op jit(solution)/shard_map/mate/ppermute | solution.py:108
  66.3 11.9 %collective-permute-start.27 = (bf16[3,128,512]{2,1,0:T(8,128)(2,1)S(1)}, bf16[3,128,512]{2,1,0:T(8,128)(2,1)S(1)}, u32[]{:S(2)}, u32[]{:S(2)}) collective-permute-start(bf16[3,128,512]{2,1,0:T(8,128)(2,1)S(1)} %get-tuple-element.140.refs_6_), channel_id=1, source_target_pairs={{0,2},{1,3},{2,0},{3,1},{4,6},{5,7},{6,4},{7,5},{8,10},{9,11},{10,... | collective-permute-start | bytes 1179656 | tf_op jit(solution)/shard_map/over_x/ppermute | solution.py:108
  67.8 10.4 %collective-permute-start.28 = (bf16[2,9,64,128]{3,2,1,0:T(8,128)(2,1)S(1)}, bf16[2,9,64,128]{3,2,1,0:T(8,128)(2,1)S(1)}, u32[]{:S(2)}, u32[]{:S(2)}) collective-permute-start(bf16[2,9,64,128]{3,2,1,0:T(8,128)(2,1)S(1)} %collective-permute-done.3), channel_id=1, source_target_pairs={{0,4},{4,0},{8,12},{12,8},{16,20},{20,16},{24,28},{28,24},{1,5},{5... | collective-permute-start | bytes 884744 | tf_op jit(solution)/shard_map/over_y/ppermute | solution.py:108
  68.9 1.4 %collective-permute-start.23 = (bf16[1,128,512]{2,1,0:T(8,128)(2,1)S(1)}, bf16[1,128,512]{2,1,0:T(8,128)(2,1)S(1)}, u32[]{:S(2)}, u32[]{:S(2)}) collective-permute-start(bf16[1,128,512]{2,1,0:T(8,128)(2,1)S(1)} %slice.41), channel_id=1, source_target_pairs={{0,1},{1,0},{2,3},{3,2},{4,5},{5,4},{6,7},{7,6},{8,9},{9,8},{10,11... | collective-permute-start | bytes 393224 | tf_op jit(solution)/shard_map/mate/ppermute | solution.py:108
  69.0 1.7 %collective-permute-start.21 = (bf16[2,128,512]{2,1,0:T(8,128)(2,1)S(1)}, bf16[2,128,512]{2,1,0:T(8,128)(2,1)S(1)}, u32[]{:S(2)}, u32[]{:S(2)}) collective-permute-start(bf16[2,128,512]{2,1,0:T(8,128)(2,1)S(1)} %get-tuple-element.174), channel_id=1, source_target_pairs={{0,1},{1,0},{2,3},{3,2},{4,5},{5,4},{6,7},{7,6},{8,9},{9,8},{10,11... | collective-permute-start | bytes 786440 | tf_op jit(solution)/shard_map/mate/ppermute | solution.py:108
  70.3 1.5 %collective-permute-start.22 = (bf16[2,128,512]{2,1,0:T(8,128)(2,1)S(1)}, bf16[2,128,512]{2,1,0:T(8,128)(2,1)S(1)}, u32[]{:S(2)}, u32[]{:S(2)}) collective-permute-start(bf16[2,128,512]{2,1,0:T(8,128)(2,1)S(1)} %get-tuple-element.173), channel_id=1, source_target_pairs={{0,1},{1,0},{2,3},{3,2},{4,5},{5,4},{6,7},{7,6},{8,9},{9,8},{10,11... | collective-permute-start | bytes 786440 | tf_op jit(solution)/shard_map/mate/ppermute | solution.py:108
  75.4 11.7 %collective-permute-start.25 = (bf16[4,128,512]{2,1,0:T(8,128)(2,1)S(1)}, bf16[4,128,512]{2,1,0:T(8,128)(2,1)S(1)}, u32[]{:S(2)}, u32[]{:S(2)}) collective-permute-start(bf16[4,128,512]{2,1,0:T(8,128)(2,1)S(1)} %get-tuple-element.160.refs_6_.refs_0_), channel_id=1, source_target_pairs={{0,1},{1,0},{2,3},{3,2},{4,5},{5,4},{6,7},{7,6},{8,9},{9,8},{10,11... | collective-permute-start | bytes 1572872 | tf_op jit(solution)/shard_map/mate/ppermute | solution.py:108
  78.3 1.8 %collective-permute-start.30 = (bf16[1,128,512]{2,1,0:T(8,128)(2,1)S(1)}, bf16[1,128,512]{2,1,0:T(8,128)(2,1)S(1)}, u32[]{:S(2)}, u32[]{:S(2)}) collective-permute-start(bf16[1,128,512]{2,1,0:T(8,128)(2,1)S(1)} %get-tuple-element.177), channel_id=1, source_target_pairs={{0,1},{1,0},{2,3},{3,2},{4,5},{5,4},{6,7},{7,6},{8,9},{9,8},{10,11... | collective-permute-start | bytes 393224 | tf_op jit(solution)/shard_map/mate/ppermute | solution.py:108
  78.7 8.4 %collective-permute-start.24 = (bf16[2,128,512]{2,1,0:T(8,128)(2,1)S(1)}, bf16[2,128,512]{2,1,0:T(8,128)(2,1)S(1)}, u32[]{:S(2)}, u32[]{:S(2)}) collective-permute-start(bf16[2,128,512]{2,1,0:T(8,128)(2,1)S(1)} %get-tuple-element.135), channel_id=1, source_target_pairs={{0,2},{1,3},{2,0},{3,1},{4,6},{5,7},{6,4},{7,5},{8,10},{9,11},{10,... | collective-permute-start | bytes 786440 | tf_op jit(solution)/shard_map/over_x/ppermute | solution.py:108
  79.6 6.3 %collective-permute-start.29 = (bf16[1,9,64,128]{3,2,1,0:T(8,128)(2,1)S(1)}, bf16[1,9,64,128]{3,2,1,0:T(8,128)(2,1)S(1)}, u32[]{:S(2)}, u32[]{:S(2)}) collective-permute-start(bf16[1,9,64,128]{3,2,1,0:T(8,128)(2,1)S(1)} %get-tuple-element.179), channel_id=1, source_target_pairs={{0,1},{1,0},{2,3},{3,2},{4,5},{5,4},{6,7},{7,6},{8,9},{9,8},{10,11... | collective-permute-start | bytes 442376 | tf_op jit(solution)/shard_map/mate/ppermute | solution.py:108
  79.8 1.4 %collective-permute-start.31 = (bf16[1,128,512]{2,1,0:T(8,128)(2,1)S(1)}, bf16[1,128,512]{2,1,0:T(8,128)(2,1)S(1)}, u32[]{:S(2)}, u32[]{:S(2)}) collective-permute-start(bf16[1,128,512]{2,1,0:T(8,128)(2,1)S(1)} %get-tuple-element.176), channel_id=1, source_target_pairs={{0,1},{1,0},{2,3},{3,2},{4,5},{5,4},{6,7},{7,6},{8,9},{9,8},{10,11... | collective-permute-start | bytes 393224 | tf_op jit(solution)/shard_map/mate/ppermute | solution.py:108
  80.1 1.3 %collective-permute-start.32 = (bf16[1,128,512]{2,1,0:T(8,128)(2,1)S(1)}, bf16[1,128,512]{2,1,0:T(8,128)(2,1)S(1)}, u32[]{:S(2)}, u32[]{:S(2)}) collective-permute-start(bf16[1,128,512]{2,1,0:T(8,128)(2,1)S(1)} %get-tuple-element.175), channel_id=1, source_target_pairs={{0,1},{1,0},{2,3},{3,2},{4,5},{5,4},{6,7},{7,6},{8,9},{9,8},{10,11... | collective-permute-start | bytes 393224 | tf_op jit(solution)/shard_map/mate/ppermute | solution.py:108
  87.1 7.5 %collective-permute-start.34 = (bf16[2,128,512]{2,1,0:T(8,128)(2,1)S(1)}, bf16[2,128,512]{2,1,0:T(8,128)(2,1)S(1)}, u32[]{:S(2)}, u32[]{:S(2)}) collective-permute-start(bf16[2,128,512]{2,1,0:T(8,128)(2,1)S(1)} %collective-permute-done.24.refs_2_), channel_id=1, source_target_pairs={{0,4},{4,0},{8,12},{12,8},{16,20},{20,16},{24,28},{28,24},{1,5},{5... | collective-permute-start | bytes 786440 | tf_op jit(solution)/shard_map/over_y/ppermute | solution.py:108
  88.1 12.9 %collective-permute-start.37 = (bf16[4,128,512]{2,1,0:T(8,128)(2,1)S(1)}, bf16[4,128,512]{2,1,0:T(8,128)(2,1)S(1)}, u32[]{:S(2)}, u32[]{:S(2)}) collective-permute-start(bf16[4,128,512]{2,1,0:T(8,128)(2,1)S(1)} %get-tuple-element.166.refs_12_.refs_6_), channel_id=1, source_target_pairs={{0,2},{1,3},{2,0},{3,1},{4,6},{5,7},{6,4},{7,5},{8,10},{9,11},{10,... | collective-permute-start | bytes 1572872 | tf_op jit(solution)/shard_map/over_x/ppermute | solution.py:108
  88.7 12.3 %collective-permute-start.33 = (bf16[4,128,512]{2,1,0:T(8,128)(2,1)S(1)}, bf16[4,128,512]{2,1,0:T(8,128)(2,1)S(1)}, u32[]{:S(2)}, u32[]{:S(2)}) collective-permute-start(bf16[4,128,512]{2,1,0:T(8,128)(2,1)S(1)} %get-tuple-element.166.refs_12_.refs_6_), channel_id=1, source_target_pairs={{0,1},{1,0},{2,3},{3,2},{4,5},{5,4},{6,7},{7,6},{8,9},{9,8},{10,11... | collective-permute-start | bytes 1572872 | tf_op jit(solution)/shard_map/mate/ppermute | solution.py:108
  88.7 6.3 %collective-permute-start.35 = (bf16[2,128,512]{2,1,0:T(8,128)(2,1)S(1)}, bf16[2,128,512]{2,1,0:T(8,128)(2,1)S(1)}, u32[]{:S(2)}, u32[]{:S(2)}) collective-permute-start(bf16[2,128,512]{2,1,0:T(8,128)(2,1)S(1)} %collective-permute-done.24.refs_2_), channel_id=1, source_target_pairs={{0,1},{1,0},{2,3},{3,2},{4,5},{5,4},{6,7},{7,6},{8,9},{9,8},{10,11... | collective-permute-start | bytes 786440 | tf_op jit(solution)/shard_map/mate/ppermute | solution.py:108
  94.6 1.5 %collective-permute-start.36 = (bf16[2,128,512]{2,1,0:T(8,128)(2,1)S(1)}, bf16[2,128,512]{2,1,0:T(8,128)(2,1)S(1)}, u32[]{:S(2)}, u32[]{:S(2)}) collective-permute-start(bf16[2,128,512]{2,1,0:T(8,128)(2,1)S(1)} %collective-permute-done.34.refs_4_), channel_id=1, source_target_pairs={{0,1},{1,0},{2,3},{3,2},{4,5},{5,4},{6,7},{7,6},{8,9},{9,8},{10,11... | collective-permute-start | bytes 786440 | tf_op jit(solution)/shard_map/mate/ppermute | solution.py:108
  101.0 1.9 %collective-permute-start.38 = (bf16[4,128,512]{2,1,0:T(8,128)(2,1)S(1)}, bf16[4,128,512]{2,1,0:T(8,128)(2,1)S(1)}, u32[]{:S(2)}, u32[]{:S(2)}) collective-permute-start(bf16[4,128,512]{2,1,0:T(8,128)(2,1)S(1)} %collective-permute-done.37.refs_8_), channel_id=1, source_target_pairs={{0,1},{1,0},{2,3},{3,2},{4,5},{5,4},{6,7},{7,6},{8,9},{9,8},{10,11... | collective-permute-start | bytes 1572872 | tf_op jit(solution)/shard_map/mate/ppermute | solution.py:108

commit v5 on v4

--- a/solution.py
+++ b/solution.py
@@ -230,6 +230,10 @@
             block_out[0] = jnp.maximum(pre, 0.0).astype(BF)
 
 
+def hold_kernel(value, out):
+    out[...] = value[...]
+
+
 def pick_kernel(weight, mate, over, sems):
     own, half = mate.shape[1], over.shape[2]
     f0, y0 = lax.axis_index("filt"), lax.axis_index("rows") & 1
@@ -387,11 +391,12 @@
         "pick_weight",
         in_spec=ANY,
     )
-    v |= {"mate": mate, "near": over_x(over)}
+    (feat_near,) = call(hold_kernel, [feat], [act(1)], [], row_flops * 2, "hold_row")
+    v |= {"mate": mate, "near": over_x(over), "feat": feat_near}
     v = wave(v)
 
     zs = (0, *zs)
-    z4 = jnp.concatenate([feat] + [v[f"z{d}"] for d in zs[1:]], axis=0)
+    z4 = jnp.concatenate([v["feat"]] + [v[f"z{d}"] for d in zs[1:]], axis=0)
     v |= {f"g{d}": swap(ograd, "rows", d) for d in zs[:0:-1]}
     v |= {"z4": z4, "x4": over_x(z4), "y4": over_y(z4)}
     v = wave(v)

time: 111 us -> 110 us (level)
  waiting for transfers between devices: 49 us -> 47.8 us
    ppermute x39, waiting for transfers between devices: 49 us -> 47.8 us  [swap(): lax.ppermute(value, axis, [(i, i ^ bits) for i in range(lax.axis_size(axi...]
    unnamed x10 -> x15, local copies, waits for them, and re-layouts: 1.28 us -> 2.25 us
    pallas_call x12 -> x13, Pallas kernels: 32 us -> 32.1 us  [call(): pl.pallas_call(kernel, out_shape=[jax.ShapeDtypeStruct(s, d) for s, d in...]
where the time goes in v5:
time: 110 us; the launch traced here: 109 us
  waiting for transfers between devices  47.8 us (43%)
  Pallas kernels  32.1 us (29%)
  starting transfers between devices  26 us (24%)
  local copies, waits for them, and re-layouts  2.41 us (2%)
    ppermute x39, waiting for transfers between devices, swap(): lax.ppermute(value, axis, [(i, i ^ bits) for i in range(lax.axis_size(axi...  47.8 us
    pallas_call x13, Pallas kernels, call(): pl.pallas_call(kernel, out_shape=[jax.ShapeDtypeStruct(s, d) for s, d in...  32.1 us
    ppermute x39, starting transfers between devices, swap(): lax.ppermute(value, axis, [(i, i ^ bits) for i in range(lax.axis_size(axi...  26 us
    unnamed x15, local copies, waits for them, and re-layouts  2.25 us
  transfers between devices with their start and end apart: 39, of which 20 were waited for; matrix products, arithmetic and copies ran while one was open for 0% of the time, Pallas kernels for 19%

profile of v5, /device:TPU:0, one launch (start us, length us, event | category | flops | bytes accessed | tf_op | source)
XLA Modules:
  0.0 109.5 jit_solution(1039905031684798472)
XLA Ops:
  0.6 1.3 %copy-done = bf16[128,3,3,512]{3,0,2,1:T(8,128)(2,1)S(1)} copy-done((bf16[128,3,3,512]{3,0,2,1:T(8,128)(2,1)S(1)}, bf16[128,3,3,512]{3,0,2,1:T(8,128)(2,1)}, u32[]{:S(2)}) %copy-start) | copy-done | bytes 1179672
  1.9 0.1 pick_weight.1
  2.0 3.0 %collective-permute-start.3 = (bf16[2,9,64,128]{3,2,1,0:T(8,128)(2,1)S(1)}, bf16[2,9,64,128]{3,2,1,0:T(8,128)(2,1)S(1)}, u32[]{:S(2)}, u32[]{:S(2)}) collective-permute-start(bf16[2,9,64,128]{3,2,1,0:T(8,128)(2,1)S(1)} %get-tuple-element.90), channel_id=1, source_target_pairs={{0,2},{1,3},{2,0},{3,1},{4,6},{5,7},{6,4},{7,5},{8,10},{9,11},{10,... | collective-permute-start | bytes 884744 | tf_op jit(solution)/shard_map/over_x/ppermute | solution.py:108
  5.1 3.6 %collective-permute-start = (bf16[1,128,512]{2,1,0:T(8,128)(2,1)}, bf16[1,128,512]{2,1,0:T(8,128)(2,1)S(1)}, u32[]{:S(2)}, u32[]{:S(2)}) collective-permute-start(bf16[1,128,512]{2,1,0:T(8,128)(2,1)} %bitcast.23), channel_id=1, source_target_pairs={{0,24},{4,28},{8,16},{12,20},{16,8},{20,12},{24,0},{28,4},{1,25},{... | collective-permute-start | bytes 393224 | tf_op jit(solution)/shard_map/along_z/ppermute | solution.py:108
  8.7 0.8 collective-permute-start.2
  9.4 0.9 copy-done.3
  10.4 3.1 %collective-permute-done = bf16[1,128,512]{2,1,0:T(8,128)(2,1)S(1)} collective-permute-done((bf16[1,128,512]{2,1,0:T(8,128)(2,1)}, bf16[1,128,512]{2,1,0:T(8,128)(2,1)S(1)}, u32[]{:S(2)}, u32[]{:S(2)}) %collective-permute-start) | collective-permute-done | bytes 131104 | tf_op jit(solution)/shard_map/along_z/ppermute | solution.py:108
  13.5 6.1 %collective-permute-done.1 = bf16[1,128,512]{2,1,0:T(8,128)(2,1)S(1)} collective-permute-done((bf16[1,128,512]{2,1,0:T(8,128)(2,1)}, bf16[1,128,512]{2,1,0:T(8,128)(2,1)S(1)}, u32[]{:S(2)}, u32[]{:S(2)}) %collective-permute-start.1) | collective-permute-done | bytes 131104 | tf_op jit(solution)/shard_map/along_z/ppermute | solution.py:108
  19.7 0.6 collective-permute-start.7
  20.3 1.5 %collective-permute-start.8 = (bf16[4,128,512]{2,1,0:T(8,128)(2,1)S(1)}, bf16[4,128,512]{2,1,0:T(8,128)(2,1)S(1)}, u32[]{:S(2)}, u32[]{:S(2)}) collective-permute-start(bf16[4,128,512]{2,1,0:T(8,128)(2,1)S(1)} %constant_dynamic-update-slice_fusion.refs_0_), channel_id=1, source_target_pairs={{0,4},{4,0},{8,12},{12,8},{16,20},{20,16},{24,28},{28,24},{1,5},{5... | collective-permute-start | bytes 1572872 | tf_op jit(solution)/shard_map/over_y/ppermute | solution.py:108
  21.9 2.5 %collective-permute-start.4 = (bf16[1,128,512]{2,1,0:T(8,128)(2,1)S(1)}, bf16[1,128,512]{2,1,0:T(8,128)(2,1)S(1)}, u32[]{:S(2)}, u32[]{:S(2)}) collective-permute-start(bf16[1,128,512]{2,1,0:T(8,128)(2,1)S(1)} %bitcast.29), channel_id=1, source_target_pairs={{0,24},{4,28},{8,16},{12,20},{16,8},{20,12},{24,0},{28,4},{1,25},{... | collective-permute-start | bytes 393224 | tf_op jit(solution)/shard_map/along_z/ppermute | solution.py:108
  24.3 1.9 %collective-permute-start.6 = (bf16[1,128,512]{2,1,0:T(8,128)(2,1)S(1)}, bf16[1,128,512]{2,1,0:T(8,128)(2,1)S(1)}, u32[]{:S(2)}, u32[]{:S(2)}) collective-permute-start(bf16[1,128,512]{2,1,0:T(8,128)(2,1)S(1)} %bitcast.31), channel_id=1, source_target_pairs={{0,8},{4,12},{8,0},{12,4},{16,24},{20,28},{24,16},{28,20},{1,9},{5... | collective-permute-start | bytes 393224 | tf_op jit(solution)/shard_map/along_z/ppermute | solution.py:108
  26.2 3.8 %collective-permute-done.4 = bf16[1,128,512]{2,1,0:T(8,128)(2,1)S(1)} collective-permute-done((bf16[1,128,512]{2,1,0:T(8,128)(2,1)S(1)}, bf16[1,128,512]{2,1,0:T(8,128)(2,1)S(1)}, u32[]{:S(2)}, u32[]{:S(2)}) %collective-permute-start.4) | collective-permute-done | bytes 131104 | tf_op jit(solution)/shard_map/along_z/ppermute | solution.py:108
  30.1 4.4 %collective-permute-done.5 = bf16[1,128,512]{2,1,0:T(8,128)(2,1)S(1)} collective-permute-done((bf16[1,128,512]{2,1,0:T(8,128)(2,1)S(1)}, bf16[1,128,512]{2,1,0:T(8,128)(2,1)S(1)}, u32[]{:S(2)}, u32[]{:S(2)}) %collective-permute-start.5) | collective-permute-done | bytes 131104 | tf_op jit(solution)/shard_map/along_z/ppermute | solution.py:108
  34.6 0.5 collective-permute-start.12
  35.1 0.1 collective-permute-start.13
  35.2 1.6 %collective-permute-start.10 = (bf16[4,64,512]{2,1,0:T(8,128)(2,1)S(1)}, bf16[4,64,512]{2,1,0:T(8,128)(2,1)S(1)}, u32[]{:S(2)}, u32[]{:S(2)}) collective-permute-start(bf16[4,64,512]{2,1,0:T(8,128)(2,1)S(1)} %slice.37), channel_id=1, source_target_pairs={{0,2},{1,3},{2,0},{3,1},{4,6},{5,7},{6,4},{7,5},{8,10},{9,11},{10,... | collective-permute-start | bytes 786440 | tf_op jit(solution)/shard_map/over_x/ppermute | solution.py:108
  36.8 0.5 collective-permute-start.9
  37.4 6.6 %collective-permute-done.10.refs_8_ = bf16[4,64,512]{2,1,0:T(8,128)(2,1)S(1)} collective-permute-done((bf16[4,64,512]{2,1,0:T(8,128)(2,1)S(1)}, bf16[4,64,512]{2,1,0:T(8,128)(2,1)S(1)}, u32[]{:S(2)}, u32[]{:S(2)}) %collective-permute-start.10) | collective-permute-done | bytes 262176 | tf_op jit(solution)/shard_map/over_x/ppermute | solution.py:108
  44.0 1.2 %collective-permute-done.9.refs_6_ = bf16[4,64,512]{2,1,0:T(8,128)(2,1)S(1)} collective-permute-done((bf16[4,64,512]{2,1,0:T(8,128)(2,1)S(1)}, bf16[4,64,512]{2,1,0:T(8,128)(2,1)S(1)}, u32[]{:S(2)}, u32[]{:S(2)}) %collective-permute-start.9) | collective-permute-done | bytes 262176 | tf_op jit(solution)/shard_map/over_y/ppermute | solution.py:108
  45.3 0.5 collective-permute-start.15
  45.8 1.0 collective-permute-done.14.refs_7_
  46.8 0.4 collective-permute-done.15.refs_9_
  47.2 3.4 %first_conv_a.1 = (bf16[8,512,512]{2,1,0:T(8,128)(2,1)S(1)}, bf16[5,128,512]{2,1,0:T(8,128)(2,1)S(1)}, bf16[5,128,512]{2,1,0:T(8,128)(2,1)S(1)}) custom-call(bf16[4,128,512]{2,1,0:T(8,128)(2,1)S(1)} %constant_dynamic-update-slice_fusion.refs_0_, bf16[4,128,512]{2,1,0:T(8,128)(2,1)S(1)} %collective-permute-done.11.refs_1_, ...), custom_call_target="tpu_custom_call" | custom-call | tf_op jit(solution)/shard_map/first_conv_a/pallas_call | solution.py:337
  50.6 0.2 collective-permute-start.16
  50.8 0.5 collective-permute-start.17
  51.3 0.5 collective-permute-start.20
  51.8 0.6 collective-permute-start.19
  52.4 2.2 %first_conv_b.1 = (bf16[3,128,512]{2,1,0:T(8,128)(2,1)S(1)}, bf16[3,128,512]{2,1,0:T(8,128)(2,1)S(1)}, bf16[512,4096]{1,0:T(8,128)(2,1)S(1)}) custom-call(bf16[8,512,512]{2,1,0:T(8,128)(2,1)S(1)} %get-tuple-element.130.full.refs_6_.refs_12_, bf16[3,384,512]{2,1,0:T(8,128)(2,1)S(1)} %bitcast.22), custom_call_target="tpu_custom_call" | custom-call | tf_op jit(solution)/shard_map/first_conv_b/pallas_call | solution.py:337
  54.6 10.6 %collective-permute-done.20.refs_8_.refs_14_ = bf16[4,128,512]{2,1,0:T(8,128)(2,1)S(1)} collective-permute-done((bf16[4,128,512]{2,1,0:T(8,128)(2,1)S(1)}, bf16[4,128,512]{2,1,0:T(8,128)(2,1)S(1)}, u32[]{:S(2)}, u32[]{:S(2)}) %collective-permute-start.20) | collective-permute-done | bytes 524320 | tf_op jit(solution)/shard_map/over_y/ppermute | solution.py:108
  65.2 1.5 %collective-permute-start.27 = (bf16[3,128,512]{2,1,0:T(8,128)(2,1)S(1)}, bf16[3,128,512]{2,1,0:T(8,128)(2,1)S(1)}, u32[]{:S(2)}, u32[]{:S(2)}) collective-permute-start(bf16[3,128,512]{2,1,0:T(8,128)(2,1)S(1)} %get-tuple-element.142.refs_6_), channel_id=1, source_target_pairs={{0,2},{1,3},{2,0},{3,1},{4,6},{5,7},{6,4},{7,5},{8,10},{9,11},{10,... | collective-permute-start | bytes 1179656 | tf_op jit(solution)/shard_map/over_x/ppermute | solution.py:108
  66.7 0.5 collective-permute-start.28
  67.2 0.5 collective-permute-done.17.refs_2_
  67.8 0.1 collective-permute-start.23
  67.9 0.6 collective-permute-start.21
  68.5 0.7 collective-permute-done.23.refs_5_
  69.2 0.1 collective-permute-start.22
  69.3 0.3 collective-permute-done.21.refs_3_
  69.6 1.1 %collective-permute-done.22.refs_4_ = bf16[2,128,512]{2,1,0:T(8,128)(2,1)S(1)} collective-permute-done((bf16[2,128,512]{2,1,0:T(8,128)(2,1)S(1)}, bf16[2,128,512]{2,1,0:T(8,128)(2,1)S(1)}, u32[]{:S(2)}, u32[]{:S(2)}) %collective-permute-start.22) | collective-permute-done | bytes 262176 | tf_op jit(solution)/shard_map/mate/ppermute | solution.py:108
  70.7 3.6 %second_conv_a.1 = (bf16[1,128,512]{2,1,0:T(8,128)(2,1)S(1)}, bf16[4,128,512]{2,1,0:T(8,128)(2,1)S(1)}, bf16[2,128,512]{2,1,0:T(8,128)(2,1)S(1)}) custom-call(bf16[5,128,512]{2,1,0:T(8,128)(2,1)S(1)} %get-tuple-element.132.refs_0_, bf16[5,128,512]{2,1,0:T(8,128)(2,1)S(1)} %collective-permute-done.16.refs_1_, ...), custom_call_target="tpu_custom_call" | custom-call | tf_op jit(solution)/shard_map/second_conv_a/pallas_call | solution.py:337
  74.3 0.2 collective-permute-start.25
  74.5 2.6 %second_terms_a.1.refs_13_ = f32[3,384,512]{2,1,0:T(8,128)S(1)} custom-call(bf16[5,128,512]{2,1,0:T(8,128)(2,1)S(1)} %get-tuple-element.132.refs_0_, bf16[5,128,512]{2,1,0:T(8,128)(2,1)S(1)} %collective-permute-done.16.refs_1_, bf16[5,128,512]{2,1,0:T(8,128)(2,1)S(1)} %collective-permute-done.17.refs_2_, ...), custom_call_target="tpu_custom_call" | custom-call | tf_op jit(solution)/shard_map/second_terms_a/pallas_call | solution.py:337
  77.2 0.4 collective-permute-start.30
  77.6 0.8 collective-permute-start.24
  78.4 0.2 collective-permute-start.29
  78.7 0.3 collective-permute-start.31
  79.0 0.2 collective-permute-start.32
  79.2 0.9 collective-permute-done.31.refs_10_
  80.1 0.3 collective-permute-done.32.refs_11_
  80.4 4.4 %second_conv_b.1 = (bf16[1,128,512]{2,1,0:T(8,128)(2,1)}, bf16[4,128,512]{2,1,0:T(8,128)(2,1)S(1)}) custom-call(bf16[5,128,512]{2,1,0:T(8,128)(2,1)S(1)} %get-tuple-element.132.refs_0_, bf16[5,128,512]{2,1,0:T(8,128)(2,1)S(1)} %collective-permute-done.16.refs_1_, bf16[5,128,512]{2,1,0:T(8,128)(2,1)S(1)} %collective-permute-done.17.refs_2_, ...), custom_call_target="tpu_custom_call" | custom-call | tf_op jit(solution)/shard_map/second_conv_b/pallas_call | solution.py:337
  84.7 1.3 %collective-permute-done.24.refs_2_ = bf16[2,128,512]{2,1,0:T(8,128)(2,1)S(1)} collective-permute-done((bf16[2,128,512]{2,1,0:T(8,128)(2,1)S(1)}, bf16[2,128,512]{2,1,0:T(8,128)(2,1)S(1)}, u32[]{:S(2)}, u32[]{:S(2)}) %collective-permute-start.24) | collective-permute-done | bytes 262176 | tf_op jit(solution)/shard_map/over_x/ppermute | solution.py:108
  86.0 1.0 collective-permute-start.34
  87.0 0.6 collective-permute-start.37
  87.6 0.5 collective-permute-start.35
  88.1 4.0 %second_terms_b.1 = f32[3,384,512]{2,1,0:T(8,128)} custom-call(bf16[5,128,512]{2,1,0:T(8,128)(2,1)S(1)} %get-tuple-element.132.refs_0_, bf16[5,128,512]{2,1,0:T(8,128)(2,1)S(1)} %collective-permute-done.16.refs_1_, bf16[5,128,512]{2,1,0:T(8,128)(2,1)S(1)} %collective-permute-done.17.refs_2_, bf16[2,128,512]{2,1,0:T(8,128)(2,1)S(1)} %collective-permute-done.21.refs_3_, ...), custom_call_target="tpu_custom_call" | custom-call | tf_op jit(solution)/shard_map/second_terms_b/pallas_call | solution.py:337
  92.1 1.4 %collective-permute-done.34.refs_4_ = bf16[2,128,512]{2,1,0:T(8,128)(2,1)S(1)} collective-permute-done((bf16[2,128,512]{2,1,0:T(8,128)(2,1)S(1)}, bf16[2,128,512]{2,1,0:T(8,128)(2,1)S(1)}, u32[]{:S(2)}, u32[]{:S(2)}) %collective-permute-start.34) | collective-permute-done | bytes 262176 | tf_op jit(solution)/shard_map/over_y/ppermute | solution.py:108
  93.5 0.4 turn_weight.1.refs_6_.refs_10_
  93.9 1.1 %collective-permute-done.36.refs_5_ = bf16[2,128,512]{2,1,0:T(8,128)(2,1)S(1)} collective-permute-done((bf16[2,128,512]{2,1,0:T(8,128)(2,1)S(1)}, bf16[2,128,512]{2,1,0:T(8,128)(2,1)S(1)}, u32[]{:S(2)}, u32[]{:S(2)}) %collective-permute-start.36) | collective-permute-done | bytes 262176 | tf_op jit(solution)/shard_map/mate/ppermute | solution.py:108
  95.1 2.1 %hidden_grad_a.1.grad = bf16[3,128,512]{2,1,0:T(8,128)(2,1)S(1)} custom-call(bf16[4,128,512]{2,1,0:T(8,128)(2,1)S(1)} %get-tuple-element.162.refs_6_.refs_0_, bf16[4,128,512]{2,1,0:T(8,128)(2,1)S(1)} %collective-permute-done.25.refs_1_, bf16[2,128,512]{2,1,0:T(8,128)(2,1)S(1)} %collective-permute-done.24.refs_2_, ...), custom_call_target="tpu_custom_call" | custom-call | tf_op jit(solution)/shard_map/hidden_grad_a/pallas_call | solution.py:337
  97.2 1.8 %first_terms_a.1.before = f32[3,384,512]{2,1,0:T(8,128)S(1)} custom-call(bf16[512,4096]{1,0:T(8,128)(2,1)S(1)} %get-tuple-element.156.flat, bf16[3,128,512]{2,1,0:T(8,128)(2,1)S(1)} %hidden_grad_a.1.grad), custom_call_target="tpu_custom_call" | custom-call | tf_op jit(solution)/shard_map/first_terms_a/pallas_call | solution.py:337
  99.0 0.8 collective-permute-done.37.refs_8_
  99.8 1.9 %collective-permute-done.38.refs_9_ = bf16[4,128,512]{2,1,0:T(8,128)(2,1)S(1)} collective-permute-done((bf16[4,128,512]{2,1,0:T(8,128)(2,1)S(1)}, bf16[4,128,512]{2,1,0:T(8,128)(2,1)S(1)}, u32[]{:S(2)}, u32[]{:S(2)}) %collective-permute-start.38) | collective-permute-done | bytes 524320 | tf_op jit(solution)/shard_map/mate/ppermute | solution.py:108
  101.8 3.6 %hidden_grad_b.1.grad = bf16[5,128,512]{2,1,0:T(8,128)(2,1)S(1)} custom-call(bf16[4,128,512]{2,1,0:T(8,128)(2,1)S(1)} %get-tuple-element.162.refs_6_.refs_0_, bf16[4,128,512]{2,1,0:T(8,128)(2,1)S(1)} %collective-permute-done.25.refs_1_, bf16[2,128,512]{2,1,0:T(8,128)(2,1)S(1)} %collective-permute-done.24.refs_2_, ...), custom_call_target="tpu_custom_call" | custom-call | flops 3019898880 | bytes 6422528 | tf_op jit(solution)/shard_map/hidden_grad_b/pallas_call | solution.py:337
  105.3 4.0 %first_terms_b.1 = f32[3,384,512]{2,1,0:T(8,128)} custom-call(bf16[512,4096]{1,0:T(8,128)(2,1)S(1)} %get-tuple-element.156.flat, bf16[5,128,512]{2,1,0:T(8,128)(2,1)S(1)} %hidden_grad_b.1.grad, f32[3,384,512]{2,1,0:T(8,128)S(1)} %first_terms_a.1.before), custom_call_target="tpu_custom_call" | custom-call | flops 3019898880 | bytes 7208960 | tf_op jit(solution)/shard_map/first_terms_b/pallas_call | solution.py:337
  (51 shorter events, 0.5 us)
Async XLA Ops:
  0.6 1.3 %copy-start = (bf16[128,3,3,512]{3,0,2,1:T(8,128)(2,1)S(1)}, bf16[128,3,3,512]{3,0,2,1:T(8,128)(2,1)}, u32[]{:S(2)}) copy-start(bf16[128,3,3,512]{3,0,2,1:T(8,128)(2,1)} %param.6) | copy-start | bytes 3538948
  2.0 17.6 %collective-permute-start.3 = (bf16[2,9,64,128]{3,2,1,0:T(8,128)(2,1)S(1)}, bf16[2,9,64,128]{3,2,1,0:T(8,128)(2,1)S(1)}, u32[]{:S(2)}, u32[]{:S(2)}) collective-permute-start(bf16[2,9,64,128]{3,2,1,0:T(8,128)(2,1)S(1)} %get-tuple-element.90), channel_id=1, source_target_pairs={{0,2},{1,3},{2,0},{3,1},{4,6},{5,7},{6,4},{7,5},{8,10},{9,11},{10,... | collective-permute-start | bytes 884744 | tf_op jit(solution)/shard_map/over_x/ppermute | solution.py:108
  5.1 8.5 %collective-permute-start = (bf16[1,128,512]{2,1,0:T(8,128)(2,1)}, bf16[1,128,512]{2,1,0:T(8,128)(2,1)S(1)}, u32[]{:S(2)}, u32[]{:S(2)}) collective-permute-start(bf16[1,128,512]{2,1,0:T(8,128)(2,1)} %bitcast.23), channel_id=1, source_target_pairs={{0,24},{4,28},{8,16},{12,20},{16,8},{20,12},{24,0},{28,4},{1,25},{... | collective-permute-start | bytes 393224 | tf_op jit(solution)/shard_map/along_z/ppermute | solution.py:108
  8.7 11.0 %collective-permute-start.1 = (bf16[1,128,512]{2,1,0:T(8,128)(2,1)}, bf16[1,128,512]{2,1,0:T(8,128)(2,1)S(1)}, u32[]{:S(2)}, u32[]{:S(2)}) collective-permute-start(bf16[1,128,512]{2,1,0:T(8,128)(2,1)} %bitcast.24), channel_id=1, source_target_pairs={{0,16},{4,20},{8,24},{12,28},{16,0},{20,4},{24,8},{28,12},{1,17},{... | collective-permute-start | bytes 393224 | tf_op jit(solution)/shard_map/along_z/ppermute | solution.py:108
  8.7 11.0 %collective-permute-start.2 = (bf16[1,128,512]{2,1,0:T(8,128)(2,1)}, bf16[1,128,512]{2,1,0:T(8,128)(2,1)S(1)}, u32[]{:S(2)}, u32[]{:S(2)}) collective-permute-start(bf16[1,128,512]{2,1,0:T(8,128)(2,1)} %bitcast.25), channel_id=1, source_target_pairs={{0,8},{4,12},{8,0},{12,4},{16,24},{20,28},{24,16},{28,20},{1,9},{5... | collective-permute-start | bytes 393224 | tf_op jit(solution)/shard_map/along_z/ppermute | solution.py:108
  9.4 0.9 copy-start.3
  10.4 11.5 %copy-start.5 = (bf16[128,1,512]{2,0,1:T(8,128)(2,1)S(1)}, bf16[128,1,512]{2,0,1:T(8,128)(2,1)}, u32[]{:S(2)}) copy-start(bf16[128,1,512]{2,0,1:T(8,128)(2,1)} %param.7) | copy-start | bytes 393220
  10.4 36.8 %copy-start.2 = (bf16[128,3,3,512]{3,0,2,1:T(8,128)(2,1)S(1)}, bf16[128,3,3,512]{3,0,2,1:T(8,128)(2,1)}, u32[]{:S(2)}) copy-start(bf16[128,3,3,512]{3,0,2,1:T(8,128)(2,1)} %param.5) | copy-start | bytes 3538948
  19.7 14.8 %collective-permute-start.7 = (bf16[4,128,512]{2,1,0:T(8,128)(2,1)S(1)}, bf16[4,128,512]{2,1,0:T(8,128)(2,1)S(1)}, u32[]{:S(2)}, u32[]{:S(2)}) collective-permute-start(bf16[4,128,512]{2,1,0:T(8,128)(2,1)S(1)} %constant_dynamic-update-slice_fusion.refs_0_), channel_id=1, source_target_pairs={{0,2},{1,3},{2,0},{3,1},{4,6},{5,7},{6,4},{7,5},{8,10},{9,11},{10,... | collective-permute-start | bytes 1572872 | tf_op jit(solution)/shard_map/over_x/ppermute | solution.py:108
  20.3 14.2 %collective-permute-start.8 = (bf16[4,128,512]{2,1,0:T(8,128)(2,1)S(1)}, bf16[4,128,512]{2,1,0:T(8,128)(2,1)S(1)}, u32[]{:S(2)}, u32[]{:S(2)}) collective-permute-start(bf16[4,128,512]{2,1,0:T(8,128)(2,1)S(1)} %constant_dynamic-update-slice_fusion.refs_0_), channel_id=1, source_target_pairs={{0,4},{4,0},{8,12},{12,8},{16,20},{20,16},{24,28},{28,24},{1,5},{5... | collective-permute-start | bytes 1572872 | tf_op jit(solution)/shard_map/over_y/ppermute | solution.py:108
  21.9 8.2 %collective-permute-start.4 = (bf16[1,128,512]{2,1,0:T(8,128)(2,1)S(1)}, bf16[1,128,512]{2,1,0:T(8,128)(2,1)S(1)}, u32[]{:S(2)}, u32[]{:S(2)}) collective-permute-start(bf16[1,128,512]{2,1,0:T(8,128)(2,1)S(1)} %bitcast.29), channel_id=1, source_target_pairs={{0,24},{4,28},{8,16},{12,20},{16,8},{20,12},{24,0},{28,4},{1,25},{... | collective-permute-start | bytes 393224 | tf_op jit(solution)/shard_map/along_z/ppermute | solution.py:108
  24.3 10.2 %collective-permute-start.5 = (bf16[1,128,512]{2,1,0:T(8,128)(2,1)S(1)}, bf16[1,128,512]{2,1,0:T(8,128)(2,1)S(1)}, u32[]{:S(2)}, u32[]{:S(2)}) collective-permute-start(bf16[1,128,512]{2,1,0:T(8,128)(2,1)S(1)} %bitcast.30), channel_id=1, source_target_pairs={{0,16},{4,20},{8,24},{12,28},{16,0},{20,4},{24,8},{28,12},{1,17},{... | collective-permute-start | bytes 393224 | tf_op jit(solution)/shard_map/along_z/ppermute | solution.py:108
  24.3 10.2 %collective-permute-start.6 = (bf16[1,128,512]{2,1,0:T(8,128)(2,1)S(1)}, bf16[1,128,512]{2,1,0:T(8,128)(2,1)S(1)}, u32[]{:S(2)}, u32[]{:S(2)}) collective-permute-start(bf16[1,128,512]{2,1,0:T(8,128)(2,1)S(1)} %bitcast.31), channel_id=1, source_target_pairs={{0,8},{4,12},{8,0},{12,4},{16,24},{20,28},{24,16},{28,20},{1,9},{5... | collective-permute-start | bytes 393224 | tf_op jit(solution)/shard_map/along_z/ppermute | solution.py:108
  34.5 10.6 %collective-permute-start.11 = (bf16[4,128,512]{2,1,0:T(8,128)(2,1)S(1)}, bf16[4,128,512]{2,1,0:T(8,128)(2,1)S(1)}, u32[]{:S(2)}, u32[]{:S(2)}) collective-permute-start(bf16[4,128,512]{2,1,0:T(8,128)(2,1)S(1)} %constant_dynamic-update-slice_fusion.refs_0_), channel_id=1, source_target_pairs={{0,1},{1,0},{2,3},{3,2},{4,5},{5,4},{6,7},{7,6},{8,9},{9,8},{10,11... | collective-permute-start | bytes 1572872 | tf_op jit(solution)/shard_map/mate/ppermute | solution.py:108
  34.6 10.6 %collective-permute-start.12 = (bf16[4,128,512]{2,1,0:T(8,128)(2,1)S(1)}, bf16[4,128,512]{2,1,0:T(8,128)(2,1)S(1)}, u32[]{:S(2)}, u32[]{:S(2)}) collective-permute-start(bf16[4,128,512]{2,1,0:T(8,128)(2,1)S(1)} %collective-permute-done.7.refs_2_), channel_id=1, source_target_pairs={{0,1},{1,0},{2,3},{3,2},{4,5},{5,4},{6,7},{7,6},{8,9},{9,8},{10,11... | collective-permute-start | bytes 1572872 | tf_op jit(solution)/shard_map/mate/ppermute | solution.py:108
  35.1 10.1 %collective-permute-start.13 = (bf16[4,128,512]{2,1,0:T(8,128)(2,1)S(1)}, bf16[4,128,512]{2,1,0:T(8,128)(2,1)S(1)}, u32[]{:S(2)}, u32[]{:S(2)}) collective-permute-start(bf16[4,128,512]{2,1,0:T(8,128)(2,1)S(1)} %collective-permute-done.8.refs_4_), channel_id=1, source_target_pairs={{0,1},{1,0},{2,3},{3,2},{4,5},{5,4},{6,7},{7,6},{8,9},{9,8},{10,11... | collective-permute-start | bytes 1572872 | tf_op jit(solution)/shard_map/mate/ppermute | solution.py:108
  35.2 8.7 %collective-permute-start.10 = (bf16[4,64,512]{2,1,0:T(8,128)(2,1)S(1)}, bf16[4,64,512]{2,1,0:T(8,128)(2,1)S(1)}, u32[]{:S(2)}, u32[]{:S(2)}) collective-permute-start(bf16[4,64,512]{2,1,0:T(8,128)(2,1)S(1)} %slice.37), channel_id=1, source_target_pairs={{0,2},{1,3},{2,0},{3,1},{4,6},{5,7},{6,4},{7,5},{8,10},{9,11},{10,... | collective-permute-start | bytes 786440 | tf_op jit(solution)/shard_map/over_x/ppermute | solution.py:108
  36.8 8.4 %collective-permute-start.9 = (bf16[4,64,512]{2,1,0:T(8,128)(2,1)S(1)}, bf16[4,64,512]{2,1,0:T(8,128)(2,1)S(1)}, u32[]{:S(2)}, u32[]{:S(2)}) collective-permute-start(bf16[4,64,512]{2,1,0:T(8,128)(2,1)S(1)} %slice.36), channel_id=1, source_target_pairs={{0,4},{4,0},{8,12},{12,8},{16,20},{20,16},{24,28},{28,24},{1,5},{5... | collective-permute-start | bytes 786440 | tf_op jit(solution)/shard_map/over_y/ppermute | solution.py:108
  45.2 1.6 %collective-permute-start.14 = (bf16[4,64,512]{2,1,0:T(8,128)(2,1)S(1)}, bf16[4,64,512]{2,1,0:T(8,128)(2,1)S(1)}, u32[]{:S(2)}, u32[]{:S(2)}) collective-permute-start(bf16[4,64,512]{2,1,0:T(8,128)(2,1)S(1)} %collective-permute-done.9.refs_6_), channel_id=1, source_target_pairs={{0,1},{1,0},{2,3},{3,2},{4,5},{5,4},{6,7},{7,6},{8,9},{9,8},{10,11... | collective-permute-start | bytes 786440 | tf_op jit(solution)/shard_map/mate/ppermute | solution.py:108
  45.3 1.9 %collective-permute-start.15 = (bf16[4,64,512]{2,1,0:T(8,128)(2,1)S(1)}, bf16[4,64,512]{2,1,0:T(8,128)(2,1)S(1)}, u32[]{:S(2)}, u32[]{:S(2)}) collective-permute-start(bf16[4,64,512]{2,1,0:T(8,128)(2,1)S(1)} %collective-permute-done.10.refs_8_), channel_id=1, source_target_pairs={{0,1},{1,0},{2,3},{3,2},{4,5},{5,4},{6,7},{7,6},{8,9},{9,8},{10,11... | collective-permute-start | bytes 786440 | tf_op jit(solution)/shard_map/mate/ppermute | solution.py:108
  50.6 16.7 %collective-permute-start.16 = (bf16[5,128,512]{2,1,0:T(8,128)(2,1)S(1)}, bf16[5,128,512]{2,1,0:T(8,128)(2,1)S(1)}, u32[]{:S(2)}, u32[]{:S(2)}) collective-permute-start(bf16[5,128,512]{2,1,0:T(8,128)(2,1)S(1)} %get-tuple-element.132.refs_0_), channel_id=1, source_target_pairs={{0,1},{1,0},{2,3},{3,2},{4,5},{5,4},{6,7},{7,6},{8,9},{9,8},{10,11... | collective-permute-start | bytes 1966088 | tf_op jit(solution)/shard_map/mate/ppermute | solution.py:108
  50.8 17.0 %collective-permute-start.17 = (bf16[5,128,512]{2,1,0:T(8,128)(2,1)S(1)}, bf16[5,128,512]{2,1,0:T(8,128)(2,1)S(1)}, u32[]{:S(2)}, u32[]{:S(2)}) collective-permute-start(bf16[5,128,512]{2,1,0:T(8,128)(2,1)S(1)} %get-tuple-element.132.refs_0_), channel_id=1, source_target_pairs={{0,2},{1,3},{2,0},{3,1},{4,6},{5,7},{6,4},{7,5},{8,10},{9,11},{10,... | collective-permute-start | bytes 1966088 | tf_op jit(solution)/shard_map/over_x/ppermute | solution.py:108
  51.3 13.9 %collective-permute-start.20 = (bf16[4,128,512]{2,1,0:T(8,128)(2,1)S(1)}, bf16[4,128,512]{2,1,0:T(8,128)(2,1)S(1)}, u32[]{:S(2)}, u32[]{:S(2)}) collective-permute-start(bf16[4,128,512]{2,1,0:T(8,128)(2,1)S(1)} %pad_maximum_fusion.refs_7_.refs_13_), channel_id=1, source_target_pairs={{0,4},{4,0},{8,12},{12,8},{16,20},{20,16},{24,28},{28,24},{1,5},{5... | collective-permute-start | bytes 1572872 | tf_op jit(solution)/shard_map/over_y/ppermute | solution.py:108
  51.8 14.9 %collective-permute-start.18 = (bf16[9,128,128]{2,1,0:T(8,128)(2,1)S(1)}, bf16[9,128,128]{2,1,0:T(8,128)(2,1)S(1)}, u32[]{:S(2)}, u32[]{:S(2)}) collective-permute-start(bf16[9,128,128]{2,1,0:T(8,128)(2,1)S(1)} %get-tuple-element.127), channel_id=1, source_target_pairs={{0,1},{1,0},{2,3},{3,2},{4,5},{5,4},{6,7},{7,6},{8,9},{9,8},{10,11... | collective-permute-start | bytes 884744 | tf_op jit(solution)/shard_map/mate/ppermute | solution.py:108
  51.8 13.4 %collective-permute-start.19 = (bf16[1,9,64,128]{3,2,1,0:T(8,128)(2,1)S(1)}, bf16[1,9,64,128]{3,2,1,0:T(8,128)(2,1)S(1)}, u32[]{:S(2)}, u32[]{:S(2)}) collective-permute-start(bf16[1,9,64,128]{3,2,1,0:T(8,128)(2,1)S(1)} %get-tuple-element.183), channel_id=1, source_target_pairs={{0,1},{1,0},{2,3},{3,2},{4,5},{5,4},{6,7},{7,6},{8,9},{9,8},{10,11... | collective-permute-start | bytes 442376 | tf_op jit(solution)/shard_map/mate/ppermute | solution.py:108
  52.4 18.3 %copy-start.1 = (bf16[128,3,3,512]{3,0,2,1:T(8,128)(2,1)S(1)}, bf16[128,3,3,512]{3,0,2,1:T(8,128)(2,1)}, u32[]{:S(2)}) copy-start(bf16[128,3,3,512]{3,0,2,1:T(8,128)(2,1)} %param.6) | copy-start | bytes 3538948
  52.4 18.3 %copy-start.4 = (bf16[128,1,512]{2,0,1:T(8,128)(2,1)S(1)}, bf16[128,1,512]{2,0,1:T(8,128)(2,1)}, u32[]{:S(2)}) copy-start(bf16[128,1,512]{2,0,1:T(8,128)(2,1)} %param.4) | copy-start | bytes 393220
  65.2 11.9 %collective-permute-start.26 = (bf16[3,128,512]{2,1,0:T(8,128)(2,1)S(1)}, bf16[3,128,512]{2,1,0:T(8,128)(2,1)S(1)}, u32[]{:S(2)}, u32[]{:S(2)}) collective-permute-start(bf16[3,128,512]{2,1,0:T(8,128)(2,1)S(1)} %get-tuple-element.142.refs_6_), channel_id=1, source_target_pairs={{0,1},{1,0},{2,3},{3,2},{4,5},{5,4},{6,7},{7,6},{8,9},{9,8},{10,11... | collective-permute-start | bytes 1179656 | tf_op jit(solution)/shard_map/mate/ppermute | solution.py:108
  65.2 11.9 %collective-permute-start.27 = (bf16[3,128,512]{2,1,0:T(8,128)(2,1)S(1)}, bf16[3,128,512]{2,1,0:T(8,128)(2,1)S(1)}, u32[]{:S(2)}, u32[]{:S(2)}) collective-permute-start(bf16[3,128,512]{2,1,0:T(8,128)(2,1)S(1)} %get-tuple-element.142.refs_6_), channel_id=1, source_target_pairs={{0,2},{1,3},{2,0},{3,1},{4,6},{5,7},{6,4},{7,5},{8,10},{9,11},{10,... | collective-permute-start | bytes 1179656 | tf_op jit(solution)/shard_map/over_x/ppermute | solution.py:108
  66.7 10.4 %collective-permute-start.28 = (bf16[2,9,64,128]{3,2,1,0:T(8,128)(2,1)S(1)}, bf16[2,9,64,128]{3,2,1,0:T(8,128)(2,1)S(1)}, u32[]{:S(2)}, u32[]{:S(2)}) collective-permute-start(bf16[2,9,64,128]{3,2,1,0:T(8,128)(2,1)S(1)} %collective-permute-done.3), channel_id=1, source_target_pairs={{0,4},{4,0},{8,12},{12,8},{16,20},{20,16},{24,28},{28,24},{1,5},{5... | collective-permute-start | bytes 884744 | tf_op jit(solution)/shard_map/over_y/ppermute | solution.py:108
  67.8 1.4 %collective-permute-start.23 = (bf16[1,128,512]{2,1,0:T(8,128)(2,1)S(1)}, bf16[1,128,512]{2,1,0:T(8,128)(2,1)S(1)}, u32[]{:S(2)}, u32[]{:S(2)}) collective-permute-start(bf16[1,128,512]{2,1,0:T(8,128)(2,1)S(1)} %slice.41), channel_id=1, source_target_pairs={{0,1},{1,0},{2,3},{3,2},{4,5},{5,4},{6,7},{7,6},{8,9},{9,8},{10,11... | collective-permute-start | bytes 393224 | tf_op jit(solution)/shard_map/mate/ppermute | solution.py:108
  67.9 1.7 %collective-permute-start.21 = (bf16[2,128,512]{2,1,0:T(8,128)(2,1)S(1)}, bf16[2,128,512]{2,1,0:T(8,128)(2,1)S(1)}, u32[]{:S(2)}, u32[]{:S(2)}) collective-permute-start(bf16[2,128,512]{2,1,0:T(8,128)(2,1)S(1)} %get-tuple-element.176), channel_id=1, source_target_pairs={{0,1},{1,0},{2,3},{3,2},{4,5},{5,4},{6,7},{7,6},{8,9},{9,8},{10,11... | collective-permute-start | bytes 786440 | tf_op jit(solution)/shard_map/mate/ppermute | solution.py:108
  69.2 1.5 %collective-permute-start.22 = (bf16[2,128,512]{2,1,0:T(8,128)(2,1)S(1)}, bf16[2,128,512]{2,1,0:T(8,128)(2,1)S(1)}, u32[]{:S(2)}, u32[]{:S(2)}) collective-permute-start(bf16[2,128,512]{2,1,0:T(8,128)(2,1)S(1)} %get-tuple-element.175), channel_id=1, source_target_pairs={{0,1},{1,0},{2,3},{3,2},{4,5},{5,4},{6,7},{7,6},{8,9},{9,8},{10,11... | collective-permute-start | bytes 786440 | tf_op jit(solution)/shard_map/mate/ppermute | solution.py:108
  74.3 11.7 %collective-permute-start.25 = (bf16[4,128,512]{2,1,0:T(8,128)(2,1)S(1)}, bf16[4,128,512]{2,1,0:T(8,128)(2,1)S(1)}, u32[]{:S(2)}, u32[]{:S(2)}) collective-permute-start(bf16[4,128,512]{2,1,0:T(8,128)(2,1)S(1)} %get-tuple-element.162.refs_6_.refs_0_), channel_id=1, source_target_pairs={{0,1},{1,0},{2,3},{3,2},{4,5},{5,4},{6,7},{7,6},{8,9},{9,8},{10,11... | collective-permute-start | bytes 1572872 | tf_op jit(solution)/shard_map/mate/ppermute | solution.py:108
  77.2 1.8 %collective-permute-start.30 = (bf16[1,128,512]{2,1,0:T(8,128)(2,1)S(1)}, bf16[1,128,512]{2,1,0:T(8,128)(2,1)S(1)}, u32[]{:S(2)}, u32[]{:S(2)}) collective-permute-start(bf16[1,128,512]{2,1,0:T(8,128)(2,1)S(1)} %get-tuple-element.179), channel_id=1, source_target_pairs={{0,1},{1,0},{2,3},{3,2},{4,5},{5,4},{6,7},{7,6},{8,9},{9,8},{10,11... | collective-permute-start | bytes 393224 | tf_op jit(solution)/shard_map/mate/ppermute | solution.py:108
  77.6 8.4 %collective-permute-start.24 = (bf16[2,128,512]{2,1,0:T(8,128)(2,1)S(1)}, bf16[2,128,512]{2,1,0:T(8,128)(2,1)S(1)}, u32[]{:S(2)}, u32[]{:S(2)}) collective-permute-start(bf16[2,128,512]{2,1,0:T(8,128)(2,1)S(1)} %get-tuple-element.137), channel_id=1, source_target_pairs={{0,2},{1,3},{2,0},{3,1},{4,6},{5,7},{6,4},{7,5},{8,10},{9,11},{10,... | collective-permute-start | bytes 786440 | tf_op jit(solution)/shard_map/over_x/ppermute | solution.py:108
  78.4 6.3 %collective-permute-start.29 = (bf16[1,9,64,128]{3,2,1,0:T(8,128)(2,1)S(1)}, bf16[1,9,64,128]{3,2,1,0:T(8,128)(2,1)S(1)}, u32[]{:S(2)}, u32[]{:S(2)}) collective-permute-start(bf16[1,9,64,128]{3,2,1,0:T(8,128)(2,1)S(1)} %get-tuple-element.181), channel_id=1, source_target_pairs={{0,1},{1,0},{2,3},{3,2},{4,5},{5,4},{6,7},{7,6},{8,9},{9,8},{10,11... | collective-permute-start | bytes 442376 | tf_op jit(solution)/shard_map/mate/ppermute | solution.py:108
  78.7 1.4 %collective-permute-start.31 = (bf16[1,128,512]{2,1,0:T(8,128)(2,1)S(1)}, bf16[1,128,512]{2,1,0:T(8,128)(2,1)S(1)}, u32[]{:S(2)}, u32[]{:S(2)}) collective-permute-start(bf16[1,128,512]{2,1,0:T(8,128)(2,1)S(1)} %get-tuple-element.178), channel_id=1, source_target_pairs={{0,1},{1,0},{2,3},{3,2},{4,5},{5,4},{6,7},{7,6},{8,9},{9,8},{10,11... | collective-permute-start | bytes 393224 | tf_op jit(solution)/shard_map/mate/ppermute | solution.py:108
  79.0 1.3 %collective-permute-start.32 = (bf16[1,128,512]{2,1,0:T(8,128)(2,1)S(1)}, bf16[1,128,512]{2,1,0:T(8,128)(2,1)S(1)}, u32[]{:S(2)}, u32[]{:S(2)}) collective-permute-start(bf16[1,128,512]{2,1,0:T(8,128)(2,1)S(1)} %get-tuple-element.177), channel_id=1, source_target_pairs={{0,1},{1,0},{2,3},{3,2},{4,5},{5,4},{6,7},{7,6},{8,9},{9,8},{10,11... | collective-permute-start | bytes 393224 | tf_op jit(solution)/shard_map/mate/ppermute | solution.py:108
  86.0 7.5 %collective-permute-start.34 = (bf16[2,128,512]{2,1,0:T(8,128)(2,1)S(1)}, bf16[2,128,512]{2,1,0:T(8,128)(2,1)S(1)}, u32[]{:S(2)}, u32[]{:S(2)}) collective-permute-start(bf16[2,128,512]{2,1,0:T(8,128)(2,1)S(1)} %collective-permute-done.24.refs_2_), channel_id=1, source_target_pairs={{0,4},{4,0},{8,12},{12,8},{16,20},{20,16},{24,28},{28,24},{1,5},{5... | collective-permute-start | bytes 786440 | tf_op jit(solution)/shard_map/over_y/ppermute | solution.py:108
  87.0 12.9 %collective-permute-start.37 = (bf16[4,128,512]{2,1,0:T(8,128)(2,1)S(1)}, bf16[4,128,512]{2,1,0:T(8,128)(2,1)S(1)}, u32[]{:S(2)}, u32[]{:S(2)}) collective-permute-start(bf16[4,128,512]{2,1,0:T(8,128)(2,1)S(1)} %get-tuple-element.168.refs_12_.refs_6_), channel_id=1, source_target_pairs={{0,2},{1,3},{2,0},{3,1},{4,6},{5,7},{6,4},{7,5},{8,10},{9,11},{10,... | collective-permute-start | bytes 1572872 | tf_op jit(solution)/shard_map/over_x/ppermute | solution.py:108
  87.6 12.3 %collective-permute-start.33 = (bf16[4,128,512]{2,1,0:T(8,128)(2,1)S(1)}, bf16[4,128,512]{2,1,0:T(8,128)(2,1)S(1)}, u32[]{:S(2)}, u32[]{:S(2)}) collective-permute-start(bf16[4,128,512]{2,1,0:T(8,128)(2,1)S(1)} %get-tuple-element.168.refs_12_.refs_6_), channel_id=1, source_target_pairs={{0,1},{1,0},{2,3},{3,2},{4,5},{5,4},{6,7},{7,6},{8,9},{9,8},{10,11... | collective-permute-start | bytes 1572872 | tf_op jit(solution)/shard_map/mate/ppermute | solution.py:108
  87.6 6.3 %collective-permute-start.35 = (bf16[2,128,512]{2,1,0:T(8,128)(2,1)S(1)}, bf16[2,128,512]{2,1,0:T(8,128)(2,1)S(1)}, u32[]{:S(2)}, u32[]{:S(2)}) collective-permute-start(bf16[2,128,512]{2,1,0:T(8,128)(2,1)S(1)} %collective-permute-done.24.refs_2_), channel_id=1, source_target_pairs={{0,1},{1,0},{2,3},{3,2},{4,5},{5,4},{6,7},{7,6},{8,9},{9,8},{10,11... | collective-permute-start | bytes 786440 | tf_op jit(solution)/shard_map/mate/ppermute | solution.py:108
  93.5 1.5 %collective-permute-start.36 = (bf16[2,128,512]{2,1,0:T(8,128)(2,1)S(1)}, bf16[2,128,512]{2,1,0:T(8,128)(2,1)S(1)}, u32[]{:S(2)}, u32[]{:S(2)}) collective-permute-start(bf16[2,128,512]{2,1,0:T(8,128)(2,1)S(1)} %collective-permute-done.34.refs_4_), channel_id=1, source_target_pairs={{0,1},{1,0},{2,3},{3,2},{4,5},{5,4},{6,7},{7,6},{8,9},{9,8},{10,11... | collective-permute-start | bytes 786440 | tf_op jit(solution)/shard_map/mate/ppermute | solution.py:108
  99.8 1.9 %collective-permute-start.38 = (bf16[4,128,512]{2,1,0:T(8,128)(2,1)S(1)}, bf16[4,128,512]{2,1,0:T(8,128)(2,1)S(1)}, u32[]{:S(2)}, u32[]{:S(2)}) collective-permute-start(bf16[4,128,512]{2,1,0:T(8,128)(2,1)S(1)} %collective-permute-done.37.refs_8_), channel_id=1, source_target_pairs={{0,1},{1,0},{2,3},{3,2},{4,5},{5,4},{6,7},{7,6},{8,9},{9,8},{10,11... | collective-permute-start | bytes 1572872 | tf_op jit(solution)/shard_map/mate/ppermute | solution.py:108

commit v6 on v5

--- a/solution.py
+++ b/solution.py
@@ -170,31 +170,28 @@
     first_rows(part, full, wide, hidden, mask)
 
 
-def first_rest_kernel(part, full, weight, hidden, mask, flat, wide):
+def first_rest_kernel(part, full, weight, hidden, mask, *refs):
+    *flats, wide = refs
     widen(weight, wide)
     first_rows(part, full, wide, hidden, mask)
     rows, _, w = full.shape
-    for r in range(rows):
-        flat[:, r * w : (r + 1) * w] = full[r]
+    for flat in flats:
+        for r in range(rows):
+            flat[:, r * w : (r + 1) * w] = full[r]
 
 
 def copy_pieces(layout, refs, put, lo, hi):
     y0, f0 = lax.axis_index("rows") & 1, lax.axis_index("filt")
+    others = {(e, base): ref for (e, base, kind), ref in zip(layout, refs) if kind == "other"}
     for (e, base, kind), ref in zip(layout, refs):
         count, own = ref.shape[:2]
         at = block_at(f0 ^ e, own)
         for n in range(count):
-            if kind == "whole":
-                if lo <= base + n < hi:
-                    put(base + n, at, ref[n])
-                continue
-            half = y0 if kind == "own" else 1 - y0
+            if kind == "whole" and lo <= base + n < hi:
+                put(base + n, at, ref[n])
             for y in (0, 1):
-                if lo <= base + y * count + n < hi:
-
-                    @pl.when(half == y)
-                    def _(ref=ref, n=n, y=y, at=at):
-                        put(base + y * count + n, at, ref[n])
+                if kind == "own" and lo <= base + y * count + n < hi:
+                    put(base + y * count + n, at, jnp.where(y0 == y, ref[n], others[e, base][n]))
 
 
 def fill_rows(x, layout, refs, lo, hi):
@@ -316,7 +313,12 @@
         out[a] = sum_terms(moved, flat, grad.shape[2], a, part)
 
 
-def first_terms_rest_kernel(part, flat, grad, before, out, moved, total, sems):
+def last_kernel(layout, part, rows, bases, *refs):
+    pieces, refs = refs[: len(layout)], refs[len(layout) :]
+    wide, mask_m, mask_b, flat, before, out, x, grad, moved, total, sems = refs
+    lo, hi = max(part[0] - 1, 0), min(part[1] + 1, rows)
+    fill_rows(x, layout, pieces, lo, hi)
+    back_rows(part, rows, lo, x, wide, list(zip(bases, (mask_m, mask_b))), grad)
     fill_moved([grad], moved)
     copies = []
     for a in range(3):
@@ -414,33 +416,40 @@
             places += [(len(pieces), k, z ^ d, e ^ core, lo) for k, z in enumerate(zs)]
             pieces.append(v["m" * core + name])
     cut_a, cut = rows // 2 + 1, rows // 2
+    start = 2
     full, h_a, mask_a = call(
-        functools.partial(first_kernel, places, len(pieces), (0, cut_a)),
+        functools.partial(first_kernel, places, len(pieces), (0, start)),
         pieces + [w1],
-        [((rows, c, w), BF), act(cut_a), act(cut_a)],
+        [((rows, c, w), BF), act(start), act(start)],
         [wide],
         0,
         "first_conv_a",
     )
-    h = {"a0": h_a, "a1": to_mate(h_a), "a2": over_x(h_a)}
+
+    def first_rest(part, with_flat, flops, name):
+        return call(
+            functools.partial(first_rest_kernel, part),
+            [full, w1],
+            [act(part[1] - part[0])] * 2 + [((c, rows * w), BF)] * with_flat,
+            [wide],
+            flops,
+            name,
+        )
+
+    x0 = over_x(h_a)
+    h_m, mask_m = first_rest((start, cut_a), 0, row_flops * 3, "first_conv_m")
     gy = over_y(v["g4"])
-    h |= {"m1": to_mate(v["mate"]), "near3": to_mate(v["near"][1:])}
-    h["gy"] = gy
-    h_b, mask_b, flat = call(
-        functools.partial(first_rest_kernel, (cut_a, rows)),
-        [full, w1],
-        [act(rows - cut_a)] * 2 + [((c, rows * w), BF)],
-        [wide],
-        0,
-        "first_conv_b",
-    )
+    h = {"h0": h_a, "h1": h_m, "x0": x0, "x1": over_x(h_m), "m0": to_mate(h_a), "m1": to_mate(h_m), "gy": gy}
+    h |= {"mate": to_mate(v["mate"]), "near3": to_mate(v["near"][1:]), "xm0": to_mate(x0)}
+    h_b, mask_b, flat = first_rest((cut_a, rows), 1, 0, "first_conv_b")
     b1, b2 = to_mate(h_b), over_x(h_b)
     h |= {"b0": h_b}
     h = wave(h)
     h |= {"b2": b2, "b1": b1}
-    cuts = [(n, min(n + 2, cut_a)) for n in range(0, cut_a, 2)]
-    layout_a = [(e, 0, "whole") for e in range(3)] + [(3, n, "whole") for n, _ in cuts]
-    spread_a = [h["a0"], h["a1"], h["a2"]] + [to_mate(h["a2"][n:m]) for n, m in cuts]
+    cuts = [(n, min(n + 2, cut_a)) for n in range(start, cut_a, 2)]
+    layout_a = [(e, 0, "whole") for e in range(4)] + [(e, start, "whole") for e in range(3)] + [(3, n, "whole") for n, _ in cuts]
+    spread_a = [h[k] for k in ("h0", "m0", "x0", "xm0", "h1", "m1", "x1")]
+    spread_a += [to_mate(h["x1"][n - start : m - start]) for n, m in cuts]
     grads = [v["g4"], h["gy"]]
     grad_places = [(p, k, z ^ p) for p in (0, 1) for k, z in enumerate(zs)]
 
@@ -488,11 +497,11 @@
     last = cut - 1
     layout = [(e, 0, "whole") for e in (0, 1)] + [(e, 0, kind) for kind in ("own", "other") for e in (2, 3)]
     names = ["a0", "a1", "s2", "s3", "t2", "t3"]
-    turned = [w2_taps, h["m1"], v["near"][:1], h["near3"], s["far"][:1], t["far3"]]
+    turned = [w2_taps, h["mate"], v["near"][:1], h["near3"], s["far"][:1], t["far3"]]
     (wide_back,) = call(turn_kernel, turned, [((3 * own, 3 * c), BF)], [], 0, "turn_weight")
     (grad_first,) = call(
-        functools.partial(back_kernel, layout, (0, last), rows, (0,)),
-        [*(t[k] for k in names), wide_back, mask_a],
+        functools.partial(back_kernel, layout, (0, last), rows, (0, start)),
+        [*(t[k] for k in names), wide_back, mask_a, mask_m],
         [act(last)],
         [vm((cut, c, w), BF)],
         0,
@@ -509,21 +518,20 @@
     t |= {"b2": b2, "terms": terms, "wide": wide_back, "grad": second_grad}
     t = wave(t)
     layout += [(e, cut, "whole") for e in range(4)]
-    (grad_first,) = call(
-        functools.partial(back_kernel, layout, (last, rows), rows, (0, cut_a)),
-        [*(t[k] for k in names), t["b0"], t["b1"], t["b2"], to_mate(t["b2"]), t["wide"], mask_a, mask_b],
-        [act(rows - last)],
-        [vm((rows - last + 1, c, w), BF)],
-        row_flops * (rows - last),
-        "hidden_grad_b",
-    )
+    n = rows - last
     (first_grad,) = call(
-        functools.partial(first_terms_rest_kernel, (last, rows)),
-        [flat, grad_first, t["terms"]],
+        functools.partial(last_kernel, layout, (last, rows), rows, (start, cut_a)),
+        [*(t[k] for k in names), t["b0"], t["b1"], t["b2"], to_mate(t["b2"]), t["wide"], mask_m, mask_b, flat, t["terms"]],
         [((3, 3 * own, c), F32)],
-        [vm((3 * own, (rows - last) * w), BF), vm((3, 3 * own, c), F32), DMA((3,))],
-        row_flops * (rows - last),
-        "first_terms_b",
+        [
+            vm((n + 1, c, w), BF),
+            vm((n, own, w), BF),
+            vm((3 * own, n * w), BF),
+            vm((3, 3 * own, c), F32),
+            DMA((3,)),
+        ],
+        2 * row_flops * n,
+        "hidden_grad_b_first_terms_b",
         out_spec=ANY,
     )
 

time: 110 us -> 107 us (0.973)
  waiting for transfers between devices: 47.8 us -> 42.3 us
  starting transfers between devices: 26 us -> 28.9 us
    ppermute x39 -> x41, waiting for transfers between devices: 47.8 us -> 42.3 us  [swap(): lax.ppermute(value, axis, [(i, i ^ bits) for i in range(lax.axis_size(axi...]
    ppermute x39 -> x41, starting transfers between devices: 26 us -> 28.9 us  [swap(): lax.ppermute(value, axis, [(i, i ^ bits) for i in range(lax.axis_size(axi...]
  transfers between devices with their start and end apart: 39 -> 41, of which waited for: 20 -> 19; matrix products, arithmetic and copies ran while one was open for 0% -> 0% of each run, Pallas kernels for 19% -> 22%
where the time goes in v6:
time: 107 us
  waiting for transfers between devices  42.3 us (40%)
  Pallas kernels  31.9 us (30%)
  starting transfers between devices  28.9 us (27%)
  local copies, waits for them, and re-layouts  2.4 us (2%)
  between operations  1.08 us (1%)
    ppermute x41, waiting for transfers between devices, swap(): lax.ppermute(value, axis, [(i, i ^ bits) for i in range(lax.axis_size(axi...  42.3 us
    pallas_call x13, Pallas kernels, call(): pl.pallas_call(kernel, out_shape=[jax.ShapeDtypeStruct(s, d) for s, d in...  31.9 us
    ppermute x41, starting transfers between devices, swap(): lax.ppermute(value, axis, [(i, i ^ bits) for i in range(lax.axis_size(axi...  28.9 us
    unnamed x15, local copies, waits for them, and re-layouts  2.25 us
  transfers between devices with their start and end apart: 41, of which 19 were waited for; matrix products, arithmetic and copies ran while one was open for 0% of the time, Pallas kernels for 22%

profile of v6, /device:TPU:0, one launch (start us, length us, event | category | flops | bytes accessed | tf_op | source)
XLA Modules:
  0.0 106.6 jit_solution(7110006575469573082)
XLA Ops:
  0.6 1.3 %copy-done = bf16[128,3,3,512]{3,0,2,1:T(8,128)(2,1)S(1)} copy-done((bf16[128,3,3,512]{3,0,2,1:T(8,128)(2,1)S(1)}, bf16[128,3,3,512]{3,0,2,1:T(8,128)(2,1)}, u32[]{:S(2)}) %copy-start) | copy-done | bytes 1179672
  1.9 0.1 pick_weight.1
  2.0 3.0 %collective-permute-start.3 = (bf16[2,9,64,128]{3,2,1,0:T(8,128)(2,1)S(1)}, bf16[2,9,64,128]{3,2,1,0:T(8,128)(2,1)S(1)}, u32[]{:S(2)}, u32[]{:S(2)}) collective-permute-start(bf16[2,9,64,128]{3,2,1,0:T(8,128)(2,1)S(1)} %get-tuple-element.96), channel_id=1, source_target_pairs={{0,2},{1,3},{2,0},{3,1},{4,6},{5,7},{6,4},{7,5},{8,10},{9,11},{10,... | collective-permute-start | bytes 884744 | tf_op jit(solution)/shard_map/over_x/ppermute | solution.py:108
  5.1 3.6 %collective-permute-start = (bf16[1,128,512]{2,1,0:T(8,128)(2,1)}, bf16[1,128,512]{2,1,0:T(8,128)(2,1)S(1)}, u32[]{:S(2)}, u32[]{:S(2)}) collective-permute-start(bf16[1,128,512]{2,1,0:T(8,128)(2,1)} %bitcast.24), channel_id=1, source_target_pairs={{0,24},{4,28},{8,16},{12,20},{16,8},{20,12},{24,0},{28,4},{1,25},{... | collective-permute-start | bytes 393224 | tf_op jit(solution)/shard_map/along_z/ppermute | solution.py:108
  8.7 0.8 collective-permute-start.2
  9.4 0.9 copy-done.3
  10.4 3.1 %collective-permute-done = bf16[1,128,512]{2,1,0:T(8,128)(2,1)S(1)} collective-permute-done((bf16[1,128,512]{2,1,0:T(8,128)(2,1)}, bf16[1,128,512]{2,1,0:T(8,128)(2,1)S(1)}, u32[]{:S(2)}, u32[]{:S(2)}) %collective-permute-start) | collective-permute-done | bytes 131104 | tf_op jit(solution)/shard_map/along_z/ppermute | solution.py:108
  13.5 6.1 %collective-permute-done.1 = bf16[1,128,512]{2,1,0:T(8,128)(2,1)S(1)} collective-permute-done((bf16[1,128,512]{2,1,0:T(8,128)(2,1)}, bf16[1,128,512]{2,1,0:T(8,128)(2,1)S(1)}, u32[]{:S(2)}, u32[]{:S(2)}) %collective-permute-start.1) | collective-permute-done | bytes 131104 | tf_op jit(solution)/shard_map/along_z/ppermute | solution.py:108
  19.7 0.6 collective-permute-start.7
  20.3 1.5 %collective-permute-start.8 = (bf16[4,128,512]{2,1,0:T(8,128)(2,1)S(1)}, bf16[4,128,512]{2,1,0:T(8,128)(2,1)S(1)}, u32[]{:S(2)}, u32[]{:S(2)}) collective-permute-start(bf16[4,128,512]{2,1,0:T(8,128)(2,1)S(1)} %constant_dynamic-update-slice_fusion.refs_0_), channel_id=1, source_target_pairs={{0,4},{4,0},{8,12},{12,8},{16,20},{20,16},{24,28},{28,24},{1,5},{5... | collective-permute-start | bytes 1572872 | tf_op jit(solution)/shard_map/over_y/ppermute | solution.py:108
  21.9 2.5 %collective-permute-start.4 = (bf16[1,128,512]{2,1,0:T(8,128)(2,1)S(1)}, bf16[1,128,512]{2,1,0:T(8,128)(2,1)S(1)}, u32[]{:S(2)}, u32[]{:S(2)}) collective-permute-start(bf16[1,128,512]{2,1,0:T(8,128)(2,1)S(1)} %bitcast.30), channel_id=1, source_target_pairs={{0,24},{4,28},{8,16},{12,20},{16,8},{20,12},{24,0},{28,4},{1,25},{... | collective-permute-start | bytes 393224 | tf_op jit(solution)/shard_map/along_z/ppermute | solution.py:108
  24.3 1.9 %collective-permute-start.6 = (bf16[1,128,512]{2,1,0:T(8,128)(2,1)S(1)}, bf16[1,128,512]{2,1,0:T(8,128)(2,1)S(1)}, u32[]{:S(2)}, u32[]{:S(2)}) collective-permute-start(bf16[1,128,512]{2,1,0:T(8,128)(2,1)S(1)} %bitcast.32), channel_id=1, source_target_pairs={{0,8},{4,12},{8,0},{12,4},{16,24},{20,28},{24,16},{28,20},{1,9},{5... | collective-permute-start | bytes 393224 | tf_op jit(solution)/shard_map/along_z/ppermute | solution.py:108
  26.2 3.8 %collective-permute-done.4 = bf16[1,128,512]{2,1,0:T(8,128)(2,1)S(1)} collective-permute-done((bf16[1,128,512]{2,1,0:T(8,128)(2,1)S(1)}, bf16[1,128,512]{2,1,0:T(8,128)(2,1)S(1)}, u32[]{:S(2)}, u32[]{:S(2)}) %collective-permute-start.4) | collective-permute-done | bytes 131104 | tf_op jit(solution)/shard_map/along_z/ppermute | solution.py:108
  30.1 4.4 %collective-permute-done.5 = bf16[1,128,512]{2,1,0:T(8,128)(2,1)S(1)} collective-permute-done((bf16[1,128,512]{2,1,0:T(8,128)(2,1)S(1)}, bf16[1,128,512]{2,1,0:T(8,128)(2,1)S(1)}, u32[]{:S(2)}, u32[]{:S(2)}) %collective-permute-start.5) | collective-permute-done | bytes 131104 | tf_op jit(solution)/shard_map/along_z/ppermute | solution.py:108
  34.5 0.1 collective-permute-start.11
  34.6 0.5 collective-permute-start.12
  35.1 0.1 collective-permute-start.13
  35.2 1.6 %collective-permute-start.10 = (bf16[4,64,512]{2,1,0:T(8,128)(2,1)S(1)}, bf16[4,64,512]{2,1,0:T(8,128)(2,1)S(1)}, u32[]{:S(2)}, u32[]{:S(2)}) collective-permute-start(bf16[4,64,512]{2,1,0:T(8,128)(2,1)S(1)} %slice.34), channel_id=1, source_target_pairs={{0,2},{1,3},{2,0},{3,1},{4,6},{5,7},{6,4},{7,5},{8,10},{9,11},{10,... | collective-permute-start | bytes 786440 | tf_op jit(solution)/shard_map/over_x/ppermute | solution.py:108
  36.8 0.5 collective-permute-start.9
  37.4 6.6 %collective-permute-done.10.refs_8_ = bf16[4,64,512]{2,1,0:T(8,128)(2,1)S(1)} collective-permute-done((bf16[4,64,512]{2,1,0:T(8,128)(2,1)S(1)}, bf16[4,64,512]{2,1,0:T(8,128)(2,1)S(1)}, u32[]{:S(2)}, u32[]{:S(2)}) %collective-permute-start.10) | collective-permute-done | bytes 262176 | tf_op jit(solution)/shard_map/over_x/ppermute | solution.py:108
  44.0 1.2 %collective-permute-done.9.refs_6_ = bf16[4,64,512]{2,1,0:T(8,128)(2,1)S(1)} collective-permute-done((bf16[4,64,512]{2,1,0:T(8,128)(2,1)S(1)}, bf16[4,64,512]{2,1,0:T(8,128)(2,1)S(1)}, u32[]{:S(2)}, u32[]{:S(2)}) %collective-permute-start.9) | collective-permute-done | bytes 262176 | tf_op jit(solution)/shard_map/over_y/ppermute | solution.py:108
  45.3 0.5 collective-permute-start.15
  45.8 1.0 collective-permute-done.14.refs_7_
  46.8 0.4 collective-permute-done.15.refs_9_
  47.2 1.6 %first_conv_a.1 = (bf16[8,512,512]{2,1,0:T(8,128)(2,1)S(1)}, bf16[2,128,512]{2,1,0:T(8,128)(2,1)S(1)}, bf16[2,128,512]{2,1,0:T(8,128)(2,1)S(1)}) custom-call(bf16[4,128,512]{2,1,0:T(8,128)(2,1)S(1)} %constant_dynamic-update-slice_fusion.refs_0_, bf16[4,128,512]{2,1,0:T(8,128)(2,1)S(1)} %collective-permute-done.11.refs_1_, ...), custom_call_target="tpu_custom_call" | custom-call | tf_op jit(solution)/shard_map/first_conv_a/pallas_call | solution.py:339
  48.7 0.6 collective-permute-start.16
  49.3 0.5 collective-permute-start.20
  49.9 0.3 collective-permute-start.22
  50.2 2.1 %first_conv_m.1 = (bf16[3,128,512]{2,1,0:T(8,128)(2,1)S(1)}, bf16[3,128,512]{2,1,0:T(8,128)(2,1)S(1)}) custom-call(bf16[8,512,512]{2,1,0:T(8,128)(2,1)S(1)} %get-tuple-element.133.full.refs_9_.refs_15_, bf16[3,384,512]{2,1,0:T(8,128)(2,1)S(1)} %bitcast.22), custom_call_target="tpu_custom_call" | custom-call | flops 1811939328 | bytes 5373952 | tf_op jit(solution)/shard_map/first_conv_m/pallas_call | solution.py:339
  52.3 0.3 collective-permute-start.21
  52.6 1.5 %collective-permute-start.17 = (bf16[3,128,512]{2,1,0:T(8,128)(2,1)S(1)}, bf16[3,128,512]{2,1,0:T(8,128)(2,1)S(1)}, u32[]{:S(2)}, u32[]{:S(2)}) collective-permute-start(bf16[3,128,512]{2,1,0:T(8,128)(2,1)S(1)} %get-tuple-element.143.refs_4_), channel_id=1, source_target_pairs={{0,2},{1,3},{2,0},{3,1},{4,6},{5,7},{6,4},{7,5},{8,10},{9,11},{10,... | collective-permute-start | bytes 1179656 | tf_op jit(solution)/shard_map/over_x/ppermute | solution.py:108
  54.1 3.8 %collective-permute-done.16.refs_2_ = bf16[2,128,512]{2,1,0:T(8,128)(2,1)S(1)} collective-permute-done((bf16[2,128,512]{2,1,0:T(8,128)(2,1)S(1)}, bf16[2,128,512]{2,1,0:T(8,128)(2,1)S(1)}, u32[]{:S(2)}, u32[]{:S(2)}) %collective-permute-start.16) | collective-permute-done | bytes 262176 | tf_op jit(solution)/shard_map/over_x/ppermute | solution.py:108
  57.9 0.5 collective-permute-start.23
  58.5 2.2 %first_conv_b.1 = (bf16[3,128,512]{2,1,0:T(8,128)(2,1)S(1)}, bf16[3,128,512]{2,1,0:T(8,128)(2,1)S(1)}, bf16[512,4096]{1,0:T(8,128)(2,1)S(1)}) custom-call(bf16[8,512,512]{2,1,0:T(8,128)(2,1)S(1)} %get-tuple-element.133.full.refs_9_.refs_15_, bf16[3,384,512]{2,1,0:T(8,128)(2,1)S(1)} %bitcast.23), custom_call_target="tpu_custom_call" | custom-call | tf_op jit(solution)/shard_map/first_conv_b/pallas_call | solution.py:339
  60.7 3.0 %collective-permute-done.20.refs_11_.refs_17_ = bf16[4,128,512]{2,1,0:T(8,128)(2,1)S(1)} collective-permute-done((bf16[4,128,512]{2,1,0:T(8,128)(2,1)S(1)}, bf16[4,128,512]{2,1,0:T(8,128)(2,1)S(1)}, u32[]{:S(2)}, u32[]{:S(2)}) %collective-permute-start.20) | collective-permute-done | bytes 524320 | tf_op jit(solution)/shard_map/over_y/ppermute | solution.py:108
  63.7 1.5 %collective-permute-start.29 = (bf16[3,128,512]{2,1,0:T(8,128)(2,1)S(1)}, bf16[3,128,512]{2,1,0:T(8,128)(2,1)S(1)}, u32[]{:S(2)}, u32[]{:S(2)}) collective-permute-start(bf16[3,128,512]{2,1,0:T(8,128)(2,1)S(1)} %get-tuple-element.153.refs_9_), channel_id=1, source_target_pairs={{0,2},{1,3},{2,0},{3,1},{4,6},{5,7},{6,4},{7,5},{8,10},{9,11},{10,... | collective-permute-start | bytes 1179656 | tf_op jit(solution)/shard_map/over_x/ppermute | solution.py:108
  65.2 0.4 collective-permute-done.17.refs_6_
  65.6 0.5 collective-permute-start.30
  66.2 0.6 collective-permute-start.25
  66.8 1.1 %collective-permute-done.25.refs_8_ = bf16[1,128,512]{2,1,0:T(8,128)(2,1)S(1)} collective-permute-done((bf16[1,128,512]{2,1,0:T(8,128)(2,1)S(1)}, bf16[1,128,512]{2,1,0:T(8,128)(2,1)S(1)}, u32[]{:S(2)}, u32[]{:S(2)}) %collective-permute-start.25) | collective-permute-done | bytes 131104 | tf_op jit(solution)/shard_map/mate/ppermute | solution.py:108
  67.9 3.7 %second_conv_a.1 = (bf16[1,128,512]{2,1,0:T(8,128)(2,1)S(1)}, bf16[4,128,512]{2,1,0:T(8,128)(2,1)S(1)}, bf16[2,128,512]{2,1,0:T(8,128)(2,1)S(1)}) custom-call(bf16[2,128,512]{2,1,0:T(8,128)(2,1)S(1)} %get-tuple-element.139.refs_0_, bf16[2,128,512]{2,1,0:T(8,128)(2,1)S(1)} %collective-permute-done.18.refs_1_, ...), custom_call_target="tpu_custom_call" | custom-call | tf_op jit(solution)/shard_map/second_conv_a/pallas_call | solution.py:339
  71.7 0.3 collective-permute-start.27
  71.9 0.8 collective-permute-start.26
  72.7 2.6 %second_terms_a.1.refs_16_ = f32[3,384,512]{2,1,0:T(8,128)S(1)} custom-call(bf16[2,128,512]{2,1,0:T(8,128)(2,1)S(1)} %get-tuple-element.139.refs_0_, bf16[2,128,512]{2,1,0:T(8,128)(2,1)S(1)} %collective-permute-done.18.refs_1_, bf16[2,128,512]{2,1,0:T(8,128)(2,1)S(1)} %collective-permute-done.16.refs_2_, ...), custom_call_target="tpu_custom_call" | custom-call | tf_op jit(solution)/shard_map/second_terms_a/pallas_call | solution.py:339
  75.4 0.1 collective-permute-start.32
  75.5 0.6 collective-permute-start.31
  76.1 0.1 collective-permute-start.33
  76.2 0.7 collective-permute-done.32.refs_12_
  76.8 0.1 collective-permute-start.34
  77.0 0.5 collective-permute-done.33.refs_13_
  77.4 0.7 collective-permute-done.34.refs_14_
  78.2 4.2 %second_conv_b.1 = (bf16[1,128,512]{2,1,0:T(8,128)(2,1)}, bf16[4,128,512]{2,1,0:T(8,128)(2,1)S(1)}) custom-call(bf16[2,128,512]{2,1,0:T(8,128)(2,1)S(1)} %get-tuple-element.139.refs_0_, bf16[2,128,512]{2,1,0:T(8,128)(2,1)S(1)} %collective-permute-done.18.refs_1_, bf16[2,128,512]{2,1,0:T(8,128)(2,1)S(1)} %collective-permute-done.16.refs_2_, ...), custom_call_target="tpu_custom_call" | custom-call | tf_op jit(solution)/shard_map/second_conv_b/pallas_call | solution.py:339
  82.4 1.3 %collective-permute-start.36 = (bf16[2,128,512]{2,1,0:T(8,128)(2,1)S(1)}, bf16[2,128,512]{2,1,0:T(8,128)(2,1)S(1)}, u32[]{:S(2)}, u32[]{:S(2)}) collective-permute-start(bf16[2,128,512]{2,1,0:T(8,128)(2,1)S(1)} %collective-permute-done.26.refs_2_), channel_id=1, source_target_pairs={{0,4},{4,0},{8,12},{12,8},{16,20},{20,16},{24,28},{28,24},{1,5},{5... | collective-permute-start | bytes 786440 | tf_op jit(solution)/shard_map/over_y/ppermute | solution.py:108
  83.7 1.5 %collective-permute-start.39 = (bf16[4,128,512]{2,1,0:T(8,128)(2,1)S(1)}, bf16[4,128,512]{2,1,0:T(8,128)(2,1)S(1)}, u32[]{:S(2)}, u32[]{:S(2)}) collective-permute-start(bf16[4,128,512]{2,1,0:T(8,128)(2,1)S(1)} %get-tuple-element.180.refs_15_.refs_6_), channel_id=1, source_target_pairs={{0,2},{1,3},{2,0},{3,1},{4,6},{5,7},{6,4},{7,5},{8,10},{9,11},{10,... | collective-permute-start | bytes 1572872 | tf_op jit(solution)/shard_map/over_x/ppermute | solution.py:108
  85.2 0.5 collective-permute-start.37
  85.7 4.0 %second_terms_b.1 = f32[3,384,512]{2,1,0:T(8,128)} custom-call(bf16[2,128,512]{2,1,0:T(8,128)(2,1)S(1)} %get-tuple-element.139.refs_0_, bf16[2,128,512]{2,1,0:T(8,128)(2,1)S(1)} %collective-permute-done.18.refs_1_, bf16[2,128,512]{2,1,0:T(8,128)(2,1)S(1)} %collective-permute-done.16.refs_2_, bf16[2,128,512]{2,1,0:T(8,128)(2,1)S(1)} %collective-permute-done.23.refs_3_, ...), custom_call_target="tpu_custom_call" | custom-call | tf_op jit(solution)/shard_map/second_terms_b/pallas_call | solution.py:339
  89.7 1.1 %collective-permute-done.36.refs_4_ = bf16[2,128,512]{2,1,0:T(8,128)(2,1)S(1)} collective-permute-done((bf16[2,128,512]{2,1,0:T(8,128)(2,1)S(1)}, bf16[2,128,512]{2,1,0:T(8,128)(2,1)S(1)}, u32[]{:S(2)}, u32[]{:S(2)}) %collective-permute-start.36) | collective-permute-done | bytes 262176 | tf_op jit(solution)/shard_map/over_y/ppermute | solution.py:108
  90.8 0.4 turn_weight.1.refs_6_.refs_10_
  91.2 1.1 %collective-permute-done.38.refs_5_ = bf16[2,128,512]{2,1,0:T(8,128)(2,1)S(1)} collective-permute-done((bf16[2,128,512]{2,1,0:T(8,128)(2,1)S(1)}, bf16[2,128,512]{2,1,0:T(8,128)(2,1)S(1)}, u32[]{:S(2)}, u32[]{:S(2)}) %collective-permute-start.38) | collective-permute-done | bytes 262176 | tf_op jit(solution)/shard_map/mate/ppermute | solution.py:108
  92.3 2.0 %hidden_grad_a.1.grad = bf16[3,128,512]{2,1,0:T(8,128)(2,1)S(1)} custom-call(bf16[4,128,512]{2,1,0:T(8,128)(2,1)S(1)} %get-tuple-element.174.refs_9_.refs_0_, bf16[4,128,512]{2,1,0:T(8,128)(2,1)S(1)} %collective-permute-done.27.refs_1_, bf16[2,128,512]{2,1,0:T(8,128)(2,1)S(1)} %collective-permute-done.26.refs_2_, ...), custom_call_target="tpu_custom_call" | custom-call | tf_op jit(solution)/shard_map/hidden_grad_a/pallas_call | solution.py:339
  94.4 1.8 %first_terms_a.1.refs_14_ = f32[3,384,512]{2,1,0:T(8,128)S(1)} custom-call(bf16[512,4096]{1,0:T(8,128)(2,1)S(1)} %get-tuple-element.167.flat.refs_13_, bf16[3,128,512]{2,1,0:T(8,128)(2,1)S(1)} %hidden_grad_a.1.grad), custom_call_target="tpu_custom_call" | custom-call | tf_op jit(solution)/shard_map/first_terms_a/pallas_call | solution.py:339
  96.2 1.2 %collective-permute-done.39.refs_8_ = bf16[4,128,512]{2,1,0:T(8,128)(2,1)S(1)} collective-permute-done((bf16[4,128,512]{2,1,0:T(8,128)(2,1)S(1)}, bf16[4,128,512]{2,1,0:T(8,128)(2,1)S(1)}, u32[]{:S(2)}, u32[]{:S(2)}) %collective-permute-start.39) | collective-permute-done | bytes 524320 | tf_op jit(solution)/shard_map/over_x/ppermute | solution.py:108
  97.4 1.9 %collective-permute-done.40.refs_9_ = bf16[4,128,512]{2,1,0:T(8,128)(2,1)S(1)} collective-permute-done((bf16[4,128,512]{2,1,0:T(8,128)(2,1)S(1)}, bf16[4,128,512]{2,1,0:T(8,128)(2,1)S(1)}, u32[]{:S(2)}, u32[]{:S(2)}) %collective-permute-start.40) | collective-permute-done | bytes 524320 | tf_op jit(solution)/shard_map/mate/ppermute | solution.py:108
  99.3 7.1 %hidden_grad_b_first_terms_b.1 = f32[3,384,512]{2,1,0:T(8,128)} custom-call(bf16[4,128,512]{2,1,0:T(8,128)(2,1)S(1)} %get-tuple-element.174.refs_9_.refs_0_, bf16[4,128,512]{2,1,0:T(8,128)(2,1)S(1)} %collective-permute-done.27.refs_1_, bf16[2,128,512]{2,1,0:T(8,128)(2,1)S(1)} %collective-permute-done.26.refs_2_, ...), custom_call_target="tpu_custom_call" | custom-call | flops 6039797760 | bytes 12713984 | tf_op jit(solution)/shard_map/hidden_grad_b_first_terms_b/pallas_call | solution.py:339
  (55 shorter events, 0.6 us)
Async XLA Ops:
  0.6 1.3 %copy-start = (bf16[128,3,3,512]{3,0,2,1:T(8,128)(2,1)S(1)}, bf16[128,3,3,512]{3,0,2,1:T(8,128)(2,1)}, u32[]{:S(2)}) copy-start(bf16[128,3,3,512]{3,0,2,1:T(8,128)(2,1)} %param.6) | copy-start | bytes 3538948
  2.0 17.6 %collective-permute-start.3 = (bf16[2,9,64,128]{3,2,1,0:T(8,128)(2,1)S(1)}, bf16[2,9,64,128]{3,2,1,0:T(8,128)(2,1)S(1)}, u32[]{:S(2)}, u32[]{:S(2)}) collective-permute-start(bf16[2,9,64,128]{3,2,1,0:T(8,128)(2,1)S(1)} %get-tuple-element.96), channel_id=1, source_target_pairs={{0,2},{1,3},{2,0},{3,1},{4,6},{5,7},{6,4},{7,5},{8,10},{9,11},{10,... | collective-permute-start | bytes 884744 | tf_op jit(solution)/shard_map/over_x/ppermute | solution.py:108
  5.1 8.5 %collective-permute-start = (bf16[1,128,512]{2,1,0:T(8,128)(2,1)}, bf16[1,128,512]{2,1,0:T(8,128)(2,1)S(1)}, u32[]{:S(2)}, u32[]{:S(2)}) collective-permute-start(bf16[1,128,512]{2,1,0:T(8,128)(2,1)} %bitcast.24), channel_id=1, source_target_pairs={{0,24},{4,28},{8,16},{12,20},{16,8},{20,12},{24,0},{28,4},{1,25},{... | collective-permute-start | bytes 393224 | tf_op jit(solution)/shard_map/along_z/ppermute | solution.py:108
  8.7 11.0 %collective-permute-start.1 = (bf16[1,128,512]{2,1,0:T(8,128)(2,1)}, bf16[1,128,512]{2,1,0:T(8,128)(2,1)S(1)}, u32[]{:S(2)}, u32[]{:S(2)}) collective-permute-start(bf16[1,128,512]{2,1,0:T(8,128)(2,1)} %bitcast.25), channel_id=1, source_target_pairs={{0,16},{4,20},{8,24},{12,28},{16,0},{20,4},{24,8},{28,12},{1,17},{... | collective-permute-start | bytes 393224 | tf_op jit(solution)/shard_map/along_z/ppermute | solution.py:108
  8.7 11.0 %collective-permute-start.2 = (bf16[1,128,512]{2,1,0:T(8,128)(2,1)}, bf16[1,128,512]{2,1,0:T(8,128)(2,1)S(1)}, u32[]{:S(2)}, u32[]{:S(2)}) collective-permute-start(bf16[1,128,512]{2,1,0:T(8,128)(2,1)} %bitcast.26), channel_id=1, source_target_pairs={{0,8},{4,12},{8,0},{12,4},{16,24},{20,28},{24,16},{28,20},{1,9},{5... | collective-permute-start | bytes 393224 | tf_op jit(solution)/shard_map/along_z/ppermute | solution.py:108
  9.4 0.9 copy-start.3
  10.4 11.5 %copy-start.5 = (bf16[128,1,512]{2,0,1:T(8,128)(2,1)S(1)}, bf16[128,1,512]{2,0,1:T(8,128)(2,1)}, u32[]{:S(2)}) copy-start(bf16[128,1,512]{2,0,1:T(8,128)(2,1)} %param.7) | copy-start | bytes 393220
  10.4 36.8 %copy-start.2 = (bf16[128,3,3,512]{3,0,2,1:T(8,128)(2,1)S(1)}, bf16[128,3,3,512]{3,0,2,1:T(8,128)(2,1)}, u32[]{:S(2)}) copy-start(bf16[128,3,3,512]{3,0,2,1:T(8,128)(2,1)} %param.5) | copy-start | bytes 3538948
  19.7 14.8 %collective-permute-start.7 = (bf16[4,128,512]{2,1,0:T(8,128)(2,1)S(1)}, bf16[4,128,512]{2,1,0:T(8,128)(2,1)S(1)}, u32[]{:S(2)}, u32[]{:S(2)}) collective-permute-start(bf16[4,128,512]{2,1,0:T(8,128)(2,1)S(1)} %constant_dynamic-update-slice_fusion.refs_0_), channel_id=1, source_target_pairs={{0,2},{1,3},{2,0},{3,1},{4,6},{5,7},{6,4},{7,5},{8,10},{9,11},{10,... | collective-permute-start | bytes 1572872 | tf_op jit(solution)/shard_map/over_x/ppermute | solution.py:108
  20.3 14.2 %collective-permute-start.8 = (bf16[4,128,512]{2,1,0:T(8,128)(2,1)S(1)}, bf16[4,128,512]{2,1,0:T(8,128)(2,1)S(1)}, u32[]{:S(2)}, u32[]{:S(2)}) collective-permute-start(bf16[4,128,512]{2,1,0:T(8,128)(2,1)S(1)} %constant_dynamic-update-slice_fusion.refs_0_), channel_id=1, source_target_pairs={{0,4},{4,0},{8,12},{12,8},{16,20},{20,16},{24,28},{28,24},{1,5},{5... | collective-permute-start | bytes 1572872 | tf_op jit(solution)/shard_map/over_y/ppermute | solution.py:108
  21.9 8.2 %collective-permute-start.4 = (bf16[1,128,512]{2,1,0:T(8,128)(2,1)S(1)}, bf16[1,128,512]{2,1,0:T(8,128)(2,1)S(1)}, u32[]{:S(2)}, u32[]{:S(2)}) collective-permute-start(bf16[1,128,512]{2,1,0:T(8,128)(2,1)S(1)} %bitcast.30), channel_id=1, source_target_pairs={{0,24},{4,28},{8,16},{12,20},{16,8},{20,12},{24,0},{28,4},{1,25},{... | collective-permute-start | bytes 393224 | tf_op jit(solution)/shard_map/along_z/ppermute | solution.py:108
  24.3 10.2 %collective-permute-start.5 = (bf16[1,128,512]{2,1,0:T(8,128)(2,1)S(1)}, bf16[1,128,512]{2,1,0:T(8,128)(2,1)S(1)}, u32[]{:S(2)}, u32[]{:S(2)}) collective-permute-start(bf16[1,128,512]{2,1,0:T(8,128)(2,1)S(1)} %bitcast.31), channel_id=1, source_target_pairs={{0,16},{4,20},{8,24},{12,28},{16,0},{20,4},{24,8},{28,12},{1,17},{... | collective-permute-start | bytes 393224 | tf_op jit(solution)/shard_map/along_z/ppermute | solution.py:108
  24.3 10.2 %collective-permute-start.6 = (bf16[1,128,512]{2,1,0:T(8,128)(2,1)S(1)}, bf16[1,128,512]{2,1,0:T(8,128)(2,1)S(1)}, u32[]{:S(2)}, u32[]{:S(2)}) collective-permute-start(bf16[1,128,512]{2,1,0:T(8,128)(2,1)S(1)} %bitcast.32), channel_id=1, source_target_pairs={{0,8},{4,12},{8,0},{12,4},{16,24},{20,28},{24,16},{28,20},{1,9},{5... | collective-permute-start | bytes 393224 | tf_op jit(solution)/shard_map/along_z/ppermute | solution.py:108
  34.5 10.6 %collective-permute-start.11 = (bf16[4,128,512]{2,1,0:T(8,128)(2,1)S(1)}, bf16[4,128,512]{2,1,0:T(8,128)(2,1)S(1)}, u32[]{:S(2)}, u32[]{:S(2)}) collective-permute-start(bf16[4,128,512]{2,1,0:T(8,128)(2,1)S(1)} %constant_dynamic-update-slice_fusion.refs_0_), channel_id=1, source_target_pairs={{0,1},{1,0},{2,3},{3,2},{4,5},{5,4},{6,7},{7,6},{8,9},{9,8},{10,11... | collective-permute-start | bytes 1572872 | tf_op jit(solution)/shard_map/mate/ppermute | solution.py:108
  34.6 10.6 %collective-permute-start.12 = (bf16[4,128,512]{2,1,0:T(8,128)(2,1)S(1)}, bf16[4,128,512]{2,1,0:T(8,128)(2,1)S(1)}, u32[]{:S(2)}, u32[]{:S(2)}) collective-permute-start(bf16[4,128,512]{2,1,0:T(8,128)(2,1)S(1)} %collective-permute-done.7.refs_2_), channel_id=1, source_target_pairs={{0,1},{1,0},{2,3},{3,2},{4,5},{5,4},{6,7},{7,6},{8,9},{9,8},{10,11... | collective-permute-start | bytes 1572872 | tf_op jit(solution)/shard_map/mate/ppermute | solution.py:108
  35.1 10.1 %collective-permute-start.13 = (bf16[4,128,512]{2,1,0:T(8,128)(2,1)S(1)}, bf16[4,128,512]{2,1,0:T(8,128)(2,1)S(1)}, u32[]{:S(2)}, u32[]{:S(2)}) collective-permute-start(bf16[4,128,512]{2,1,0:T(8,128)(2,1)S(1)} %collective-permute-done.8.refs_4_), channel_id=1, source_target_pairs={{0,1},{1,0},{2,3},{3,2},{4,5},{5,4},{6,7},{7,6},{8,9},{9,8},{10,11... | collective-permute-start | bytes 1572872 | tf_op jit(solution)/shard_map/mate/ppermute | solution.py:108
  35.2 8.7 %collective-permute-start.10 = (bf16[4,64,512]{2,1,0:T(8,128)(2,1)S(1)}, bf16[4,64,512]{2,1,0:T(8,128)(2,1)S(1)}, u32[]{:S(2)}, u32[]{:S(2)}) collective-permute-start(bf16[4,64,512]{2,1,0:T(8,128)(2,1)S(1)} %slice.34), channel_id=1, source_target_pairs={{0,2},{1,3},{2,0},{3,1},{4,6},{5,7},{6,4},{7,5},{8,10},{9,11},{10,... | collective-permute-start | bytes 786440 | tf_op jit(solution)/shard_map/over_x/ppermute | solution.py:108
  36.8 8.4 %collective-permute-start.9 = (bf16[4,64,512]{2,1,0:T(8,128)(2,1)S(1)}, bf16[4,64,512]{2,1,0:T(8,128)(2,1)S(1)}, u32[]{:S(2)}, u32[]{:S(2)}) collective-permute-start(bf16[4,64,512]{2,1,0:T(8,128)(2,1)S(1)} %slice.33), channel_id=1, source_target_pairs={{0,4},{4,0},{8,12},{12,8},{16,20},{20,16},{24,28},{28,24},{1,5},{5... | collective-permute-start | bytes 786440 | tf_op jit(solution)/shard_map/over_y/ppermute | solution.py:108
  45.2 1.6 %collective-permute-start.14 = (bf16[4,64,512]{2,1,0:T(8,128)(2,1)S(1)}, bf16[4,64,512]{2,1,0:T(8,128)(2,1)S(1)}, u32[]{:S(2)}, u32[]{:S(2)}) collective-permute-start(bf16[4,64,512]{2,1,0:T(8,128)(2,1)S(1)} %collective-permute-done.9.refs_6_), channel_id=1, source_target_pairs={{0,1},{1,0},{2,3},{3,2},{4,5},{5,4},{6,7},{7,6},{8,9},{9,8},{10,11... | collective-permute-start | bytes 786440 | tf_op jit(solution)/shard_map/mate/ppermute | solution.py:108
  45.3 1.9 %collective-permute-start.15 = (bf16[4,64,512]{2,1,0:T(8,128)(2,1)S(1)}, bf16[4,64,512]{2,1,0:T(8,128)(2,1)S(1)}, u32[]{:S(2)}, u32[]{:S(2)}) collective-permute-start(bf16[4,64,512]{2,1,0:T(8,128)(2,1)S(1)} %collective-permute-done.10.refs_8_), channel_id=1, source_target_pairs={{0,1},{1,0},{2,3},{3,2},{4,5},{5,4},{6,7},{7,6},{8,9},{9,8},{10,11... | collective-permute-start | bytes 786440 | tf_op jit(solution)/shard_map/mate/ppermute | solution.py:108
  48.7 9.2 %collective-permute-start.16 = (bf16[2,128,512]{2,1,0:T(8,128)(2,1)S(1)}, bf16[2,128,512]{2,1,0:T(8,128)(2,1)S(1)}, u32[]{:S(2)}, u32[]{:S(2)}) collective-permute-start(bf16[2,128,512]{2,1,0:T(8,128)(2,1)S(1)} %get-tuple-element.139.refs_0_), channel_id=1, source_target_pairs={{0,2},{1,3},{2,0},{3,1},{4,6},{5,7},{6,4},{7,5},{8,10},{9,11},{10,... | collective-permute-start | bytes 786440 | tf_op jit(solution)/shard_map/over_x/ppermute | solution.py:108
  49.3 8.6 %collective-permute-start.18 = (bf16[2,128,512]{2,1,0:T(8,128)(2,1)S(1)}, bf16[2,128,512]{2,1,0:T(8,128)(2,1)S(1)}, u32[]{:S(2)}, u32[]{:S(2)}) collective-permute-start(bf16[2,128,512]{2,1,0:T(8,128)(2,1)S(1)} %get-tuple-element.139.refs_0_), channel_id=1, source_target_pairs={{0,1},{1,0},{2,3},{3,2},{4,5},{5,4},{6,7},{7,6},{8,9},{9,8},{10,11... | collective-permute-start | bytes 786440 | tf_op jit(solution)/shard_map/mate/ppermute | solution.py:108
  49.3 14.3 %collective-permute-start.20 = (bf16[4,128,512]{2,1,0:T(8,128)(2,1)S(1)}, bf16[4,128,512]{2,1,0:T(8,128)(2,1)S(1)}, u32[]{:S(2)}, u32[]{:S(2)}) collective-permute-start(bf16[4,128,512]{2,1,0:T(8,128)(2,1)S(1)} %pad_maximum_fusion.refs_10_.refs_16_), channel_id=1, source_target_pairs={{0,4},{4,0},{8,12},{12,8},{16,20},{20,16},{24,28},{28,24},{1,5},{5... | collective-permute-start | bytes 1572872 | tf_op jit(solution)/shard_map/over_y/ppermute | solution.py:108
  49.9 2.7 %collective-permute-start.22 = (bf16[1,9,64,128]{3,2,1,0:T(8,128)(2,1)S(1)}, bf16[1,9,64,128]{3,2,1,0:T(8,128)(2,1)S(1)}, u32[]{:S(2)}, u32[]{:S(2)}) collective-permute-start(bf16[1,9,64,128]{3,2,1,0:T(8,128)(2,1)S(1)} %get-tuple-element.193), channel_id=1, source_target_pairs={{0,1},{1,0},{2,3},{3,2},{4,5},{5,4},{6,7},{7,6},{8,9},{9,8},{10,11... | collective-permute-start | bytes 442376 | tf_op jit(solution)/shard_map/mate/ppermute | solution.py:108
  52.3 8.4 %collective-permute-start.21 = (bf16[9,128,128]{2,1,0:T(8,128)(2,1)S(1)}, bf16[9,128,128]{2,1,0:T(8,128)(2,1)S(1)}, u32[]{:S(2)}, u32[]{:S(2)}) collective-permute-start(bf16[9,128,128]{2,1,0:T(8,128)(2,1)S(1)} %get-tuple-element.136), channel_id=1, source_target_pairs={{0,1},{1,0},{2,3},{3,2},{4,5},{5,4},{6,7},{7,6},{8,9},{9,8},{10,11... | collective-permute-start | bytes 884744 | tf_op jit(solution)/shard_map/mate/ppermute | solution.py:108
  52.6 15.3 %copy-start.1 = (bf16[128,3,3,512]{3,0,2,1:T(8,128)(2,1)S(1)}, bf16[128,3,3,512]{3,0,2,1:T(8,128)(2,1)}, u32[]{:S(2)}) copy-start(bf16[128,3,3,512]{3,0,2,1:T(8,128)(2,1)} %param.6) | copy-start | bytes 3538948
  52.6 15.3 %copy-start.4 = (bf16[128,1,512]{2,0,1:T(8,128)(2,1)S(1)}, bf16[128,1,512]{2,0,1:T(8,128)(2,1)}, u32[]{:S(2)}) copy-start(bf16[128,1,512]{2,0,1:T(8,128)(2,1)} %param.4) | copy-start | bytes 393220
  52.6 13.0 %collective-permute-start.17 = (bf16[3,128,512]{2,1,0:T(8,128)(2,1)S(1)}, bf16[3,128,512]{2,1,0:T(8,128)(2,1)S(1)}, u32[]{:S(2)}, u32[]{:S(2)}) collective-permute-start(bf16[3,128,512]{2,1,0:T(8,128)(2,1)S(1)} %get-tuple-element.143.refs_4_), channel_id=1, source_target_pairs={{0,2},{1,3},{2,0},{3,1},{4,6},{5,7},{6,4},{7,5},{8,10},{9,11},{10,... | collective-permute-start | bytes 1179656 | tf_op jit(solution)/shard_map/over_x/ppermute | solution.py:108
  57.9 8.1 %collective-permute-start.19 = (bf16[3,128,512]{2,1,0:T(8,128)(2,1)S(1)}, bf16[3,128,512]{2,1,0:T(8,128)(2,1)S(1)}, u32[]{:S(2)}, u32[]{:S(2)}) collective-permute-start(bf16[3,128,512]{2,1,0:T(8,128)(2,1)S(1)} %get-tuple-element.143.refs_4_), channel_id=1, source_target_pairs={{0,1},{1,0},{2,3},{3,2},{4,5},{5,4},{6,7},{7,6},{8,9},{9,8},{10,11... | collective-permute-start | bytes 1179656 | tf_op jit(solution)/shard_map/mate/ppermute | solution.py:108
  57.9 8.1 %collective-permute-start.23 = (bf16[2,128,512]{2,1,0:T(8,128)(2,1)S(1)}, bf16[2,128,512]{2,1,0:T(8,128)(2,1)S(1)}, u32[]{:S(2)}, u32[]{:S(2)}) collective-permute-start(bf16[2,128,512]{2,1,0:T(8,128)(2,1)S(1)} %collective-permute-done.16.refs_2_), channel_id=1, source_target_pairs={{0,1},{1,0},{2,3},{3,2},{4,5},{5,4},{6,7},{7,6},{8,9},{9,8},{10,11... | collective-permute-start | bytes 786440 | tf_op jit(solution)/shard_map/mate/ppermute | solution.py:108
  60.6 14.7 %collective-permute-start.28 = (bf16[3,128,512]{2,1,0:T(8,128)(2,1)S(1)}, bf16[3,128,512]{2,1,0:T(8,128)(2,1)S(1)}, u32[]{:S(2)}, u32[]{:S(2)}) collective-permute-start(bf16[3,128,512]{2,1,0:T(8,128)(2,1)S(1)} %get-tuple-element.153.refs_9_), channel_id=1, source_target_pairs={{0,1},{1,0},{2,3},{3,2},{4,5},{5,4},{6,7},{7,6},{8,9},{9,8},{10,11... | collective-permute-start | bytes 1179656 | tf_op jit(solution)/shard_map/mate/ppermute | solution.py:108
  63.7 11.7 %collective-permute-start.29 = (bf16[3,128,512]{2,1,0:T(8,128)(2,1)S(1)}, bf16[3,128,512]{2,1,0:T(8,128)(2,1)S(1)}, u32[]{:S(2)}, u32[]{:S(2)}) collective-permute-start(bf16[3,128,512]{2,1,0:T(8,128)(2,1)S(1)} %get-tuple-element.153.refs_9_), channel_id=1, source_target_pairs={{0,2},{1,3},{2,0},{3,1},{4,6},{5,7},{6,4},{7,5},{8,10},{9,11},{10,... | collective-permute-start | bytes 1179656 | tf_op jit(solution)/shard_map/over_x/ppermute | solution.py:108
  65.6 9.8 %collective-permute-start.30 = (bf16[2,9,64,128]{3,2,1,0:T(8,128)(2,1)S(1)}, bf16[2,9,64,128]{3,2,1,0:T(8,128)(2,1)S(1)}, u32[]{:S(2)}, u32[]{:S(2)}) collective-permute-start(bf16[2,9,64,128]{3,2,1,0:T(8,128)(2,1)S(1)} %collective-permute-done.3), channel_id=1, source_target_pairs={{0,4},{4,0},{8,12},{12,8},{16,20},{20,16},{24,28},{28,24},{1,5},{5... | collective-permute-start | bytes 884744 | tf_op jit(solution)/shard_map/over_y/ppermute | solution.py:108
  66.1 1.8 %collective-permute-start.24 = (bf16[2,128,512]{2,1,0:T(8,128)(2,1)S(1)}, bf16[2,128,512]{2,1,0:T(8,128)(2,1)S(1)}, u32[]{:S(2)}, u32[]{:S(2)}) collective-permute-start(bf16[2,128,512]{2,1,0:T(8,128)(2,1)S(1)} %slice.36), channel_id=1, source_target_pairs={{0,1},{1,0},{2,3},{3,2},{4,5},{5,4},{6,7},{7,6},{8,9},{9,8},{10,11... | collective-permute-start | bytes 786440 | tf_op jit(solution)/shard_map/mate/ppermute | solution.py:108
  66.2 1.7 %collective-permute-start.25 = (bf16[1,128,512]{2,1,0:T(8,128)(2,1)S(1)}, bf16[1,128,512]{2,1,0:T(8,128)(2,1)S(1)}, u32[]{:S(2)}, u32[]{:S(2)}) collective-permute-start(bf16[1,128,512]{2,1,0:T(8,128)(2,1)S(1)} %slice.37), channel_id=1, source_target_pairs={{0,1},{1,0},{2,3},{3,2},{4,5},{5,4},{6,7},{7,6},{8,9},{9,8},{10,11... | collective-permute-start | bytes 393224 | tf_op jit(solution)/shard_map/mate/ppermute | solution.py:108
  71.7 10.7 %collective-permute-start.27 = (bf16[4,128,512]{2,1,0:T(8,128)(2,1)S(1)}, bf16[4,128,512]{2,1,0:T(8,128)(2,1)S(1)}, u32[]{:S(2)}, u32[]{:S(2)}) collective-permute-start(bf16[4,128,512]{2,1,0:T(8,128)(2,1)S(1)} %get-tuple-element.174.refs_9_.refs_0_), channel_id=1, source_target_pairs={{0,1},{1,0},{2,3},{3,2},{4,5},{5,4},{6,7},{7,6},{8,9},{9,8},{10,11... | collective-permute-start | bytes 1572872 | tf_op jit(solution)/shard_map/mate/ppermute | solution.py:108
  71.9 10.4 %collective-permute-start.26 = (bf16[2,128,512]{2,1,0:T(8,128)(2,1)S(1)}, bf16[2,128,512]{2,1,0:T(8,128)(2,1)S(1)}, u32[]{:S(2)}, u32[]{:S(2)}) collective-permute-start(bf16[2,128,512]{2,1,0:T(8,128)(2,1)S(1)} %get-tuple-element.148), channel_id=1, source_target_pairs={{0,2},{1,3},{2,0},{3,1},{4,6},{5,7},{6,4},{7,5},{8,10},{9,11},{10,... | collective-permute-start | bytes 786440 | tf_op jit(solution)/shard_map/over_x/ppermute | solution.py:108
  75.4 1.4 %collective-permute-start.32 = (bf16[1,128,512]{2,1,0:T(8,128)(2,1)S(1)}, bf16[1,128,512]{2,1,0:T(8,128)(2,1)S(1)}, u32[]{:S(2)}, u32[]{:S(2)}) collective-permute-start(bf16[1,128,512]{2,1,0:T(8,128)(2,1)S(1)} %get-tuple-element.189), channel_id=1, source_target_pairs={{0,1},{1,0},{2,3},{3,2},{4,5},{5,4},{6,7},{7,6},{8,9},{9,8},{10,11... | collective-permute-start | bytes 393224 | tf_op jit(solution)/shard_map/mate/ppermute | solution.py:108
  75.5 6.8 %collective-permute-start.31 = (bf16[1,9,64,128]{3,2,1,0:T(8,128)(2,1)S(1)}, bf16[1,9,64,128]{3,2,1,0:T(8,128)(2,1)S(1)}, u32[]{:S(2)}, u32[]{:S(2)}) collective-permute-start(bf16[1,9,64,128]{3,2,1,0:T(8,128)(2,1)S(1)} %get-tuple-element.191), channel_id=1, source_target_pairs={{0,1},{1,0},{2,3},{3,2},{4,5},{5,4},{6,7},{7,6},{8,9},{9,8},{10,11... | collective-permute-start | bytes 442376 | tf_op jit(solution)/shard_map/mate/ppermute | solution.py:108
  76.1 1.3 %collective-permute-start.33 = (bf16[1,128,512]{2,1,0:T(8,128)(2,1)S(1)}, bf16[1,128,512]{2,1,0:T(8,128)(2,1)S(1)}, u32[]{:S(2)}, u32[]{:S(2)}) collective-permute-start(bf16[1,128,512]{2,1,0:T(8,128)(2,1)S(1)} %get-tuple-element.188), channel_id=1, source_target_pairs={{0,1},{1,0},{2,3},{3,2},{4,5},{5,4},{6,7},{7,6},{8,9},{9,8},{10,11... | collective-permute-start | bytes 393224 | tf_op jit(solution)/shard_map/mate/ppermute | solution.py:108
  76.8 1.3 %collective-permute-start.34 = (bf16[1,128,512]{2,1,0:T(8,128)(2,1)S(1)}, bf16[1,128,512]{2,1,0:T(8,128)(2,1)S(1)}, u32[]{:S(2)}, u32[]{:S(2)}) collective-permute-start(bf16[1,128,512]{2,1,0:T(8,128)(2,1)S(1)} %get-tuple-element.187), channel_id=1, source_target_pairs={{0,1},{1,0},{2,3},{3,2},{4,5},{5,4},{6,7},{7,6},{8,9},{9,8},{10,11... | collective-permute-start | bytes 393224 | tf_op jit(solution)/shard_map/mate/ppermute | solution.py:108
  82.4 8.4 %collective-permute-start.36 = (bf16[2,128,512]{2,1,0:T(8,128)(2,1)S(1)}, bf16[2,128,512]{2,1,0:T(8,128)(2,1)S(1)}, u32[]{:S(2)}, u32[]{:S(2)}) collective-permute-start(bf16[2,128,512]{2,1,0:T(8,128)(2,1)S(1)} %collective-permute-done.26.refs_2_), channel_id=1, source_target_pairs={{0,4},{4,0},{8,12},{12,8},{16,20},{20,16},{24,28},{28,24},{1,5},{5... | collective-permute-start | bytes 786440 | tf_op jit(solution)/shard_map/over_y/ppermute | solution.py:108
  83.7 13.7 %collective-permute-start.39 = (bf16[4,128,512]{2,1,0:T(8,128)(2,1)S(1)}, bf16[4,128,512]{2,1,0:T(8,128)(2,1)S(1)}, u32[]{:S(2)}, u32[]{:S(2)}) collective-permute-start(bf16[4,128,512]{2,1,0:T(8,128)(2,1)S(1)} %get-tuple-element.180.refs_15_.refs_6_), channel_id=1, source_target_pairs={{0,2},{1,3},{2,0},{3,1},{4,6},{5,7},{6,4},{7,5},{8,10},{9,11},{10,... | collective-permute-start | bytes 1572872 | tf_op jit(solution)/shard_map/over_x/ppermute | solution.py:108
  85.2 12.2 %collective-permute-start.35 = (bf16[4,128,512]{2,1,0:T(8,128)(2,1)S(1)}, bf16[4,128,512]{2,1,0:T(8,128)(2,1)S(1)}, u32[]{:S(2)}, u32[]{:S(2)}) collective-permute-start(bf16[4,128,512]{2,1,0:T(8,128)(2,1)S(1)} %get-tuple-element.180.refs_15_.refs_6_), channel_id=1, source_target_pairs={{0,1},{1,0},{2,3},{3,2},{4,5},{5,4},{6,7},{7,6},{8,9},{9,8},{10,11... | collective-permute-start | bytes 1572872 | tf_op jit(solution)/shard_map/mate/ppermute | solution.py:108
  85.2 6.0 %collective-permute-start.37 = (bf16[2,128,512]{2,1,0:T(8,128)(2,1)S(1)}, bf16[2,128,512]{2,1,0:T(8,128)(2,1)S(1)}, u32[]{:S(2)}, u32[]{:S(2)}) collective-permute-start(bf16[2,128,512]{2,1,0:T(8,128)(2,1)S(1)} %collective-permute-done.26.refs_2_), channel_id=1, source_target_pairs={{0,1},{1,0},{2,3},{3,2},{4,5},{5,4},{6,7},{7,6},{8,9},{9,8},{10,11... | collective-permute-start | bytes 786440 | tf_op jit(solution)/shard_map/mate/ppermute | solution.py:108
  90.8 1.5 %collective-permute-start.38 = (bf16[2,128,512]{2,1,0:T(8,128)(2,1)S(1)}, bf16[2,128,512]{2,1,0:T(8,128)(2,1)S(1)}, u32[]{:S(2)}, u32[]{:S(2)}) collective-permute-start(bf16[2,128,512]{2,1,0:T(8,128)(2,1)S(1)} %collective-permute-done.36.refs_4_), channel_id=1, source_target_pairs={{0,1},{1,0},{2,3},{3,2},{4,5},{5,4},{6,7},{7,6},{8,9},{9,8},{10,11... | collective-permute-start | bytes 786440 | tf_op jit(solution)/shard_map/mate/ppermute | solution.py:108
  97.4 1.9 %collective-permute-start.40 = (bf16[4,128,512]{2,1,0:T(8,128)(2,1)S(1)}, bf16[4,128,512]{2,1,0:T(8,128)(2,1)S(1)}, u32[]{:S(2)}, u32[]{:S(2)}) collective-permute-start(bf16[4,128,512]{2,1,0:T(8,128)(2,1)S(1)} %collective-permute-done.39.refs_8_), channel_id=1, source_target_pairs={{0,1},{1,0},{2,3},{3,2},{4,5},{5,4},{6,7},{7,6},{8,9},{9,8},{10,11... | collective-permute-start | bytes 1572872 | tf_op jit(solution)/shard_map/mate/ppermute | solution.py:108

commit v7 on v6

--- a/solution.py
+++ b/solution.py
@@ -313,9 +313,13 @@
         out[a] = sum_terms(moved, flat, grad.shape[2], a, part)
 
 
+def fill_kernel(layout, lo, hi, *refs):
+    fill_rows(refs[-1], layout, refs[:-1], lo, hi)
+
+
 def last_kernel(layout, part, rows, bases, *refs):
     pieces, refs = refs[: len(layout)], refs[len(layout) :]
-    wide, mask_m, mask_b, flat, before, out, x, grad, moved, total, sems = refs
+    wide, mask_m, mask_b, flat, before, _, out, x, grad, moved, total, sems = refs
     lo, hi = max(part[0] - 1, 0), min(part[1] + 1, rows)
     fill_rows(x, layout, pieces, lo, hi)
     back_rows(part, rows, lo, x, wide, list(zip(bases, (mask_m, mask_b))), grad)
@@ -334,13 +338,14 @@
 DMA = pltpu.SemaphoreType.DMA
 
 
-def call(kernel, ins, outs, scratch, flops, name, in_spec=VM, out_spec=VM):
+def call(kernel, ins, outs, scratch, flops, name, in_spec=VM, out_spec=VM, aliases=None):
     nbytes = sum(v.size * v.dtype.itemsize for v in ins) if flops else 0
     return pl.pallas_call(
         kernel,
         out_shape=[jax.ShapeDtypeStruct(s, d) for s, d in outs],
         in_specs=[in_spec] * len(ins),
-        out_specs=[out_spec] * len(outs),
+        out_specs=[out_spec] + [VM] * (len(outs) - 1),
+        input_output_aliases=aliases or {},
         scratch_shapes=scratch,
         compiler_params=pltpu.CompilerParams(vmem_limit_bytes=VMEM_BYTES),
         cost_estimate=pl.CostEstimate(flops=flops, bytes_accessed=nbytes, transcendentals=0),
@@ -515,24 +520,27 @@
         0,
         "first_terms_a",
     )
-    t |= {"b2": b2, "terms": terms, "wide": wide_back, "grad": second_grad}
+    n = rows - last
+    known = layout + [(e, cut, "whole") for e in (0, 1)]
+    (x,) = call(
+        functools.partial(fill_kernel, known, last - 1, rows),
+        [*(t[k] for k in names), t["b0"], t["b1"]],
+        [((n + 1, c, w), BF)],
+        [],
+        0,
+        "known_rows",
+    )
+    t |= {"b2": b2, "terms": terms, "wide": wide_back, "grad": second_grad, "x": x}
     t = wave(t)
-    layout += [(e, cut, "whole") for e in range(4)]
-    n = rows - last
-    (first_grad,) = call(
-        functools.partial(last_kernel, layout, (last, rows), rows, (start, cut_a)),
-        [*(t[k] for k in names), t["b0"], t["b1"], t["b2"], to_mate(t["b2"]), t["wide"], mask_m, mask_b, flat, t["terms"]],
-        [((3, 3 * own, c), F32)],
-        [
-            vm((n + 1, c, w), BF),
-            vm((n, own, w), BF),
-            vm((3 * own, n * w), BF),
-            vm((3, 3 * own, c), F32),
-            DMA((3,)),
-        ],
+    first_grad, _ = call(
+        functools.partial(last_kernel, [(e, cut, "whole") for e in (2, 3)], (last, rows), rows, (start, cut_a)),
+        [t["b2"], to_mate(t["b2"]), t["wide"], mask_m, mask_b, flat, t["terms"], t["x"]],
+        [((3, 3 * own, c), F32), ((n + 1, c, w), BF)],
+        [vm((n, own, w), BF), vm((3 * own, n * w), BF), vm((3, 3 * own, c), F32), DMA((3,))],
         2 * row_flops * n,
         "hidden_grad_b_first_terms_b",
         out_spec=ANY,
+        aliases={7: 1},
     )
 
     def as_weight(value):

time: 107 us -> 107 us (level)
  waiting for transfers between devices: 42.3 us -> 44.6 us
  starting transfers between devices: 28.9 us -> 26.8 us
    ppermute x41, waiting for transfers between devices: 42.3 us -> 44.6 us  [swap(): lax.ppermute(value, axis, [(i, i ^ bits) for i in range(lax.axis_size(axi...]
    ppermute x41, starting transfers between devices: 28.9 us -> 26.8 us  [swap(): lax.ppermute(value, axis, [(i, i ^ bits) for i in range(lax.axis_size(axi...]
    pallas_call x13 -> x14, Pallas kernels: 31.9 us -> 31.9 us  [call(): pl.pallas_call(kernel, out_shape=[jax.ShapeDtypeStruct(s, d) for s, d in...]
where the time goes in v7:
time: 107 us
  waiting for transfers between devices  44.6 us (42%)
  Pallas kernels  31.9 us (30%)
  starting transfers between devices  26.8 us (25%)
  local copies, waits for them, and re-layouts  2.4 us (2%)
  between operations  1.11 us (1%)
    ppermute x41, waiting for transfers between devices, swap(): lax.ppermute(value, axis, [(i, i ^ bits) for i in range(lax.axis_size(axi...  44.6 us
    pallas_call x14, Pallas kernels, call(): pl.pallas_call(kernel, out_shape=[jax.ShapeDtypeStruct(s, d) for s, d in...  31.9 us
    ppermute x41, starting transfers between devices, swap(): lax.ppermute(value, axis, [(i, i ^ bits) for i in range(lax.axis_size(axi...  26.8 us
    unnamed x15, local copies, waits for them, and re-layouts  2.26 us
  transfers between devices with their start and end apart: 41, of which 19 were waited for; matrix products, arithmetic and copies ran while one was open for 0% of the time, Pallas kernels for 22%

profile of v7, /device:TPU:0, one launch (start us, length us, event | category | flops | bytes accessed | tf_op | source)
XLA Modules:
  0.0 106.9 jit_solution(146069371950013501)
XLA Ops:
  0.6 1.3 %copy-done = bf16[128,3,3,512]{3,0,2,1:T(8,128)(2,1)S(1)} copy-done((bf16[128,3,3,512]{3,0,2,1:T(8,128)(2,1)S(1)}, bf16[128,3,3,512]{3,0,2,1:T(8,128)(2,1)}, u32[]{:S(2)}) %copy-start) | copy-done | bytes 1179672
  1.9 0.1 pick_weight.1
  2.0 3.0 %collective-permute-start.3 = (bf16[2,9,64,128]{3,2,1,0:T(8,128)(2,1)S(1)}, bf16[2,9,64,128]{3,2,1,0:T(8,128)(2,1)S(1)}, u32[]{:S(2)}, u32[]{:S(2)}) collective-permute-start(bf16[2,9,64,128]{3,2,1,0:T(8,128)(2,1)S(1)} %get-tuple-element.90), channel_id=1, source_target_pairs={{0,2},{1,3},{2,0},{3,1},{4,6},{5,7},{6,4},{7,5},{8,10},{9,11},{10,... | collective-permute-start | bytes 884744 | tf_op jit(solution)/shard_map/over_x/ppermute | solution.py:108
  5.1 1.6 %collective-permute-start.2 = (bf16[1,128,512]{2,1,0:T(8,128)(2,1)}, bf16[1,128,512]{2,1,0:T(8,128)(2,1)S(1)}, u32[]{:S(2)}, u32[]{:S(2)}) collective-permute-start(bf16[1,128,512]{2,1,0:T(8,128)(2,1)} %bitcast.24), channel_id=1, source_target_pairs={{0,8},{4,12},{8,0},{12,4},{16,24},{20,28},{24,16},{28,20},{1,9},{5... | collective-permute-start | bytes 393224 | tf_op jit(solution)/shard_map/along_z/ppermute | solution.py:108
  6.6 2.6 %collective-permute-start.1 = (bf16[1,128,512]{2,1,0:T(8,128)(2,1)}, bf16[1,128,512]{2,1,0:T(8,128)(2,1)S(1)}, u32[]{:S(2)}, u32[]{:S(2)}) collective-permute-start(bf16[1,128,512]{2,1,0:T(8,128)(2,1)} %bitcast.25), channel_id=1, source_target_pairs={{0,16},{4,20},{8,24},{12,28},{16,0},{20,4},{24,8},{28,12},{1,17},{... | collective-permute-start | bytes 393224 | tf_op jit(solution)/shard_map/along_z/ppermute | solution.py:108
  9.2 0.2 collective-permute-start
  9.4 0.9 copy-done.3
  10.4 1.3 %collective-permute-done.2 = bf16[1,128,512]{2,1,0:T(8,128)(2,1)S(1)} collective-permute-done((bf16[1,128,512]{2,1,0:T(8,128)(2,1)}, bf16[1,128,512]{2,1,0:T(8,128)(2,1)S(1)}, u32[]{:S(2)}, u32[]{:S(2)}) %collective-permute-start.2) | collective-permute-done | bytes 131104 | tf_op jit(solution)/shard_map/along_z/ppermute | solution.py:108
  11.7 7.8 %collective-permute-done.1 = bf16[1,128,512]{2,1,0:T(8,128)(2,1)S(1)} collective-permute-done((bf16[1,128,512]{2,1,0:T(8,128)(2,1)}, bf16[1,128,512]{2,1,0:T(8,128)(2,1)S(1)}, u32[]{:S(2)}, u32[]{:S(2)}) %collective-permute-start.1) | collective-permute-done | bytes 131104 | tf_op jit(solution)/shard_map/along_z/ppermute | solution.py:108
  19.6 1.6 %collective-permute-start.8 = (bf16[4,128,512]{2,1,0:T(8,128)(2,1)S(1)}, bf16[4,128,512]{2,1,0:T(8,128)(2,1)S(1)}, u32[]{:S(2)}, u32[]{:S(2)}) collective-permute-start(bf16[4,128,512]{2,1,0:T(8,128)(2,1)S(1)} %constant_dynamic-update-slice_fusion.refs_0_), channel_id=1, source_target_pairs={{0,4},{4,0},{8,12},{12,8},{16,20},{20,16},{24,28},{28,24},{1,5},{5... | collective-permute-start | bytes 1572872 | tf_op jit(solution)/shard_map/over_y/ppermute | solution.py:108
  21.2 0.5 collective-permute-start.7
  21.7 2.0 %collective-permute-start.6 = (bf16[1,128,512]{2,1,0:T(8,128)(2,1)S(1)}, bf16[1,128,512]{2,1,0:T(8,128)(2,1)S(1)}, u32[]{:S(2)}, u32[]{:S(2)}) collective-permute-start(bf16[1,128,512]{2,1,0:T(8,128)(2,1)S(1)} %bitcast.30), channel_id=1, source_target_pairs={{0,8},{4,12},{8,0},{12,4},{16,24},{20,28},{24,16},{28,20},{1,9},{5... | collective-permute-start | bytes 393224 | tf_op jit(solution)/shard_map/along_z/ppermute | solution.py:108
  23.7 1.0 collective-permute-start.5
  24.7 1.4 %collective-permute-start.4 = (bf16[1,128,512]{2,1,0:T(8,128)(2,1)S(1)}, bf16[1,128,512]{2,1,0:T(8,128)(2,1)S(1)}, u32[]{:S(2)}, u32[]{:S(2)}) collective-permute-start(bf16[1,128,512]{2,1,0:T(8,128)(2,1)S(1)} %bitcast.32), channel_id=1, source_target_pairs={{0,24},{4,28},{8,16},{12,20},{16,8},{20,12},{24,0},{28,4},{1,25},{... | collective-permute-start | bytes 393224 | tf_op jit(solution)/shard_map/along_z/ppermute | solution.py:108
  26.1 1.4 %collective-permute-done.6 = bf16[1,128,512]{2,1,0:T(8,128)(2,1)S(1)} collective-permute-done((bf16[1,128,512]{2,1,0:T(8,128)(2,1)S(1)}, bf16[1,128,512]{2,1,0:T(8,128)(2,1)S(1)}, u32[]{:S(2)}, u32[]{:S(2)}) %collective-permute-start.6) | collective-permute-done | bytes 131104 | tf_op jit(solution)/shard_map/along_z/ppermute | solution.py:108
  27.5 7.2 %collective-permute-done.5 = bf16[1,128,512]{2,1,0:T(8,128)(2,1)S(1)} collective-permute-done((bf16[1,128,512]{2,1,0:T(8,128)(2,1)S(1)}, bf16[1,128,512]{2,1,0:T(8,128)(2,1)S(1)}, u32[]{:S(2)}, u32[]{:S(2)}) %collective-permute-start.5) | collective-permute-done | bytes 131104 | tf_op jit(solution)/shard_map/along_z/ppermute | solution.py:108
  34.8 0.5 collective-permute-start.12
  35.4 1.6 %collective-permute-start.10 = (bf16[4,64,512]{2,1,0:T(8,128)(2,1)S(1)}, bf16[4,64,512]{2,1,0:T(8,128)(2,1)S(1)}, u32[]{:S(2)}, u32[]{:S(2)}) collective-permute-start(bf16[4,64,512]{2,1,0:T(8,128)(2,1)S(1)} %slice.34), channel_id=1, source_target_pairs={{0,2},{1,3},{2,0},{3,1},{4,6},{5,7},{6,4},{7,5},{8,10},{9,11},{10,... | collective-permute-start | bytes 786440 | tf_op jit(solution)/shard_map/over_x/ppermute | solution.py:108
  37.0 0.5 collective-permute-start.9
  37.6 6.6 %collective-permute-done.10.refs_8_ = bf16[4,64,512]{2,1,0:T(8,128)(2,1)S(1)} collective-permute-done((bf16[4,64,512]{2,1,0:T(8,128)(2,1)S(1)}, bf16[4,64,512]{2,1,0:T(8,128)(2,1)S(1)}, u32[]{:S(2)}, u32[]{:S(2)}) %collective-permute-start.10) | collective-permute-done | bytes 262176 | tf_op jit(solution)/shard_map/over_x/ppermute | solution.py:108
  44.1 1.2 %collective-permute-done.9.refs_6_ = bf16[4,64,512]{2,1,0:T(8,128)(2,1)S(1)} collective-permute-done((bf16[4,64,512]{2,1,0:T(8,128)(2,1)S(1)}, bf16[4,64,512]{2,1,0:T(8,128)(2,1)S(1)}, u32[]{:S(2)}, u32[]{:S(2)}) %collective-permute-start.9) | collective-permute-done | bytes 262176 | tf_op jit(solution)/shard_map/over_y/ppermute | solution.py:108
  45.4 0.5 collective-permute-start.15
  45.9 1.0 collective-permute-done.14.refs_7_
  47.0 0.4 collective-permute-done.15.refs_9_
  47.3 1.6 %first_conv_a.1 = (bf16[8,512,512]{2,1,0:T(8,128)(2,1)S(1)}, bf16[2,128,512]{2,1,0:T(8,128)(2,1)S(1)}, bf16[2,128,512]{2,1,0:T(8,128)(2,1)S(1)}) custom-call(bf16[4,128,512]{2,1,0:T(8,128)(2,1)S(1)} %constant_dynamic-update-slice_fusion.refs_0_, bf16[4,128,512]{2,1,0:T(8,128)(2,1)S(1)} %collective-permute-done.11.refs_1_, ...), custom_call_target="tpu_custom_call" | custom-call | tf_op jit(solution)/shard_map/first_conv_a/pallas_call | solution.py:343
  48.9 0.2 collective-permute-start.18
  49.1 0.5 collective-permute-start.16
  49.7 0.5 collective-permute-start.20
  50.3 0.5 collective-permute-start.21
  50.8 2.1 %first_conv_m.1 = (bf16[3,128,512]{2,1,0:T(8,128)(2,1)S(1)}, bf16[3,128,512]{2,1,0:T(8,128)(2,1)S(1)}) custom-call(bf16[8,512,512]{2,1,0:T(8,128)(2,1)S(1)} %get-tuple-element.127.full.refs_9_.refs_15_, bf16[3,384,512]{2,1,0:T(8,128)(2,1)S(1)} %bitcast.22), custom_call_target="tpu_custom_call" | custom-call | flops 1811939328 | bytes 5373952 | tf_op jit(solution)/shard_map/first_conv_m/pallas_call | solution.py:343
  52.9 0.1 collective-permute-start.19
  53.1 1.5 %collective-permute-start.17 = (bf16[3,128,512]{2,1,0:T(8,128)(2,1)S(1)}, bf16[3,128,512]{2,1,0:T(8,128)(2,1)S(1)}, u32[]{:S(2)}, u32[]{:S(2)}) collective-permute-start(bf16[3,128,512]{2,1,0:T(8,128)(2,1)S(1)} %get-tuple-element.137.refs_4_), channel_id=1, source_target_pairs={{0,2},{1,3},{2,0},{3,1},{4,6},{5,7},{6,4},{7,5},{8,10},{9,11},{10,... | collective-permute-start | bytes 1179656 | tf_op jit(solution)/shard_map/over_x/ppermute | solution.py:108
  54.6 3.7 %collective-permute-done.16.refs_2_ = bf16[2,128,512]{2,1,0:T(8,128)(2,1)S(1)} collective-permute-done((bf16[2,128,512]{2,1,0:T(8,128)(2,1)S(1)}, bf16[2,128,512]{2,1,0:T(8,128)(2,1)S(1)}, u32[]{:S(2)}, u32[]{:S(2)}) %collective-permute-start.16) | collective-permute-done | bytes 262176 | tf_op jit(solution)/shard_map/over_x/ppermute | solution.py:108
  58.3 2.2 %first_conv_b.1 = (bf16[3,128,512]{2,1,0:T(8,128)(2,1)S(1)}, bf16[3,128,512]{2,1,0:T(8,128)(2,1)S(1)}, bf16[512,4096]{1,0:T(8,128)(2,1)S(1)}) custom-call(bf16[8,512,512]{2,1,0:T(8,128)(2,1)S(1)} %get-tuple-element.127.full.refs_9_.refs_15_, bf16[3,384,512]{2,1,0:T(8,128)(2,1)S(1)} %bitcast.23), custom_call_target="tpu_custom_call" | custom-call | tf_op jit(solution)/shard_map/first_conv_b/pallas_call | solution.py:343
  60.4 0.6 collective-permute-start.29
  61.0 2.5 %collective-permute-done.20.refs_11_.refs_17_ = bf16[4,128,512]{2,1,0:T(8,128)(2,1)S(1)} collective-permute-done((bf16[4,128,512]{2,1,0:T(8,128)(2,1)S(1)}, bf16[4,128,512]{2,1,0:T(8,128)(2,1)S(1)}, u32[]{:S(2)}, u32[]{:S(2)}) %collective-permute-start.20) | collective-permute-done | bytes 524320 | tf_op jit(solution)/shard_map/over_y/ppermute | solution.py:108
  63.6 0.5 collective-permute-start.30
  64.1 2.6 %collective-permute-done.17.refs_6_ = bf16[3,128,512]{2,1,0:T(8,128)(2,1)S(1)} collective-permute-done((bf16[3,128,512]{2,1,0:T(8,128)(2,1)S(1)}, bf16[3,128,512]{2,1,0:T(8,128)(2,1)S(1)}, u32[]{:S(2)}, u32[]{:S(2)}) %collective-permute-start.17) | collective-permute-done | bytes 393248 | tf_op jit(solution)/shard_map/over_x/ppermute | solution.py:108
  66.8 0.6 collective-permute-start.25
  67.4 1.1 %collective-permute-done.25.refs_8_ = bf16[1,128,512]{2,1,0:T(8,128)(2,1)S(1)} collective-permute-done((bf16[1,128,512]{2,1,0:T(8,128)(2,1)S(1)}, bf16[1,128,512]{2,1,0:T(8,128)(2,1)S(1)}, u32[]{:S(2)}, u32[]{:S(2)}) %collective-permute-start.25) | collective-permute-done | bytes 131104 | tf_op jit(solution)/shard_map/mate/ppermute | solution.py:108
  68.5 3.7 %second_conv_a.1 = (bf16[1,128,512]{2,1,0:T(8,128)(2,1)S(1)}, bf16[4,128,512]{2,1,0:T(8,128)(2,1)S(1)}, bf16[2,128,512]{2,1,0:T(8,128)(2,1)S(1)}) custom-call(bf16[2,128,512]{2,1,0:T(8,128)(2,1)S(1)} %get-tuple-element.133.refs_0_, bf16[2,128,512]{2,1,0:T(8,128)(2,1)S(1)} %collective-permute-done.18.refs_1_, ...), custom_call_target="tpu_custom_call" | custom-call | tf_op jit(solution)/shard_map/second_conv_a/pallas_call | solution.py:343
  72.3 0.6 collective-permute-start.26
  72.9 2.6 %second_terms_a.1.refs_16_ = f32[3,384,512]{2,1,0:T(8,128)S(1)} custom-call(bf16[2,128,512]{2,1,0:T(8,128)(2,1)S(1)} %get-tuple-element.133.refs_0_, bf16[2,128,512]{2,1,0:T(8,128)(2,1)S(1)} %collective-permute-done.18.refs_1_, bf16[2,128,512]{2,1,0:T(8,128)(2,1)S(1)} %collective-permute-done.16.refs_2_, ...), custom_call_target="tpu_custom_call" | custom-call | tf_op jit(solution)/shard_map/second_terms_a/pallas_call | solution.py:343
  75.5 0.6 collective-permute-start.34
  76.1 0.1 collective-permute-start.31
  76.2 0.5 collective-permute-start.33
  76.7 0.4 collective-permute-done.34.refs_14_
  77.1 0.4 collective-permute-start.32
  77.5 0.3 collective-permute-done.33.refs_13_
  77.8 0.7 collective-permute-done.32.refs_12_
  78.5 4.2 %second_conv_b.1 = (bf16[1,128,512]{2,1,0:T(8,128)(2,1)}, bf16[4,128,512]{2,1,0:T(8,128)(2,1)S(1)}) custom-call(bf16[2,128,512]{2,1,0:T(8,128)(2,1)S(1)} %get-tuple-element.133.refs_0_, bf16[2,128,512]{2,1,0:T(8,128)(2,1)S(1)} %collective-permute-done.18.refs_1_, bf16[2,128,512]{2,1,0:T(8,128)(2,1)S(1)} %collective-permute-done.16.refs_2_, ...), custom_call_target="tpu_custom_call" | custom-call | tf_op jit(solution)/shard_map/second_conv_b/pallas_call | solution.py:343
  82.7 0.9 collective-permute-start.36
  83.6 1.2 %collective-permute-start.39 = (bf16[4,128,512]{2,1,0:T(8,128)(2,1)S(1)}, bf16[4,128,512]{2,1,0:T(8,128)(2,1)S(1)}, u32[]{:S(2)}, u32[]{:S(2)}) collective-permute-start(bf16[4,128,512]{2,1,0:T(8,128)(2,1)S(1)} %get-tuple-element.158.refs_15_.refs_6_), channel_id=1, source_target_pairs={{0,2},{1,3},{2,0},{3,1},{4,6},{5,7},{6,4},{7,5},{8,10},{9,11},{10,... | collective-permute-start | bytes 1572872 | tf_op jit(solution)/shard_map/over_x/ppermute | solution.py:108
  84.8 0.2 collective-permute-start.37
  85.0 4.0 %second_terms_b.1 = f32[3,384,512]{2,1,0:T(8,128)} custom-call(bf16[2,128,512]{2,1,0:T(8,128)(2,1)S(1)} %get-tuple-element.133.refs_0_, bf16[2,128,512]{2,1,0:T(8,128)(2,1)S(1)} %collective-permute-done.18.refs_1_, bf16[2,128,512]{2,1,0:T(8,128)(2,1)S(1)} %collective-permute-done.16.refs_2_, bf16[2,128,512]{2,1,0:T(8,128)(2,1)S(1)} %collective-permute-done.23.refs_3_, ...), custom_call_target="tpu_custom_call" | custom-call | tf_op jit(solution)/shard_map/second_terms_b/pallas_call | solution.py:343
  89.0 2.3 %collective-permute-done.36.refs_4_ = bf16[2,128,512]{2,1,0:T(8,128)(2,1)S(1)} collective-permute-done((bf16[2,128,512]{2,1,0:T(8,128)(2,1)S(1)}, bf16[2,128,512]{2,1,0:T(8,128)(2,1)S(1)}, u32[]{:S(2)}, u32[]{:S(2)}) %collective-permute-start.36) | collective-permute-done | bytes 262176 | tf_op jit(solution)/shard_map/over_y/ppermute | solution.py:108
  91.3 0.4 turn_weight.1.refs_6_.refs_2_
  91.7 1.1 %collective-permute-done.38.refs_5_ = bf16[2,128,512]{2,1,0:T(8,128)(2,1)S(1)} collective-permute-done((bf16[2,128,512]{2,1,0:T(8,128)(2,1)S(1)}, bf16[2,128,512]{2,1,0:T(8,128)(2,1)S(1)}, u32[]{:S(2)}, u32[]{:S(2)}) %collective-permute-start.38) | collective-permute-done | bytes 262176 | tf_op jit(solution)/shard_map/mate/ppermute | solution.py:108
  92.8 2.0 %hidden_grad_a.1.grad = bf16[3,128,512]{2,1,0:T(8,128)(2,1)S(1)} custom-call(bf16[4,128,512]{2,1,0:T(8,128)(2,1)S(1)} %get-tuple-element.153.refs_9_.refs_0_, bf16[4,128,512]{2,1,0:T(8,128)(2,1)S(1)} %collective-permute-done.27.refs_1_, bf16[2,128,512]{2,1,0:T(8,128)(2,1)S(1)} %collective-permute-done.26.refs_2_, ...), custom_call_target="tpu_custom_call" | custom-call | tf_op jit(solution)/shard_map/hidden_grad_a/pallas_call | solution.py:343
  94.9 1.8 %first_terms_a.1.refs_6_ = f32[3,384,512]{2,1,0:T(8,128)S(1)} custom-call(bf16[512,4096]{1,0:T(8,128)(2,1)S(1)} %get-tuple-element.161.flat.refs_5_, bf16[3,128,512]{2,1,0:T(8,128)(2,1)S(1)} %hidden_grad_a.1.grad), custom_call_target="tpu_custom_call" | custom-call | tf_op jit(solution)/shard_map/first_terms_a/pallas_call | solution.py:343
  96.7 0.2 known_rows.1.refs_7_
  96.9 0.9 collective-permute-done.39.refs_0_
  97.9 1.9 %collective-permute-done.40.refs_1_ = bf16[4,128,512]{2,1,0:T(8,128)(2,1)S(1)} collective-permute-done((bf16[4,128,512]{2,1,0:T(8,128)(2,1)S(1)}, bf16[4,128,512]{2,1,0:T(8,128)(2,1)S(1)}, u32[]{:S(2)}, u32[]{:S(2)}) %collective-permute-start.40) | collective-permute-done | bytes 524320 | tf_op jit(solution)/shard_map/mate/ppermute | solution.py:108
  99.8 7.0 %hidden_grad_b_first_terms_b.1 = (f32[3,384,512]{2,1,0:T(8,128)}, bf16[6,512,512]{2,1,0:T(8,128)(2,1)S(1)}) custom-call(bf16[4,128,512]{2,1,0:T(8,128)(2,1)S(1)} %collective-permute-done.39.refs_0_, bf16[4,128,512]{2,1,0:T(8,128)(2,1)S(1)} %collective-permute-done.40.refs_1_, ...), custom_call_target="tpu_custom_call", output_to_operand_aliasing={{1}: (7, {})} | custom-call | flops 6039797760 | bytes 12713984 | tf_op jit(solution)/shard_map/hidden_grad_b_first_terms_b/pallas_call | solution.py:343
  (56 shorter events, 0.8 us)
Async XLA Ops:
  0.6 1.3 %copy-start = (bf16[128,3,3,512]{3,0,2,1:T(8,128)(2,1)S(1)}, bf16[128,3,3,512]{3,0,2,1:T(8,128)(2,1)}, u32[]{:S(2)}) copy-start(bf16[128,3,3,512]{3,0,2,1:T(8,128)(2,1)} %param.6) | copy-start | bytes 3538948
  2.0 17.5 %collective-permute-start.3 = (bf16[2,9,64,128]{3,2,1,0:T(8,128)(2,1)S(1)}, bf16[2,9,64,128]{3,2,1,0:T(8,128)(2,1)S(1)}, u32[]{:S(2)}, u32[]{:S(2)}) collective-permute-start(bf16[2,9,64,128]{3,2,1,0:T(8,128)(2,1)S(1)} %get-tuple-element.90), channel_id=1, source_target_pairs={{0,2},{1,3},{2,0},{3,1},{4,6},{5,7},{6,4},{7,5},{8,10},{9,11},{10,... | collective-permute-start | bytes 884744 | tf_op jit(solution)/shard_map/over_x/ppermute | solution.py:108
  5.1 6.6 %collective-permute-start.2 = (bf16[1,128,512]{2,1,0:T(8,128)(2,1)}, bf16[1,128,512]{2,1,0:T(8,128)(2,1)S(1)}, u32[]{:S(2)}, u32[]{:S(2)}) collective-permute-start(bf16[1,128,512]{2,1,0:T(8,128)(2,1)} %bitcast.24), channel_id=1, source_target_pairs={{0,8},{4,12},{8,0},{12,4},{16,24},{20,28},{24,16},{28,20},{1,9},{5... | collective-permute-start | bytes 393224 | tf_op jit(solution)/shard_map/along_z/ppermute | solution.py:108
  6.6 12.9 %collective-permute-start.1 = (bf16[1,128,512]{2,1,0:T(8,128)(2,1)}, bf16[1,128,512]{2,1,0:T(8,128)(2,1)S(1)}, u32[]{:S(2)}, u32[]{:S(2)}) collective-permute-start(bf16[1,128,512]{2,1,0:T(8,128)(2,1)} %bitcast.25), channel_id=1, source_target_pairs={{0,16},{4,20},{8,24},{12,28},{16,0},{20,4},{24,8},{28,12},{1,17},{... | collective-permute-start | bytes 393224 | tf_op jit(solution)/shard_map/along_z/ppermute | solution.py:108
  9.2 10.3 %collective-permute-start = (bf16[1,128,512]{2,1,0:T(8,128)(2,1)}, bf16[1,128,512]{2,1,0:T(8,128)(2,1)S(1)}, u32[]{:S(2)}, u32[]{:S(2)}) collective-permute-start(bf16[1,128,512]{2,1,0:T(8,128)(2,1)} %bitcast.26), channel_id=1, source_target_pairs={{0,24},{4,28},{8,16},{12,20},{16,8},{20,12},{24,0},{28,4},{1,25},{... | collective-permute-start | bytes 393224 | tf_op jit(solution)/shard_map/along_z/ppermute | solution.py:108
  9.4 0.9 copy-start.3
  10.4 11.3 %copy-start.5 = (bf16[128,1,512]{2,0,1:T(8,128)(2,1)S(1)}, bf16[128,1,512]{2,0,1:T(8,128)(2,1)}, u32[]{:S(2)}) copy-start(bf16[128,1,512]{2,0,1:T(8,128)(2,1)} %param.7) | copy-start | bytes 393220
  10.4 37.0 %copy-start.2 = (bf16[128,3,3,512]{3,0,2,1:T(8,128)(2,1)S(1)}, bf16[128,3,3,512]{3,0,2,1:T(8,128)(2,1)}, u32[]{:S(2)}) copy-start(bf16[128,3,3,512]{3,0,2,1:T(8,128)(2,1)} %param.5) | copy-start | bytes 3538948
  19.6 15.1 %collective-permute-start.8 = (bf16[4,128,512]{2,1,0:T(8,128)(2,1)S(1)}, bf16[4,128,512]{2,1,0:T(8,128)(2,1)S(1)}, u32[]{:S(2)}, u32[]{:S(2)}) collective-permute-start(bf16[4,128,512]{2,1,0:T(8,128)(2,1)S(1)} %constant_dynamic-update-slice_fusion.refs_0_), channel_id=1, source_target_pairs={{0,4},{4,0},{8,12},{12,8},{16,20},{20,16},{24,28},{28,24},{1,5},{5... | collective-permute-start | bytes 1572872 | tf_op jit(solution)/shard_map/over_y/ppermute | solution.py:108
  21.2 13.5 %collective-permute-start.7 = (bf16[4,128,512]{2,1,0:T(8,128)(2,1)S(1)}, bf16[4,128,512]{2,1,0:T(8,128)(2,1)S(1)}, u32[]{:S(2)}, u32[]{:S(2)}) collective-permute-start(bf16[4,128,512]{2,1,0:T(8,128)(2,1)S(1)} %constant_dynamic-update-slice_fusion.refs_0_), channel_id=1, source_target_pairs={{0,2},{1,3},{2,0},{3,1},{4,6},{5,7},{6,4},{7,5},{8,10},{9,11},{10,... | collective-permute-start | bytes 1572872 | tf_op jit(solution)/shard_map/over_x/ppermute | solution.py:108
  21.7 5.8 %collective-permute-start.6 = (bf16[1,128,512]{2,1,0:T(8,128)(2,1)S(1)}, bf16[1,128,512]{2,1,0:T(8,128)(2,1)S(1)}, u32[]{:S(2)}, u32[]{:S(2)}) collective-permute-start(bf16[1,128,512]{2,1,0:T(8,128)(2,1)S(1)} %bitcast.30), channel_id=1, source_target_pairs={{0,8},{4,12},{8,0},{12,4},{16,24},{20,28},{24,16},{28,20},{1,9},{5... | collective-permute-start | bytes 393224 | tf_op jit(solution)/shard_map/along_z/ppermute | solution.py:108
  23.7 11.0 %collective-permute-start.5 = (bf16[1,128,512]{2,1,0:T(8,128)(2,1)S(1)}, bf16[1,128,512]{2,1,0:T(8,128)(2,1)S(1)}, u32[]{:S(2)}, u32[]{:S(2)}) collective-permute-start(bf16[1,128,512]{2,1,0:T(8,128)(2,1)S(1)} %bitcast.31), channel_id=1, source_target_pairs={{0,16},{4,20},{8,24},{12,28},{16,0},{20,4},{24,8},{28,12},{1,17},{... | collective-permute-start | bytes 393224 | tf_op jit(solution)/shard_map/along_z/ppermute | solution.py:108
  24.7 10.0 %collective-permute-start.4 = (bf16[1,128,512]{2,1,0:T(8,128)(2,1)S(1)}, bf16[1,128,512]{2,1,0:T(8,128)(2,1)S(1)}, u32[]{:S(2)}, u32[]{:S(2)}) collective-permute-start(bf16[1,128,512]{2,1,0:T(8,128)(2,1)S(1)} %bitcast.32), channel_id=1, source_target_pairs={{0,24},{4,28},{8,16},{12,20},{16,8},{20,12},{24,0},{28,4},{1,25},{... | collective-permute-start | bytes 393224 | tf_op jit(solution)/shard_map/along_z/ppermute | solution.py:108
  34.7 10.6 %collective-permute-start.11 = (bf16[4,128,512]{2,1,0:T(8,128)(2,1)S(1)}, bf16[4,128,512]{2,1,0:T(8,128)(2,1)S(1)}, u32[]{:S(2)}, u32[]{:S(2)}) collective-permute-start(bf16[4,128,512]{2,1,0:T(8,128)(2,1)S(1)} %constant_dynamic-update-slice_fusion.refs_0_), channel_id=1, source_target_pairs={{0,1},{1,0},{2,3},{3,2},{4,5},{5,4},{6,7},{7,6},{8,9},{9,8},{10,11... | collective-permute-start | bytes 1572872 | tf_op jit(solution)/shard_map/mate/ppermute | solution.py:108
  34.8 10.6 %collective-permute-start.12 = (bf16[4,128,512]{2,1,0:T(8,128)(2,1)S(1)}, bf16[4,128,512]{2,1,0:T(8,128)(2,1)S(1)}, u32[]{:S(2)}, u32[]{:S(2)}) collective-permute-start(bf16[4,128,512]{2,1,0:T(8,128)(2,1)S(1)} %collective-permute-done.7.refs_2_), channel_id=1, source_target_pairs={{0,1},{1,0},{2,3},{3,2},{4,5},{5,4},{6,7},{7,6},{8,9},{9,8},{10,11... | collective-permute-start | bytes 1572872 | tf_op jit(solution)/shard_map/mate/ppermute | solution.py:108
  35.3 10.1 %collective-permute-start.13 = (bf16[4,128,512]{2,1,0:T(8,128)(2,1)S(1)}, bf16[4,128,512]{2,1,0:T(8,128)(2,1)S(1)}, u32[]{:S(2)}, u32[]{:S(2)}) collective-permute-start(bf16[4,128,512]{2,1,0:T(8,128)(2,1)S(1)} %collective-permute-done.8.refs_4_), channel_id=1, source_target_pairs={{0,1},{1,0},{2,3},{3,2},{4,5},{5,4},{6,7},{7,6},{8,9},{9,8},{10,11... | collective-permute-start | bytes 1572872 | tf_op jit(solution)/shard_map/mate/ppermute | solution.py:108
  35.4 8.7 %collective-permute-start.10 = (bf16[4,64,512]{2,1,0:T(8,128)(2,1)S(1)}, bf16[4,64,512]{2,1,0:T(8,128)(2,1)S(1)}, u32[]{:S(2)}, u32[]{:S(2)}) collective-permute-start(bf16[4,64,512]{2,1,0:T(8,128)(2,1)S(1)} %slice.34), channel_id=1, source_target_pairs={{0,2},{1,3},{2,0},{3,1},{4,6},{5,7},{6,4},{7,5},{8,10},{9,11},{10,... | collective-permute-start | bytes 786440 | tf_op jit(solution)/shard_map/over_x/ppermute | solution.py:108
  37.0 8.4 %collective-permute-start.9 = (bf16[4,64,512]{2,1,0:T(8,128)(2,1)S(1)}, bf16[4,64,512]{2,1,0:T(8,128)(2,1)S(1)}, u32[]{:S(2)}, u32[]{:S(2)}) collective-permute-start(bf16[4,64,512]{2,1,0:T(8,128)(2,1)S(1)} %slice.33), channel_id=1, source_target_pairs={{0,4},{4,0},{8,12},{12,8},{16,20},{20,16},{24,28},{28,24},{1,5},{5... | collective-permute-start | bytes 786440 | tf_op jit(solution)/shard_map/over_y/ppermute | solution.py:108
  45.4 1.6 %collective-permute-start.14 = (bf16[4,64,512]{2,1,0:T(8,128)(2,1)S(1)}, bf16[4,64,512]{2,1,0:T(8,128)(2,1)S(1)}, u32[]{:S(2)}, u32[]{:S(2)}) collective-permute-start(bf16[4,64,512]{2,1,0:T(8,128)(2,1)S(1)} %collective-permute-done.9.refs_6_), channel_id=1, source_target_pairs={{0,1},{1,0},{2,3},{3,2},{4,5},{5,4},{6,7},{7,6},{8,9},{9,8},{10,11... | collective-permute-start | bytes 786440 | tf_op jit(solution)/shard_map/mate/ppermute | solution.py:108
  45.4 1.9 %collective-permute-start.15 = (bf16[4,64,512]{2,1,0:T(8,128)(2,1)S(1)}, bf16[4,64,512]{2,1,0:T(8,128)(2,1)S(1)}, u32[]{:S(2)}, u32[]{:S(2)}) collective-permute-start(bf16[4,64,512]{2,1,0:T(8,128)(2,1)S(1)} %collective-permute-done.10.refs_8_), channel_id=1, source_target_pairs={{0,1},{1,0},{2,3},{3,2},{4,5},{5,4},{6,7},{7,6},{8,9},{9,8},{10,11... | collective-permute-start | bytes 786440 | tf_op jit(solution)/shard_map/mate/ppermute | solution.py:108
  48.9 4.1 %collective-permute-start.18 = (bf16[2,128,512]{2,1,0:T(8,128)(2,1)S(1)}, bf16[2,128,512]{2,1,0:T(8,128)(2,1)S(1)}, u32[]{:S(2)}, u32[]{:S(2)}) collective-permute-start(bf16[2,128,512]{2,1,0:T(8,128)(2,1)S(1)} %get-tuple-element.133.refs_0_), channel_id=1, source_target_pairs={{0,1},{1,0},{2,3},{3,2},{4,5},{5,4},{6,7},{7,6},{8,9},{9,8},{10,11... | collective-permute-start | bytes 786440 | tf_op jit(solution)/shard_map/mate/ppermute | solution.py:108
  49.1 9.1 %collective-permute-start.16 = (bf16[2,128,512]{2,1,0:T(8,128)(2,1)S(1)}, bf16[2,128,512]{2,1,0:T(8,128)(2,1)S(1)}, u32[]{:S(2)}, u32[]{:S(2)}) collective-permute-start(bf16[2,128,512]{2,1,0:T(8,128)(2,1)S(1)} %get-tuple-element.133.refs_0_), channel_id=1, source_target_pairs={{0,2},{1,3},{2,0},{3,1},{4,6},{5,7},{6,4},{7,5},{8,10},{9,11},{10,... | collective-permute-start | bytes 786440 | tf_op jit(solution)/shard_map/over_x/ppermute | solution.py:108
  49.7 13.9 %collective-permute-start.20 = (bf16[4,128,512]{2,1,0:T(8,128)(2,1)S(1)}, bf16[4,128,512]{2,1,0:T(8,128)(2,1)S(1)}, u32[]{:S(2)}, u32[]{:S(2)}) collective-permute-start(bf16[4,128,512]{2,1,0:T(8,128)(2,1)S(1)} %pad_maximum_fusion.refs_10_.refs_16_), channel_id=1, source_target_pairs={{0,4},{4,0},{8,12},{12,8},{16,20},{20,16},{24,28},{28,24},{1,5},{5... | collective-permute-start | bytes 1572872 | tf_op jit(solution)/shard_map/over_y/ppermute | solution.py:108
  50.2 2.7 %collective-permute-start.22 = (bf16[1,9,64,128]{3,2,1,0:T(8,128)(2,1)S(1)}, bf16[1,9,64,128]{3,2,1,0:T(8,128)(2,1)S(1)}, u32[]{:S(2)}, u32[]{:S(2)}) collective-permute-start(bf16[1,9,64,128]{3,2,1,0:T(8,128)(2,1)S(1)} %get-tuple-element.181), channel_id=1, source_target_pairs={{0,1},{1,0},{2,3},{3,2},{4,5},{5,4},{6,7},{7,6},{8,9},{9,8},{10,11... | collective-permute-start | bytes 442376 | tf_op jit(solution)/shard_map/mate/ppermute | solution.py:108
  50.3 10.1 %collective-permute-start.21 = (bf16[9,128,128]{2,1,0:T(8,128)(2,1)S(1)}, bf16[9,128,128]{2,1,0:T(8,128)(2,1)S(1)}, u32[]{:S(2)}, u32[]{:S(2)}) collective-permute-start(bf16[9,128,128]{2,1,0:T(8,128)(2,1)S(1)} %get-tuple-element.130), channel_id=1, source_target_pairs={{0,1},{1,0},{2,3},{3,2},{4,5},{5,4},{6,7},{7,6},{8,9},{9,8},{10,11... | collective-permute-start | bytes 884744 | tf_op jit(solution)/shard_map/mate/ppermute | solution.py:108
  52.9 15.6 %copy-start.1 = (bf16[128,3,3,512]{3,0,2,1:T(8,128)(2,1)S(1)}, bf16[128,3,3,512]{3,0,2,1:T(8,128)(2,1)}, u32[]{:S(2)}) copy-start(bf16[128,3,3,512]{3,0,2,1:T(8,128)(2,1)} %param.6) | copy-start | bytes 3538948
  52.9 15.6 %copy-start.4 = (bf16[128,1,512]{2,0,1:T(8,128)(2,1)S(1)}, bf16[128,1,512]{2,0,1:T(8,128)(2,1)}, u32[]{:S(2)}) copy-start(bf16[128,1,512]{2,0,1:T(8,128)(2,1)} %param.4) | copy-start | bytes 393220
  52.9 10.7 %collective-permute-start.19 = (bf16[3,128,512]{2,1,0:T(8,128)(2,1)S(1)}, bf16[3,128,512]{2,1,0:T(8,128)(2,1)S(1)}, u32[]{:S(2)}, u32[]{:S(2)}) collective-permute-start(bf16[3,128,512]{2,1,0:T(8,128)(2,1)S(1)} %get-tuple-element.137.refs_4_), channel_id=1, source_target_pairs={{0,1},{1,0},{2,3},{3,2},{4,5},{5,4},{6,7},{7,6},{8,9},{9,8},{10,11... | collective-permute-start | bytes 1179656 | tf_op jit(solution)/shard_map/mate/ppermute | solution.py:108
  53.1 13.6 %collective-permute-start.17 = (bf16[3,128,512]{2,1,0:T(8,128)(2,1)S(1)}, bf16[3,128,512]{2,1,0:T(8,128)(2,1)S(1)}, u32[]{:S(2)}, u32[]{:S(2)}) collective-permute-start(bf16[3,128,512]{2,1,0:T(8,128)(2,1)S(1)} %get-tuple-element.137.refs_4_), channel_id=1, source_target_pairs={{0,2},{1,3},{2,0},{3,1},{4,6},{5,7},{6,4},{7,5},{8,10},{9,11},{10,... | collective-permute-start | bytes 1179656 | tf_op jit(solution)/shard_map/over_x/ppermute | solution.py:108
  58.3 8.4 %collective-permute-start.23 = (bf16[2,128,512]{2,1,0:T(8,128)(2,1)S(1)}, bf16[2,128,512]{2,1,0:T(8,128)(2,1)S(1)}, u32[]{:S(2)}, u32[]{:S(2)}) collective-permute-start(bf16[2,128,512]{2,1,0:T(8,128)(2,1)S(1)} %collective-permute-done.16.refs_2_), channel_id=1, source_target_pairs={{0,1},{1,0},{2,3},{3,2},{4,5},{5,4},{6,7},{7,6},{8,9},{9,8},{10,11... | collective-permute-start | bytes 786440 | tf_op jit(solution)/shard_map/mate/ppermute | solution.py:108
  60.4 15.1 %collective-permute-start.29 = (bf16[3,128,512]{2,1,0:T(8,128)(2,1)S(1)}, bf16[3,128,512]{2,1,0:T(8,128)(2,1)S(1)}, u32[]{:S(2)}, u32[]{:S(2)}) collective-permute-start(bf16[3,128,512]{2,1,0:T(8,128)(2,1)S(1)} %get-tuple-element.147.refs_9_), channel_id=1, source_target_pairs={{0,2},{1,3},{2,0},{3,1},{4,6},{5,7},{6,4},{7,5},{8,10},{9,11},{10,... | collective-permute-start | bytes 1179656 | tf_op jit(solution)/shard_map/over_x/ppermute | solution.py:108
  63.6 11.9 %collective-permute-start.28 = (bf16[3,128,512]{2,1,0:T(8,128)(2,1)S(1)}, bf16[3,128,512]{2,1,0:T(8,128)(2,1)S(1)}, u32[]{:S(2)}, u32[]{:S(2)}) collective-permute-start(bf16[3,128,512]{2,1,0:T(8,128)(2,1)S(1)} %get-tuple-element.147.refs_9_), channel_id=1, source_target_pairs={{0,1},{1,0},{2,3},{3,2},{4,5},{5,4},{6,7},{7,6},{8,9},{9,8},{10,11... | collective-permute-start | bytes 1179656 | tf_op jit(solution)/shard_map/mate/ppermute | solution.py:108
  63.6 11.9 %collective-permute-start.30 = (bf16[2,9,64,128]{3,2,1,0:T(8,128)(2,1)S(1)}, bf16[2,9,64,128]{3,2,1,0:T(8,128)(2,1)S(1)}, u32[]{:S(2)}, u32[]{:S(2)}) collective-permute-start(bf16[2,9,64,128]{3,2,1,0:T(8,128)(2,1)S(1)} %collective-permute-done.3), channel_id=1, source_target_pairs={{0,4},{4,0},{8,12},{12,8},{16,20},{20,16},{24,28},{28,24},{1,5},{5... | collective-permute-start | bytes 884744 | tf_op jit(solution)/shard_map/over_y/ppermute | solution.py:108
  66.7 1.8 %collective-permute-start.24 = (bf16[2,128,512]{2,1,0:T(8,128)(2,1)S(1)}, bf16[2,128,512]{2,1,0:T(8,128)(2,1)S(1)}, u32[]{:S(2)}, u32[]{:S(2)}) collective-permute-start(bf16[2,128,512]{2,1,0:T(8,128)(2,1)S(1)} %slice.36), channel_id=1, source_target_pairs={{0,1},{1,0},{2,3},{3,2},{4,5},{5,4},{6,7},{7,6},{8,9},{9,8},{10,11... | collective-permute-start | bytes 786440 | tf_op jit(solution)/shard_map/mate/ppermute | solution.py:108
  66.8 1.7 %collective-permute-start.25 = (bf16[1,128,512]{2,1,0:T(8,128)(2,1)S(1)}, bf16[1,128,512]{2,1,0:T(8,128)(2,1)S(1)}, u32[]{:S(2)}, u32[]{:S(2)}) collective-permute-start(bf16[1,128,512]{2,1,0:T(8,128)(2,1)S(1)} %slice.37), channel_id=1, source_target_pairs={{0,1},{1,0},{2,3},{3,2},{4,5},{5,4},{6,7},{7,6},{8,9},{9,8},{10,11... | collective-permute-start | bytes 393224 | tf_op jit(solution)/shard_map/mate/ppermute | solution.py:108
  72.3 10.4 %collective-permute-start.26 = (bf16[2,128,512]{2,1,0:T(8,128)(2,1)S(1)}, bf16[2,128,512]{2,1,0:T(8,128)(2,1)S(1)}, u32[]{:S(2)}, u32[]{:S(2)}) collective-permute-start(bf16[2,128,512]{2,1,0:T(8,128)(2,1)S(1)} %get-tuple-element.142), channel_id=1, source_target_pairs={{0,2},{1,3},{2,0},{3,1},{4,6},{5,7},{6,4},{7,5},{8,10},{9,11},{10,... | collective-permute-start | bytes 786440 | tf_op jit(solution)/shard_map/over_x/ppermute | solution.py:108
  72.9 9.8 %collective-permute-start.27 = (bf16[4,128,512]{2,1,0:T(8,128)(2,1)S(1)}, bf16[4,128,512]{2,1,0:T(8,128)(2,1)S(1)}, u32[]{:S(2)}, u32[]{:S(2)}) collective-permute-start(bf16[4,128,512]{2,1,0:T(8,128)(2,1)S(1)} %get-tuple-element.153.refs_9_.refs_0_), channel_id=1, source_target_pairs={{0,1},{1,0},{2,3},{3,2},{4,5},{5,4},{6,7},{7,6},{8,9},{9,8},{10,11... | collective-permute-start | bytes 1572872 | tf_op jit(solution)/shard_map/mate/ppermute | solution.py:108
  75.5 1.6 %collective-permute-start.34 = (bf16[1,128,512]{2,1,0:T(8,128)(2,1)S(1)}, bf16[1,128,512]{2,1,0:T(8,128)(2,1)S(1)}, u32[]{:S(2)}, u32[]{:S(2)}) collective-permute-start(bf16[1,128,512]{2,1,0:T(8,128)(2,1)S(1)} %get-tuple-element.175), channel_id=1, source_target_pairs={{0,1},{1,0},{2,3},{3,2},{4,5},{5,4},{6,7},{7,6},{8,9},{9,8},{10,11... | collective-permute-start | bytes 393224 | tf_op jit(solution)/shard_map/mate/ppermute | solution.py:108
  76.1 6.5 %collective-permute-start.31 = (bf16[1,9,64,128]{3,2,1,0:T(8,128)(2,1)S(1)}, bf16[1,9,64,128]{3,2,1,0:T(8,128)(2,1)S(1)}, u32[]{:S(2)}, u32[]{:S(2)}) collective-permute-start(bf16[1,9,64,128]{3,2,1,0:T(8,128)(2,1)S(1)} %get-tuple-element.179), channel_id=1, source_target_pairs={{0,1},{1,0},{2,3},{3,2},{4,5},{5,4},{6,7},{7,6},{8,9},{9,8},{10,11... | collective-permute-start | bytes 442376 | tf_op jit(solution)/shard_map/mate/ppermute | solution.py:108
  76.2 1.5 %collective-permute-start.33 = (bf16[1,128,512]{2,1,0:T(8,128)(2,1)S(1)}, bf16[1,128,512]{2,1,0:T(8,128)(2,1)S(1)}, u32[]{:S(2)}, u32[]{:S(2)}) collective-permute-start(bf16[1,128,512]{2,1,0:T(8,128)(2,1)S(1)} %get-tuple-element.176), channel_id=1, source_target_pairs={{0,1},{1,0},{2,3},{3,2},{4,5},{5,4},{6,7},{7,6},{8,9},{9,8},{10,11... | collective-permute-start | bytes 393224 | tf_op jit(solution)/shard_map/mate/ppermute | solution.py:108
  77.1 1.3 %collective-permute-start.32 = (bf16[1,128,512]{2,1,0:T(8,128)(2,1)S(1)}, bf16[1,128,512]{2,1,0:T(8,128)(2,1)S(1)}, u32[]{:S(2)}, u32[]{:S(2)}) collective-permute-start(bf16[1,128,512]{2,1,0:T(8,128)(2,1)S(1)} %get-tuple-element.177), channel_id=1, source_target_pairs={{0,1},{1,0},{2,3},{3,2},{4,5},{5,4},{6,7},{7,6},{8,9},{9,8},{10,11... | collective-permute-start | bytes 393224 | tf_op jit(solution)/shard_map/mate/ppermute | solution.py:108
  82.7 8.6 %collective-permute-start.36 = (bf16[2,128,512]{2,1,0:T(8,128)(2,1)S(1)}, bf16[2,128,512]{2,1,0:T(8,128)(2,1)S(1)}, u32[]{:S(2)}, u32[]{:S(2)}) collective-permute-start(bf16[2,128,512]{2,1,0:T(8,128)(2,1)S(1)} %collective-permute-done.26.refs_2_), channel_id=1, source_target_pairs={{0,4},{4,0},{8,12},{12,8},{16,20},{20,16},{24,28},{28,24},{1,5},{5... | collective-permute-start | bytes 786440 | tf_op jit(solution)/shard_map/over_y/ppermute | solution.py:108
  83.5 13.2 %collective-permute-start.35 = (bf16[4,128,512]{2,1,0:T(8,128)(2,1)S(1)}, bf16[4,128,512]{2,1,0:T(8,128)(2,1)S(1)}, u32[]{:S(2)}, u32[]{:S(2)}) collective-permute-start(bf16[4,128,512]{2,1,0:T(8,128)(2,1)S(1)} %get-tuple-element.158.refs_15_.refs_6_), channel_id=1, source_target_pairs={{0,1},{1,0},{2,3},{3,2},{4,5},{5,4},{6,7},{7,6},{8,9},{9,8},{10,11... | collective-permute-start | bytes 1572872 | tf_op jit(solution)/shard_map/mate/ppermute | solution.py:108
  83.6 14.3 %collective-permute-start.39 = (bf16[4,128,512]{2,1,0:T(8,128)(2,1)S(1)}, bf16[4,128,512]{2,1,0:T(8,128)(2,1)S(1)}, u32[]{:S(2)}, u32[]{:S(2)}) collective-permute-start(bf16[4,128,512]{2,1,0:T(8,128)(2,1)S(1)} %get-tuple-element.158.refs_15_.refs_6_), channel_id=1, source_target_pairs={{0,2},{1,3},{2,0},{3,1},{4,6},{5,7},{6,4},{7,5},{8,10},{9,11},{10,... | collective-permute-start | bytes 1572872 | tf_op jit(solution)/shard_map/over_x/ppermute | solution.py:108
  84.8 6.9 %collective-permute-start.37 = (bf16[2,128,512]{2,1,0:T(8,128)(2,1)S(1)}, bf16[2,128,512]{2,1,0:T(8,128)(2,1)S(1)}, u32[]{:S(2)}, u32[]{:S(2)}) collective-permute-start(bf16[2,128,512]{2,1,0:T(8,128)(2,1)S(1)} %collective-permute-done.26.refs_2_), channel_id=1, source_target_pairs={{0,1},{1,0},{2,3},{3,2},{4,5},{5,4},{6,7},{7,6},{8,9},{9,8},{10,11... | collective-permute-start | bytes 786440 | tf_op jit(solution)/shard_map/mate/ppermute | solution.py:108
  91.3 1.5 %collective-permute-start.38 = (bf16[2,128,512]{2,1,0:T(8,128)(2,1)S(1)}, bf16[2,128,512]{2,1,0:T(8,128)(2,1)S(1)}, u32[]{:S(2)}, u32[]{:S(2)}) collective-permute-start(bf16[2,128,512]{2,1,0:T(8,128)(2,1)S(1)} %collective-permute-done.36.refs_4_), channel_id=1, source_target_pairs={{0,1},{1,0},{2,3},{3,2},{4,5},{5,4},{6,7},{7,6},{8,9},{9,8},{10,11... | collective-permute-start | bytes 786440 | tf_op jit(solution)/shard_map/mate/ppermute | solution.py:108
  97.8 1.9 %collective-permute-start.40 = (bf16[4,128,512]{2,1,0:T(8,128)(2,1)S(1)}, bf16[4,128,512]{2,1,0:T(8,128)(2,1)S(1)}, u32[]{:S(2)}, u32[]{:S(2)}) collective-permute-start(bf16[4,128,512]{2,1,0:T(8,128)(2,1)S(1)} %collective-permute-done.39.refs_0_), channel_id=1, source_target_pairs={{0,1},{1,0},{2,3},{3,2},{4,5},{5,4},{6,7},{7,6},{8,9},{9,8},{10,11... | collective-permute-start | bytes 1572872 | tf_op jit(solution)/shard_map/mate/ppermute | solution.py:108
